TPU v7x, 256 devices: a whole 4x4x8 slice. The times are simulated.
256 devices in a mesh: replica: 16 (over z_hi, y, core), fsdp: 16 (over z_lo, x).
Axes of the slice: x: 4, y: 4, z: 8 (z_hi: 2, z_lo: 4; z = z_hi * 4 + z_lo), core: 2. Of those that a mesh axis runs over, the one named last changes fastest.
Arguments:
- tokens: bfloat16 [131072, 4096], P(('replica', 'fsdp')), may hold values from -24 to 24
- key_grad: bfloat16 [131072, 1024], P(('replica', 'fsdp')), may hold values from -0.0625 to 0.0625
- key_weight: bfloat16 [16, 4096, 1024], P('replica', 'fsdp'), may hold values from -0.09375 to 0.09375
- adam_first: float32 [16, 4096, 1024], P('replica', 'fsdp'), may hold values from -4 to 4
- adam_second: float32 [16, 4096, 1024], P('replica', 'fsdp'), may hold values from 0.1 to 4
- local_params: bfloat16 [16, 4096, 1024], P('replica', 'fsdp'), may hold values from -4 to 4
- anchor: float32 [4096, 1024], P('fsdp'), may hold values from -4 to 4
- outer_momentum: float32 [4096, 1024], P('fsdp'), may hold values from -3 to 3
Outputs:
- keys: bfloat16 [131072, 1024], P(('replica', 'fsdp'))
- new_weight: bfloat16 [16, 4096, 1024], P('replica', 'fsdp')
- new_first: float32 [16, 4096, 1024], P('replica', 'fsdp')
- new_second: float32 [16, 4096, 1024], P('replica', 'fsdp')
- new_anchor: float32 [4096, 1024], P('fsdp')
- new_momentum: float32 [4096, 1024], P('fsdp')
All inputs are finite; a program needn't handle non-finite values.
Results may differ from a plain program's by a relative error of at most 0.0085.
Values may be sent and summed in bfloat16 or wider, within the bound.
No kernel may reach another device: no remote copies, remote signals or barrier semaphores. Data moves between devices by JAX's collectives and lax.ppermute only.
A program may use at most 128 MiB of HBM per device.

v0:
```python
import jax
import jax.numpy as jnp
from jax import lax
from jax.sharding import PartitionSpec as P

learn_rate = 0.001
weight_decay = 0.1
first_decay = 0.9
second_decay = 0.95
adam_floor = 1e-08
outer_rate = 0.7
outer_decay = 0.9


def outer_update(drift, momentum, anchor):
    new_momentum = outer_decay * momentum + drift
    new_anchor = anchor - outer_rate * (drift + outer_decay * new_momentum)
    return (new_anchor, new_momentum)


def on_device(
    tokens, key_grad, key_weight, adam_first, adam_second, local_params, anchor, outer_momentum
):
    weight = key_weight[0]
    columns = tokens
    keys = jnp.dot(
        columns,
        lax.all_gather(weight, "fsdp", axis=0, tiled=True),
        preferred_element_type=jnp.float32,
    ).astype(jnp.bfloat16)
    columns = tokens
    gradient = lax.psum_scatter(
        lax.dot_general(
            columns, key_grad, (((0,), (0,)), ((), ())), preferred_element_type=jnp.float32
        ).astype(jnp.bfloat16),
        "fsdp",
        scatter_dimension=0,
        tiled=True,
    ).astype(jnp.float32)
    new_first = first_decay * adam_first[0] + (1.0 - first_decay) * gradient
    new_second = second_decay * adam_second[0] + (1.0 - second_decay) * gradient * gradient
    master = weight.astype(jnp.float32)
    update = new_first / (jnp.sqrt(new_second) + adam_floor) + weight_decay * master
    new_weight = (master - learn_rate * update).astype(jnp.bfloat16)
    own_drift = anchor - local_params[0].astype(jnp.float32)
    replicas = lax.axis_size("replica")
    drift = lax.psum(own_drift, "replica") / replicas
    new_anchor, new_momentum = outer_update(drift, outer_momentum, anchor)
    return (keys, new_weight[None], new_first[None], new_second[None], new_anchor, new_momentum)


def solution(mesh):
    placed = (
        P(("replica", "fsdp"), None),
        P(("replica", "fsdp"), None),
        P("replica", "fsdp", None),
        P("replica", "fsdp", None),
        P("replica", "fsdp", None),
        P("replica", "fsdp", None),
        P("fsdp", None),
        P("fsdp", None),
    )
    return jax.shard_map(
        on_device,
        mesh=mesh,
        in_specs=placed,
        out_specs=(
            P(("replica", "fsdp"), None),
            P("replica", "fsdp", None),
            P("replica", "fsdp", None),
            P("replica", "fsdp", None),
            P("fsdp", None),
            P("fsdp", None),
        ),
        check_vma=False,
    )
```

profile of v0, /device:TPU:1, one launch (start us, length us, event | category | flops | bytes accessed | tf_op | source)
XLA Modules:
  0.0 322.5 jit_solution(14422761831779927001)
XLA Ops:
  8.0 0.0 copy-start
  8.0 0.0 all-reduce.2.cloned.1.call-start
  8.1 2.6 convert_subtract_fusion.1
  10.7 0.0 all-reduce.2.cloned.1.call-update
  10.7 0.0 all-gather.3.cloned.1.call-start
  10.7 0.5 all-gather.3.cloned.1.call-update
  11.3 0.0 reduce-scatter.2.cloned.1.call-start
  11.3 0.0 copy-done
  11.3 9.0 %convolution_convert_fusion = bf16[4096,1024]{1,0:T(8,128)(2,1)} fusion(bf16[512,4096]{1,0:T(8,128)(2,1)} %param.8, bf16[512,1024]{1,0:T(8,128)(2,1)S(1)} %copy-done), kind=kOutput, calls=%fused_computation.2 | convolution fusion | flops 4299161600 | bytes 13631488 | tf_op jit(solution)/shard_map/dot_general | solution.py:33
  20.3 0.0 copy-start.1
  20.3 0.0 copy-start.3
  20.3 0.0 reduce-scatter.2.cloned.1.call-update
  20.4 277.9 %all-reduce.2.cloned.1.call-done = f32[256,1024]{1,0:T(8,128)} async-done(((f32[256,1024]{1,0:T(8,128)}), f32[256,1024]{1,0:T(8,128)}) %all-reduce.2.cloned.1.call-update) | async-done | bytes 1048592 | tf_op jit(solution)/shard_map/psum | solution.py:47
  298.3 0.0 copy-done.1
  298.3 0.0 copy-done.3
  298.3 2.9 multiply_subtract_fusion
  301.2 0.0 copy-start.2
  301.2 0.0 copy-start.4
  301.2 0.0 all-gather.3.cloned.1.call-done
  301.2 10.2 %fusion.2 = bf16[512,1024]{1,0:T(8,128)(2,1)} fusion(bf16[512,4096]{1,0:T(8,128)(2,1)} %param.8, bf16[1,4096,1024]{2,1,0:T(8,128)(2,1)} %all-gather.3.cloned.1.call-done), kind=kOutput, calls=%fused_computation.4 | convolution fusion | flops 4295491584 | bytes 13631488 | tf_op jit(solution)/shard_map/dot_general | solution.py:26
  311.4 0.0 reduce-scatter.2.cloned.1.call-done
  311.4 0.0 copy-done.2
  311.4 0.0 copy-done.4
  311.4 3.7 %fusion.11 = (f32[1,256,1024]{2,1,0:T(8,128)}, bf16[1,256,1024]{2,1,0:T(8,128)(2,1)}, f32[1,256,1024]{2,1,0:T(8,128)}) fusion(bf16[256,1024]{1,0:T(8,128)(2,1)} %reduce-scatter.2.cloned.1.call-done, f32[1,256,1024]{2,1,0:T(8,128)S(1)} %copy-done.4, f32[1,256,1024]{2,1,0:T(8,128)} %param.11, bf16[1,256,1024]{2,1,0:T(8,128)(2,1)S(1)} %copy-done.2), kind=kLoop, calls=%fused_computation.17 | loop fusion | flops 4194304 | bytes 5767168 | tf_op jit(solution)/shard_map/broadcast_in_dim | solution.py:49
Async XLA Ops:
  8.0 3.3 %copy-start = (bf16[512,1024]{1,0:T(8,128)(2,1)S(1)}, bf16[512,1024]{1,0:T(8,128)(2,1)}, u32[]{:S(2)}) copy-start(bf16[512,1024]{1,0:T(8,128)(2,1)} %param.9) | copy-start | bytes 3145732
  8.0 290.2 %all-reduce.2.cloned.1.call-start = ((), (), s32[]{:S(2)}) async-start(), calls=%async_computation.2 | async-start | bytes 2097152 | tf_op jit(solution)/shard_map/psum | solution.py:47
  10.7 290.5 %all-gather.3.cloned.1.call-start = ((), (), s32[]{:S(2)}) async-start(), calls=%async_computation.3 | async-start | bytes 8912896 | tf_op jit(solution)/shard_map/all_gather | solution.py:28
  11.3 300.1 %reduce-scatter.2.cloned.1.call-start = ((), (), s32[]{:S(2)}) async-start(), calls=%async_computation.1 | async-start | bytes 8912896 | tf_op jit(solution)/shard_map/reduce_scatter | solution.py:32
  20.3 277.9 %copy-start.1 = (f32[256,1024]{1,0:T(8,128)S(1)}, f32[256,1024]{1,0:T(8,128)}, u32[]{:S(2)}) copy-start(f32[256,1024]{1,0:T(8,128)} %param.14) | copy-start | bytes 3145732
  20.3 277.9 %copy-start.3 = (f32[256,1024]{1,0:T(8,128)S(1)}, f32[256,1024]{1,0:T(8,128)}, u32[]{:S(2)}) copy-start(f32[256,1024]{1,0:T(8,128)} %param.15) | copy-start | bytes 3145732
  301.2 10.2 %copy-start.2 = (bf16[1,256,1024]{2,1,0:T(8,128)(2,1)S(1)}, bf16[1,256,1024]{2,1,0:T(8,128)(2,1)}, u32[]{:S(2)}) copy-start(bf16[1,256,1024]{2,1,0:T(8,128)(2,1)} %param.10) | copy-start | bytes 1572868
  301.2 10.2 %copy-start.4 = (f32[1,256,1024]{2,1,0:T(8,128)S(1)}, f32[1,256,1024]{2,1,0:T(8,128)}, u32[]{:S(2)}) copy-start(f32[1,256,1024]{2,1,0:T(8,128)} %param.12) | copy-start | bytes 3145732
Sparse Core Ops, SparseCore 0:
  12.1 286.1 all-reduce.1
Sparse Core Ops, SparseCore 1:
  12.9 107.2 all-gather.2
  122.6 105.3 reduce-scatter.1
where the time goes:
time: 324 us; the launch traced here: 323 us
  waiting for transfers between devices  278 us (86%)
  matrix products  19.2 us (6%)
  between operations  15.5 us (5%)
  other arithmetic  9.17 us (3%)
    psum x1, waiting for transfers between devices, on_device(): drift = lax.psum(own_drift, 'replica') / replicas  278 us
    dot_general x1, matrix products, on_device(): jnp.dot(columns, lax.all_gather(weight, 'fsdp', axis=0, tiled=True), pref...  10.2 us
    dot_general x1, matrix products, on_device(): lax.dot_general(columns, key_grad, (((0,), (0,)), ((), ())), preferred_el...  9.01 us
  transfers between devices with their start and end apart: 3, of which 1 were waited for; matrix products, arithmetic and copies ran while one was open for 7% of the time, Pallas kernels for 0%

commit v1 on v0

v1 whole, which is shorter than its diff:
```python
import jax
import jax.numpy as jnp
from jax import lax
from jax.sharding import Mesh, PartitionSpec as P

learn_rate = 0.001
weight_decay = 0.1
first_decay = 0.9
second_decay = 0.95
adam_floor = 1e-08
outer_rate = 0.7
outer_decay = 0.9

bf16, f32 = jnp.bfloat16, jnp.float32
ALPHA = 128

HOME = (0, 1, 1, 0)
SWAP = [(c * 4 + x, (1 - c) * 4 + (x ^ 1)) for c in range(2) for x in range(4) if c != HOME[x]]
CORE = [(0, 1), (1, 0)]
ACROSS = [(x, 3 - x) for x in range(4)]
ENDS_IN = [(0, 1), (3, 2)]
ENDS_OUT = [(1, 0), (2, 3)]
PAIRS = ENDS_IN + ENDS_OUT
MIDDLE = [(1, 2), (2, 1)]
ORDER = ((3, 2, 1, 0), (3, 2, 0, 1), (0, 1, 3, 2), (0, 1, 2, 3))


def swap(v):
    return lax.ppermute(v, ("c", "x"), SWAP)


def core(v):
    return lax.ppermute(v, "c", CORE)


def across(v):
    return lax.ppermute(v, "x", ACROSS)


def line(v, pairs):
    return lax.ppermute(v, "zl", pairs)


def line_gather(own):
    beside = line(own, PAIRS)
    mid = line(own, MIDDLE)
    far = line(beside, MIDDLE)
    return [far + line(far, ENDS_OUT), mid + line(mid, ENDS_OUT), beside, own]


def dot(a, b):
    return jnp.dot(a, b, preferred_element_type=f32)


def dot_t(a, b):
    return lax.dot_general(a, b, (((0,), (0,)), ((), ())), preferred_element_type=f32)


def drift_sum(own, c, y, zh):
    def halve(v, axis, perm, bit, kind=f32):
        n = v.shape[0] // 2
        keep = lax.dynamic_slice_in_dim(v, bit * n, n, 0)
        send = lax.dynamic_slice_in_dim(v, (1 - bit) * n, n, 0).astype(kind)
        return keep + lax.ppermute(send, axis, perm).astype(f32)

    def double(v, axis, perm, bit):
        other = lax.ppermute(v, axis, perm)
        return jnp.where(bit == 0, jnp.concatenate([v, other]), jnp.concatenate([other, v]))

    near = [(i, i ^ 1) for i in range(4)]
    wide = [(i, i ^ 2) for i in range(4)]
    steps = (("c", CORE, c), ("y", near, y % 2), ("y", wide, y // 2))
    v = own
    for axis, perm, bit in steps:
        v = halve(v, axis, perm, bit)
    v = double(halve(v, "zh", CORE, zh, bf16), "zh", CORE, zh)
    for axis, perm, bit in steps[::-1]:
        v = double(v, axis, perm, bit)
    return v


def on_device(
    tokens, key_grad, key_weight, adam_first, adam_second, local_params, anchor, outer_momentum
):
    c, x, z, y, zh = (lax.axis_index(a) for a in ("c", "x", "zl", "y", "zh"))
    weight = key_weight[0]
    stays = c == jnp.where((x == 1) | (x == 2), 1, 0)
    mine = jnp.where(x < 2, c, 3 - c)
    theirs = jnp.where(x < 2, 1 - c, 2 + c)
    order = jnp.asarray(ORDER, jnp.int32)[z]

    def settle(v, arrived=None):
        return jnp.where(stays, v, swap(v) if arrived is None else arrived)

    w = settle(weight)
    g_own = settle(key_grad)
    blocks = [
        settle(lax.dynamic_slice_in_dim(tokens, order[k] * 1024, 1024, 1)) for k in range(4)
    ]
    g_other = core(g_own)

    def pick(v, quarter):
        return jnp.concatenate(
            [
                lax.dynamic_slice_in_dim(v, q * 256, 256, 1) for q in (quarter, 3 - quarter)
            ],
            axis=1,
        )

    x_own = [pick(b, mine) for b in blocks]
    x_other = [core(pick(b, theirs)) for b in blocks]

    first = line_gather(w[:ALPHA])
    low = [across(jnp.concatenate(first[2:])), across(jnp.concatenate(first[:2]))]
    low_far = [low[1][:ALPHA], low[1][ALPHA:], low[0][:ALPHA], low[0][ALPHA:]]
    rest = w[ALPHA:]
    second = line_gather(jnp.concatenate([rest, across(rest)]))
    n = 256 - ALPHA
    rows = [
        jnp.concatenate([first[k], second[k][:n], low_far[k], second[k][n:]]) for k in range(4)
    ]
    halves = [sum(dot(xs[k], rows[k]) for k in (3, 2, 1, 0)) for xs in (x_own, x_other)]
    keys_work = (halves[0] + core(halves[1].astype(bf16)).astype(f32)).astype(bf16)
    keys = settle(keys_work)

    part = []
    for k in range(4):
        whole = dot_t(x_own[k], g_own) + dot_t(x_other[k], g_other)
        part.append(whole[:256] + across(whole[256:].astype(bf16)).astype(f32))
    send = lambda v, pairs: line(v.astype(bf16), pairs).astype(f32)
    r0 = send(part[0], ENDS_IN)
    r1 = send(part[1], ENDS_IN)
    r2 = send(part[2], ENDS_IN)
    m0 = send(part[0] + r0, MIDDLE)
    m1 = send(part[1] + r1, MIDDLE)
    e0 = send(part[2] + m0, ENDS_OUT)
    total = part[3] + r2 + m1 + e0
    gradient = jnp.where(stays, total, swap(total.astype(bf16)).astype(f32))

    new_first = first_decay * adam_first[0] + (1.0 - first_decay) * gradient
    new_second = second_decay * adam_second[0] + (1.0 - second_decay) * gradient * gradient
    master = weight.astype(f32)
    update = new_first / (jnp.sqrt(new_second) + adam_floor) + weight_decay * master
    new_weight = (master - learn_rate * update).astype(bf16)

    drift = drift_sum(anchor - local_params[0].astype(f32), c, y, zh) / 16
    new_momentum = outer_decay * outer_momentum + drift
    new_anchor = anchor - outer_rate * (drift + outer_decay * new_momentum)
    return (keys, new_weight[None], new_first[None], new_second[None], new_anchor, new_momentum)


def solution(mesh):
    fine = Mesh(mesh.devices.reshape(2, 4, 2, 4, 4), ("zh", "y", "c", "zl", "x"))
    replica, fsdp = ("zh", "y", "c"), ("zl", "x")
    tokens, stacked, shared = P(replica + fsdp, None), P(replica, fsdp, None), P(fsdp, None)
    return jax.shard_map(
        on_device,
        mesh=fine,
        in_specs=(tokens, tokens, stacked, stacked, stacked, stacked, shared, shared),
        out_specs=(tokens, stacked, stacked, stacked, shared, shared),
        check_vma=False,
    )
```

time: 324 us -> 219 us (0.68)
  waiting for transfers between devices: 278 us -> 70.9 us
  starting transfers between devices: 0.12 us -> 95.8 us
  other arithmetic: 9.17 us -> 25.1 us
  between operations: 15.5 us -> 4.13 us
  local copies, waits for them, and re-layouts: 0.02 us -> 8.52 us
  matrix products: 19.2 us -> 11.8 us
    psum x1 -> x0, waiting for transfers between devices: 278 us -> none  [on_device(): drift = lax.psum(own_drift, 'replica') / replicas]
    ppermute x0 -> x45, starting transfers between devices: none -> 95.8 us  [the longest x16 27.7 us: line(): return lax.ppermute(v, 'zl', pairs)]
    ppermute x0 -> x45, waiting for transfers between devices: none -> 70.9 us  [the longest x16 35.3 us: line(): return lax.ppermute(v, 'zl', pairs)]
    select_n x0 -> x10, other arithmetic: none -> 9.8 us  [the longest x7 7.85 us: settle(): return jnp.where(stays, v, swap(v) if arrived is None else arrived)]
    dot_general x2 -> x16, matrix products: 19.2 us -> 11.8 us  [the longest x8 5.92 us: dot(): return jnp.dot(a, b, preferred_element_type=f32)]
    dynamic_slice x0 -> x9, local copies, waits for them, and re-layouts: none -> 5.89 us  [the longest x1 3.6 us: on_device(): lax.dynamic_slice_in_dim(tokens, order[k] * 1024, 1024, 1)]
    convert_element_type x0 -> x6, other arithmetic: none -> 4.93 us  [the longest x5 2.83 us: on_device(): send = lambda v, pairs: line(v.astype(bf16), pairs).astype(f32)]
  transfers between devices with their start and end apart: 3 -> 45, of which waited for: 1 -> 15; matrix products, arithmetic and copies ran while one was open for 7% -> 18% of each run, Pallas kernels for 0% -> 0%
where the time goes in v1:
time: 219 us; the launch traced here: 216 us
  starting transfers between devices  95.8 us (44%)
  waiting for transfers between devices  70.9 us (32%)
  other arithmetic  25.1 us (11%)
  matrix products  11.8 us (5%)
  local copies, waits for them, and re-layouts  8.52 us (4%)
  between operations  4.13 us (2%)
    ppermute x16, waiting for transfers between devices, line(): return lax.ppermute(v, 'zl', pairs)  35.3 us
    ppermute x16, starting transfers between devices, line(): return lax.ppermute(v, 'zl', pairs)  27.7 us
    ppermute x8, starting transfers between devices, swap(): return lax.ppermute(v, ('c', 'x'), SWAP)  25.7 us
    ppermute x7, waiting for transfers between devices, across(): return lax.ppermute(v, 'x', ACROSS)  21.1 us
    ppermute x7, starting transfers between devices, across(): return lax.ppermute(v, 'x', ACROSS)  11.9 us
    ppermute x4, starting transfers between devices, double(): other = lax.ppermute(v, axis, perm)  11.3 us
    ppermute x4, starting transfers between devices, halve(): return keep + lax.ppermute(send, axis, perm).astype(f32)  11.3 us
    ppermute x4, waiting for transfers between devices, halve(): return keep + lax.ppermute(send, axis, perm).astype(f32)  8.37 us
  transfers between devices with their start and end apart: 45, of which 15 were waited for; matrix products, arithmetic and copies ran while one was open for 18% of the time, Pallas kernels for 0%

profile of v1, /device:TPU:1, one launch (start us, length us, event | category | flops | bytes accessed | tf_op | source)
XLA Modules:
  0.0 216.1 jit_solution(5035236668531435800)
XLA Ops:
  3.1 3.2 %collective-permute-start.37 = (f32[128,1024]{1,0:T(8,128)}, f32[128,1024]{1,0:T(8,128)}, u32[]{:S(2)}, u32[]{:S(2)}) collective-permute-start(f32[128,1024]{1,0:T(8,128)} %constant_dynamic-slice_fusion.2), channel_id=1, source_target_pairs={{0,16},{16,0},{1,17},{17,1},{2,18},{18,2},{3,19},{19,3},{4,20},{20... | collective-permute-start | bytes 1572872 | tf_op jit(solution)/shard_map/ppermute | solution.py:64
  12.2 3.6 %constant_dynamic-slice_fusion.13 = (bf16[512,1024]{1,0:T(8,128)(2,1)S(1)}, bf16[512,1024]{1,0:T(8,128)(2,1)S(1)}, bf16[512,1024]{1,0:T(8,128)(2,1)S(1)}, bf16[512,1024]{1,0:T(8,128)(2,1)}) fusion(bf16[512,4096]{1,0:T(8,128)(2,1)} %param.9, s32[]{:T(128)S(6)} %select_n.170, s32[]{:T(128)S(6)} %select_n.166, s32[]{:T(128)S(6)} %select_n.159, s32[]{:T(128)S(6)} %select_n.168), kind=kLoop, calls=%fused_computation.89 | loop fusion | bytes 8388624 | tf_op jit(solution)/shard_map/dynamic_slice | solution.py:98
  15.8 3.6 %collective-permute-start.7 = (bf16[512,1024]{1,0:T(8,128)(2,1)}, bf16[512,1024]{1,0:T(8,128)(2,1)}, u32[]{:S(2)}, u32[]{:S(2)}) collective-permute-start(bf16[512,1024]{1,0:T(8,128)(2,1)} %get-tuple-element.13), channel_id=1, source_target_pairs={{1,16},{2,19},{16,1},{19,2},{5,20},{6,23},{20,5},{23,6},{9,24},{10... | collective-permute-start | bytes 3145736 | tf_op jit(solution)/shard_map/ppermute | solution.py:29
  21.4 3.6 %collective-permute-start.5 = (bf16[512,1024]{1,0:T(8,128)(2,1)S(1)}, bf16[512,1024]{1,0:T(8,128)(2,1)}, u32[]{:S(2)}, u32[]{:S(2)}) collective-permute-start(bf16[512,1024]{1,0:T(8,128)(2,1)S(1)} %get-tuple-element.11), channel_id=1, source_target_pairs={{1,16},{2,19},{16,1},{19,2},{5,20},{6,23},{20,5},{23,6},{9,24},{10... | collective-permute-start | bytes 3145736 | tf_op jit(solution)/shard_map/ppermute | solution.py:29
  27.8 4.4 %collective-permute-done.38 = f32[64,1024]{1,0:T(8,128)S(1)} collective-permute-done((f32[64,1024]{1,0:T(8,128)S(1)}, f32[64,1024]{1,0:T(8,128)S(1)}, u32[]{:S(2)}, u32[]{:S(2)}) %collective-permute-start.38) | collective-permute-done | bytes 262176 | tf_op jit(solution)/shard_map/ppermute | solution.py:64
  33.1 3.2 %collective-permute-start.4 = (bf16[128,1024]{1,0:T(8,128)(2,1)S(1)}, bf16[128,1024]{1,0:T(8,128)(2,1)S(1)}, u32[]{:S(2)}, u32[]{:S(2)}) collective-permute-start(bf16[128,1024]{1,0:T(8,128)(2,1)S(1)} %get-tuple-element.46), channel_id=1, source_target_pairs={{0,3},{1,2},{2,1},{3,0},{4,7},{5,6},{6,5},{7,4},{8,11},{9,10},{10,... | collective-permute-start | bytes 786440 | tf_op jit(solution)/shard_map/ppermute | solution.py:37
  40.0 7.1 %collective-permute-start.40 = (bf16[16,1024]{1,0:T(8,128)(2,1)S(1)}, bf16[16,1024]{1,0:T(8,128)(2,1)S(1)}, u32[]{:S(2)}, u32[]{:S(2)}) collective-permute-start(bf16[16,1024]{1,0:T(8,128)(2,1)S(1)} %dynamic-slice_convert_fusion), channel_id=1, source_target_pairs={{0,128},{128,0},{1,129},{129,1},{2,130},{130,2},{3,131},{131,3},{4... | collective-permute-start | bytes 98312 | tf_op jit(solution)/shard_map/ppermute | solution.py:64
  47.1 2.6 %collective-permute-done.40 = bf16[16,1024]{1,0:T(8,128)(2,1)S(1)} collective-permute-done((bf16[16,1024]{1,0:T(8,128)(2,1)S(1)}, bf16[16,1024]{1,0:T(8,128)(2,1)S(1)}, u32[]{:S(2)}, u32[]{:S(2)}) %collective-permute-start.40) | collective-permute-done | bytes 32800 | tf_op jit(solution)/shard_map/ppermute | solution.py:64
  49.8 5.1 %collective-permute-start.15 = (bf16[512,1024]{1,0:T(8,128)(2,1)S(1)}, bf16[512,1024]{1,0:T(8,128)(2,1)S(1)}, u32[]{:S(2)}, u32[]{:S(2)}) collective-permute-start(bf16[512,1024]{1,0:T(8,128)(2,1)S(1)} %get-tuple-element.10), channel_id=1, source_target_pairs={{1,16},{2,19},{16,1},{19,2},{5,20},{6,23},{20,5},{23,6},{9,24},{10... | collective-permute-start | bytes 3145736 | tf_op jit(solution)/shard_map/ppermute | solution.py:29
  54.9 5.7 %collective-permute-start.41 = (f32[16,1024]{1,0:T(8,128)S(1)}, f32[16,1024]{1,0:T(8,128)S(1)}, u32[]{:S(2)}, u32[]{:S(2)}) collective-permute-start(f32[16,1024]{1,0:T(8,128)S(1)} %convert_add_fusion), channel_id=1, source_target_pairs={{0,128},{128,0},{1,129},{129,1},{2,130},{130,2},{3,131},{131,3},{4... | collective-permute-start | bytes 196616 | tf_op jit(solution)/shard_map/ppermute | solution.py:67
  62.2 2.9 %collective-permute-start.24 = (bf16[512,1024]{1,0:T(8,128)(2,1)S(1)}, bf16[512,1024]{1,0:T(8,128)(2,1)S(1)}, u32[]{:S(2)}, u32[]{:S(2)}) collective-permute-start(bf16[512,1024]{1,0:T(8,128)(2,1)S(1)} %copy-done.2), channel_id=1, source_target_pairs={{1,16},{2,19},{16,1},{19,2},{5,20},{6,23},{20,5},{23,6},{9,24},{10... | collective-permute-start | bytes 3145736 | tf_op jit(solution)/shard_map/ppermute | solution.py:29
  75.1 3.9 %collective-permute-start.42 = (f32[32,1024]{1,0:T(8,128)S(1)}, f32[32,1024]{1,0:T(8,128)S(1)}, u32[]{:S(2)}, u32[]{:S(2)}) collective-permute-start(f32[32,1024]{1,0:T(8,128)S(1)} %maximum_select_fusion.3), channel_id=1, source_target_pairs={{0,64},{32,96},{64,0},{96,32},{1,65},{33,97},{65,1},{97,33},{2,66}... | collective-permute-start | bytes 393224 | tf_op jit(solution)/shard_map/ppermute | solution.py:67
  80.8 5.6 %collective-permute-done.9 = bf16[128,1024]{1,0:T(8,128)(2,1)S(1)} collective-permute-done((bf16[128,1024]{1,0:T(8,128)(2,1)S(1)}, bf16[128,1024]{1,0:T(8,128)(2,1)S(1)}, u32[]{:S(2)}, u32[]{:S(2)}) %collective-permute-start.9) | collective-permute-done | bytes 262176 | tf_op jit(solution)/shard_map/ppermute | solution.py:41
  86.4 5.3 %collective-permute-start.6 = (bf16[256,1024]{1,0:T(8,128)(2,1)S(1)}, bf16[256,1024]{1,0:T(8,128)(2,1)S(1)}, u32[]{:S(2)}, u32[]{:S(2)}) collective-permute-start(bf16[256,1024]{1,0:T(8,128)(2,1)S(1)} %pad_maximum_fusion.7), channel_id=1, source_target_pairs={{0,4},{12,8},{4,0},{8,12},{1,5},{13,9},{5,1},{9,13},{2,6},{14,10},... | collective-permute-start | bytes 1572872 | tf_op jit(solution)/shard_map/ppermute | solution.py:41
  91.9 6.0 %collective-permute-done.13 = bf16[128,1024]{1,0:T(8,128)(2,1)S(1)} collective-permute-done((bf16[128,1024]{1,0:T(8,128)(2,1)S(1)}, bf16[128,1024]{1,0:T(8,128)(2,1)S(1)}, u32[]{:S(2)}, u32[]{:S(2)}) %collective-permute-start.13) | collective-permute-done | bytes 262176 | tf_op jit(solution)/shard_map/ppermute | solution.py:41
  99.3 3.9 %collective-permute-done.6 = bf16[256,1024]{1,0:T(8,128)(2,1)S(1)} collective-permute-done((bf16[256,1024]{1,0:T(8,128)(2,1)S(1)}, bf16[256,1024]{1,0:T(8,128)(2,1)S(1)}, u32[]{:S(2)}, u32[]{:S(2)}) %collective-permute-start.6) | collective-permute-done | bytes 524320 | tf_op jit(solution)/shard_map/ppermute | solution.py:41
  104.1 3.9 %collective-permute-start.14 = (bf16[256,1024]{1,0:T(8,128)(2,1)S(1)}, bf16[256,1024]{1,0:T(8,128)(2,1)S(1)}, u32[]{:S(2)}, u32[]{:S(2)}) collective-permute-start(bf16[256,1024]{1,0:T(8,128)(2,1)S(1)} %pad_maximum_fusion.9), channel_id=1, source_target_pairs={{0,3},{1,2},{2,1},{3,0},{4,7},{5,6},{6,5},{7,4},{8,11},{9,10},{10,... | collective-permute-start | bytes 1572872 | tf_op jit(solution)/shard_map/ppermute | solution.py:37
  111.4 11.1 %collective-permute-done.11 = bf16[256,1024]{1,0:T(8,128)(2,1)S(1)} collective-permute-done((bf16[256,1024]{1,0:T(8,128)(2,1)S(1)}, bf16[256,1024]{1,0:T(8,128)(2,1)S(1)}, u32[]{:S(2)}, u32[]{:S(2)}) %collective-permute-start.11) | collective-permute-done | bytes 524320 | tf_op jit(solution)/shard_map/ppermute | solution.py:41
  130.6 2.7 %collective-permute-start.32 = (bf16[256,1024]{1,0:T(8,128)(2,1)S(1)}, bf16[256,1024]{1,0:T(8,128)(2,1)S(1)}, u32[]{:S(2)}, u32[]{:S(2)}) collective-permute-start(bf16[256,1024]{1,0:T(8,128)(2,1)S(1)} %slice.151), channel_id=1, source_target_pairs={{0,3},{1,2},{2,1},{3,0},{4,7},{5,6},{6,5},{7,4},{8,11},{9,10},{10,... | collective-permute-start | bytes 1572872 | tf_op jit(solution)/shard_map/ppermute | solution.py:37
  135.7 2.8 %collective-permute-done.17 = bf16[256,1024]{1,0:T(8,128)(2,1)S(1)} collective-permute-done((bf16[256,1024]{1,0:T(8,128)(2,1)S(1)}, bf16[256,1024]{1,0:T(8,128)(2,1)S(1)}, u32[]{:S(2)}, u32[]{:S(2)}) %collective-permute-start.17) | collective-permute-done | bytes 524320 | tf_op jit(solution)/shard_map/ppermute | solution.py:41
  138.7 16.3 %collective-permute-done.32 = bf16[256,1024]{1,0:T(8,128)(2,1)S(1)} collective-permute-done((bf16[256,1024]{1,0:T(8,128)(2,1)S(1)}, bf16[256,1024]{1,0:T(8,128)(2,1)S(1)}, u32[]{:S(2)}, u32[]{:S(2)}) %collective-permute-start.32) | collective-permute-done | bytes 524320 | tf_op jit(solution)/shard_map/ppermute | solution.py:37
  158.1 5.4 %collective-permute-start.22 = (bf16[512,1024]{1,0:T(8,128)(2,1)S(1)}, bf16[512,1024]{1,0:T(8,128)(2,1)S(1)}, u32[]{:S(2)}, u32[]{:S(2)}) collective-permute-start(bf16[512,1024]{1,0:T(8,128)(2,1)S(1)} %add_convert_fusion.1), channel_id=1, source_target_pairs={{0,16},{16,0},{1,17},{17,1},{2,18},{18,2},{3,19},{19,3},{4,20},{20... | collective-permute-start | bytes 3145736 | tf_op jit(solution)/shard_map/ppermute | solution.py:33
  163.5 2.7 %collective-permute-done.29 = bf16[256,1024]{1,0:T(8,128)(2,1)S(1)} collective-permute-done((bf16[256,1024]{1,0:T(8,128)(2,1)S(1)}, bf16[256,1024]{1,0:T(8,128)(2,1)S(1)}, u32[]{:S(2)}, u32[]{:S(2)}) %collective-permute-start.29) | collective-permute-done | bytes 524320 | tf_op jit(solution)/shard_map/ppermute | solution.py:37
  166.4 2.2 %collective-permute-start.30 = (bf16[256,1024]{1,0:T(8,128)(2,1)S(1)}, bf16[256,1024]{1,0:T(8,128)(2,1)S(1)}, u32[]{:S(2)}, u32[]{:S(2)}) collective-permute-start(bf16[256,1024]{1,0:T(8,128)(2,1)S(1)} %fusion.9), channel_id=1, source_target_pairs={{0,4},{12,8},{1,5},{13,9},{2,6},{14,10},{3,7},{15,11},{16,20},{28,... | collective-permute-start | bytes 1572872 | tf_op jit(solution)/shard_map/ppermute | solution.py:41
  171.2 6.0 %collective-permute-done.30 = bf16[256,1024]{1,0:T(8,128)(2,1)S(1)} collective-permute-done((bf16[256,1024]{1,0:T(8,128)(2,1)S(1)}, bf16[256,1024]{1,0:T(8,128)(2,1)S(1)}, u32[]{:S(2)}, u32[]{:S(2)}) %collective-permute-start.30) | collective-permute-done | bytes 524320 | tf_op jit(solution)/shard_map/ppermute | solution.py:41
  182.3 6.4 %collective-permute-start.28 = (bf16[256,1024]{1,0:T(8,128)(2,1)}, bf16[256,1024]{1,0:T(8,128)(2,1)}, u32[]{:S(2)}, u32[]{:S(2)}) collective-permute-start(bf16[256,1024]{1,0:T(8,128)(2,1)} %get-tuple-element.17), channel_id=1, source_target_pairs={{0,4},{12,8},{1,5},{13,9},{2,6},{14,10},{3,7},{15,11},{16,20},{28,... | collective-permute-start | bytes 1572872 | tf_op jit(solution)/shard_map/ppermute | solution.py:41
  190.3 4.4 %collective-permute-start.23 = (bf16[512,1024]{1,0:T(8,128)(2,1)S(1)}, bf16[512,1024]{1,0:T(8,128)(2,1)}, u32[]{:S(2)}, u32[]{:S(2)}) collective-permute-start(bf16[512,1024]{1,0:T(8,128)(2,1)S(1)} %add_convert_fusion), channel_id=1, source_target_pairs={{1,16},{2,19},{16,1},{19,2},{5,20},{6,23},{20,5},{23,6},{9,24},{10... | collective-permute-start | bytes 3145736 | tf_op jit(solution)/shard_map/ppermute | solution.py:29
  200.3 2.3 %collective-permute-start.36 = (bf16[256,1024]{1,0:T(8,128)(2,1)S(1)}, bf16[256,1024]{1,0:T(8,128)(2,1)S(1)}, u32[]{:S(2)}, u32[]{:S(2)}) collective-permute-start(bf16[256,1024]{1,0:T(8,128)(2,1)S(1)} %get-tuple-element.8), channel_id=1, source_target_pairs={{1,16},{2,19},{16,1},{19,2},{5,20},{6,23},{20,5},{23,6},{9,24},{10... | collective-permute-start | bytes 1572872 | tf_op jit(solution)/shard_map/ppermute | solution.py:29
  202.6 3.4 %multiply_subtract_fusion = (f32[256,1024]{1,0:T(8,128)}, f32[256,1024]{1,0:T(8,128)}) fusion(f32[256,1024]{1,0:T(8,128)S(1)} %copy-done.1, f32[128,1024]{1,0:T(8,128)} %maximum_select_fusion.1, f32[128,1024]{1,0:T(8,128)} %collective-permute-done.44, pred[]{:T(512)S(6)} %eq.26, f32[256,1024]{1,0:T(8,128)S(1)} %copy-done.3), kind=kLoop, calls=%fused_computation.32 | loop fusion | flops 2621440 | bytes 5242881 | tf_op jit(solution)/shard_map/sub | solution.py:148
  207.2 2.3 %broadcast_select_fusion.1 = bf16[512,1024]{1,0:T(8,128)(2,1)} fusion(bf16[512,1024]{1,0:T(8,128)(2,1)S(1)} %add_convert_fusion, bf16[512,1024]{1,0:T(8,128)(2,1)} %collective-permute-done.23, pred[]{:T(512)S(6)} %eq.25), kind=kLoop, calls=%fused_computation.39 | loop fusion | flops 524288 | bytes 3145729 | tf_op jit(solution)/shard_map/jit(_where)/select_n | solution.py:93
  209.5 3.2 %collective-permute-done.36 = bf16[256,1024]{1,0:T(8,128)(2,1)S(1)} collective-permute-done((bf16[256,1024]{1,0:T(8,128)(2,1)S(1)}, bf16[256,1024]{1,0:T(8,128)(2,1)S(1)}, u32[]{:S(2)}, u32[]{:S(2)}) %collective-permute-start.36) | collective-permute-done | bytes 524320 | tf_op jit(solution)/shard_map/ppermute | solution.py:29
  212.8 3.4 %fusion.32 = (f32[1,256,1024]{2,1,0:T(8,128)}, bf16[1,256,1024]{2,1,0:T(8,128)(2,1)}, f32[1,256,1024]{2,1,0:T(8,128)}) fusion(f32[256,1024]{1,0:T(8,128)S(1)} %get-tuple-element.9, bf16[256,1024]{1,0:T(8,128)(2,1)S(1)} %collective-permute-done.36, pred[]{:T(512)S(6)} %eq.25, f32[1,256,1024]{2,1,0:T(8,128)S(1)} %copy-done.4, ...), kind=kLoop, calls=%fused_computation.112 | loop fusion | flops 4456448 | bytes 6815745 | tf_op jit(solution)/shard_map/broadcast_in_dim | solution.py:149
  (143 shorter events, 63.8 us)
Async XLA Ops:
  3.1 22.0 %collective-permute-start.37 = (f32[128,1024]{1,0:T(8,128)}, f32[128,1024]{1,0:T(8,128)}, u32[]{:S(2)}, u32[]{:S(2)}) collective-permute-start(f32[128,1024]{1,0:T(8,128)} %constant_dynamic-slice_fusion.2), channel_id=1, source_target_pairs={{0,16},{16,0},{1,17},{17,1},{2,18},{18,2},{3,19},{19,3},{4,20},{20... | collective-permute-start | bytes 1572872 | tf_op jit(solution)/shard_map/ppermute | solution.py:64
  6.3 20.1 %collective-permute-start.1 = (bf16[256,1024]{1,0:T(8,128)(2,1)}, bf16[256,1024]{1,0:T(8,128)(2,1)}, u32[]{:S(2)}, u32[]{:S(2)}) collective-permute-start(bf16[256,1024]{1,0:T(8,128)(2,1)} %bitcast.1), channel_id=1, source_target_pairs={{1,16},{2,19},{16,1},{19,2},{5,20},{6,23},{20,5},{23,6},{9,24},{10... | collective-permute-start | bytes 1572872 | tf_op jit(solution)/shard_map/ppermute | solution.py:29
  15.8 49.4 %collective-permute-start.7 = (bf16[512,1024]{1,0:T(8,128)(2,1)}, bf16[512,1024]{1,0:T(8,128)(2,1)}, u32[]{:S(2)}, u32[]{:S(2)}) collective-permute-start(bf16[512,1024]{1,0:T(8,128)(2,1)} %get-tuple-element.13), channel_id=1, source_target_pairs={{1,16},{2,19},{16,1},{19,2},{5,20},{6,23},{20,5},{23,6},{9,24},{10... | collective-permute-start | bytes 3145736 | tf_op jit(solution)/shard_map/ppermute | solution.py:29
  19.4 47.8 %collective-permute-start = (bf16[512,1024]{1,0:T(8,128)(2,1)S(1)}, bf16[512,1024]{1,0:T(8,128)(2,1)}, u32[]{:S(2)}, u32[]{:S(2)}) collective-permute-start(bf16[512,1024]{1,0:T(8,128)(2,1)S(1)} %get-tuple-element.12), channel_id=1, source_target_pairs={{1,16},{2,19},{16,1},{19,2},{5,20},{6,23},{20,5},{23,6},{9,24},{10... | collective-permute-start | bytes 3145736 | tf_op jit(solution)/shard_map/ppermute | solution.py:29
  21.4 48.3 %collective-permute-start.5 = (bf16[512,1024]{1,0:T(8,128)(2,1)S(1)}, bf16[512,1024]{1,0:T(8,128)(2,1)}, u32[]{:S(2)}, u32[]{:S(2)}) collective-permute-start(bf16[512,1024]{1,0:T(8,128)(2,1)S(1)} %get-tuple-element.11), channel_id=1, source_target_pairs={{1,16},{2,19},{16,1},{19,2},{5,20},{6,23},{20,5},{23,6},{9,24},{10... | collective-permute-start | bytes 3145736 | tf_op jit(solution)/shard_map/ppermute | solution.py:29
  37.6 17.2 %collective-permute-start.2 = (bf16[128,1024]{1,0:T(8,128)(2,1)S(1)}, bf16[128,1024]{1,0:T(8,128)(2,1)S(1)}, u32[]{:S(2)}, u32[]{:S(2)}) collective-permute-start(bf16[128,1024]{1,0:T(8,128)(2,1)S(1)} %get-tuple-element.45), channel_id=1, source_target_pairs={{0,4},{12,8},{4,0},{8,12},{1,5},{13,9},{5,1},{9,13},{2,6},{14,10},... | collective-permute-start | bytes 786440 | tf_op jit(solution)/shard_map/ppermute | solution.py:41
  49.8 23.9 %collective-permute-start.15 = (bf16[512,1024]{1,0:T(8,128)(2,1)S(1)}, bf16[512,1024]{1,0:T(8,128)(2,1)S(1)}, u32[]{:S(2)}, u32[]{:S(2)}) collective-permute-start(bf16[512,1024]{1,0:T(8,128)(2,1)S(1)} %get-tuple-element.10), channel_id=1, source_target_pairs={{1,16},{2,19},{16,1},{19,2},{5,20},{6,23},{20,5},{23,6},{9,24},{10... | collective-permute-start | bytes 3145736 | tf_op jit(solution)/shard_map/ppermute | solution.py:29
  62.2 16.8 %collective-permute-start.24 = (bf16[512,1024]{1,0:T(8,128)(2,1)S(1)}, bf16[512,1024]{1,0:T(8,128)(2,1)S(1)}, u32[]{:S(2)}, u32[]{:S(2)}) collective-permute-start(bf16[512,1024]{1,0:T(8,128)(2,1)S(1)} %copy-done.2), channel_id=1, source_target_pairs={{1,16},{2,19},{16,1},{19,2},{5,20},{6,23},{20,5},{23,6},{9,24},{10... | collective-permute-start | bytes 3145736 | tf_op jit(solution)/shard_map/ppermute | solution.py:29
  67.2 36.8 %collective-permute-start.10 = (bf16[256,1024]{1,0:T(8,128)(2,1)S(1)}, bf16[256,1024]{1,0:T(8,128)(2,1)S(1)}, u32[]{:S(2)}, u32[]{:S(2)}) collective-permute-start(bf16[256,1024]{1,0:T(8,128)(2,1)S(1)} %pad_maximum_fusion.7), channel_id=1, source_target_pairs={{4,8},{8,4},{5,9},{9,5},{6,10},{10,6},{7,11},{11,7},{20,24},{24,20... | collective-permute-start | bytes 1572872 | tf_op jit(solution)/shard_map/ppermute | solution.py:41
  69.7 28.3 %collective-permute-start.3 = (bf16[256,1024]{1,0:T(8,128)(2,1)S(1)}, bf16[256,1024]{1,0:T(8,128)(2,1)S(1)}, u32[]{:S(2)}, u32[]{:S(2)}) collective-permute-start(bf16[256,1024]{1,0:T(8,128)(2,1)S(1)} %pad_maximum_fusion.5), channel_id=1, source_target_pairs={{0,3},{1,2},{2,1},{3,0},{4,7},{5,6},{6,5},{7,4},{8,11},{9,10},{10,... | collective-permute-start | bytes 1572872 | tf_op jit(solution)/shard_map/ppermute | solution.py:37
  73.6 12.7 %collective-permute-start.9 = (bf16[128,1024]{1,0:T(8,128)(2,1)S(1)}, bf16[128,1024]{1,0:T(8,128)(2,1)S(1)}, u32[]{:S(2)}, u32[]{:S(2)}) collective-permute-start(bf16[128,1024]{1,0:T(8,128)(2,1)S(1)} %collective-permute-done.8), channel_id=1, source_target_pairs={{4,0},{8,12},{5,1},{9,13},{6,2},{10,14},{7,3},{11,15},{20,16},{24,... | collective-permute-start | bytes 786440 | tf_op jit(solution)/shard_map/ppermute | solution.py:41
  75.1 16.7 %collective-permute-start.42 = (f32[32,1024]{1,0:T(8,128)S(1)}, f32[32,1024]{1,0:T(8,128)S(1)}, u32[]{:S(2)}, u32[]{:S(2)}) collective-permute-start(f32[32,1024]{1,0:T(8,128)S(1)} %maximum_select_fusion.3), channel_id=1, source_target_pairs={{0,64},{32,96},{64,0},{96,32},{1,65},{33,97},{65,1},{97,33},{2,66}... | collective-permute-start | bytes 393224 | tf_op jit(solution)/shard_map/ppermute | solution.py:67
  79.0 18.8 %collective-permute-start.13 = (bf16[128,1024]{1,0:T(8,128)(2,1)S(1)}, bf16[128,1024]{1,0:T(8,128)(2,1)S(1)}, u32[]{:S(2)}, u32[]{:S(2)}) collective-permute-start(bf16[128,1024]{1,0:T(8,128)(2,1)S(1)} %collective-permute-done.12), channel_id=1, source_target_pairs={{4,0},{8,12},{5,1},{9,13},{6,2},{10,14},{7,3},{11,15},{20,16},{24,... | collective-permute-start | bytes 786440 | tf_op jit(solution)/shard_map/ppermute | solution.py:41
  86.4 16.9 %collective-permute-start.6 = (bf16[256,1024]{1,0:T(8,128)(2,1)S(1)}, bf16[256,1024]{1,0:T(8,128)(2,1)S(1)}, u32[]{:S(2)}, u32[]{:S(2)}) collective-permute-start(bf16[256,1024]{1,0:T(8,128)(2,1)S(1)} %pad_maximum_fusion.7), channel_id=1, source_target_pairs={{0,4},{12,8},{4,0},{8,12},{1,5},{13,9},{5,1},{9,13},{2,6},{14,10},... | collective-permute-start | bytes 1572872 | tf_op jit(solution)/shard_map/ppermute | solution.py:41
  91.8 34.8 %collective-permute-start.20 = (bf16[512,512]{1,0:T(8,128)(2,1)S(1)}, bf16[512,512]{1,0:T(8,128)(2,1)S(1)}, u32[]{:S(2)}, u32[]{:S(2)}) collective-permute-start(bf16[512,512]{1,0:T(8,128)(2,1)S(1)} %pad_maximum_fusion.13), channel_id=1, source_target_pairs={{0,16},{16,0},{1,17},{17,1},{2,18},{18,2},{3,19},{19,3},{4,20},{20... | collective-permute-start | bytes 1572872 | tf_op jit(solution)/shard_map/ppermute | solution.py:33
  103.3 24.1 %collective-permute-start.25 = (bf16[512,1024]{1,0:T(8,128)(2,1)S(1)}, bf16[512,1024]{1,0:T(8,128)(2,1)S(1)}, u32[]{:S(2)}, u32[]{:S(2)}) collective-permute-start(bf16[512,1024]{1,0:T(8,128)(2,1)S(1)} %broadcast_select_fusion), channel_id=1, source_target_pairs={{0,16},{16,0},{1,17},{17,1},{2,18},{18,2},{3,19},{19,3},{4,20},{20... | collective-permute-start | bytes 3145736 | tf_op jit(solution)/shard_map/ppermute | solution.py:33
  104.1 20.3 %collective-permute-start.14 = (bf16[256,1024]{1,0:T(8,128)(2,1)S(1)}, bf16[256,1024]{1,0:T(8,128)(2,1)S(1)}, u32[]{:S(2)}, u32[]{:S(2)}) collective-permute-start(bf16[256,1024]{1,0:T(8,128)(2,1)S(1)} %pad_maximum_fusion.9), channel_id=1, source_target_pairs={{0,3},{1,2},{2,1},{3,0},{4,7},{5,6},{6,5},{7,4},{8,11},{9,10},{10,... | collective-permute-start | bytes 1572872 | tf_op jit(solution)/shard_map/ppermute | solution.py:37
  107.9 14.5 %collective-permute-start.11 = (bf16[256,1024]{1,0:T(8,128)(2,1)S(1)}, bf16[256,1024]{1,0:T(8,128)(2,1)S(1)}, u32[]{:S(2)}, u32[]{:S(2)}) collective-permute-start(bf16[256,1024]{1,0:T(8,128)(2,1)S(1)} %collective-permute-done.10), channel_id=1, source_target_pairs={{4,0},{8,12},{5,1},{9,13},{6,2},{10,14},{7,3},{11,15},{20,16},{24,... | collective-permute-start | bytes 1572872 | tf_op jit(solution)/shard_map/ppermute | solution.py:41
  110.0 14.6 %collective-permute-start.16 = (bf16[256,1024]{1,0:T(8,128)(2,1)S(1)}, bf16[256,1024]{1,0:T(8,128)(2,1)S(1)}, u32[]{:S(2)}, u32[]{:S(2)}) collective-permute-start(bf16[256,1024]{1,0:T(8,128)(2,1)S(1)} %collective-permute-done.6), channel_id=1, source_target_pairs={{4,8},{8,4},{5,9},{9,5},{6,10},{10,6},{7,11},{11,7},{20,24},{24,20... | collective-permute-start | bytes 1572872 | tf_op jit(solution)/shard_map/ppermute | solution.py:41
  124.4 65.2 %collective-permute-start.43 = (f32[64,1024]{1,0:T(8,128)S(1)}, f32[64,1024]{1,0:T(8,128)S(1)}, u32[]{:S(2)}, u32[]{:S(2)}) collective-permute-start(f32[64,1024]{1,0:T(8,128)S(1)} %maximum_select_fusion.2), channel_id=1, source_target_pairs={{0,32},{32,0},{64,96},{96,64},{1,33},{33,1},{65,97},{97,65},{2,34}... | collective-permute-start | bytes 786440 | tf_op jit(solution)/shard_map/ppermute | solution.py:67
  124.5 13.9 %collective-permute-start.17 = (bf16[256,1024]{1,0:T(8,128)(2,1)S(1)}, bf16[256,1024]{1,0:T(8,128)(2,1)S(1)}, u32[]{:S(2)}, u32[]{:S(2)}) collective-permute-start(bf16[256,1024]{1,0:T(8,128)(2,1)S(1)} %collective-permute-done.16), channel_id=1, source_target_pairs={{4,0},{8,12},{5,1},{9,13},{6,2},{10,14},{7,3},{11,15},{20,16},{24,... | collective-permute-start | bytes 1572872 | tf_op jit(solution)/shard_map/ppermute | solution.py:41
  128.9 49.4 %collective-permute-start.27 = (bf16[256,1024]{1,0:T(8,128)(2,1)S(1)}, bf16[256,1024]{1,0:T(8,128)(2,1)S(1)}, u32[]{:S(2)}, u32[]{:S(2)}) collective-permute-start(bf16[256,1024]{1,0:T(8,128)(2,1)S(1)} %slice.153), channel_id=1, source_target_pairs={{0,3},{1,2},{2,1},{3,0},{4,7},{5,6},{6,5},{7,4},{8,11},{9,10},{10,... | collective-permute-start | bytes 1572872 | tf_op jit(solution)/shard_map/ppermute | solution.py:37
  130.6 24.4 %collective-permute-start.32 = (bf16[256,1024]{1,0:T(8,128)(2,1)S(1)}, bf16[256,1024]{1,0:T(8,128)(2,1)S(1)}, u32[]{:S(2)}, u32[]{:S(2)}) collective-permute-start(bf16[256,1024]{1,0:T(8,128)(2,1)S(1)} %slice.151), channel_id=1, source_target_pairs={{0,3},{1,2},{2,1},{3,0},{4,7},{5,6},{6,5},{7,4},{8,11},{9,10},{10,... | collective-permute-start | bytes 1572872 | tf_op jit(solution)/shard_map/ppermute | solution.py:37
  134.8 31.4 %collective-permute-start.29 = (bf16[256,1024]{1,0:T(8,128)(2,1)S(1)}, bf16[256,1024]{1,0:T(8,128)(2,1)S(1)}, u32[]{:S(2)}, u32[]{:S(2)}) collective-permute-start(bf16[256,1024]{1,0:T(8,128)(2,1)S(1)} %slice.152), channel_id=1, source_target_pairs={{0,3},{1,2},{2,1},{3,0},{4,7},{5,6},{6,5},{7,4},{8,11},{9,10},{10,... | collective-permute-start | bytes 1572872 | tf_op jit(solution)/shard_map/ppermute | solution.py:37
  155.1 13.5 %collective-permute-start.33 = (bf16[256,1024]{1,0:T(8,128)(2,1)S(1)}, bf16[256,1024]{1,0:T(8,128)(2,1)S(1)}, u32[]{:S(2)}, u32[]{:S(2)}) collective-permute-start(bf16[256,1024]{1,0:T(8,128)(2,1)S(1)} %fusion.10), channel_id=1, source_target_pairs={{0,4},{12,8},{1,5},{13,9},{2,6},{14,10},{3,7},{15,11},{16,20},{28,... | collective-permute-start | bytes 1572872 | tf_op jit(solution)/shard_map/ppermute | solution.py:41
  158.1 24.2 %collective-permute-start.22 = (bf16[512,1024]{1,0:T(8,128)(2,1)S(1)}, bf16[512,1024]{1,0:T(8,128)(2,1)S(1)}, u32[]{:S(2)}, u32[]{:S(2)}) collective-permute-start(bf16[512,1024]{1,0:T(8,128)(2,1)S(1)} %add_convert_fusion.1), channel_id=1, source_target_pairs={{0,16},{16,0},{1,17},{17,1},{2,18},{18,2},{3,19},{19,3},{4,20},{20... | collective-permute-start | bytes 3145736 | tf_op jit(solution)/shard_map/ppermute | solution.py:33
  177.2 19.4 %collective-permute-start.26 = (bf16[256,1024]{1,0:T(8,128)(2,1)}, bf16[256,1024]{1,0:T(8,128)(2,1)}, u32[]{:S(2)}, u32[]{:S(2)}) collective-permute-start(bf16[256,1024]{1,0:T(8,128)(2,1)} %slice.154), channel_id=1, source_target_pairs={{0,3},{1,2},{2,1},{3,0},{4,7},{5,6},{6,5},{7,4},{8,11},{9,10},{10,... | collective-permute-start | bytes 1572872 | tf_op jit(solution)/shard_map/ppermute | solution.py:37
  178.2 19.9 %collective-permute-start.31 = (bf16[256,1024]{1,0:T(8,128)(2,1)}, bf16[256,1024]{1,0:T(8,128)(2,1)}, u32[]{:S(2)}, u32[]{:S(2)}) collective-permute-start(bf16[256,1024]{1,0:T(8,128)(2,1)} %add_convert_fusion.4), channel_id=1, source_target_pairs={{4,8},{8,4},{5,9},{9,5},{6,10},{10,6},{7,11},{11,7},{20,24},{24,20... | collective-permute-start | bytes 1572872 | tf_op jit(solution)/shard_map/ppermute | solution.py:41
  181.0 17.2 %collective-permute-start.35 = (bf16[256,1024]{1,0:T(8,128)(2,1)}, bf16[256,1024]{1,0:T(8,128)(2,1)}, u32[]{:S(2)}, u32[]{:S(2)}) collective-permute-start(bf16[256,1024]{1,0:T(8,128)(2,1)} %get-tuple-element.18), channel_id=1, source_target_pairs={{4,0},{8,12},{5,1},{9,13},{6,2},{10,14},{7,3},{11,15},{20,16},{24,... | collective-permute-start | bytes 1572872 | tf_op jit(solution)/shard_map/ppermute | solution.py:41
  182.3 15.9 %collective-permute-start.28 = (bf16[256,1024]{1,0:T(8,128)(2,1)}, bf16[256,1024]{1,0:T(8,128)(2,1)}, u32[]{:S(2)}, u32[]{:S(2)}) collective-permute-start(bf16[256,1024]{1,0:T(8,128)(2,1)} %get-tuple-element.17), channel_id=1, source_target_pairs={{0,4},{12,8},{1,5},{13,9},{2,6},{14,10},{3,7},{15,11},{16,20},{28,... | collective-permute-start | bytes 1572872 | tf_op jit(solution)/shard_map/ppermute | solution.py:41
  190.3 16.9 %collective-permute-start.23 = (bf16[512,1024]{1,0:T(8,128)(2,1)S(1)}, bf16[512,1024]{1,0:T(8,128)(2,1)}, u32[]{:S(2)}, u32[]{:S(2)}) collective-permute-start(bf16[512,1024]{1,0:T(8,128)(2,1)S(1)} %add_convert_fusion), channel_id=1, source_target_pairs={{1,16},{2,19},{16,1},{19,2},{5,20},{6,23},{20,5},{23,6},{9,24},{10... | collective-permute-start | bytes 3145736 | tf_op jit(solution)/shard_map/ppermute | solution.py:29
  200.3 12.5 %collective-permute-start.36 = (bf16[256,1024]{1,0:T(8,128)(2,1)S(1)}, bf16[256,1024]{1,0:T(8,128)(2,1)S(1)}, u32[]{:S(2)}, u32[]{:S(2)}) collective-permute-start(bf16[256,1024]{1,0:T(8,128)(2,1)S(1)} %get-tuple-element.8), channel_id=1, source_target_pairs={{1,16},{2,19},{16,1},{19,2},{5,20},{6,23},{20,5},{23,6},{9,24},{10... | collective-permute-start | bytes 1572872 | tf_op jit(solution)/shard_map/ppermute | solution.py:29
  (20 other events, 164.4 us)

commit v2 on v1

v2 whole, which is shorter than its diff:
```python
import jax
import jax.numpy as jnp
from jax import lax
from jax.sharding import Mesh, PartitionSpec as P

learn_rate = 0.001
weight_decay = 0.1
first_decay = 0.9
second_decay = 0.95
adam_floor = 1e-08
outer_rate = 0.7
outer_decay = 0.9

bf16, f32 = jnp.bfloat16, jnp.float32
ALPHA = 96

HOME = (0, 1, 1, 0)
SWAP = [(c * 4 + x, (1 - c) * 4 + (x ^ 1)) for c in range(2) for x in range(4) if c != HOME[x]]
CORE = [(0, 1), (1, 0)]
ACROSS = [(x, 3 - x) for x in range(4)]
BESIDE = [(x, x ^ 1) for x in range(4)]
ENDS_OUT = [(1, 0), (2, 3)]
PAIRS = [(0, 1), (1, 0), (2, 3), (3, 2)]
MIDDLE = [(1, 2), (2, 1)]
ORDER = ((3, 2, 1, 0), (3, 2, 0, 1), (0, 1, 3, 2), (0, 1, 2, 3))


def swap(v):
    return lax.ppermute(v, ("c", "x"), SWAP)


def core(v):
    return lax.ppermute(v, "c", CORE)


def beside(v):
    return lax.ppermute(v, "x", BESIDE)


def across(v):
    return lax.ppermute(v, "x", ACROSS)


def line(v, pairs):
    return lax.ppermute(v, "zl", pairs)


def dot(a, b):
    return jnp.dot(a, b, preferred_element_type=f32)


def dot_t(a, b):
    return lax.dot_general(a, b, (((0,), (0,)), ((), ())), preferred_element_type=f32)


def together(*arrays):
    return lax.optimization_barrier(arrays)


class Drift:
    def __init__(self, own, c, y, zh):
        near = [(i, i ^ 1) for i in range(4)]
        wide = [(i, i ^ 2) for i in range(4)]
        self.v = own
        self.steps = [("c", CORE, c), ("y", near, y % 2), ("y", wide, y // 2), ("zh", CORE, zh)]
        self.at = 0

    def send(self):
        if self.at < 4:
            bit = self.steps[self.at][2]
            n = self.v.shape[0] // 2
            sent = lax.dynamic_slice_in_dim(self.v, (1 - bit) * n, n, 0)
            return sent.astype(bf16) if self.at == 3 else sent
        return self.v

    def step(self, sent):
        axis, perm, _ = self.steps[min(self.at, 7 - self.at)]
        return lax.ppermute(sent, axis, perm)

    def take(self, got):
        bit = self.steps[min(self.at, 7 - self.at)][2]
        if self.at < 4:
            n = self.v.shape[0] // 2
            self.v = lax.dynamic_slice_in_dim(self.v, bit * n, n, 0) + got.astype(f32)
        else:
            v = self.v
            self.v = jnp.where(bit == 0, jnp.concatenate([v, got]), jnp.concatenate([got, v]))
        self.at += 1


def on_device(
    tokens, key_grad, key_weight, adam_first, adam_second, local_params, anchor, outer_momentum
):
    c, x, z, y, zh = (lax.axis_index(a) for a in ("c", "x", "zl", "y", "zh"))
    weight = key_weight[0]
    stays = c == jnp.where((x == 1) | (x == 2), 1, 0)
    end = (z == 0) | (z == 3)
    mine = jnp.where(x < 2, c, 3 - c)
    theirs = jnp.where(x < 2, 1 - c, 2 + c)
    order = [
        jnp.where(z < 2, 3, 0),
        jnp.where(z < 2, 2, 1),
        jnp.where(z == 0, 1, jnp.where(z == 1, 0, jnp.where(z == 2, 3, 2))),
        z,
    ]

    def half(quarter):
        return jnp.concatenate(
            [
                lax.dynamic_slice_in_dim(tokens, order[k] * 1024 + q * 256, 256, 1)
                for k in range(4)
                for q in (quarter, 3 - quarter)
            ],
            axis=1,
        )

    w = jnp.where(stays, weight, swap(weight))
    g_sib = core(key_grad)
    x_own, x_sib = half(mine), core(half(theirs))
    drift = Drift(anchor - local_params[0].astype(f32), c, y, zh)
    drift.take(drift.step(drift.send()))
    x_a = jnp.where(stays, x_own, x_sib)
    x_l = jnp.where(stays, x_sib, x_own)
    g_a = jnp.where(stays, key_grad, g_sib)
    g_l = lax.dynamic_slice_in_dim(jnp.where(stays, g_sib, key_grad), c * 256, 256, 0)
    leave = [x_l[:, 512 * k : 512 * k + 512] for k in range(4)]
    keep = [x_a[:, 512 * k : 512 * k + 512] for k in range(4)]
    base = [dot_t(k, g_a) for k in keep]

    got = (beside(g_l), across(w), line(w, PAIRS), line(w, MIDDLE), drift.step(drift.send()))
    got, leave, drift.v = together(got, leave, drift.v)
    g_half, q_own, e_own, m_own, d = got
    drift.take(d)

    g_rest = core(g_half)
    g_b = jnp.where(
        c == 0, jnp.concatenate([g_half, g_rest]), jnp.concatenate([g_rest, g_half])
    )
    q_beta = q_own[ALPHA:]
    pad = jnp.zeros((ALPHA, 1024), bf16)
    got = (
        beside(leave[0]),
        line(jnp.where(end, jnp.concatenate([q_beta, pad]), m_own), PAIRS),
        line(e_own, MIDDLE),
        across(e_own[:ALPHA]),
        drift.step(drift.send()),
    )
    got, leave, drift.v, g_b = together(got, leave, drift.v, g_b)
    x_b = [got[0]]
    _, e2, m2, q2, d = got
    drift.take(d)

    def whole(k):
        v = base[k] + dot_t(x_b[k], g_b)
        return v[:256], v[256:].astype(bf16)

    mid = jnp.where(end, e2, m_own)
    stay0, go0 = whole(0)
    got = (
        beside(leave[1]),
        line(m2, ENDS_OUT),
        line(q_beta, MIDDLE),
        across(jnp.concatenate([go0, mid[:ALPHA]])),
        drift.step(drift.send()),
    )
    got, leave, drift.v, stay0 = together(got, leave, drift.v, stay0)
    x_b.append(got[0])
    _, e3, m3, q3, d = got
    drift.take(d)
    part0 = stay0 + q3[:256].astype(f32)

    far = jnp.where(end, e3, m2)
    stay1, go1 = whole(1)
    cut = 256 - (256 - ALPHA)
    got = (
        beside(leave[2]),
        line(
            jnp.where(end, part0.astype(bf16), jnp.concatenate([q_beta, m3[:cut]])), PAIRS
        ),
        line(e2[: 256 - ALPHA], MIDDLE),
        across(jnp.concatenate([go1, far[:ALPHA]])),
        drift.step(drift.send()),
    )
    got, leave, drift.v, stay1, part0 = together(got, leave, drift.v, stay1, part0)
    x_b.append(got[0])
    _, e4, m4, q4, d = got
    drift.take(d)
    part1 = stay1 + q4[:256].astype(f32)

    stay2, go2 = whole(2)
    fill = jnp.zeros((2 * ALPHA + cut - 256, 1024), bf16)
    got = (
        beside(leave[3]),
        line(
            jnp.where(
                end, part1.astype(bf16), jnp.concatenate([m3[cut:], m4, fill])
            ),
            PAIRS,
        ),
        line((part0 + e4.astype(f32)).astype(bf16), MIDDLE),
        across(go2),
        drift.step(drift.send()),
    )
    got, drift.v, stay2, part1 = together(got, drift.v, stay2, part1)
    x_b.append(got[0])
    _, e5, m5, q5, d = got
    drift.take(d)
    part2 = stay2 + q5.astype(f32)

    n = 256 - ALPHA
    beta1 = jnp.where(end, jnp.concatenate([e4[n:], e5[: n - cut]]), m3)
    beta0 = jnp.where(end, e5[n - cut : 2 * n - cut], m4)
    beta2 = jnp.where(end, e4[:n], e2[:n])
    rows = [
        jnp.concatenate([far, q4[256:], beta0]),
        jnp.concatenate([mid, q3[256:], beta1]),
        jnp.concatenate([e_own, q2, beta2]),
        jnp.concatenate([w, q_own]),
    ]
    k_a = sum(dot(keep[k], rows[k]) for k in (3, 2, 1, 0))
    k_b = sum(dot(x_b[k], rows[k]) for k in (2, 1, 0, 3))
    k_got = core(jnp.where(stays, k_b, k_a).astype(bf16))
    keys_work = (jnp.where(stays, k_a, k_b) + k_got.astype(f32)).astype(bf16)

    stay3, go3 = whole(3)
    got = (
        swap(keys_work),
        line((part2 + m5.astype(f32)).astype(bf16), PAIRS),
        line((part1 + e5.astype(f32)).astype(bf16), MIDDLE),
        across(go3),
        drift.step(drift.send()),
    )
    k_back, e6, m6, q6, d = got
    drift.take(d)
    keys = jnp.where(stays, keys_work, k_back)
    total = stay3 + q6.astype(f32) + e6.astype(f32) + m6.astype(f32)
    gradient = jnp.where(stays, total, swap(total.astype(bf16)).astype(f32))
    drift.take(drift.step(drift.send()))

    new_first = first_decay * adam_first[0] + (1.0 - first_decay) * gradient
    new_second = second_decay * adam_second[0] + (1.0 - second_decay) * gradient * gradient
    master = weight.astype(f32)
    update = new_first / (jnp.sqrt(new_second) + adam_floor) + weight_decay * master
    new_weight = (master - learn_rate * update).astype(bf16)

    mean = drift.v / 16
    new_momentum = outer_decay * outer_momentum + mean
    new_anchor = anchor - outer_rate * (mean + outer_decay * new_momentum)
    return (keys, new_weight[None], new_first[None], new_second[None], new_anchor, new_momentum)


def solution(mesh):
    fine = Mesh(mesh.devices.reshape(2, 4, 2, 4, 4), ("zh", "y", "c", "zl", "x"))
    replica, fsdp = ("zh", "y", "c"), ("zl", "x")
    tokens, stacked, shared = P(replica + fsdp, None), P(replica, fsdp, None), P(fsdp, None)
    return jax.shard_map(
        on_device,
        mesh=fine,
        in_specs=(tokens, tokens, stacked, stacked, stacked, stacked, shared, shared),
        out_specs=(tokens, stacked, stacked, stacked, shared, shared),
        check_vma=False,
    )
```

time: 219 us -> 199 us (0.909)
  starting transfers between devices: 95.8 us -> 62.3 us
  local copies, waits for them, and re-layouts: 8.52 us -> 29.7 us
  waiting for transfers between devices: 70.9 us -> 53.7 us
  matrix products: 11.8 us -> 19.9 us
  other arithmetic: 25.1 us -> 30.1 us
  between operations: 4.13 us -> 1.64 us
    ppermute x16 -> x12, waiting for transfers between devices: 35.3 us -> 2.58 us  [line(): return lax.ppermute(v, 'zl', pairs)]
    ppermute x8 -> x3, starting transfers between devices: 25.7 us -> 6.01 us  [swap(): return lax.ppermute(v, ('c', 'x'), SWAP)]
    unnamed x14 -> x84, local copies, waits for them, and re-layouts: 0.72 us -> 19.4 us
    ppermute x8 -> x13, waiting for transfers between devices: 10 us -> 25.6 us  [the longest x8 14 us: step(): return lax.ppermute(sent, axis, perm)]
    ppermute x8 -> x3, waiting for transfers between devices: 4.43 us -> 19.2 us  [swap(): return lax.ppermute(v, ('c', 'x'), SWAP)]
    ppermute x7 -> x6, waiting for transfers between devices: 21.1 us -> 6.38 us  [across(): return lax.ppermute(v, 'x', ACROSS)]
    ppermute x8 -> x13, starting transfers between devices: 22.6 us -> 16.7 us  [the longest x8 14.8 us: step(): return lax.ppermute(sent, axis, perm)]
    dynamic_slice x9 -> x3, local copies, waits for them, and re-layouts: 5.89 us -> 0.09 us  [send(): sent = lax.dynamic_slice_in_dim(self.v, (1 - bit) * n, n, 0)]
  transfers between devices with their start and end apart: 45 -> 38, of which waited for: 15 -> 13; matrix products, arithmetic and copies ran while one was open for 18% -> 23% of each run, Pallas kernels for 0% -> 0%
where the time goes in v2:
time: 199 us; the launch traced here: 197 us
  starting transfers between devices  62.3 us (31%)
  waiting for transfers between devices  53.7 us (27%)
  other arithmetic  30.1 us (15%)
  local copies, waits for them, and re-layouts  29.7 us (15%)
  matrix products  19.9 us (10%)
    ppermute x12, starting transfers between devices, line(): return lax.ppermute(v, 'zl', pairs)  22.5 us
    unnamed x84, local copies, waits for them, and re-layouts  19.4 us
    ppermute x3, waiting for transfers between devices, swap(): return lax.ppermute(v, ('c', 'x'), SWAP)  19.2 us
    ppermute x8, starting transfers between devices, step(): return lax.ppermute(sent, axis, perm)  14.8 us
    ppermute x8, waiting for transfers between devices, step(): return lax.ppermute(sent, axis, perm)  14 us
    ppermute x5, waiting for transfers between devices, beside(): return lax.ppermute(v, 'x', BESIDE)  11.6 us
    dot_general x8, matrix products, dot(): return jnp.dot(a, b, preferred_element_type=f32)  10.9 us
    ppermute x4, starting transfers between devices, core(): return lax.ppermute(v, 'c', CORE)  9.85 us
  transfers between devices with their start and end apart: 38, of which 13 were waited for; matrix products, arithmetic and copies ran while one was open for 23% of the time, Pallas kernels for 0%

profile of v2, /device:TPU:1, one launch (start us, length us, event | category | flops | bytes accessed | tf_op | source)
XLA Modules:
  0.0 197.4 jit_solution(3496915255539431055)
XLA Ops:
  2.6 1.9 dynamic-slice_dynamic-update-slice_fusion.13
  9.5 2.1 %dynamic-slice_dynamic-update-slice_fusion.10 = (bf16[512,2048]{1,0:T(8,128)(2,1)}, bf16[512,2048]{1,0:T(8,128)(2,1)}) fusion(bf16[512,2048]{1,0:T(8,128)(2,1)} %copy-done.16, bf16[512,4096]{1,0:T(8,128)(2,1)} %param.8, s32[]{:T(128)S(6)} %select_n.252, bf16[512,2048]{1,0:T(8,128)(2,1)} %get-tuple-element.115, s32[]{:T(128)S(6)} %select_n.259), kind=kLoop, calls=%fused_computation.86 | loop fusion | bytes 1048584
  11.5 1.9 dynamic-slice_dynamic-update-slice_fusion.9
  13.5 1.9 dynamic-slice_dynamic-update-slice_fusion.8
  18.8 3.2 %collective-permute-start = (bf16[512,2048]{1,0:T(8,128)(2,1)}, bf16[512,2048]{1,0:T(8,128)(2,1)}, u32[]{:S(2)}, u32[]{:S(2)}) collective-permute-start(bf16[512,2048]{1,0:T(8,128)(2,1)} %dynamic-slice_dynamic-update-slice_fusion), channel_id=1, source_target_pairs={{0,16},{16,0},{1,17},{17,1},{2,18},{18,2},{3,19},{19,3},{4,20},{20... | collective-permute-start | bytes 6291464 | tf_op jit(solution)/shard_map/ppermute | solution.py:33
  22.0 1.9 collective-permute-start.1
  24.4 8.4 %collective-permute-done.1 = bf16[256,1024]{1,0:T(8,128)(2,1)} collective-permute-done((bf16[256,1024]{1,0:T(8,128)(2,1)S(1)}, bf16[256,1024]{1,0:T(8,128)(2,1)}, u32[]{:S(2)}, u32[]{:S(2)}) %collective-permute-start.1) | collective-permute-done | bytes 524320 | tf_op jit(solution)/shard_map/ppermute | solution.py:29
  40.1 2.1 %broadcast_select_fusion.1 = (bf16[512,2048]{1,0:T(8,128)(2,1)S(1)}, bf16[512,2048]{1,0:T(8,128)(2,1)S(1)}) fusion(bf16[512,2048]{1,0:T(8,128)(2,1)S(1)} %copy-done.17, bf16[512,2048]{1,0:T(8,128)(2,1)} %collective-permute-done, pred[]{:T(512)S(6)} %eq.39), kind=kLoop, calls=%fused_computation.5 | loop fusion | flops 2097152 | bytes 8388609 | tf_op jit(solution)/shard_map/jit(_where)/select_n | solution.py:122
  43.6 10.1 %collective-permute-done.3 = bf16[256,1024]{1,0:T(8,128)(2,1)S(1)} collective-permute-done((bf16[256,1024]{1,0:T(8,128)(2,1)S(1)}, bf16[256,1024]{1,0:T(8,128)(2,1)S(1)}, u32[]{:S(2)}, u32[]{:S(2)}) %collective-permute-start.3) | collective-permute-done | bytes 524320 | tf_op jit(solution)/shard_map/ppermute | solution.py:37
  53.9 4.8 %collective-permute-start.10 = (bf16[256,1024]{1,0:T(8,128)(2,1)S(1)}, bf16[256,1024]{1,0:T(8,128)(2,1)S(1)}, u32[]{:S(2)}, u32[]{:S(2)}) collective-permute-start(bf16[256,1024]{1,0:T(8,128)(2,1)S(1)} %pad_select_fusion), channel_id=1, source_target_pairs={{0,4},{4,0},{8,12},{12,8},{1,5},{5,1},{9,13},{13,9},{2,6},{6,2},{1... | collective-permute-start | bytes 1572872 | tf_op jit(solution)/shard_map/ppermute | solution.py:45
  63.6 2.6 %collective-permute-start.13 = (f32[32,1024]{1,0:T(8,128)S(1)}, f32[32,1024]{1,0:T(8,128)S(1)}, u32[]{:S(2)}, u32[]{:S(2)}) collective-permute-start(f32[32,1024]{1,0:T(8,128)S(1)} %constant_dynamic-slice_fusion), channel_id=1, source_target_pairs={{0,64},{32,96},{64,0},{96,32},{1,65},{33,97},{65,1},{97,33},{2,66}... | collective-permute-start | bytes 393224 | tf_op jit(solution)/shard_map/ppermute | solution.py:78
  66.7 3.2 %collective-permute-done.13 = f32[32,1024]{1,0:T(8,128)S(1)} collective-permute-done((f32[32,1024]{1,0:T(8,128)S(1)}, f32[32,1024]{1,0:T(8,128)S(1)}, u32[]{:S(2)}, u32[]{:S(2)}) %collective-permute-start.13) | collective-permute-done | bytes 131104 | tf_op jit(solution)/shard_map/ppermute | solution.py:78
  74.5 2.0 %collective-permute-start.18 = (bf16[352,1024]{1,0:T(8,128)(2,1)}, bf16[352,1024]{1,0:T(8,128)(2,1)}, u32[]{:S(2)}, u32[]{:S(2)}) collective-permute-start(bf16[352,1024]{1,0:T(8,128)(2,1)} %pad_maximum_fusion.4), channel_id=1, source_target_pairs={{0,3},{1,2},{2,1},{3,0},{4,7},{5,6},{6,5},{7,4},{8,11},{9,10},{10,... | collective-permute-start | bytes 2162696 | tf_op jit(solution)/shard_map/ppermute | solution.py:41
  80.7 4.2 %collective-permute-start.19 = (bf16[16,1024]{1,0:T(8,128)(2,1)S(1)}, bf16[16,1024]{1,0:T(8,128)(2,1)S(1)}, u32[]{:S(2)}, u32[]{:S(2)}) collective-permute-start(bf16[16,1024]{1,0:T(8,128)(2,1)S(1)} %dynamic-slice_convert_fusion), channel_id=1, source_target_pairs={{0,128},{128,0},{1,129},{129,1},{2,130},{130,2},{3,131},{131,3},{4... | collective-permute-start | bytes 98312 | tf_op jit(solution)/shard_map/ppermute | solution.py:78
  84.9 2.6 %collective-permute-done.19 = bf16[16,1024]{1,0:T(8,128)(2,1)S(1)} collective-permute-done((bf16[16,1024]{1,0:T(8,128)(2,1)S(1)}, bf16[16,1024]{1,0:T(8,128)(2,1)S(1)}, u32[]{:S(2)}, u32[]{:S(2)}) %collective-permute-start.19) | collective-permute-done | bytes 32800 | tf_op jit(solution)/shard_map/ppermute | solution.py:78
  88.9 2.6 %collective-permute-done.16 = bf16[256,1024]{1,0:T(8,128)(2,1)} collective-permute-done((bf16[256,1024]{1,0:T(8,128)(2,1)}, bf16[256,1024]{1,0:T(8,128)(2,1)}, u32[]{:S(2)}, u32[]{:S(2)}) %collective-permute-start.16) | collective-permute-done | bytes 524320 | tf_op jit(solution)/shard_map/ppermute | solution.py:45
  99.2 1.9 collective-permute-start.23
  101.1 2.4 %maximum_select_fusion.2 = (bf16[256,1024]{1,0:T(8,128)(2,1)}, f32[256,1024]{1,0:T(8,128)}) fusion(bf16[96,1024]{1,0:T(8,128)(2,1)S(1)} %slice-done.3, bf16[160,1024]{1,0:T(8,128)(2,1)S(1)} %slice.104, pred[]{:T(512)S(6)} %or.7, f32[256,1024]{1,0:T(8,128)S(1)} %slice-done, bf16[352,1024]{1,0:T(8,128)(2,1)} %collective-permute-done.18), kind=kLoop, calls=%fused_computation.48 | loop fusion | flops 2097152 | bytes 3670017 | tf_op jit(solution)/shard_map/jit(_where)/select_n | solution.py:178
  103.6 4.1 %collective-permute-start.21 = (bf16[256,1024]{1,0:T(8,128)(2,1)}, bf16[256,1024]{1,0:T(8,128)(2,1)}, u32[]{:S(2)}, u32[]{:S(2)}) collective-permute-start(bf16[256,1024]{1,0:T(8,128)(2,1)} %get-tuple-element.104), channel_id=1, source_target_pairs={{0,4},{4,0},{8,12},{12,8},{1,5},{5,1},{9,13},{13,9},{2,6},{6,2},{1... | collective-permute-start | bytes 1572872 | tf_op jit(solution)/shard_map/ppermute | solution.py:45
  115.0 5.4 %collective-permute-done.24 = f32[16,1024]{1,0:T(8,128)S(1)} collective-permute-done((f32[16,1024]{1,0:T(8,128)S(1)}, f32[16,1024]{1,0:T(8,128)S(1)}, u32[]{:S(2)}, u32[]{:S(2)}) %collective-permute-start.24) | collective-permute-done | bytes 65568 | tf_op jit(solution)/shard_map/ppermute | solution.py:78
  130.4 2.9 %collective-permute-start.29 = (f32[32,1024]{1,0:T(8,128)S(1)}, f32[32,1024]{1,0:T(8,128)S(1)}, u32[]{:S(2)}, u32[]{:S(2)}) collective-permute-start(f32[32,1024]{1,0:T(8,128)S(1)} %maximum_select_fusion.7), channel_id=1, source_target_pairs={{0,64},{32,96},{64,0},{96,32},{1,65},{33,97},{65,1},{97,33},{2,66}... | collective-permute-start | bytes 393224 | tf_op jit(solution)/shard_map/ppermute | solution.py:78
  140.0 1.9 fusion.24
  143.4 2.6 %select_convert_fusion = (bf16[512,1024]{1,0:T(8,128)(2,1)}, f32[512,1024]{1,0:T(8,128)}) fusion(f32[512,1024]{1,0:T(8,128)S(1)} %add_add_fusion.1, pred[]{:T(512)S(6)} %eq.39, bf16[512,512]{1,0:T(8,128)(2,1)S(1)} %collective-permute-done.25, bf16[256,1024]{1,0:T(8,128)(2,1)S(1)} %collective-permute-done.4, ...), kind=kOutput, calls=%fused_computation.1 | convolution fusion | flops 541065216 | bytes 13107201 | tf_op jit(solution)/shard_map/dot_general | solution.py:49
  146.0 5.5 %collective-permute-start.30 = (bf16[512,1024]{1,0:T(8,128)(2,1)}, bf16[512,1024]{1,0:T(8,128)(2,1)S(1)}, u32[]{:S(2)}, u32[]{:S(2)}) collective-permute-start(bf16[512,1024]{1,0:T(8,128)(2,1)} %get-tuple-element.127), channel_id=1, source_target_pairs={{0,16},{16,0},{1,17},{17,1},{2,18},{18,2},{3,19},{19,3},{4,20},{20... | collective-permute-start | bytes 3145736 | tf_op jit(solution)/shard_map/ppermute | solution.py:33
  155.1 4.5 %collective-permute-start.33 = (bf16[256,1024]{1,0:T(8,128)(2,1)}, bf16[256,1024]{1,0:T(8,128)(2,1)}, u32[]{:S(2)}, u32[]{:S(2)}) collective-permute-start(bf16[256,1024]{1,0:T(8,128)(2,1)} %add_convert_fusion.2), channel_id=1, source_target_pairs={{0,4},{4,0},{8,12},{12,8},{1,5},{5,1},{9,13},{13,9},{2,6},{6,2},{1... | collective-permute-start | bytes 1572872 | tf_op jit(solution)/shard_map/ppermute | solution.py:45
  164.3 2.8 %collective-permute-done.36 = f32[64,1024]{1,0:T(8,128)} collective-permute-done((f32[64,1024]{1,0:T(8,128)S(1)}, f32[64,1024]{1,0:T(8,128)}, u32[]{:S(2)}, u32[]{:S(2)}) %collective-permute-start.36) | collective-permute-done | bytes 262176 | tf_op jit(solution)/shard_map/ppermute | solution.py:78
  169.7 2.3 %add_convert_fusion = bf16[512,1024]{1,0:T(8,128)(2,1)S(1)} fusion(bf16[512,1024]{1,0:T(8,128)(2,1)S(1)} %collective-permute-done.30, f32[512,1024]{1,0:T(8,128)S(1)} %copy-done.1, f32[512,1024]{1,0:T(8,128)} %get-tuple-element.128, pred[]{:T(512)S(6)} %eq.39), kind=kLoop, calls=%fused_computation | loop fusion | flops 2097152 | bytes 6291457 | tf_op jit(solution)/shard_map/convert_element_type | solution.py:223
  172.1 2.1 %collective-permute-start.31 = (bf16[512,1024]{1,0:T(8,128)(2,1)S(1)}, bf16[512,1024]{1,0:T(8,128)(2,1)S(1)}, u32[]{:S(2)}, u32[]{:S(2)}) collective-permute-start(bf16[512,1024]{1,0:T(8,128)(2,1)S(1)} %add_convert_fusion), channel_id=1, source_target_pairs={{1,16},{2,19},{16,1},{19,2},{5,20},{6,23},{20,5},{23,6},{9,24},{10... | collective-permute-start | bytes 3145736 | tf_op jit(solution)/shard_map/ppermute | solution.py:29
  174.2 3.5 %collective-permute-done.32 = bf16[256,1024]{1,0:T(8,128)(2,1)} collective-permute-done((bf16[256,1024]{1,0:T(8,128)(2,1)}, bf16[256,1024]{1,0:T(8,128)(2,1)}, u32[]{:S(2)}, u32[]{:S(2)}) %collective-permute-start.32) | collective-permute-done | bytes 524320 | tf_op jit(solution)/shard_map/ppermute | solution.py:41
  179.4 2.1 %collective-permute-start.35 = (bf16[256,1024]{1,0:T(8,128)(2,1)S(1)}, bf16[256,1024]{1,0:T(8,128)(2,1)S(1)}, u32[]{:S(2)}, u32[]{:S(2)}) collective-permute-start(bf16[256,1024]{1,0:T(8,128)(2,1)S(1)} %get-tuple-element.100), channel_id=1, source_target_pairs={{1,16},{2,19},{16,1},{19,2},{5,20},{6,23},{20,5},{23,6},{9,24},{10... | collective-permute-start | bytes 1572872 | tf_op jit(solution)/shard_map/ppermute | solution.py:29
  183.2 10.7 %collective-permute-done.35 = bf16[256,1024]{1,0:T(8,128)(2,1)S(1)} collective-permute-done((bf16[256,1024]{1,0:T(8,128)(2,1)S(1)}, bf16[256,1024]{1,0:T(8,128)(2,1)S(1)}, u32[]{:S(2)}, u32[]{:S(2)}) %collective-permute-start.35) | collective-permute-done | bytes 524320 | tf_op jit(solution)/shard_map/ppermute | solution.py:29
  194.0 2.3 %fusion.35 = (f32[1,256,1024]{2,1,0:T(8,128)}, bf16[1,256,1024]{2,1,0:T(8,128)(2,1)}, f32[1,256,1024]{2,1,0:T(8,128)}) fusion(f32[256,1024]{1,0:T(8,128)S(1)} %get-tuple-element.101, bf16[256,1024]{1,0:T(8,128)(2,1)S(1)} %collective-permute-done.35, pred[]{:T(512)S(6)} %eq.39, f32[1,256,1024]{2,1,0:T(8,128)S(1)} %copy-done.24, ...), kind=kLoop, calls=%fused_computation.108 | loop fusion | flops 4456448 | bytes 6815745 | tf_op jit(solution)/shard_map/broadcast_in_dim | solution.py:249
  (207 shorter events, 83.0 us)
Async XLA Ops:
  18.8 21.2 %collective-permute-start = (bf16[512,2048]{1,0:T(8,128)(2,1)}, bf16[512,2048]{1,0:T(8,128)(2,1)}, u32[]{:S(2)}, u32[]{:S(2)}) collective-permute-start(bf16[512,2048]{1,0:T(8,128)(2,1)} %dynamic-slice_dynamic-update-slice_fusion), channel_id=1, source_target_pairs={{0,16},{16,0},{1,17},{17,1},{2,18},{18,2},{3,19},{19,3},{4,20},{20... | collective-permute-start | bytes 6291464 | tf_op jit(solution)/shard_map/ppermute | solution.py:33
  22.0 15.2 %collective-permute-start.2 = (bf16[512,1024]{1,0:T(8,128)(2,1)}, bf16[512,1024]{1,0:T(8,128)(2,1)}, u32[]{:S(2)}, u32[]{:S(2)}) collective-permute-start(bf16[512,1024]{1,0:T(8,128)(2,1)} %param.9), channel_id=1, source_target_pairs={{0,16},{16,0},{1,17},{17,1},{2,18},{18,2},{3,19},{19,3},{4,20},{20... | collective-permute-start | bytes 3145736 | tf_op jit(solution)/shard_map/ppermute | solution.py:33
  22.0 10.8 %collective-permute-start.1 = (bf16[256,1024]{1,0:T(8,128)(2,1)S(1)}, bf16[256,1024]{1,0:T(8,128)(2,1)}, u32[]{:S(2)}, u32[]{:S(2)}) collective-permute-start(bf16[256,1024]{1,0:T(8,128)(2,1)S(1)} %bitcast.40), channel_id=1, source_target_pairs={{1,16},{2,19},{16,1},{19,2},{5,20},{6,23},{20,5},{23,6},{9,24},{10... | collective-permute-start | bytes 1572872 | tf_op jit(solution)/shard_map/ppermute | solution.py:29
  24.2 12.2 %collective-permute-start.7 = (f32[128,1024]{1,0:T(8,128)S(1)}, f32[128,1024]{1,0:T(8,128)S(1)}, u32[]{:S(2)}, u32[]{:S(2)}) collective-permute-start(f32[128,1024]{1,0:T(8,128)S(1)} %constant_dynamic-slice_fusion.2), channel_id=1, source_target_pairs={{0,16},{16,0},{1,17},{17,1},{2,18},{18,2},{3,19},{19,3},{4,20},{20... | collective-permute-start | bytes 1572872 | tf_op jit(solution)/shard_map/ppermute | solution.py:78
  33.9 9.6 %collective-permute-start.4 = (bf16[256,1024]{1,0:T(8,128)(2,1)S(1)}, bf16[256,1024]{1,0:T(8,128)(2,1)S(1)}, u32[]{:S(2)}, u32[]{:S(2)}) collective-permute-start(bf16[256,1024]{1,0:T(8,128)(2,1)S(1)} %broadcast_select_fusion.6), channel_id=1, source_target_pairs={{0,3},{1,2},{2,1},{3,0},{4,7},{5,6},{6,5},{7,4},{8,11},{9,10},{10,... | collective-permute-start | bytes 1572872 | tf_op jit(solution)/shard_map/ppermute | solution.py:41
  34.8 8.8 %collective-permute-start.5 = (bf16[256,1024]{1,0:T(8,128)(2,1)S(1)}, bf16[256,1024]{1,0:T(8,128)(2,1)S(1)}, u32[]{:S(2)}, u32[]{:S(2)}) collective-permute-start(bf16[256,1024]{1,0:T(8,128)(2,1)S(1)} %broadcast_select_fusion.6), channel_id=1, source_target_pairs={{0,4},{4,0},{8,12},{12,8},{1,5},{5,1},{9,13},{13,9},{2,6},{6,2},{1... | collective-permute-start | bytes 1572872 | tf_op jit(solution)/shard_map/ppermute | solution.py:45
  36.4 7.1 %collective-permute-start.6 = (bf16[256,1024]{1,0:T(8,128)(2,1)S(1)}, bf16[256,1024]{1,0:T(8,128)(2,1)S(1)}, u32[]{:S(2)}, u32[]{:S(2)}) collective-permute-start(bf16[256,1024]{1,0:T(8,128)(2,1)S(1)} %broadcast_select_fusion.6), channel_id=1, source_target_pairs={{4,8},{8,4},{5,9},{9,5},{6,10},{10,6},{7,11},{11,7},{20,24},{24,20... | collective-permute-start | bytes 1572872 | tf_op jit(solution)/shard_map/ppermute | solution.py:45
  40.0 13.7 %collective-permute-start.3 = (bf16[256,1024]{1,0:T(8,128)(2,1)S(1)}, bf16[256,1024]{1,0:T(8,128)(2,1)S(1)}, u32[]{:S(2)}, u32[]{:S(2)}) collective-permute-start(bf16[256,1024]{1,0:T(8,128)(2,1)S(1)} %dynamic-slice_select_fusion), channel_id=1, source_target_pairs={{0,1},{1,0},{2,3},{3,2},{4,5},{5,4},{6,7},{7,6},{8,9},{9,8},{10,11... | collective-permute-start | bytes 1572872 | tf_op jit(solution)/shard_map/ppermute | solution.py:37
  53.7 16.7 %collective-permute-start.9 = (bf16[512,512]{1,0:T(8,128)(2,1)S(1)}, bf16[512,512]{1,0:T(8,128)(2,1)S(1)}, u32[]{:S(2)}, u32[]{:S(2)}) collective-permute-start(bf16[512,512]{1,0:T(8,128)(2,1)S(1)} %get-tuple-element.54), channel_id=1, source_target_pairs={{0,1},{1,0},{2,3},{3,2},{4,5},{5,4},{6,7},{7,6},{8,9},{9,8},{10,11... | collective-permute-start | bytes 1572872 | tf_op jit(solution)/shard_map/ppermute | solution.py:37
  53.9 16.6 %collective-permute-start.10 = (bf16[256,1024]{1,0:T(8,128)(2,1)S(1)}, bf16[256,1024]{1,0:T(8,128)(2,1)S(1)}, u32[]{:S(2)}, u32[]{:S(2)}) collective-permute-start(bf16[256,1024]{1,0:T(8,128)(2,1)S(1)} %pad_select_fusion), channel_id=1, source_target_pairs={{0,4},{4,0},{8,12},{12,8},{1,5},{5,1},{9,13},{13,9},{2,6},{6,2},{1... | collective-permute-start | bytes 1572872 | tf_op jit(solution)/shard_map/ppermute | solution.py:45
  58.7 11.7 %collective-permute-start.11 = (bf16[256,1024]{1,0:T(8,128)(2,1)S(1)}, bf16[256,1024]{1,0:T(8,128)(2,1)}, u32[]{:S(2)}, u32[]{:S(2)}) collective-permute-start(bf16[256,1024]{1,0:T(8,128)(2,1)S(1)} %collective-permute-done.5), channel_id=1, source_target_pairs={{4,8},{8,4},{5,9},{9,5},{6,10},{10,6},{7,11},{11,7},{20,24},{24,20... | collective-permute-start | bytes 1572872 | tf_op jit(solution)/shard_map/ppermute | solution.py:45
  62.6 7.8 %collective-permute-start.12 = (bf16[96,1024]{1,0:T(8,128)(2,1)S(1)}, bf16[96,1024]{1,0:T(8,128)(2,1)S(1)}, u32[]{:S(2)}, u32[]{:S(2)}) collective-permute-start(bf16[96,1024]{1,0:T(8,128)(2,1)S(1)} %slice.105), channel_id=1, source_target_pairs={{0,3},{1,2},{2,1},{3,0},{4,7},{5,6},{6,5},{7,4},{8,11},{9,10},{10,... | collective-permute-start | bytes 589832 | tf_op jit(solution)/shard_map/ppermute | solution.py:41
  74.5 18.1 %collective-permute-start.18 = (bf16[352,1024]{1,0:T(8,128)(2,1)}, bf16[352,1024]{1,0:T(8,128)(2,1)}, u32[]{:S(2)}, u32[]{:S(2)}) collective-permute-start(bf16[352,1024]{1,0:T(8,128)(2,1)} %pad_maximum_fusion.4), channel_id=1, source_target_pairs={{0,3},{1,2},{2,1},{3,0},{4,7},{5,6},{6,5},{7,4},{8,11},{9,10},{10,... | collective-permute-start | bytes 2162696 | tf_op jit(solution)/shard_map/ppermute | solution.py:41
  76.6 12.4 %collective-permute-start.15 = (bf16[512,512]{1,0:T(8,128)(2,1)}, bf16[512,512]{1,0:T(8,128)(2,1)}, u32[]{:S(2)}, u32[]{:S(2)}) collective-permute-start(bf16[512,512]{1,0:T(8,128)(2,1)} %get-tuple-element.63), channel_id=1, source_target_pairs={{0,1},{1,0},{2,3},{3,2},{4,5},{5,4},{6,7},{7,6},{8,9},{9,8},{10,11... | collective-permute-start | bytes 1572872 | tf_op jit(solution)/shard_map/ppermute | solution.py:37
  76.8 14.7 %collective-permute-start.16 = (bf16[256,1024]{1,0:T(8,128)(2,1)}, bf16[256,1024]{1,0:T(8,128)(2,1)}, u32[]{:S(2)}, u32[]{:S(2)}) collective-permute-start(bf16[256,1024]{1,0:T(8,128)(2,1)} %collective-permute-done.11), channel_id=1, source_target_pairs={{4,0},{8,12},{5,1},{9,13},{6,2},{10,14},{7,3},{11,15},{20,16},{24,... | collective-permute-start | bytes 1572872 | tf_op jit(solution)/shard_map/ppermute | solution.py:45
  92.7 27.7 %collective-permute-start.20 = (bf16[512,512]{1,0:T(8,128)(2,1)}, bf16[512,512]{1,0:T(8,128)(2,1)}, u32[]{:S(2)}, u32[]{:S(2)}) collective-permute-start(bf16[512,512]{1,0:T(8,128)(2,1)} %get-tuple-element.72), channel_id=1, source_target_pairs={{0,1},{1,0},{2,3},{3,2},{4,5},{5,4},{6,7},{7,6},{8,9},{9,8},{10,11... | collective-permute-start | bytes 1572872 | tf_op jit(solution)/shard_map/ppermute | solution.py:37
  99.2 21.2 %collective-permute-start.23 = (bf16[352,1024]{1,0:T(8,128)(2,1)}, bf16[352,1024]{1,0:T(8,128)(2,1)}, u32[]{:S(2)}, u32[]{:S(2)}) collective-permute-start(bf16[352,1024]{1,0:T(8,128)(2,1)} %pad_maximum_fusion.5), channel_id=1, source_target_pairs={{0,3},{1,2},{2,1},{3,0},{4,7},{5,6},{6,5},{7,4},{8,11},{9,10},{10,... | collective-permute-start | bytes 2162696 | tf_op jit(solution)/shard_map/ppermute | solution.py:41
  103.6 16.8 %collective-permute-start.21 = (bf16[256,1024]{1,0:T(8,128)(2,1)}, bf16[256,1024]{1,0:T(8,128)(2,1)}, u32[]{:S(2)}, u32[]{:S(2)}) collective-permute-start(bf16[256,1024]{1,0:T(8,128)(2,1)} %get-tuple-element.104), channel_id=1, source_target_pairs={{0,4},{4,0},{8,12},{12,8},{1,5},{5,1},{9,13},{13,9},{2,6},{6,2},{1... | collective-permute-start | bytes 1572872 | tf_op jit(solution)/shard_map/ppermute | solution.py:45
  110.3 10.0 %collective-permute-start.24 = (f32[16,1024]{1,0:T(8,128)S(1)}, f32[16,1024]{1,0:T(8,128)S(1)}, u32[]{:S(2)}, u32[]{:S(2)}) collective-permute-start(f32[16,1024]{1,0:T(8,128)S(1)} %convert_add_fusion.2), channel_id=1, source_target_pairs={{0,128},{128,0},{1,129},{129,1},{2,130},{130,2},{3,131},{131,3},{4... | collective-permute-start | bytes 196616 | tf_op jit(solution)/shard_map/ppermute | solution.py:78
  120.4 17.5 %collective-permute-start.25 = (bf16[512,512]{1,0:T(8,128)(2,1)S(1)}, bf16[512,512]{1,0:T(8,128)(2,1)S(1)}, u32[]{:S(2)}, u32[]{:S(2)}) collective-permute-start(bf16[512,512]{1,0:T(8,128)(2,1)S(1)} %copy-done.31), channel_id=1, source_target_pairs={{0,1},{1,0},{2,3},{3,2},{4,5},{5,4},{6,7},{7,6},{8,9},{9,8},{10,11... | collective-permute-start | bytes 1572872 | tf_op jit(solution)/shard_map/ppermute | solution.py:37
  123.2 14.7 %collective-permute-start.26 = (bf16[256,1024]{1,0:T(8,128)(2,1)S(1)}, bf16[256,1024]{1,0:T(8,128)(2,1)S(1)}, u32[]{:S(2)}, u32[]{:S(2)}) collective-permute-start(bf16[256,1024]{1,0:T(8,128)(2,1)S(1)} %get-tuple-element.102), channel_id=1, source_target_pairs={{0,4},{4,0},{8,12},{12,8},{1,5},{5,1},{9,13},{13,9},{2,6},{6,2},{1... | collective-permute-start | bytes 1572872 | tf_op jit(solution)/shard_map/ppermute | solution.py:45
  125.5 12.3 %collective-permute-start.27 = (bf16[256,1024]{1,0:T(8,128)(2,1)S(1)}, bf16[256,1024]{1,0:T(8,128)(2,1)S(1)}, u32[]{:S(2)}, u32[]{:S(2)}) collective-permute-start(bf16[256,1024]{1,0:T(8,128)(2,1)S(1)} %add_convert_fusion.3), channel_id=1, source_target_pairs={{4,8},{8,4},{5,9},{9,5},{6,10},{10,6},{7,11},{11,7},{20,24},{24,20... | collective-permute-start | bytes 1572872 | tf_op jit(solution)/shard_map/ppermute | solution.py:45
  129.0 10.1 %collective-permute-start.28 = (bf16[256,1024]{1,0:T(8,128)(2,1)S(1)}, bf16[256,1024]{1,0:T(8,128)(2,1)S(1)}, u32[]{:S(2)}, u32[]{:S(2)}) collective-permute-start(bf16[256,1024]{1,0:T(8,128)(2,1)S(1)} %slice.180), channel_id=1, source_target_pairs={{0,3},{1,2},{2,1},{3,0},{4,7},{5,6},{6,5},{7,4},{8,11},{9,10},{10,... | collective-permute-start | bytes 1572872 | tf_op jit(solution)/shard_map/ppermute | solution.py:41
  130.4 7.4 %collective-permute-start.29 = (f32[32,1024]{1,0:T(8,128)S(1)}, f32[32,1024]{1,0:T(8,128)S(1)}, u32[]{:S(2)}, u32[]{:S(2)}) collective-permute-start(f32[32,1024]{1,0:T(8,128)S(1)} %maximum_select_fusion.7), channel_id=1, source_target_pairs={{0,64},{32,96},{64,0},{96,32},{1,65},{33,97},{65,1},{97,33},{2,66}... | collective-permute-start | bytes 393224 | tf_op jit(solution)/shard_map/ppermute | solution.py:78
  146.0 23.7 %collective-permute-start.30 = (bf16[512,1024]{1,0:T(8,128)(2,1)}, bf16[512,1024]{1,0:T(8,128)(2,1)S(1)}, u32[]{:S(2)}, u32[]{:S(2)}) collective-permute-start(bf16[512,1024]{1,0:T(8,128)(2,1)} %get-tuple-element.127), channel_id=1, source_target_pairs={{0,16},{16,0},{1,17},{17,1},{2,18},{18,2},{3,19},{19,3},{4,20},{20... | collective-permute-start | bytes 3145736 | tf_op jit(solution)/shard_map/ppermute | solution.py:33
  152.5 21.6 %collective-permute-start.34 = (bf16[256,1024]{1,0:T(8,128)(2,1)}, bf16[256,1024]{1,0:T(8,128)(2,1)}, u32[]{:S(2)}, u32[]{:S(2)}) collective-permute-start(bf16[256,1024]{1,0:T(8,128)(2,1)} %add_convert_fusion.1), channel_id=1, source_target_pairs={{4,8},{8,4},{5,9},{9,5},{6,10},{10,6},{7,11},{11,7},{20,24},{24,20... | collective-permute-start | bytes 1572872 | tf_op jit(solution)/shard_map/ppermute | solution.py:45
  155.1 19.1 %collective-permute-start.33 = (bf16[256,1024]{1,0:T(8,128)(2,1)}, bf16[256,1024]{1,0:T(8,128)(2,1)}, u32[]{:S(2)}, u32[]{:S(2)}) collective-permute-start(bf16[256,1024]{1,0:T(8,128)(2,1)} %add_convert_fusion.2), channel_id=1, source_target_pairs={{0,4},{4,0},{8,12},{12,8},{1,5},{5,1},{9,13},{13,9},{2,6},{6,2},{1... | collective-permute-start | bytes 1572872 | tf_op jit(solution)/shard_map/ppermute | solution.py:45
  159.6 7.5 %collective-permute-start.36 = (f32[64,1024]{1,0:T(8,128)S(1)}, f32[64,1024]{1,0:T(8,128)}, u32[]{:S(2)}, u32[]{:S(2)}) collective-permute-start(f32[64,1024]{1,0:T(8,128)S(1)} %maximum_select_fusion.6), channel_id=1, source_target_pairs={{0,32},{32,0},{64,96},{96,64},{1,33},{33,1},{65,97},{97,65},{2,34}... | collective-permute-start | bytes 786440 | tf_op jit(solution)/shard_map/ppermute | solution.py:78
  163.5 14.1 %collective-permute-start.32 = (bf16[256,1024]{1,0:T(8,128)(2,1)}, bf16[256,1024]{1,0:T(8,128)(2,1)}, u32[]{:S(2)}, u32[]{:S(2)}) collective-permute-start(bf16[256,1024]{1,0:T(8,128)(2,1)} %slice.179), channel_id=1, source_target_pairs={{0,3},{1,2},{2,1},{3,0},{4,7},{5,6},{6,5},{7,4},{8,11},{9,10},{10,... | collective-permute-start | bytes 1572872 | tf_op jit(solution)/shard_map/ppermute | solution.py:41
  168.2 13.3 %collective-permute-start.37 = (f32[128,1024]{1,0:T(8,128)S(1)}, f32[128,1024]{1,0:T(8,128)S(1)}, u32[]{:S(2)}, u32[]{:S(2)}) collective-permute-start(f32[128,1024]{1,0:T(8,128)S(1)} %maximum_select_fusion.4), channel_id=1, source_target_pairs={{0,16},{16,0},{1,17},{17,1},{2,18},{18,2},{3,19},{19,3},{4,20},{20... | collective-permute-start | bytes 1572872 | tf_op jit(solution)/shard_map/ppermute | solution.py:78
  172.1 24.2 %collective-permute-start.31 = (bf16[512,1024]{1,0:T(8,128)(2,1)S(1)}, bf16[512,1024]{1,0:T(8,128)(2,1)S(1)}, u32[]{:S(2)}, u32[]{:S(2)}) collective-permute-start(bf16[512,1024]{1,0:T(8,128)(2,1)S(1)} %add_convert_fusion), channel_id=1, source_target_pairs={{1,16},{2,19},{16,1},{19,2},{5,20},{6,23},{20,5},{23,6},{9,24},{10... | collective-permute-start | bytes 3145736 | tf_op jit(solution)/shard_map/ppermute | solution.py:29
  179.4 14.5 %collective-permute-start.35 = (bf16[256,1024]{1,0:T(8,128)(2,1)S(1)}, bf16[256,1024]{1,0:T(8,128)(2,1)S(1)}, u32[]{:S(2)}, u32[]{:S(2)}) collective-permute-start(bf16[256,1024]{1,0:T(8,128)(2,1)S(1)} %get-tuple-element.100), channel_id=1, source_target_pairs={{1,16},{2,19},{16,1},{19,2},{5,20},{6,23},{20,5},{23,6},{9,24},{10... | collective-permute-start | bytes 1572872 | tf_op jit(solution)/shard_map/ppermute | solution.py:29
  (49 other events, 320.5 us)

commit v3 on v2

v3 whole, which is shorter than its diff:
```python
import jax
import jax.numpy as jnp
from jax import lax
from jax.experimental import pallas as pl
from jax.experimental.pallas import tpu as pltpu
from jax.sharding import Mesh, PartitionSpec as P

learn_rate = 0.001
weight_decay = 0.1
first_decay = 0.9
second_decay = 0.95
adam_floor = 1e-08
outer_rate = 0.7
outer_decay = 0.9

bf16, f32 = jnp.bfloat16, jnp.float32

HOME = (0, 1, 1, 0)
SWAP = [(c * 4 + x, (1 - c) * 4 + (x ^ 1)) for c in range(2) for x in range(4) if c != HOME[x]]
CORE = [(0, 1), (1, 0)]
ACROSS = [(x, 3 - x) for x in range(4)]
BESIDE = [(x, x ^ 1) for x in range(4)]
ENDS_OUT = [(1, 0), (2, 3)]
PAIRS = [(0, 1), (1, 0), (2, 3), (3, 2)]
MIDDLE = [(1, 2), (2, 1)]
ORDER = ((3, 2, 1, 0), (3, 2, 0, 1), (0, 1, 3, 2), (0, 1, 2, 3))


def swap(v):
    return lax.ppermute(v, ("c", "x"), SWAP)


def core(v):
    return lax.ppermute(v, "c", CORE)


def beside(v):
    return lax.ppermute(v, "x", BESIDE)


def across(v):
    return lax.ppermute(v, "x", ACROSS)


def line(v, pairs):
    return lax.ppermute(v, "zl", pairs)


def dot(a, b):
    return jnp.dot(a, b, preferred_element_type=f32)


def dot_t(a, b):
    return lax.dot_general(a, b, (((0,), (0,)), ((), ())), preferred_element_type=f32)


def together(*arrays):
    return lax.optimization_barrier(arrays)


def move(_, a, b, to_a, to_b):
    to_a[0] = a[...]
    to_b[0] = b[...]


def halves(tokens, blocks):
    spec = lambda i: pl.BlockSpec((512, 256), lambda n, table: (0, table[i, n]))
    out = pl.BlockSpec((1, 512, 256), lambda n, table: (n // 2, 0, n % 2))
    kind = jax.ShapeDtypeStruct((4, 512, 512), bf16)
    return pl.pallas_call(
        move,
        grid_spec=pltpu.PrefetchScalarGridSpec(
            num_scalar_prefetch=1,
            grid=(8,),
            in_specs=[spec(0), spec(1)],
            out_specs=[out, out],
        ),
        out_shape=[kind, kind],
        cost_estimate=pl.CostEstimate(flops=0, bytes_accessed=16 << 20, transcendentals=0),
    )(blocks, tokens, tokens)


class Drift:
    def __init__(self, own, c, y):
        near = [(i, i ^ 1) for i in range(4)]
        wide = [(i, i ^ 2) for i in range(4)]
        self.v = own
        self.steps = [("c", CORE, c), ("y", near, y % 2), ("y", wide, y // 2), ("zh", CORE, c)]
        self.at = 0

    def send(self):
        if self.at < 3:
            bit = self.steps[self.at][2]
            n = self.v.shape[0] // 2
            self.sent = lax.dynamic_slice_in_dim(self.v, (1 - bit) * n, n, 0)
        elif self.at == 3:
            (self.sent,) = together(self.v.astype(bf16))
        else:
            self.sent = self.v
        axis, perm, _ = self.steps[min(self.at, 6 - self.at)]
        return lax.ppermute(self.sent, axis, perm)

    def take(self, got):
        bit = self.steps[min(self.at, 6 - self.at)][2]
        v = self.v
        if self.at < 3:
            n = v.shape[0] // 2
            self.v = lax.dynamic_slice_in_dim(v, bit * n, n, 0) + got
        elif self.at == 3:
            self.v = self.sent.astype(f32) + got.astype(f32)
        else:
            self.v = jnp.where(bit == 0, jnp.concatenate([v, got]), jnp.concatenate([got, v]))
        self.at += 1


def on_device(
    tokens, key_grad, key_weight, adam_first, adam_second, local_params, anchor, outer_momentum
):
    c, x, z, y = (lax.axis_index(a) for a in ("c", "x", "zl", "y"))
    weight = key_weight[0]
    stays = c == jnp.where((x == 1) | (x == 2), 1, 0)
    end = (z == 0) | (z == 3)
    mine = jnp.where(x < 2, c, 3 - c)
    theirs = jnp.where(x < 2, 1 - c, 2 + c)
    order = [
        jnp.where(z < 2, 3, 0),
        jnp.where(z < 2, 2, 1),
        jnp.where(z == 0, 1, jnp.where(z == 1, 0, jnp.where(z == 2, 3, 2))),
        z,
    ]
    blocks = jnp.stack(
        [4 * order[k] + q for half in (theirs, mine) for k in range(4) for q in (half, 3 - half)]
    ).reshape(2, 8)

    w = jnp.where(stays, weight, swap(weight))
    g_sib = core(key_grad)
    x_give, x_own = halves(tokens, blocks.astype(jnp.int32))
    x_sib = core(x_give)
    drift = Drift(anchor - local_params[0].astype(f32), c, y)
    drift.take(drift.send())
    g_a = jnp.where(stays, key_grad, g_sib)
    g_l = lax.dynamic_slice_in_dim(jnp.where(stays, g_sib, key_grad), c * 256, 256, 0)

    got = (beside(g_l), line(w, PAIRS), line(w, MIDDLE), across(w), drift.send())
    leave = [jnp.where(stays, x_sib[k], x_own[k]) for k in range(4)]
    keep = [jnp.where(stays, x_own[k], x_sib[k]) for k in range(4)]
    got, leave, drift.v = together(got, leave, drift.v)
    g_half, e_own, m_own, q_own, d = got
    drift.take(d)

    got = (beside(leave[0]), line(m_own, ENDS_OUT), line(e_own, MIDDLE), across(e_own), drift.send())
    g_rest = core(g_half)
    g_b = jnp.where(
        c == 0, jnp.concatenate([g_half, g_rest]), jnp.concatenate([g_rest, g_half])
    )
    base = [dot_t(k, g_a) for k in keep]
    sent = drift.v
    got, leave, sent, g_b, base = together(got, leave, sent, g_b, base)
    drift.v = sent
    x_b = [got[0]]
    _, e2, m2, q2, d = got
    drift.take(d)
    mid = jnp.where(end, e2, m_own)

    def going(k):
        return (base[k][256:] + dot_t(x_b[k][:, 256:], g_b)).astype(bf16)

    def staying(k):
        return base[k][:256] + dot_t(x_b[k][:, :256], g_b)

    def cat(*arrays):
        return jnp.concatenate(arrays, axis=-1)

    got = (beside(leave[1]), line(m2, ENDS_OUT), line(q_own, MIDDLE), across(going(0)), drift.send())
    rows = [None, None, jnp.concatenate([e_own, q2]), jnp.concatenate([w, q_own])]
    k_a = dot(cat(keep[2], keep[3]), jnp.concatenate(rows[2:]))
    stay = staying(0)
    got, leave, drift.v, drift.sent, stay, k_a = together(got, leave, drift.v, drift.sent, stay, k_a)
    x_b.append(got[0])
    _, e3, m3, q3, d = got
    drift.take(d)
    part0 = stay + q3.astype(f32)

    got = (
        beside(leave[2]),
        line(jnp.where(end, part0.astype(bf16), m3), PAIRS),
        line(q2, MIDDLE),
        across(going(1)),
        drift.send(),
    )
    stay = staying(1)
    got, leave, drift.v, stay, part0 = together(got, leave, drift.v, stay, part0)
    x_b.append(got[0])
    _, e4, m4, q4, d = got
    drift.take(d)
    part1 = stay + q4.astype(f32)

    got = (
        beside(leave[3]),
        line(jnp.where(end, part1.astype(bf16), m4), PAIRS),
        line((part0 + e4.astype(f32)).astype(bf16), MIDDLE),
        across(going(2)),
        drift.send(),
    )
    rows[1] = jnp.concatenate([mid, jnp.where(end, e4, m3)])
    k_a = k_a + dot(keep[1], rows[1])
    k_b = dot(cat(x_b[1], x_b[2]), jnp.concatenate(rows[1:3]))
    stay = staying(2)
    got, drift.v, stay, part1, k_a, k_b = together(got, drift.v, stay, part1, k_a, k_b)
    x_b.append(got[0])
    _, e5, m5, q5, d = got
    drift.take(d)
    part2 = stay + q5.astype(f32)

    got = (
        line((part2 + m5.astype(f32)).astype(bf16), PAIRS),
        line((part1 + e5.astype(f32)).astype(bf16), MIDDLE),
        across(going(3)),
    )
    rows[0] = jnp.concatenate([jnp.where(end, e3, m2), jnp.where(end, e5, m4)])
    k_a = k_a + dot(keep[0], rows[0])
    k_b = k_b + dot(cat(x_b[0], x_b[3]), jnp.concatenate([rows[0], rows[3]]))
    k_got = core(jnp.where(stays, k_b, k_a).astype(bf16))
    keys_work = (jnp.where(stays, k_a, k_b) + k_got.astype(f32)).astype(bf16)
    keys = jnp.where(stays, keys_work, swap(keys_work))
    e6, m6, q6 = got
    total = staying(3) + q6.astype(f32) + e6.astype(f32) + m6.astype(f32)
    gradient = jnp.where(stays, total, swap(total.astype(bf16)).astype(f32))
    drift.take(drift.send())

    new_first = first_decay * adam_first[0] + (1.0 - first_decay) * gradient
    new_second = second_decay * adam_second[0] + (1.0 - second_decay) * gradient * gradient
    master = weight.astype(f32)
    update = new_first / (jnp.sqrt(new_second) + adam_floor) + weight_decay * master
    new_weight = (master - learn_rate * update).astype(bf16)

    mean = drift.v / 16
    new_momentum = outer_decay * outer_momentum + mean
    new_anchor = anchor - outer_rate * (mean + outer_decay * new_momentum)
    return (keys, new_weight[None], new_first[None], new_second[None], new_anchor, new_momentum)


def solution(mesh):
    fine = Mesh(mesh.devices.reshape(2, 4, 2, 4, 4), ("zh", "y", "c", "zl", "x"))
    replica, fsdp = ("zh", "y", "c"), ("zl", "x")
    tokens, stacked, shared = P(replica + fsdp, None), P(replica, fsdp, None), P(fsdp, None)
    return jax.shard_map(
        on_device,
        mesh=fine,
        in_specs=(tokens, tokens, stacked, stacked, stacked, stacked, shared, shared),
        out_specs=(tokens, stacked, stacked, stacked, shared, shared),
        check_vma=False,
    )
```

time: 199 us -> 159 us (0.80)
  local copies, waits for them, and re-layouts: 29.7 us -> 1.65 us
  other arithmetic: 30.1 us -> 17.4 us
  matrix products: 19.9 us -> 12 us
  Pallas kernels: 0 us -> 7.37 us
  waiting for transfers between devices: 53.7 us -> 56.8 us
    unnamed x84 -> x10, local copies, waits for them, and re-layouts: 19.4 us -> 0.03 us
    ppermute x6, waiting for transfers between devices: 6.38 us -> 19.2 us  [across(): return lax.ppermute(v, 'x', ACROSS)]
    ppermute x12, waiting for transfers between devices: 2.58 us -> 11.2 us  [line(): return lax.ppermute(v, 'zl', pairs)]
    pallas_call x0 -> x1, Pallas kernels: none -> 7.37 us  [halves(): pl.pallas_call(move, grid_spec=pltpu.PrefetchScalarGridSpec(num_scalar_pr...]
    select_n x9 -> x7, other arithmetic: 9.37 us -> 2.14 us  [the longest x1 1.11 us: on_device(): keys = jnp.where(stays, keys_work, swap(keys_work))]
    ppermute x5, waiting for transfers between devices: 11.6 us -> 5.14 us  [beside(): return lax.ppermute(v, 'x', BESIDE)]
    ppermute x3, waiting for transfers between devices: 19.2 us -> 12.7 us  [swap(): return lax.ppermute(v, ('c', 'x'), SWAP)]
    slice x24 -> x0, local copies, waits for them, and re-layouts: 6.46 us -> none  [the longest x1 1.25 us: on_device(): leave = [x_l[:, 512 * k:512 * k + 512] for k in range(4)]]
  transfers between devices with their start and end apart: 38 -> 37, of which waited for: 13 -> 15; matrix products, arithmetic and copies ran while one was open for 23% -> 17% of each run, Pallas kernels for 0% -> 0%
where the time goes in v3:
time: 159 us; the launch traced here: 158 us
  starting transfers between devices  62 us (39%)
  waiting for transfers between devices  56.8 us (36%)
  other arithmetic  17.4 us (11%)
  matrix products  12 us (8%)
  Pallas kernels  7.37 us (5%)
  local copies, waits for them, and re-layouts  1.65 us (1%)
    ppermute x6, waiting for transfers between devices, across(): return lax.ppermute(v, 'x', ACROSS)  19.2 us
    ppermute x12, starting transfers between devices, line(): return lax.ppermute(v, 'zl', pairs)  18.5 us
    ppermute x7, starting transfers between devices, send(): return lax.ppermute(self.sent, axis, perm)  14.5 us
    ppermute x3, waiting for transfers between devices, swap(): return lax.ppermute(v, ('c', 'x'), SWAP)  12.7 us
    ppermute x12, waiting for transfers between devices, line(): return lax.ppermute(v, 'zl', pairs)  11.2 us
    ppermute x4, starting transfers between devices, core(): return lax.ppermute(v, 'c', CORE)  10.6 us
    ppermute x3, starting transfers between devices, swap(): return lax.ppermute(v, ('c', 'x'), SWAP)  8.73 us
    ppermute x7, waiting for transfers between devices, send(): return lax.ppermute(self.sent, axis, perm)  8.57 us
  transfers between devices with their start and end apart: 37, of which 15 were waited for; matrix products, arithmetic and copies ran while one was open for 17% of the time, Pallas kernels for 0%

profile of v3, /device:TPU:1, one launch (start us, length us, event | category | flops | bytes accessed | tf_op | source)
XLA Modules:
  0.0 158.4 jit_solution(6914363055146916183)
XLA Ops:
  1.4 7.4 %shard_map.127 = (bf16[4,512,512]{2,1,0:T(8,128)(2,1)}, bf16[4,512,512]{2,1,0:T(8,128)(2,1)}) custom-call(s32[2,8]{1,0:T(2,128)} %reshape.37._, bf16[512,4096]{1,0:T(8,128)(2,1)} %b.1, bf16[512,4096]{1,0:T(8,128)(2,1)} %b.1), custom_call_target="tpu_custom_call" | custom-call | bytes 16777216 | tf_op jit(solution)/shard_map/pallas_call | solution.py:70
  8.8 3.2 %collective-permute-start.8 = (bf16[4,512,512]{2,1,0:T(8,128)(2,1)}, bf16[4,512,512]{2,1,0:T(8,128)(2,1)S(1)}, u32[]{:S(2)}, u32[]{:S(2)}) collective-permute-start(bf16[4,512,512]{2,1,0:T(8,128)(2,1)} %get-tuple-element.61), channel_id=1, source_target_pairs={{0,16},{16,0},{1,17},{17,1},{2,18},{18,2},{3,19},{19,3},{4,20},{20... | collective-permute-start | bytes 6291464 | tf_op jit(solution)/shard_map/ppermute | solution.py:34
  12.0 1.9 %collective-permute-start.2 = (bf16[256,1024]{1,0:T(8,128)(2,1)}, bf16[256,1024]{1,0:T(8,128)(2,1)}, u32[]{:S(2)}, u32[]{:S(2)}) collective-permute-start(bf16[256,1024]{1,0:T(8,128)(2,1)} %bitcast), channel_id=1, source_target_pairs={{1,16},{2,19},{16,1},{19,2},{5,20},{6,23},{20,5},{23,6},{9,24},{10... | collective-permute-start | bytes 1572872 | tf_op jit(solution)/shard_map/ppermute | solution.py:30
  14.1 1.5 convert_subtract_fusion.1
  16.9 6.1 %collective-permute-done.2 = bf16[256,1024]{1,0:T(8,128)(2,1)} collective-permute-done((bf16[256,1024]{1,0:T(8,128)(2,1)}, bf16[256,1024]{1,0:T(8,128)(2,1)}, u32[]{:S(2)}, u32[]{:S(2)}) %collective-permute-start.2) | collective-permute-done | bytes 524320 | tf_op jit(solution)/shard_map/ppermute | solution.py:30
  25.8 4.6 %collective-permute-start.3 = (bf16[256,1024]{1,0:T(8,128)(2,1)S(1)}, bf16[256,1024]{1,0:T(8,128)(2,1)S(1)}, u32[]{:S(2)}, u32[]{:S(2)}) collective-permute-start(bf16[256,1024]{1,0:T(8,128)(2,1)S(1)} %broadcast_select_fusion.2), channel_id=1, source_target_pairs={{0,4},{4,0},{8,12},{12,8},{1,5},{5,1},{9,13},{13,9},{2,6},{6,2},{1... | collective-permute-start | bytes 1572872 | tf_op jit(solution)/shard_map/ppermute | solution.py:46
  31.6 1.5 dynamic-slice_select_fusion
  34.6 1.4 collective-permute-start.7
  36.3 5.3 %collective-permute-done.7 = f32[64,1024]{1,0:T(8,128)S(1)} collective-permute-done((f32[64,1024]{1,0:T(8,128)S(1)}, f32[64,1024]{1,0:T(8,128)S(1)}, u32[]{:S(2)}, u32[]{:S(2)}) %collective-permute-start.7) | collective-permute-done | bytes 262176 | tf_op jit(solution)/shard_map/ppermute | solution.py:101
  41.6 4.5 %collective-permute-done.1 = bf16[256,1024]{1,0:T(8,128)(2,1)S(1)} collective-permute-done((bf16[256,1024]{1,0:T(8,128)(2,1)S(1)}, bf16[256,1024]{1,0:T(8,128)(2,1)S(1)}, u32[]{:S(2)}, u32[]{:S(2)}) %collective-permute-start.1) | collective-permute-done | bytes 524320 | tf_op jit(solution)/shard_map/ppermute | solution.py:38
  53.1 3.0 %collective-permute-start.13 = (f32[32,1024]{1,0:T(8,128)S(1)}, f32[32,1024]{1,0:T(8,128)S(1)}, u32[]{:S(2)}, u32[]{:S(2)}) collective-permute-start(f32[32,1024]{1,0:T(8,128)S(1)} %constant_dynamic-slice_fusion), channel_id=1, source_target_pairs={{0,64},{32,96},{64,0},{96,32},{1,65},{33,97},{65,1},{97,33},{2,66}... | collective-permute-start | bytes 393224 | tf_op jit(solution)/shard_map/ppermute | solution.py:101
  56.6 3.2 %collective-permute-done.13 = f32[32,1024]{1,0:T(8,128)S(1)} collective-permute-done((f32[32,1024]{1,0:T(8,128)S(1)}, f32[32,1024]{1,0:T(8,128)S(1)}, u32[]{:S(2)}, u32[]{:S(2)}) %collective-permute-start.13) | collective-permute-done | bytes 131104 | tf_op jit(solution)/shard_map/ppermute | solution.py:101
  60.5 1.8 %collective-permute-done.10 = bf16[256,1024]{1,0:T(8,128)(2,1)S(1)} collective-permute-done((bf16[256,1024]{1,0:T(8,128)(2,1)S(1)}, bf16[256,1024]{1,0:T(8,128)(2,1)S(1)}, u32[]{:S(2)}, u32[]{:S(2)}) %collective-permute-start.10) | collective-permute-done | bytes 524320 | tf_op jit(solution)/shard_map/ppermute | solution.py:46
  63.3 5.2 %collective-permute-start.19 = (bf16[32,1024]{1,0:T(8,128)(2,1)S(1)}, bf16[32,1024]{1,0:T(8,128)(2,1)S(1)}, u32[]{:S(2)}, u32[]{:S(2)}) collective-permute-start(bf16[32,1024]{1,0:T(8,128)(2,1)S(1)} %dynamic-slice_add_fusion.2), channel_id=1, source_target_pairs={{0,128},{128,0},{1,129},{129,1},{2,130},{130,2},{3,131},{131,3},{4... | collective-permute-start | bytes 196616 | tf_op jit(solution)/shard_map/ppermute | solution.py:101
  69.8 1.6 %collective-permute-start.15 = (bf16[512,512]{1,0:T(8,128)(2,1)S(1)}, bf16[512,512]{1,0:T(8,128)(2,1)S(1)}, u32[]{:S(2)}, u32[]{:S(2)}) collective-permute-start(bf16[512,512]{1,0:T(8,128)(2,1)S(1)} %get-tuple-element.72), channel_id=1, source_target_pairs={{0,1},{1,0},{2,3},{3,2},{4,5},{5,4},{6,7},{7,6},{8,9},{9,8},{10,11... | collective-permute-start | bytes 1572872 | tf_op jit(solution)/shard_map/ppermute | solution.py:38
  74.7 6.4 %collective-permute-done.18 = bf16[256,1024]{1,0:T(8,128)(2,1)S(1)} collective-permute-done((bf16[256,1024]{1,0:T(8,128)(2,1)S(1)}, bf16[256,1024]{1,0:T(8,128)(2,1)S(1)}, u32[]{:S(2)}, u32[]{:S(2)}) %collective-permute-start.18) | collective-permute-done | bytes 524320 | tf_op jit(solution)/shard_map/ppermute | solution.py:42
  81.1 3.3 %collective-permute-done.16 = bf16[256,1024]{1,0:T(8,128)(2,1)S(1)} collective-permute-done((bf16[256,1024]{1,0:T(8,128)(2,1)S(1)}, bf16[256,1024]{1,0:T(8,128)(2,1)S(1)}, u32[]{:S(2)}, u32[]{:S(2)}) %collective-permute-start.16) | collective-permute-done | bytes 524320 | tf_op jit(solution)/shard_map/ppermute | solution.py:46
  84.4 3.0 %collective-permute-start.24 = (f32[32,1024]{1,0:T(8,128)S(1)}, f32[32,1024]{1,0:T(8,128)S(1)}, u32[]{:S(2)}, u32[]{:S(2)}) collective-permute-start(f32[32,1024]{1,0:T(8,128)S(1)} %convert_add_fusion.3), channel_id=1, source_target_pairs={{0,64},{32,96},{64,0},{96,32},{1,65},{33,97},{65,1},{97,33},{2,66}... | collective-permute-start | bytes 393224 | tf_op jit(solution)/shard_map/ppermute | solution.py:101
  87.9 1.9 %collective-permute-start.23 = (bf16[256,1024]{1,0:T(8,128)(2,1)S(1)}, bf16[256,1024]{1,0:T(8,128)(2,1)S(1)}, u32[]{:S(2)}, u32[]{:S(2)}) collective-permute-start(bf16[256,1024]{1,0:T(8,128)(2,1)S(1)} %add_convert_fusion.6), channel_id=1, source_target_pairs={{0,3},{1,2},{2,1},{3,0},{4,7},{5,6},{6,5},{7,4},{8,11},{9,10},{10,... | collective-permute-start | bytes 1572872 | tf_op jit(solution)/shard_map/ppermute | solution.py:42
  91.3 7.7 %collective-permute-done.23 = bf16[256,1024]{1,0:T(8,128)(2,1)S(1)} collective-permute-done((bf16[256,1024]{1,0:T(8,128)(2,1)S(1)}, bf16[256,1024]{1,0:T(8,128)(2,1)S(1)}, u32[]{:S(2)}, u32[]{:S(2)}) %collective-permute-start.23) | collective-permute-done | bytes 524320 | tf_op jit(solution)/shard_map/ppermute | solution.py:42
  104.5 3.1 %collective-permute-start.26 = (bf16[256,1024]{1,0:T(8,128)(2,1)S(1)}, bf16[256,1024]{1,0:T(8,128)(2,1)S(1)}, u32[]{:S(2)}, u32[]{:S(2)}) collective-permute-start(bf16[256,1024]{1,0:T(8,128)(2,1)S(1)} %get-tuple-element.120), channel_id=1, source_target_pairs={{0,4},{4,0},{8,12},{12,8},{1,5},{5,1},{9,13},{13,9},{2,6},{6,2},{1... | collective-permute-start | bytes 1572872 | tf_op jit(solution)/shard_map/ppermute | solution.py:46
  110.7 1.7 %collective-permute-done.28 = bf16[256,1024]{1,0:T(8,128)(2,1)S(1)} collective-permute-done((bf16[256,1024]{1,0:T(8,128)(2,1)S(1)}, bf16[256,1024]{1,0:T(8,128)(2,1)S(1)}, u32[]{:S(2)}, u32[]{:S(2)}) %collective-permute-start.28) | collective-permute-done | bytes 524320 | tf_op jit(solution)/shard_map/ppermute | solution.py:42
  112.4 2.1 %collective-permute-done.26 = bf16[256,1024]{1,0:T(8,128)(2,1)S(1)} collective-permute-done((bf16[256,1024]{1,0:T(8,128)(2,1)S(1)}, bf16[256,1024]{1,0:T(8,128)(2,1)S(1)}, u32[]{:S(2)}, u32[]{:S(2)}) %collective-permute-start.26) | collective-permute-done | bytes 524320 | tf_op jit(solution)/shard_map/ppermute | solution.py:46
  116.7 6.3 %collective-permute-start.30 = (bf16[512,1024]{1,0:T(8,128)(2,1)S(1)}, bf16[512,1024]{1,0:T(8,128)(2,1)S(1)}, u32[]{:S(2)}, u32[]{:S(2)}) collective-permute-start(bf16[512,1024]{1,0:T(8,128)(2,1)S(1)} %get-tuple-element.133), channel_id=1, source_target_pairs={{0,16},{16,0},{1,17},{17,1},{2,18},{18,2},{3,19},{19,3},{4,20},{20... | collective-permute-start | bytes 3145736 | tf_op jit(solution)/shard_map/ppermute | solution.py:34
  125.8 3.7 %collective-permute-start.33 = (bf16[256,1024]{1,0:T(8,128)(2,1)S(1)}, bf16[256,1024]{1,0:T(8,128)(2,1)S(1)}, u32[]{:S(2)}, u32[]{:S(2)}) collective-permute-start(bf16[256,1024]{1,0:T(8,128)(2,1)S(1)} %add_convert_fusion.2), channel_id=1, source_target_pairs={{0,4},{4,0},{8,12},{12,8},{1,5},{5,1},{9,13},{13,9},{2,6},{6,2},{1... | collective-permute-start | bytes 1572872 | tf_op jit(solution)/shard_map/ppermute | solution.py:46
  132.1 2.9 %collective-permute-start.31 = (bf16[512,1024]{1,0:T(8,128)(2,1)S(1)}, bf16[512,1024]{1,0:T(8,128)(2,1)S(1)}, u32[]{:S(2)}, u32[]{:S(2)}) collective-permute-start(bf16[512,1024]{1,0:T(8,128)(2,1)S(1)} %add_convert_fusion), channel_id=1, source_target_pairs={{1,16},{2,19},{16,1},{19,2},{5,20},{6,23},{20,5},{23,6},{9,24},{10... | collective-permute-start | bytes 3145736 | tf_op jit(solution)/shard_map/ppermute | solution.py:30
  134.9 3.4 %collective-permute-done.32 = bf16[256,1024]{1,0:T(8,128)(2,1)S(1)} collective-permute-done((bf16[256,1024]{1,0:T(8,128)(2,1)S(1)}, bf16[256,1024]{1,0:T(8,128)(2,1)S(1)}, u32[]{:S(2)}, u32[]{:S(2)}) %collective-permute-start.32) | collective-permute-done | bytes 524320 | tf_op jit(solution)/shard_map/ppermute | solution.py:42
  138.3 2.9 %collective-permute-done.33 = bf16[256,1024]{1,0:T(8,128)(2,1)S(1)} collective-permute-done((bf16[256,1024]{1,0:T(8,128)(2,1)S(1)}, bf16[256,1024]{1,0:T(8,128)(2,1)S(1)}, u32[]{:S(2)}, u32[]{:S(2)}) %collective-permute-start.33) | collective-permute-done | bytes 524320 | tf_op jit(solution)/shard_map/ppermute | solution.py:46
  141.7 4.0 %collective-permute-start.35 = (bf16[256,1024]{1,0:T(8,128)(2,1)S(1)}, bf16[256,1024]{1,0:T(8,128)(2,1)S(1)}, u32[]{:S(2)}, u32[]{:S(2)}) collective-permute-start(bf16[256,1024]{1,0:T(8,128)(2,1)S(1)} %get-tuple-element.118), channel_id=1, source_target_pairs={{1,16},{2,19},{16,1},{19,2},{5,20},{6,23},{20,5},{23,6},{9,24},{10... | collective-permute-start | bytes 1572872 | tf_op jit(solution)/shard_map/ppermute | solution.py:30
  145.6 1.7 %multiply_subtract_fusion = (f32[256,1024]{1,0:T(8,128)}, f32[256,1024]{1,0:T(8,128)}) fusion(f32[256,1024]{1,0:T(8,128)S(1)} %copy-done.1, f32[128,1024]{1,0:T(8,128)S(1)} %maximum_select_fusion.2, f32[128,1024]{1,0:T(8,128)S(1)} %collective-permute-done.36, pred[]{:T(512)S(6)} %eq.40, f32[256,1024]{1,0:T(8,128)S(1)} %copy-done.2), kind=kLoop, calls=%fused_computation.51 | loop fusion | flops 2621440 | bytes 5242881 | tf_op jit(solution)/shard_map/sub | solution.py:239
  147.4 6.5 %collective-permute-done.35 = bf16[256,1024]{1,0:T(8,128)(2,1)S(1)} collective-permute-done((bf16[256,1024]{1,0:T(8,128)(2,1)S(1)}, bf16[256,1024]{1,0:T(8,128)(2,1)S(1)}, u32[]{:S(2)}, u32[]{:S(2)}) %collective-permute-start.35) | collective-permute-done | bytes 524320 | tf_op jit(solution)/shard_map/ppermute | solution.py:30
  153.9 3.4 %fusion.81 = (f32[1,256,1024]{2,1,0:T(8,128)}, bf16[1,256,1024]{2,1,0:T(8,128)(2,1)}, f32[1,256,1024]{2,1,0:T(8,128)}) fusion(f32[256,1024]{1,0:T(8,128)S(1)} %get-tuple-element.119, bf16[256,1024]{1,0:T(8,128)(2,1)S(1)} %collective-permute-done.35, pred[]{:T(512)S(6)} %eq.36, f32[1,256,1024]{2,1,0:T(8,128)S(1)} %copy-done.3, ...), kind=kLoop, calls=%fused_computation.123 | loop fusion | flops 4456448 | bytes 6815745 | tf_op jit(solution)/shard_map/broadcast_in_dim | solution.py:240
  (102 shorter events, 40.9 us)
Async XLA Ops:
  8.8 25.8 %collective-permute-start.8 = (bf16[4,512,512]{2,1,0:T(8,128)(2,1)}, bf16[4,512,512]{2,1,0:T(8,128)(2,1)S(1)}, u32[]{:S(2)}, u32[]{:S(2)}) collective-permute-start(bf16[4,512,512]{2,1,0:T(8,128)(2,1)} %get-tuple-element.61), channel_id=1, source_target_pairs={{0,16},{16,0},{1,17},{17,1},{2,18},{18,2},{3,19},{19,3},{4,20},{20... | collective-permute-start | bytes 6291464 | tf_op jit(solution)/shard_map/ppermute | solution.py:34
  12.0 11.0 %collective-permute-start.2 = (bf16[256,1024]{1,0:T(8,128)(2,1)}, bf16[256,1024]{1,0:T(8,128)(2,1)}, u32[]{:S(2)}, u32[]{:S(2)}) collective-permute-start(bf16[256,1024]{1,0:T(8,128)(2,1)} %bitcast), channel_id=1, source_target_pairs={{1,16},{2,19},{16,1},{19,2},{5,20},{6,23},{20,5},{23,6},{9,24},{10... | collective-permute-start | bytes 1572872 | tf_op jit(solution)/shard_map/ppermute | solution.py:30
  14.0 17.6 %collective-permute-start = (bf16[512,1024]{1,0:T(8,128)(2,1)}, bf16[512,1024]{1,0:T(8,128)(2,1)}, u32[]{:S(2)}, u32[]{:S(2)}) collective-permute-start(bf16[512,1024]{1,0:T(8,128)(2,1)} %param.9), channel_id=1, source_target_pairs={{0,16},{16,0},{1,17},{17,1},{2,18},{18,2},{3,19},{19,3},{4,20},{20... | collective-permute-start | bytes 3145736 | tf_op jit(solution)/shard_map/ppermute | solution.py:34
  16.4 9.4 %collective-permute-start.6 = (f32[128,1024]{1,0:T(8,128)}, f32[128,1024]{1,0:T(8,128)}, u32[]{:S(2)}, u32[]{:S(2)}) collective-permute-start(f32[128,1024]{1,0:T(8,128)} %constant_dynamic-slice_fusion.2), channel_id=1, source_target_pairs={{0,16},{16,0},{1,17},{17,1},{2,18},{18,2},{3,19},{19,3},{4,20},{20... | collective-permute-start | bytes 1572872 | tf_op jit(solution)/shard_map/ppermute | solution.py:101
  24.3 17.3 %collective-permute-start.5 = (bf16[256,1024]{1,0:T(8,128)(2,1)S(1)}, bf16[256,1024]{1,0:T(8,128)(2,1)S(1)}, u32[]{:S(2)}, u32[]{:S(2)}) collective-permute-start(bf16[256,1024]{1,0:T(8,128)(2,1)S(1)} %broadcast_select_fusion.2), channel_id=1, source_target_pairs={{0,3},{1,2},{2,1},{3,0},{4,7},{5,6},{6,5},{7,4},{8,11},{9,10},{10,... | collective-permute-start | bytes 1572872 | tf_op jit(solution)/shard_map/ppermute | solution.py:42
  25.1 16.5 %collective-permute-start.4 = (bf16[256,1024]{1,0:T(8,128)(2,1)S(1)}, bf16[256,1024]{1,0:T(8,128)(2,1)S(1)}, u32[]{:S(2)}, u32[]{:S(2)}) collective-permute-start(bf16[256,1024]{1,0:T(8,128)(2,1)S(1)} %broadcast_select_fusion.2), channel_id=1, source_target_pairs={{4,8},{8,4},{5,9},{9,5},{6,10},{10,6},{7,11},{11,7},{20,24},{24,20... | collective-permute-start | bytes 1572872 | tf_op jit(solution)/shard_map/ppermute | solution.py:46
  25.8 15.8 %collective-permute-start.3 = (bf16[256,1024]{1,0:T(8,128)(2,1)S(1)}, bf16[256,1024]{1,0:T(8,128)(2,1)S(1)}, u32[]{:S(2)}, u32[]{:S(2)}) collective-permute-start(bf16[256,1024]{1,0:T(8,128)(2,1)S(1)} %broadcast_select_fusion.2), channel_id=1, source_target_pairs={{0,4},{4,0},{8,12},{12,8},{1,5},{5,1},{9,13},{13,9},{2,6},{6,2},{1... | collective-permute-start | bytes 1572872 | tf_op jit(solution)/shard_map/ppermute | solution.py:46
  33.1 13.1 %collective-permute-start.1 = (bf16[256,1024]{1,0:T(8,128)(2,1)S(1)}, bf16[256,1024]{1,0:T(8,128)(2,1)S(1)}, u32[]{:S(2)}, u32[]{:S(2)}) collective-permute-start(bf16[256,1024]{1,0:T(8,128)(2,1)S(1)} %dynamic-slice_select_fusion), channel_id=1, source_target_pairs={{0,1},{1,0},{2,3},{3,2},{4,5},{5,4},{6,7},{7,6},{8,9},{9,8},{10,11... | collective-permute-start | bytes 1572872 | tf_op jit(solution)/shard_map/ppermute | solution.py:38
  46.2 16.2 %collective-permute-start.12 = (bf16[256,1024]{1,0:T(8,128)(2,1)S(1)}, bf16[256,1024]{1,0:T(8,128)(2,1)S(1)}, u32[]{:S(2)}, u32[]{:S(2)}) collective-permute-start(bf16[256,1024]{1,0:T(8,128)(2,1)S(1)} %collective-permute-done.3), channel_id=1, source_target_pairs={{0,3},{1,2},{2,1},{3,0},{4,7},{5,6},{6,5},{7,4},{8,11},{9,10},{10,... | collective-permute-start | bytes 1572872 | tf_op jit(solution)/shard_map/ppermute | solution.py:42
  47.0 15.3 %collective-permute-start.11 = (bf16[256,1024]{1,0:T(8,128)(2,1)S(1)}, bf16[256,1024]{1,0:T(8,128)(2,1)S(1)}, u32[]{:S(2)}, u32[]{:S(2)}) collective-permute-start(bf16[256,1024]{1,0:T(8,128)(2,1)S(1)} %collective-permute-done.3), channel_id=1, source_target_pairs={{4,8},{8,4},{5,9},{9,5},{6,10},{10,6},{7,11},{11,7},{20,24},{24,20... | collective-permute-start | bytes 1572872 | tf_op jit(solution)/shard_map/ppermute | solution.py:46
  47.7 12.8 %collective-permute-start.9 = (bf16[512,512]{1,0:T(8,128)(2,1)S(1)}, bf16[512,512]{1,0:T(8,128)(2,1)S(1)}, u32[]{:S(2)}, u32[]{:S(2)}) collective-permute-start(bf16[512,512]{1,0:T(8,128)(2,1)S(1)} %get-tuple-element.63), channel_id=1, source_target_pairs={{0,1},{1,0},{2,3},{3,2},{4,5},{5,4},{6,7},{7,6},{8,9},{9,8},{10,11... | collective-permute-start | bytes 1572872 | tf_op jit(solution)/shard_map/ppermute | solution.py:38
  47.8 14.5 %collective-permute-start.10 = (bf16[256,1024]{1,0:T(8,128)(2,1)S(1)}, bf16[256,1024]{1,0:T(8,128)(2,1)S(1)}, u32[]{:S(2)}, u32[]{:S(2)}) collective-permute-start(bf16[256,1024]{1,0:T(8,128)(2,1)S(1)} %collective-permute-done.4), channel_id=1, source_target_pairs={{4,0},{8,12},{5,1},{9,13},{6,2},{10,14},{7,3},{11,15},{20,16},{24,... | collective-permute-start | bytes 1572872 | tf_op jit(solution)/shard_map/ppermute | solution.py:46
  59.8 14.2 %collective-permute-start.17 = (bf16[256,1024]{1,0:T(8,128)(2,1)S(1)}, bf16[256,1024]{1,0:T(8,128)(2,1)S(1)}, u32[]{:S(2)}, u32[]{:S(2)}) collective-permute-start(bf16[256,1024]{1,0:T(8,128)(2,1)S(1)} %collective-permute-done.5), channel_id=1, source_target_pairs={{4,8},{8,4},{5,9},{9,5},{6,10},{10,6},{7,11},{11,7},{20,24},{24,20... | collective-permute-start | bytes 1572872 | tf_op jit(solution)/shard_map/ppermute | solution.py:46
  63.3 11.4 %collective-permute-start.19 = (bf16[32,1024]{1,0:T(8,128)(2,1)S(1)}, bf16[32,1024]{1,0:T(8,128)(2,1)S(1)}, u32[]{:S(2)}, u32[]{:S(2)}) collective-permute-start(bf16[32,1024]{1,0:T(8,128)(2,1)S(1)} %dynamic-slice_add_fusion.2), channel_id=1, source_target_pairs={{0,128},{128,0},{1,129},{129,1},{2,130},{130,2},{3,131},{131,3},{4... | collective-permute-start | bytes 196616 | tf_op jit(solution)/shard_map/ppermute | solution.py:101
  68.5 12.6 %collective-permute-start.18 = (bf16[256,1024]{1,0:T(8,128)(2,1)S(1)}, bf16[256,1024]{1,0:T(8,128)(2,1)S(1)}, u32[]{:S(2)}, u32[]{:S(2)}) collective-permute-start(bf16[256,1024]{1,0:T(8,128)(2,1)S(1)} %add_convert_fusion.7), channel_id=1, source_target_pairs={{0,3},{1,2},{2,1},{3,0},{4,7},{5,6},{6,5},{7,4},{8,11},{9,10},{10,... | collective-permute-start | bytes 1572872 | tf_op jit(solution)/shard_map/ppermute | solution.py:42
  69.8 11.3 %collective-permute-start.15 = (bf16[512,512]{1,0:T(8,128)(2,1)S(1)}, bf16[512,512]{1,0:T(8,128)(2,1)S(1)}, u32[]{:S(2)}, u32[]{:S(2)}) collective-permute-start(bf16[512,512]{1,0:T(8,128)(2,1)S(1)} %get-tuple-element.72), channel_id=1, source_target_pairs={{0,1},{1,0},{2,3},{3,2},{4,5},{5,4},{6,7},{7,6},{8,9},{9,8},{10,11... | collective-permute-start | bytes 1572872 | tf_op jit(solution)/shard_map/ppermute | solution.py:38
  71.4 13.0 %collective-permute-start.16 = (bf16[256,1024]{1,0:T(8,128)(2,1)S(1)}, bf16[256,1024]{1,0:T(8,128)(2,1)S(1)}, u32[]{:S(2)}, u32[]{:S(2)}) collective-permute-start(bf16[256,1024]{1,0:T(8,128)(2,1)S(1)} %collective-permute-done.11), channel_id=1, source_target_pairs={{4,0},{8,12},{5,1},{9,13},{6,2},{10,14},{7,3},{11,15},{20,16},{24,... | collective-permute-start | bytes 1572872 | tf_op jit(solution)/shard_map/ppermute | solution.py:46
  74.0 17.3 %collective-permute-start.22 = (bf16[256,1024]{1,0:T(8,128)(2,1)S(1)}, bf16[256,1024]{1,0:T(8,128)(2,1)S(1)}, u32[]{:S(2)}, u32[]{:S(2)}) collective-permute-start(bf16[256,1024]{1,0:T(8,128)(2,1)S(1)} %collective-permute-done.12), channel_id=1, source_target_pairs={{4,8},{8,4},{5,9},{9,5},{6,10},{10,6},{7,11},{11,7},{20,24},{24,20... | collective-permute-start | bytes 1572872 | tf_op jit(solution)/shard_map/ppermute | solution.py:46
  87.9 11.2 %collective-permute-start.23 = (bf16[256,1024]{1,0:T(8,128)(2,1)S(1)}, bf16[256,1024]{1,0:T(8,128)(2,1)S(1)}, u32[]{:S(2)}, u32[]{:S(2)}) collective-permute-start(bf16[256,1024]{1,0:T(8,128)(2,1)S(1)} %add_convert_fusion.6), channel_id=1, source_target_pairs={{0,3},{1,2},{2,1},{3,0},{4,7},{5,6},{6,5},{7,4},{8,11},{9,10},{10,... | collective-permute-start | bytes 1572872 | tf_op jit(solution)/shard_map/ppermute | solution.py:42
  90.0 10.2 %collective-permute-start.21 = (bf16[256,1024]{1,0:T(8,128)(2,1)S(1)}, bf16[256,1024]{1,0:T(8,128)(2,1)S(1)}, u32[]{:S(2)}, u32[]{:S(2)}) collective-permute-start(bf16[256,1024]{1,0:T(8,128)(2,1)S(1)} %get-tuple-element.122), channel_id=1, source_target_pairs={{0,4},{4,0},{8,12},{12,8},{1,5},{5,1},{9,13},{13,9},{2,6},{6,2},{1... | collective-permute-start | bytes 1572872 | tf_op jit(solution)/shard_map/ppermute | solution.py:46
  90.5 10.3 %collective-permute-start.20 = (bf16[512,512]{1,0:T(8,128)(2,1)S(1)}, bf16[512,512]{1,0:T(8,128)(2,1)S(1)}, u32[]{:S(2)}, u32[]{:S(2)}) collective-permute-start(bf16[512,512]{1,0:T(8,128)(2,1)S(1)} %get-tuple-element.83), channel_id=1, source_target_pairs={{0,1},{1,0},{2,3},{3,2},{4,5},{5,4},{6,7},{7,6},{8,9},{9,8},{10,11... | collective-permute-start | bytes 1572872 | tf_op jit(solution)/shard_map/ppermute | solution.py:38
  100.9 9.8 %collective-permute-start.29 = (f32[64,1024]{1,0:T(8,128)S(1)}, f32[64,1024]{1,0:T(8,128)S(1)}, u32[]{:S(2)}, u32[]{:S(2)}) collective-permute-start(f32[64,1024]{1,0:T(8,128)S(1)} %maximum_select_fusion.3), channel_id=1, source_target_pairs={{0,32},{32,0},{64,96},{96,64},{1,33},{33,1},{65,97},{97,65},{2,34}... | collective-permute-start | bytes 786440 | tf_op jit(solution)/shard_map/ppermute | solution.py:101
  102.0 10.4 %collective-permute-start.28 = (bf16[256,1024]{1,0:T(8,128)(2,1)S(1)}, bf16[256,1024]{1,0:T(8,128)(2,1)S(1)}, u32[]{:S(2)}, u32[]{:S(2)}) collective-permute-start(bf16[256,1024]{1,0:T(8,128)(2,1)S(1)} %add_convert_fusion.4), channel_id=1, source_target_pairs={{0,3},{1,2},{2,1},{3,0},{4,7},{5,6},{6,5},{7,4},{8,11},{9,10},{10,... | collective-permute-start | bytes 1572872 | tf_op jit(solution)/shard_map/ppermute | solution.py:42
  103.0 9.4 %collective-permute-start.27 = (bf16[256,1024]{1,0:T(8,128)(2,1)S(1)}, bf16[256,1024]{1,0:T(8,128)(2,1)S(1)}, u32[]{:S(2)}, u32[]{:S(2)}) collective-permute-start(bf16[256,1024]{1,0:T(8,128)(2,1)S(1)} %add_convert_fusion.5), channel_id=1, source_target_pairs={{4,8},{8,4},{5,9},{9,5},{6,10},{10,6},{7,11},{11,7},{20,24},{24,20... | collective-permute-start | bytes 1572872 | tf_op jit(solution)/shard_map/ppermute | solution.py:46
  104.5 10.0 %collective-permute-start.26 = (bf16[256,1024]{1,0:T(8,128)(2,1)S(1)}, bf16[256,1024]{1,0:T(8,128)(2,1)S(1)}, u32[]{:S(2)}, u32[]{:S(2)}) collective-permute-start(bf16[256,1024]{1,0:T(8,128)(2,1)S(1)} %get-tuple-element.120), channel_id=1, source_target_pairs={{0,4},{4,0},{8,12},{12,8},{1,5},{5,1},{9,13},{13,9},{2,6},{6,2},{1... | collective-permute-start | bytes 1572872 | tf_op jit(solution)/shard_map/ppermute | solution.py:46
  116.7 14.2 %collective-permute-start.30 = (bf16[512,1024]{1,0:T(8,128)(2,1)S(1)}, bf16[512,1024]{1,0:T(8,128)(2,1)S(1)}, u32[]{:S(2)}, u32[]{:S(2)}) collective-permute-start(bf16[512,1024]{1,0:T(8,128)(2,1)S(1)} %get-tuple-element.133), channel_id=1, source_target_pairs={{0,16},{16,0},{1,17},{17,1},{2,18},{18,2},{3,19},{19,3},{4,20},{20... | collective-permute-start | bytes 3145736 | tf_op jit(solution)/shard_map/ppermute | solution.py:34
  123.5 14.8 %collective-permute-start.32 = (bf16[256,1024]{1,0:T(8,128)(2,1)S(1)}, bf16[256,1024]{1,0:T(8,128)(2,1)S(1)}, u32[]{:S(2)}, u32[]{:S(2)}) collective-permute-start(bf16[256,1024]{1,0:T(8,128)(2,1)S(1)} %add_convert_fusion.3), channel_id=1, source_target_pairs={{0,3},{1,2},{2,1},{3,0},{4,7},{5,6},{6,5},{7,4},{8,11},{9,10},{10,... | collective-permute-start | bytes 1572872 | tf_op jit(solution)/shard_map/ppermute | solution.py:42
  124.8 13.5 %collective-permute-start.34 = (bf16[256,1024]{1,0:T(8,128)(2,1)S(1)}, bf16[256,1024]{1,0:T(8,128)(2,1)S(1)}, u32[]{:S(2)}, u32[]{:S(2)}) collective-permute-start(bf16[256,1024]{1,0:T(8,128)(2,1)S(1)} %add_convert_fusion.1), channel_id=1, source_target_pairs={{4,8},{8,4},{5,9},{9,5},{6,10},{10,6},{7,11},{11,7},{20,24},{24,20... | collective-permute-start | bytes 1572872 | tf_op jit(solution)/shard_map/ppermute | solution.py:46
  125.8 15.4 %collective-permute-start.33 = (bf16[256,1024]{1,0:T(8,128)(2,1)S(1)}, bf16[256,1024]{1,0:T(8,128)(2,1)S(1)}, u32[]{:S(2)}, u32[]{:S(2)}) collective-permute-start(bf16[256,1024]{1,0:T(8,128)(2,1)S(1)} %add_convert_fusion.2), channel_id=1, source_target_pairs={{0,4},{4,0},{8,12},{12,8},{1,5},{5,1},{9,13},{13,9},{2,6},{6,2},{1... | collective-permute-start | bytes 1572872 | tf_op jit(solution)/shard_map/ppermute | solution.py:46
  129.9 15.7 %collective-permute-start.36 = (f32[128,1024]{1,0:T(8,128)S(1)}, f32[128,1024]{1,0:T(8,128)S(1)}, u32[]{:S(2)}, u32[]{:S(2)}) collective-permute-start(f32[128,1024]{1,0:T(8,128)S(1)} %maximum_select_fusion.2), channel_id=1, source_target_pairs={{0,16},{16,0},{1,17},{17,1},{2,18},{18,2},{3,19},{19,3},{4,20},{20... | collective-permute-start | bytes 1572872 | tf_op jit(solution)/shard_map/ppermute | solution.py:101
  132.1 25.2 %collective-permute-start.31 = (bf16[512,1024]{1,0:T(8,128)(2,1)S(1)}, bf16[512,1024]{1,0:T(8,128)(2,1)S(1)}, u32[]{:S(2)}, u32[]{:S(2)}) collective-permute-start(bf16[512,1024]{1,0:T(8,128)(2,1)S(1)} %add_convert_fusion), channel_id=1, source_target_pairs={{1,16},{2,19},{16,1},{19,2},{5,20},{6,23},{20,5},{23,6},{9,24},{10... | collective-permute-start | bytes 3145736 | tf_op jit(solution)/shard_map/ppermute | solution.py:30
  141.7 12.3 %collective-permute-start.35 = (bf16[256,1024]{1,0:T(8,128)(2,1)S(1)}, bf16[256,1024]{1,0:T(8,128)(2,1)S(1)}, u32[]{:S(2)}, u32[]{:S(2)}) collective-permute-start(bf16[256,1024]{1,0:T(8,128)(2,1)S(1)} %get-tuple-element.118), channel_id=1, source_target_pairs={{1,16},{2,19},{16,1},{19,2},{5,20},{6,23},{20,5},{23,6},{9,24},{10... | collective-permute-start | bytes 1572872 | tf_op jit(solution)/shard_map/ppermute | solution.py:30
  (10 other events, 89.6 us)

commit v4 on v3

--- a/solution.py
+++ b/solution.py
@@ -58,26 +58,24 @@
     return lax.optimization_barrier(arrays)
 
 
-def move(_, a, b, to_a, to_b):
-    to_a[0] = a[...]
-    to_b[0] = b[...]
-
-
-def halves(tokens, blocks):
-    spec = lambda i: pl.BlockSpec((512, 256), lambda n, table: (0, table[i, n]))
+def sort_columns(table, own, sib, leave, keep):
+    stays = table[8] == 1
+    leave[0] = jnp.where(stays, sib[...], own[...])
+    keep[0] = jnp.where(stays, own[...], sib[...])
+
+
+def halves(table, own, sib):
+    block = pl.BlockSpec((512, 256), lambda n, table: (0, table[n]))
     out = pl.BlockSpec((1, 512, 256), lambda n, table: (n // 2, 0, n % 2))
     kind = jax.ShapeDtypeStruct((4, 512, 512), bf16)
     return pl.pallas_call(
-        move,
+        sort_columns,
         grid_spec=pltpu.PrefetchScalarGridSpec(
-            num_scalar_prefetch=1,
-            grid=(8,),
-            in_specs=[spec(0), spec(1)],
-            out_specs=[out, out],
+            num_scalar_prefetch=1, grid=(8,), in_specs=[block, block], out_specs=[out, out]
         ),
         out_shape=[kind, kind],
-        cost_estimate=pl.CostEstimate(flops=0, bytes_accessed=16 << 20, transcendentals=0),
-    )(blocks, tokens, tokens)
+        cost_estimate=pl.CostEstimate(flops=0, bytes_accessed=0, transcendentals=0),
+    )(table, own, sib)
 
 
 class Drift:
@@ -88,7 +86,8 @@
         self.steps = [("c", CORE, c), ("y", near, y % 2), ("y", wide, y // 2), ("zh", CORE, c)]
         self.at = 0
 
-    def send(self):
+    def send(self, after):
+        self.v, _ = together(self.v, after)
         if self.at < 3:
             bit = self.steps[self.at][2]
             n = self.v.shape[0] // 2
@@ -121,39 +120,47 @@
     stays = c == jnp.where((x == 1) | (x == 2), 1, 0)
     end = (z == 0) | (z == 3)
     mine = jnp.where(x < 2, c, 3 - c)
-    theirs = jnp.where(x < 2, 1 - c, 2 + c)
     order = [
         jnp.where(z < 2, 3, 0),
         jnp.where(z < 2, 2, 1),
         jnp.where(z == 0, 1, jnp.where(z == 1, 0, jnp.where(z == 2, 3, 2))),
         z,
     ]
-    blocks = jnp.stack(
-        [4 * order[k] + q for half in (theirs, mine) for k in range(4) for q in (half, 3 - half)]
-    ).reshape(2, 8)
+    table = jnp.stack(
+        [4 * order[k] + q for k in range(4) for q in (mine, 3 - mine)] + [stays.astype(jnp.int32)]
+    ).astype(jnp.int32)
 
     w = jnp.where(stays, weight, swap(weight))
-    g_sib = core(key_grad)
-    x_give, x_own = halves(tokens, blocks.astype(jnp.int32))
-    x_sib = core(x_give)
+    g_mine = lax.dynamic_slice_in_dim(key_grad, c * 256, 256, 0)
+    g_first = core(lax.dynamic_slice_in_dim(key_grad, (1 - c) * 256, 256, 0))
+    g_l = jnp.where(stays, g_first, g_mine)
+    x_sib = core(tokens)
     drift = Drift(anchor - local_params[0].astype(f32), c, y)
-    drift.take(drift.send())
-    g_a = jnp.where(stays, key_grad, g_sib)
-    g_l = lax.dynamic_slice_in_dim(jnp.where(stays, g_sib, key_grad), c * 256, 256, 0)
-
-    got = (beside(g_l), line(w, PAIRS), line(w, MIDDLE), across(w), drift.send())
-    leave = [jnp.where(stays, x_sib[k], x_own[k]) for k in range(4)]
-    keep = [jnp.where(stays, x_own[k], x_sib[k]) for k in range(4)]
-    got, leave, drift.v = together(got, leave, drift.v)
+    drift.take(drift.send(w))
+
+    x_l, x_k = halves(table, tokens, x_sib)
+    leave, keep = ([v[k] for k in range(4)] for v in (x_l, x_k))
+    g_mine, _ = together(g_mine, x_sib)
+    g_second = core(g_mine)
+    got = (beside(g_l), line(w, PAIRS), line(w, MIDDLE), across(w), drift.send(leave[0]))
+    got, leave, g_second, drift.v = together(got, leave, g_second, drift.v)
     g_half, e_own, m_own, q_own, d = got
     drift.take(d)
 
-    got = (beside(leave[0]), line(m_own, ENDS_OUT), line(e_own, MIDDLE), across(e_own), drift.send())
-    g_rest = core(g_half)
-    g_b = jnp.where(
-        c == 0, jnp.concatenate([g_half, g_rest]), jnp.concatenate([g_rest, g_half])
-    )
+    def in_order(a, b):
+        return jnp.where(c == 0, jnp.concatenate([a, b]), jnp.concatenate([b, a]))
+
+    g_a = jnp.where(stays, key_grad, in_order(g_first, g_second))
+    g_b = in_order(g_half, core(g_half))
+    g_a, g_b = together(g_a, g_b)
     base = [dot_t(k, g_a) for k in keep]
+    got = (
+        beside(leave[0]),
+        line(m_own, ENDS_OUT),
+        line(e_own, MIDDLE),
+        across(e_own),
+        drift.send(g_b),
+    )
     sent = drift.v
     got, leave, sent, g_b, base = together(got, leave, sent, g_b, base)
     drift.v = sent
@@ -171,45 +178,49 @@
     def cat(*arrays):
         return jnp.concatenate(arrays, axis=-1)
 
-    got = (beside(leave[1]), line(m2, ENDS_OUT), line(q_own, MIDDLE), across(going(0)), drift.send())
+    stay = staying(0)
+    got = (
+        beside(leave[1]),
+        line(m2, ENDS_OUT),
+        line(q_own, MIDDLE),
+        across(going(0)),
+        drift.send(stay),
+    )
     rows = [None, None, jnp.concatenate([e_own, q2]), jnp.concatenate([w, q_own])]
     k_a = dot(cat(keep[2], keep[3]), jnp.concatenate(rows[2:]))
-    stay = staying(0)
     got, leave, drift.v, drift.sent, stay, k_a = together(got, leave, drift.v, drift.sent, stay, k_a)
     x_b.append(got[0])
     _, e3, m3, q3, d = got
     drift.take(d)
     part0 = stay + q3.astype(f32)
 
+    stay = staying(1)
     got = (
         beside(leave[2]),
         line(jnp.where(end, part0.astype(bf16), m3), PAIRS),
         line(q2, MIDDLE),
         across(going(1)),
-        drift.send(),
-    )
-    stay = staying(1)
+        drift.send(stay),
+    )
     got, leave, drift.v, stay, part0 = together(got, leave, drift.v, stay, part0)
     x_b.append(got[0])
     _, e4, m4, q4, d = got
     drift.take(d)
     part1 = stay + q4.astype(f32)
 
+    stay = staying(2)
+    rows[1] = jnp.concatenate([mid, jnp.where(end, e4, m3)])
+    k_a = k_a + dot(keep[1], rows[1])
+    k_b = dot(cat(x_b[1], x_b[2]), jnp.concatenate(rows[1:3]))
     got = (
         beside(leave[3]),
         line(jnp.where(end, part1.astype(bf16), m4), PAIRS),
         line((part0 + e4.astype(f32)).astype(bf16), MIDDLE),
         across(going(2)),
-        drift.send(),
-    )
-    rows[1] = jnp.concatenate([mid, jnp.where(end, e4, m3)])
-    k_a = k_a + dot(keep[1], rows[1])
-    k_b = dot(cat(x_b[1], x_b[2]), jnp.concatenate(rows[1:3]))
-    stay = staying(2)
-    got, drift.v, stay, part1, k_a, k_b = together(got, drift.v, stay, part1, k_a, k_b)
+    )
+    got, stay, part1, k_a, k_b = together(got, stay, part1, k_a, k_b)
     x_b.append(got[0])
-    _, e5, m5, q5, d = got
-    drift.take(d)
+    _, e5, m5, q5 = got
     part2 = stay + q5.astype(f32)
 
     got = (
@@ -222,11 +233,13 @@
     k_b = k_b + dot(cat(x_b[0], x_b[3]), jnp.concatenate([rows[0], rows[3]]))
     k_got = core(jnp.where(stays, k_b, k_a).astype(bf16))
     keys_work = (jnp.where(stays, k_a, k_b) + k_got.astype(f32)).astype(bf16)
-    keys = jnp.where(stays, keys_work, swap(keys_work))
-    e6, m6, q6 = got
+    k_back = swap(keys_work)
+    drift.take(drift.send(keys_work))
+    keys = jnp.where(stays, keys_work, k_back)
+    (e6, m6, q6), _ = together(got, k_back)
     total = staying(3) + q6.astype(f32) + e6.astype(f32) + m6.astype(f32)
     gradient = jnp.where(stays, total, swap(total.astype(bf16)).astype(f32))
-    drift.take(drift.send())
+    drift.take(drift.send(k_back))
 
     new_first = first_decay * adam_first[0] + (1.0 - first_decay) * gradient
     new_second = second_decay * adam_second[0] + (1.0 - second_decay) * gradient * gradient

time: 159 us -> 168 us (1.057)
  matrix products: 12 us -> 22.4 us
  waiting for transfers between devices: 56.8 us -> 47.6 us
  local copies, waits for them, and re-layouts: 1.65 us -> 7.3 us
  other arithmetic: 17.4 us -> 22.2 us
  starting transfers between devices: 62 us -> 59.4 us
    ppermute x6, waiting for transfers between devices: 19.2 us -> 10.9 us  [across(): return lax.ppermute(v, 'x', ACROSS)]
    ppermute x7, waiting for transfers between devices: 8.57 us -> 15.7 us  [send(): return lax.ppermute(self.sent, axis, perm)]
    dot_general x5, matrix products: 5.34 us -> 11.8 us  [dot(): return jnp.dot(a, b, preferred_element_type=f32)]
    ppermute x5, waiting for transfers between devices: 5.14 us -> 0.77 us  [beside(): return lax.ppermute(v, 'x', BESIDE)]
    dot_general x12, matrix products: 6.66 us -> 10.6 us  [dot_t(): lax.dot_general(a, b, (((0,), (0,)), ((), ())), preferred_element_type=f32)]
    squeeze x0 -> x2, local copies, waits for them, and re-layouts: none -> 3.08 us  [on_device(): leave, keep = ([v[k] for k in range(4)] for v in (x_l, x_k))]
    ppermute x12, waiting for transfers between devices: 11.2 us -> 8.51 us  [line(): return lax.ppermute(v, 'zl', pairs)]
    convert_element_type x1, other arithmetic: 1.16 us -> 3.75 us  [on_device(): keys_work = (jnp.where(stays, k_a, k_b) + k_got.astype(f32)).astype(bf16)]
  transfers between devices with their start and end apart: 37 -> 38, of which waited for: 15 -> 15; matrix products, arithmetic and copies ran while one was open for 17% -> 25% of each run, Pallas kernels for 0% -> 4%
where the time goes in v4:
time: 168 us; the launch traced here: 167 us
  starting transfers between devices  59.4 us (35%)
  waiting for transfers between devices  47.6 us (28%)
  matrix products  22.4 us (13%)
  other arithmetic  22.2 us (13%)
  Pallas kernels  7.33 us (4%)
  local copies, waits for them, and re-layouts  7.3 us (4%)
    ppermute x12, starting transfers between devices, line(): return lax.ppermute(v, 'zl', pairs)  17.4 us
    ppermute x7, waiting for transfers between devices, send(): return lax.ppermute(self.sent, axis, perm)  15.7 us
    ppermute x7, starting transfers between devices, send(): return lax.ppermute(self.sent, axis, perm)  13 us
    dot_general x5, matrix products, dot(): return jnp.dot(a, b, preferred_element_type=f32)  11.8 us
    ppermute x3, waiting for transfers between devices, swap(): return lax.ppermute(v, ('c', 'x'), SWAP)  11.6 us
    ppermute x6, waiting for transfers between devices, across(): return lax.ppermute(v, 'x', ACROSS)  10.9 us
    ppermute x5, starting transfers between devices, core(): return lax.ppermute(v, 'c', CORE)  10.9 us
    dot_general x12, matrix products, dot_t(): lax.dot_general(a, b, (((0,), (0,)), ((), ())), preferred_element_type=f32)  10.6 us
  transfers between devices with their start and end apart: 38, of which 15 were waited for; matrix products, arithmetic and copies ran while one was open for 25% of the time, Pallas kernels for 4%

profile of v4, /device:TPU:1, one launch (start us, length us, event | category | flops | bytes accessed | tf_op | source)
XLA Modules:
  0.0 167.4 jit_solution(14579430882968511867)
XLA Ops:
  0.6 3.3 %collective-permute-start.7 = (bf16[512,4096]{1,0:T(8,128)(2,1)}, bf16[512,4096]{1,0:T(8,128)(2,1)}, u32[]{:S(2)}, u32[]{:S(2)}) collective-permute-start(bf16[512,4096]{1,0:T(8,128)(2,1)} %own.1), channel_id=1, source_target_pairs={{0,16},{16,0},{1,17},{17,1},{2,18},{18,2},{3,19},{19,3},{4,20},{20... | collective-permute-start | bytes 12582920 | tf_op jit(solution)/shard_map/ppermute | solution.py:34
  4.0 1.9 %collective-permute-start.2 = (bf16[256,1024]{1,0:T(8,128)(2,1)}, bf16[256,1024]{1,0:T(8,128)(2,1)}, u32[]{:S(2)}, u32[]{:S(2)}) collective-permute-start(bf16[256,1024]{1,0:T(8,128)(2,1)} %bitcast.69), channel_id=1, source_target_pairs={{1,16},{2,19},{16,1},{19,2},{5,20},{6,23},{20,5},{23,6},{9,24},{10... | collective-permute-start | bytes 1572872 | tf_op jit(solution)/shard_map/ppermute | solution.py:30
  9.4 5.4 %collective-permute-done.2 = bf16[256,1024]{1,0:T(8,128)(2,1)} collective-permute-done((bf16[256,1024]{1,0:T(8,128)(2,1)}, bf16[256,1024]{1,0:T(8,128)(2,1)}, u32[]{:S(2)}, u32[]{:S(2)}) %collective-permute-start.2) | collective-permute-done | bytes 524320 | tf_op jit(solution)/shard_map/ppermute | solution.py:30
  14.8 1.9 %broadcast_select_fusion.5 = bf16[256,1024]{1,0:T(8,128)(2,1)} fusion(bf16[256,1024]{1,0:T(8,128)(2,1)} %collective-permute-done.2, pred[]{:T(512)S(6)} %eq.37, bf16[1,256,1024]{2,1,0:T(8,128)(2,1)S(1)} %copy-done.15), kind=kLoop, calls=%fused_computation.90 | loop fusion | flops 262144 | bytes 1572865 | tf_op jit(solution)/shard_map/jit(_where)/select_n | solution.py:133
  20.3 3.8 %collective-permute-start.3 = (bf16[256,1024]{1,0:T(8,128)(2,1)}, bf16[256,1024]{1,0:T(8,128)(2,1)}, u32[]{:S(2)}, u32[]{:S(2)}) collective-permute-start(bf16[256,1024]{1,0:T(8,128)(2,1)} %broadcast_select_fusion.5), channel_id=1, source_target_pairs={{0,4},{4,0},{8,12},{12,8},{1,5},{5,1},{9,13},{13,9},{2,6},{6,2},{1... | collective-permute-start | bytes 1572872 | tf_op jit(solution)/shard_map/ppermute | solution.py:46
  27.6 7.3 %shard_map.127 = (bf16[4,512,512]{2,1,0:T(8,128)(2,1)}, bf16[4,512,512]{2,1,0:T(8,128)(2,1)}) custom-call(s32[9]{0:T(128)} %stack.43.table, bf16[512,4096]{1,0:T(8,128)(2,1)} %own.1, bf16[512,4096]{1,0:T(8,128)(2,1)} %collective-permute-done.7.sib), custom_call_target="tpu_custom_call" | custom-call | tf_op jit(solution)/shard_map/pallas_call | solution.py:71
  34.9 3.0 %slice_bitcast_fusion.2 = (bf16[512,512]{1,0:T(8,128)(2,1)}, bf16[512,512]{1,0:T(8,128)(2,1)}, bf16[512,512]{1,0:T(8,128)(2,1)}, bf16[512,512]{1,0:T(8,128)(2,1)}) fusion(bf16[4,512,512]{2,1,0:T(8,128)(2,1)} %get-tuple-element.74), kind=kLoop, calls=%fused_computation.81 | loop fusion | bytes 4194304 | tf_op jit(solution)/shard_map/squeeze | solution.py:142
  39.4 6.7 %collective-permute-done.8 = f32[64,1024]{1,0:T(8,128)} collective-permute-done((f32[64,1024]{1,0:T(8,128)S(1)}, f32[64,1024]{1,0:T(8,128)}, u32[]{:S(2)}, u32[]{:S(2)}) %collective-permute-start.8) | collective-permute-done | bytes 262176 | tf_op jit(solution)/shard_map/ppermute | solution.py:100
  55.4 2.0 %fusion.88 = f32[512,1024]{1,0:T(8,128)} fusion(bf16[512,1024]{1,0:T(8,128)(2,1)S(1)} %fusion.20, bf16[4,512,512]{2,1,0:T(8,128)(2,1)S(1)} %copy-done), kind=kOutput, calls=%fused_computation.130 | convolution fusion | flops 536870912 | bytes 3670016 | tf_op jit(solution)/shard_map/dot_general | solution.py:54
  58.2 3.0 %collective-permute-start.15 = (f32[32,1024]{1,0:T(8,128)S(1)}, f32[32,1024]{1,0:T(8,128)S(1)}, u32[]{:S(2)}, u32[]{:S(2)}) collective-permute-start(f32[32,1024]{1,0:T(8,128)S(1)} %constant_dynamic-slice_fusion), channel_id=1, source_target_pairs={{0,64},{32,96},{64,0},{96,32},{1,65},{33,97},{65,1},{97,33},{2,66}... | collective-permute-start | bytes 393224 | tf_op jit(solution)/shard_map/ppermute | solution.py:100
  65.9 5.2 %collective-permute-start.20 = (bf16[32,1024]{1,0:T(8,128)(2,1)S(1)}, bf16[32,1024]{1,0:T(8,128)(2,1)S(1)}, u32[]{:S(2)}, u32[]{:S(2)}) collective-permute-start(bf16[32,1024]{1,0:T(8,128)(2,1)S(1)} %dynamic-slice_add_fusion.2), channel_id=1, source_target_pairs={{0,128},{128,0},{1,129},{129,1},{2,130},{130,2},{3,131},{131,3},{4... | collective-permute-start | bytes 196616 | tf_op jit(solution)/shard_map/ppermute | solution.py:100
  74.2 2.5 %fusion = f32[512,1024]{1,0:T(8,128)S(1)} fusion(bf16[256,1024]{1,0:T(8,128)(2,1)} %collective-permute-done.5, bf16[256,1024]{1,0:T(8,128)(2,1)S(1)} %copy-done.24, bf16[256,1024]{1,0:T(8,128)(2,1)S(1)} %collective-permute-done.13, bf16[256,1024]{1,0:T(8,128)(2,1)} %collective-permute-done.3, bf16[512,512]{1,0:T(8,128)(2,1)S(1)} %get-tuple-element.154, ...), kind=kOutput, calls=%fused_computation.4 | convolution fusion | flops 1084227584 | bytes 5242880 | tf_op jit(solution)/shard_map/dot_general | solution.py:50
  77.5 6.9 %collective-permute-done.19 = bf16[256,1024]{1,0:T(8,128)(2,1)S(1)} collective-permute-done((bf16[256,1024]{1,0:T(8,128)(2,1)S(1)}, bf16[256,1024]{1,0:T(8,128)(2,1)S(1)}, u32[]{:S(2)}, u32[]{:S(2)}) %collective-permute-start.19) | collective-permute-done | bytes 524320 | tf_op jit(solution)/shard_map/ppermute | solution.py:42
  84.4 3.0 %collective-permute-done.17 = bf16[256,1024]{1,0:T(8,128)(2,1)S(1)} collective-permute-done((bf16[256,1024]{1,0:T(8,128)(2,1)S(1)}, bf16[256,1024]{1,0:T(8,128)(2,1)S(1)}, u32[]{:S(2)}, u32[]{:S(2)}) %collective-permute-start.17) | collective-permute-done | bytes 524320 | tf_op jit(solution)/shard_map/ppermute | solution.py:46
  87.8 2.0 %collective-permute-start.24 = (bf16[256,1024]{1,0:T(8,128)(2,1)S(1)}, bf16[256,1024]{1,0:T(8,128)(2,1)S(1)}, u32[]{:S(2)}, u32[]{:S(2)}) collective-permute-start(bf16[256,1024]{1,0:T(8,128)(2,1)S(1)} %add_convert_fusion.6), channel_id=1, source_target_pairs={{0,3},{1,2},{2,1},{3,0},{4,7},{5,6},{6,5},{7,4},{8,11},{9,10},{10,... | collective-permute-start | bytes 1572872 | tf_op jit(solution)/shard_map/ppermute | solution.py:42
  90.8 2.5 %collective-permute-start.25 = (f32[32,1024]{1,0:T(8,128)S(1)}, f32[32,1024]{1,0:T(8,128)S(1)}, u32[]{:S(2)}, u32[]{:S(2)}) collective-permute-start(f32[32,1024]{1,0:T(8,128)S(1)} %convert_add_fusion.3), channel_id=1, source_target_pairs={{0,64},{32,96},{64,0},{96,32},{1,65},{33,97},{65,1},{97,33},{2,66}... | collective-permute-start | bytes 393224 | tf_op jit(solution)/shard_map/ppermute | solution.py:100
  93.4 2.8 %collective-permute-done.25 = f32[32,1024]{1,0:T(8,128)S(1)} collective-permute-done((f32[32,1024]{1,0:T(8,128)S(1)}, f32[32,1024]{1,0:T(8,128)S(1)}, u32[]{:S(2)}, u32[]{:S(2)}) %collective-permute-start.25) | collective-permute-done | bytes 131104 | tf_op jit(solution)/shard_map/ppermute | solution.py:100
  96.2 3.8 %collective-permute-done.24 = bf16[256,1024]{1,0:T(8,128)(2,1)S(1)} collective-permute-done((bf16[256,1024]{1,0:T(8,128)(2,1)S(1)}, bf16[256,1024]{1,0:T(8,128)(2,1)S(1)}, u32[]{:S(2)}, u32[]{:S(2)}) %collective-permute-start.24) | collective-permute-done | bytes 524320 | tf_op jit(solution)/shard_map/ppermute | solution.py:42
  105.3 2.2 %collective-permute-start.27 = (bf16[256,1024]{1,0:T(8,128)(2,1)S(1)}, bf16[256,1024]{1,0:T(8,128)(2,1)S(1)}, u32[]{:S(2)}, u32[]{:S(2)}) collective-permute-start(bf16[256,1024]{1,0:T(8,128)(2,1)S(1)} %get-tuple-element.144), channel_id=1, source_target_pairs={{0,4},{4,0},{8,12},{12,8},{1,5},{5,1},{9,13},{13,9},{2,6},{6,2},{1... | collective-permute-start | bytes 1572872 | tf_op jit(solution)/shard_map/ppermute | solution.py:46
  108.7 2.7 %fusion.5 = f32[512,1024]{1,0:T(8,128)S(1)} fusion(bf16[256,1024]{1,0:T(8,128)(2,1)S(1)} %collective-permute-done.13, bf16[256,1024]{1,0:T(8,128)(2,1)} %collective-permute-done.3, bf16[256,1024]{1,0:T(8,128)(2,1)S(1)} %broadcast_select_fusion.3, bf16[256,1024]{1,0:T(8,128)(2,1)S(1)} %broadcast_select_fusion.4, ...), kind=kOutput, calls=%fused_computation.9 | convolution fusion | flops 1084227584 | bytes 5242880 | tf_op jit(solution)/shard_map/dot_general | solution.py:50
  117.4 4.1 %select_convert_fusion = (bf16[512,1024]{1,0:T(8,128)(2,1)}, f32[512,1024]{1,0:T(8,128)}) fusion(pred[]{:T(512)S(6)} %eq.37, f32[512,1024]{1,0:T(8,128)S(1)} %fusion.5, f32[512,1024]{1,0:T(8,128)S(1)} %add.179, f32[512,1024]{1,0:T(8,128)S(1)} %fusion.31, bf16[256,1024]{1,0:T(8,128)(2,1)} %collective-permute-done.5, bf16[256,1024]{1,0:T(8,128)(2,1)S(1)} %copy-done.24, ...), kind=kOutput, calls=%fused_computation.21 | convolution fusion | flops 1086324736 | bytes 12582913 | tf_op jit(solution)/shard_map/dot_general | solution.py:50
  121.6 5.5 %collective-permute-start.30 = (bf16[512,1024]{1,0:T(8,128)(2,1)}, bf16[512,1024]{1,0:T(8,128)(2,1)}, u32[]{:S(2)}, u32[]{:S(2)}) collective-permute-start(bf16[512,1024]{1,0:T(8,128)(2,1)} %get-tuple-element.159), channel_id=1, source_target_pairs={{0,16},{16,0},{1,17},{17,1},{2,18},{18,2},{3,19},{19,3},{4,20},{20... | collective-permute-start | bytes 3145736 | tf_op jit(solution)/shard_map/ppermute | solution.py:34
  127.1 1.9 %add_convert_fusion.1 = bf16[256,1024]{1,0:T(8,128)(2,1)S(1)} fusion(f32[512,1024]{1,0:T(8,128)} %fusion.88, bf16[512,1024]{1,0:T(8,128)(2,1)S(1)} %maximum_select_fusion.1, bf16[512,512]{1,0:T(8,128)(2,1)} %copy-done.25), kind=kOutput, calls=%fused_computation.57 | convolution fusion | flops 268959744 | bytes 2883584 | tf_op jit(solution)/shard_map/dot_general | solution.py:54
  129.0 2.6 %collective-permute-start.34 = (bf16[256,1024]{1,0:T(8,128)(2,1)S(1)}, bf16[256,1024]{1,0:T(8,128)(2,1)S(1)}, u32[]{:S(2)}, u32[]{:S(2)}) collective-permute-start(bf16[256,1024]{1,0:T(8,128)(2,1)S(1)} %add_convert_fusion.1), channel_id=1, source_target_pairs={{0,3},{1,2},{2,1},{3,0},{4,7},{5,6},{6,5},{7,4},{8,11},{9,10},{10,... | collective-permute-start | bytes 1572872 | tf_op jit(solution)/shard_map/ppermute | solution.py:42
  131.6 3.8 %add_convert_fusion = bf16[512,1024]{1,0:T(8,128)(2,1)S(1)} fusion(bf16[512,1024]{1,0:T(8,128)(2,1)} %collective-permute-done.30, pred[]{:T(512)S(6)} %eq.37, f32[512,1024]{1,0:T(8,128)} %copy-done.12, f32[512,1024]{1,0:T(8,128)} %get-tuple-element.160, f32[512,1024]{1,0:T(8,128)S(1)} %copy-done.3, f32[512,1024]{1,0:T(8,128)S(1)} %fusion.31), kind=kLoop, calls=%fused_computation.20 | loop fusion | flops 3145728 | bytes 10485761 | tf_op jit(solution)/shard_map/convert_element_type | solution.py:235
  135.4 3.1 %collective-permute-start.31 = (bf16[512,1024]{1,0:T(8,128)(2,1)S(1)}, bf16[512,1024]{1,0:T(8,128)(2,1)S(1)}, u32[]{:S(2)}, u32[]{:S(2)}) collective-permute-start(bf16[512,1024]{1,0:T(8,128)(2,1)S(1)} %add_convert_fusion), channel_id=1, source_target_pairs={{1,16},{2,19},{16,1},{19,2},{5,20},{6,23},{20,5},{23,6},{9,24},{10... | collective-permute-start | bytes 3145736 | tf_op jit(solution)/shard_map/ppermute | solution.py:30
  139.8 3.5 %collective-permute-start.32 = (bf16[256,1024]{1,0:T(8,128)(2,1)S(1)}, bf16[256,1024]{1,0:T(8,128)(2,1)S(1)}, u32[]{:S(2)}, u32[]{:S(2)}) collective-permute-start(bf16[256,1024]{1,0:T(8,128)(2,1)S(1)} %add_convert_fusion.3), channel_id=1, source_target_pairs={{0,4},{4,0},{8,12},{12,8},{1,5},{5,1},{9,13},{13,9},{2,6},{6,2},{1... | collective-permute-start | bytes 1572872 | tf_op jit(solution)/shard_map/ppermute | solution.py:46
  144.6 6.2 %collective-permute-done.36 = f32[64,1024]{1,0:T(8,128)S(1)} collective-permute-done((f32[64,1024]{1,0:T(8,128)S(1)}, f32[64,1024]{1,0:T(8,128)S(1)}, u32[]{:S(2)}, u32[]{:S(2)}) %collective-permute-start.36) | collective-permute-done | bytes 262176 | tf_op jit(solution)/shard_map/ppermute | solution.py:100
  151.9 2.0 %collective-permute-done.32 = bf16[256,1024]{1,0:T(8,128)(2,1)S(1)} collective-permute-done((bf16[256,1024]{1,0:T(8,128)(2,1)S(1)}, bf16[256,1024]{1,0:T(8,128)(2,1)S(1)}, u32[]{:S(2)}, u32[]{:S(2)}) %collective-permute-start.32) | collective-permute-done | bytes 524320 | tf_op jit(solution)/shard_map/ppermute | solution.py:46
  154.5 2.7 %collective-permute-start.35 = (bf16[256,1024]{1,0:T(8,128)(2,1)S(1)}, bf16[256,1024]{1,0:T(8,128)(2,1)S(1)}, u32[]{:S(2)}, u32[]{:S(2)}) collective-permute-start(bf16[256,1024]{1,0:T(8,128)(2,1)S(1)} %get-tuple-element.142), channel_id=1, source_target_pairs={{1,16},{2,19},{16,1},{19,2},{5,20},{6,23},{20,5},{23,6},{9,24},{10... | collective-permute-start | bytes 1572872 | tf_op jit(solution)/shard_map/ppermute | solution.py:30
  160.0 5.1 %collective-permute-done.35 = bf16[256,1024]{1,0:T(8,128)(2,1)S(1)} collective-permute-done((bf16[256,1024]{1,0:T(8,128)(2,1)S(1)}, bf16[256,1024]{1,0:T(8,128)(2,1)S(1)}, u32[]{:S(2)}, u32[]{:S(2)}) %collective-permute-start.35) | collective-permute-done | bytes 524320 | tf_op jit(solution)/shard_map/ppermute | solution.py:30
  165.1 2.3 %fusion.86 = (f32[1,256,1024]{2,1,0:T(8,128)}, bf16[1,256,1024]{2,1,0:T(8,128)(2,1)}, f32[1,256,1024]{2,1,0:T(8,128)}) fusion(f32[256,1024]{1,0:T(8,128)S(1)} %get-tuple-element.143, bf16[256,1024]{1,0:T(8,128)(2,1)S(1)} %collective-permute-done.35, pred[]{:T(512)S(6)} %eq.37, f32[1,256,1024]{2,1,0:T(8,128)S(1)} %copy-done.18, ...), kind=kLoop, calls=%fused_computation.128 | loop fusion | flops 4456448 | bytes 6815745 | tf_op jit(solution)/shard_map/broadcast_in_dim | solution.py:253
  (157 shorter events, 51.3 us)
Async XLA Ops:
  0.6 25.7 %collective-permute-start.7 = (bf16[512,4096]{1,0:T(8,128)(2,1)}, bf16[512,4096]{1,0:T(8,128)(2,1)}, u32[]{:S(2)}, u32[]{:S(2)}) collective-permute-start(bf16[512,4096]{1,0:T(8,128)(2,1)} %own.1), channel_id=1, source_target_pairs={{0,16},{16,0},{1,17},{17,1},{2,18},{18,2},{3,19},{19,3},{4,20},{20... | collective-permute-start | bytes 12582920 | tf_op jit(solution)/shard_map/ppermute | solution.py:34
  4.0 10.8 %collective-permute-start.2 = (bf16[256,1024]{1,0:T(8,128)(2,1)}, bf16[256,1024]{1,0:T(8,128)(2,1)}, u32[]{:S(2)}, u32[]{:S(2)}) collective-permute-start(bf16[256,1024]{1,0:T(8,128)(2,1)} %bitcast.69), channel_id=1, source_target_pairs={{1,16},{2,19},{16,1},{19,2},{5,20},{6,23},{20,5},{23,6},{9,24},{10... | collective-permute-start | bytes 1572872 | tf_op jit(solution)/shard_map/ppermute | solution.py:30
  7.8 12.6 %collective-permute-start = (bf16[256,1024]{1,0:T(8,128)(2,1)}, bf16[256,1024]{1,0:T(8,128)(2,1)S(1)}, u32[]{:S(2)}, u32[]{:S(2)}) collective-permute-start(bf16[256,1024]{1,0:T(8,128)(2,1)} %constant_dynamic-slice_fusion.4), channel_id=1, source_target_pairs={{0,16},{16,0},{1,17},{17,1},{2,18},{18,2},{3,19},{19,3},{4,20},{20... | collective-permute-start | bytes 1572872 | tf_op jit(solution)/shard_map/ppermute | solution.py:34
  18.1 19.8 %collective-permute-start.5 = (bf16[256,1024]{1,0:T(8,128)(2,1)}, bf16[256,1024]{1,0:T(8,128)(2,1)}, u32[]{:S(2)}, u32[]{:S(2)}) collective-permute-start(bf16[256,1024]{1,0:T(8,128)(2,1)} %broadcast_select_fusion.5), channel_id=1, source_target_pairs={{0,3},{1,2},{2,1},{3,0},{4,7},{5,6},{6,5},{7,4},{8,11},{9,10},{10,... | collective-permute-start | bytes 1572872 | tf_op jit(solution)/shard_map/ppermute | solution.py:42
  18.9 20.5 %collective-permute-start.4 = (bf16[256,1024]{1,0:T(8,128)(2,1)}, bf16[256,1024]{1,0:T(8,128)(2,1)}, u32[]{:S(2)}, u32[]{:S(2)}) collective-permute-start(bf16[256,1024]{1,0:T(8,128)(2,1)} %broadcast_select_fusion.5), channel_id=1, source_target_pairs={{4,8},{8,4},{5,9},{9,5},{6,10},{10,6},{7,11},{11,7},{20,24},{24,20... | collective-permute-start | bytes 1572872 | tf_op jit(solution)/shard_map/ppermute | solution.py:46
  20.3 19.0 %collective-permute-start.3 = (bf16[256,1024]{1,0:T(8,128)(2,1)}, bf16[256,1024]{1,0:T(8,128)(2,1)}, u32[]{:S(2)}, u32[]{:S(2)}) collective-permute-start(bf16[256,1024]{1,0:T(8,128)(2,1)} %broadcast_select_fusion.5), channel_id=1, source_target_pairs={{0,4},{4,0},{8,12},{12,8},{1,5},{5,1},{9,13},{13,9},{2,6},{6,2},{1... | collective-permute-start | bytes 1572872 | tf_op jit(solution)/shard_map/ppermute | solution.py:46
  25.4 14.0 %collective-permute-start.1 = (bf16[256,1024]{1,0:T(8,128)(2,1)}, bf16[256,1024]{1,0:T(8,128)(2,1)}, u32[]{:S(2)}, u32[]{:S(2)}) collective-permute-start(bf16[256,1024]{1,0:T(8,128)(2,1)} %get-tuple-element.148), channel_id=1, source_target_pairs={{0,1},{1,0},{2,3},{3,2},{4,5},{5,4},{6,7},{7,6},{8,9},{9,8},{10,11... | collective-permute-start | bytes 1572872 | tf_op jit(solution)/shard_map/ppermute | solution.py:38
  26.3 19.8 %collective-permute-start.9 = (bf16[256,1024]{1,0:T(8,128)(2,1)}, bf16[256,1024]{1,0:T(8,128)(2,1)}, u32[]{:S(2)}, u32[]{:S(2)}) collective-permute-start(bf16[256,1024]{1,0:T(8,128)(2,1)} %get-tuple-element.76), channel_id=1, source_target_pairs={{0,16},{16,0},{1,17},{17,1},{2,18},{18,2},{3,19},{19,3},{4,20},{20... | collective-permute-start | bytes 1572872 | tf_op jit(solution)/shard_map/ppermute | solution.py:34
  38.0 8.1 %collective-permute-start.8 = (f32[64,1024]{1,0:T(8,128)S(1)}, f32[64,1024]{1,0:T(8,128)}, u32[]{:S(2)}, u32[]{:S(2)}) collective-permute-start(f32[64,1024]{1,0:T(8,128)S(1)} %constant_dynamic-slice_fusion.1), channel_id=1, source_target_pairs={{0,32},{32,0},{64,96},{96,64},{1,33},{33,1},{65,97},{97,65},{2,34}... | collective-permute-start | bytes 786440 | tf_op jit(solution)/shard_map/ppermute | solution.py:100
  47.0 18.0 %collective-permute-start.13 = (bf16[256,1024]{1,0:T(8,128)(2,1)}, bf16[256,1024]{1,0:T(8,128)(2,1)S(1)}, u32[]{:S(2)}, u32[]{:S(2)}) collective-permute-start(bf16[256,1024]{1,0:T(8,128)(2,1)} %collective-permute-done.3), channel_id=1, source_target_pairs={{0,3},{1,2},{2,1},{3,0},{4,7},{5,6},{6,5},{7,4},{8,11},{9,10},{10,... | collective-permute-start | bytes 1572872 | tf_op jit(solution)/shard_map/ppermute | solution.py:42
  47.8 17.2 %collective-permute-start.12 = (bf16[256,1024]{1,0:T(8,128)(2,1)}, bf16[256,1024]{1,0:T(8,128)(2,1)S(1)}, u32[]{:S(2)}, u32[]{:S(2)}) collective-permute-start(bf16[256,1024]{1,0:T(8,128)(2,1)} %collective-permute-done.3), channel_id=1, source_target_pairs={{4,8},{8,4},{5,9},{9,5},{6,10},{10,6},{7,11},{11,7},{20,24},{24,20... | collective-permute-start | bytes 1572872 | tf_op jit(solution)/shard_map/ppermute | solution.py:46
  48.5 14.1 %collective-permute-start.10 = (bf16[512,512]{1,0:T(8,128)(2,1)S(1)}, bf16[512,512]{1,0:T(8,128)(2,1)S(1)}, u32[]{:S(2)}, u32[]{:S(2)}) collective-permute-start(bf16[512,512]{1,0:T(8,128)(2,1)S(1)} %copy-done.30), channel_id=1, source_target_pairs={{0,1},{1,0},{2,3},{3,2},{4,5},{5,4},{6,7},{7,6},{8,9},{9,8},{10,11... | collective-permute-start | bytes 1572872 | tf_op jit(solution)/shard_map/ppermute | solution.py:38
  49.6 15.3 %collective-permute-start.11 = (bf16[256,1024]{1,0:T(8,128)(2,1)}, bf16[256,1024]{1,0:T(8,128)(2,1)S(1)}, u32[]{:S(2)}, u32[]{:S(2)}) collective-permute-start(bf16[256,1024]{1,0:T(8,128)(2,1)} %collective-permute-done.4), channel_id=1, source_target_pairs={{4,0},{8,12},{5,1},{9,13},{6,2},{10,14},{7,3},{11,15},{20,16},{24,... | collective-permute-start | bytes 1572872 | tf_op jit(solution)/shard_map/ppermute | solution.py:46
  62.6 14.1 %collective-permute-start.18 = (bf16[256,1024]{1,0:T(8,128)(2,1)}, bf16[256,1024]{1,0:T(8,128)(2,1)S(1)}, u32[]{:S(2)}, u32[]{:S(2)}) collective-permute-start(bf16[256,1024]{1,0:T(8,128)(2,1)} %collective-permute-done.5), channel_id=1, source_target_pairs={{4,8},{8,4},{5,9},{9,5},{6,10},{10,6},{7,11},{11,7},{20,24},{24,20... | collective-permute-start | bytes 1572872 | tf_op jit(solution)/shard_map/ppermute | solution.py:46
  65.9 11.5 %collective-permute-start.20 = (bf16[32,1024]{1,0:T(8,128)(2,1)S(1)}, bf16[32,1024]{1,0:T(8,128)(2,1)S(1)}, u32[]{:S(2)}, u32[]{:S(2)}) collective-permute-start(bf16[32,1024]{1,0:T(8,128)(2,1)S(1)} %dynamic-slice_add_fusion.2), channel_id=1, source_target_pairs={{0,128},{128,0},{1,129},{129,1},{2,130},{130,2},{3,131},{131,3},{4... | collective-permute-start | bytes 196616 | tf_op jit(solution)/shard_map/ppermute | solution.py:100
  71.1 13.2 %collective-permute-start.19 = (bf16[256,1024]{1,0:T(8,128)(2,1)S(1)}, bf16[256,1024]{1,0:T(8,128)(2,1)S(1)}, u32[]{:S(2)}, u32[]{:S(2)}) collective-permute-start(bf16[256,1024]{1,0:T(8,128)(2,1)S(1)} %add_convert_fusion.7), channel_id=1, source_target_pairs={{0,3},{1,2},{2,1},{3,0},{4,7},{5,6},{6,5},{7,4},{8,11},{9,10},{10,... | collective-permute-start | bytes 1572872 | tf_op jit(solution)/shard_map/ppermute | solution.py:42
  72.9 11.5 %collective-permute-start.16 = (bf16[512,512]{1,0:T(8,128)(2,1)S(1)}, bf16[512,512]{1,0:T(8,128)(2,1)S(1)}, u32[]{:S(2)}, u32[]{:S(2)}) collective-permute-start(bf16[512,512]{1,0:T(8,128)(2,1)S(1)} %copy-done.29), channel_id=1, source_target_pairs={{0,1},{1,0},{2,3},{3,2},{4,5},{5,4},{6,7},{7,6},{8,9},{9,8},{10,11... | collective-permute-start | bytes 1572872 | tf_op jit(solution)/shard_map/ppermute | solution.py:38
  72.9 14.5 %collective-permute-start.17 = (bf16[256,1024]{1,0:T(8,128)(2,1)S(1)}, bf16[256,1024]{1,0:T(8,128)(2,1)S(1)}, u32[]{:S(2)}, u32[]{:S(2)}) collective-permute-start(bf16[256,1024]{1,0:T(8,128)(2,1)S(1)} %collective-permute-done.12), channel_id=1, source_target_pairs={{4,0},{8,12},{5,1},{9,13},{6,2},{10,14},{7,3},{11,15},{20,16},{24,... | collective-permute-start | bytes 1572872 | tf_op jit(solution)/shard_map/ppermute | solution.py:46
  76.7 16.6 %collective-permute-start.23 = (bf16[256,1024]{1,0:T(8,128)(2,1)S(1)}, bf16[256,1024]{1,0:T(8,128)(2,1)S(1)}, u32[]{:S(2)}, u32[]{:S(2)}) collective-permute-start(bf16[256,1024]{1,0:T(8,128)(2,1)S(1)} %collective-permute-done.13), channel_id=1, source_target_pairs={{4,8},{8,4},{5,9},{9,5},{6,10},{10,6},{7,11},{11,7},{20,24},{24,20... | collective-permute-start | bytes 1572872 | tf_op jit(solution)/shard_map/ppermute | solution.py:46
  87.8 12.1 %collective-permute-start.24 = (bf16[256,1024]{1,0:T(8,128)(2,1)S(1)}, bf16[256,1024]{1,0:T(8,128)(2,1)S(1)}, u32[]{:S(2)}, u32[]{:S(2)}) collective-permute-start(bf16[256,1024]{1,0:T(8,128)(2,1)S(1)} %add_convert_fusion.6), channel_id=1, source_target_pairs={{0,3},{1,2},{2,1},{3,0},{4,7},{5,6},{6,5},{7,4},{8,11},{9,10},{10,... | collective-permute-start | bytes 1572872 | tf_op jit(solution)/shard_map/ppermute | solution.py:42
  90.1 11.2 %collective-permute-start.22 = (bf16[256,1024]{1,0:T(8,128)(2,1)S(1)}, bf16[256,1024]{1,0:T(8,128)(2,1)S(1)}, u32[]{:S(2)}, u32[]{:S(2)}) collective-permute-start(bf16[256,1024]{1,0:T(8,128)(2,1)S(1)} %get-tuple-element.146), channel_id=1, source_target_pairs={{0,4},{4,0},{8,12},{12,8},{1,5},{5,1},{9,13},{13,9},{2,6},{6,2},{1... | collective-permute-start | bytes 1572872 | tf_op jit(solution)/shard_map/ppermute | solution.py:46
  90.2 11.1 %collective-permute-start.21 = (bf16[512,512]{1,0:T(8,128)(2,1)S(1)}, bf16[512,512]{1,0:T(8,128)(2,1)S(1)}, u32[]{:S(2)}, u32[]{:S(2)}) collective-permute-start(bf16[512,512]{1,0:T(8,128)(2,1)S(1)} %copy-done.28), channel_id=1, source_target_pairs={{0,1},{1,0},{2,3},{3,2},{4,5},{5,4},{6,7},{7,6},{8,9},{9,8},{10,11... | collective-permute-start | bytes 1572872 | tf_op jit(solution)/shard_map/ppermute | solution.py:38
  102.0 11.3 %collective-permute-start.29 = (bf16[256,1024]{1,0:T(8,128)(2,1)S(1)}, bf16[256,1024]{1,0:T(8,128)(2,1)S(1)}, u32[]{:S(2)}, u32[]{:S(2)}) collective-permute-start(bf16[256,1024]{1,0:T(8,128)(2,1)S(1)} %add_convert_fusion.4), channel_id=1, source_target_pairs={{0,3},{1,2},{2,1},{3,0},{4,7},{5,6},{6,5},{7,4},{8,11},{9,10},{10,... | collective-permute-start | bytes 1572872 | tf_op jit(solution)/shard_map/ppermute | solution.py:42
  103.2 10.1 %collective-permute-start.28 = (bf16[256,1024]{1,0:T(8,128)(2,1)S(1)}, bf16[256,1024]{1,0:T(8,128)(2,1)S(1)}, u32[]{:S(2)}, u32[]{:S(2)}) collective-permute-start(bf16[256,1024]{1,0:T(8,128)(2,1)S(1)} %add_convert_fusion.5), channel_id=1, source_target_pairs={{4,8},{8,4},{5,9},{9,5},{6,10},{10,6},{7,11},{11,7},{20,24},{24,20... | collective-permute-start | bytes 1572872 | tf_op jit(solution)/shard_map/ppermute | solution.py:46
  103.9 10.2 %collective-permute-start.26 = (bf16[512,512]{1,0:T(8,128)(2,1)S(1)}, bf16[512,512]{1,0:T(8,128)(2,1)S(1)}, u32[]{:S(2)}, u32[]{:S(2)}) collective-permute-start(bf16[512,512]{1,0:T(8,128)(2,1)S(1)} %copy-done.27), channel_id=1, source_target_pairs={{0,1},{1,0},{2,3},{3,2},{4,5},{5,4},{6,7},{7,6},{8,9},{9,8},{10,11... | collective-permute-start | bytes 1572872 | tf_op jit(solution)/shard_map/ppermute | solution.py:38
  105.3 9.6 %collective-permute-start.27 = (bf16[256,1024]{1,0:T(8,128)(2,1)S(1)}, bf16[256,1024]{1,0:T(8,128)(2,1)S(1)}, u32[]{:S(2)}, u32[]{:S(2)}) collective-permute-start(bf16[256,1024]{1,0:T(8,128)(2,1)S(1)} %get-tuple-element.144), channel_id=1, source_target_pairs={{0,4},{4,0},{8,12},{12,8},{1,5},{5,1},{9,13},{13,9},{2,6},{6,2},{1... | collective-permute-start | bytes 1572872 | tf_op jit(solution)/shard_map/ppermute | solution.py:46
  121.6 10.0 %collective-permute-start.30 = (bf16[512,1024]{1,0:T(8,128)(2,1)}, bf16[512,1024]{1,0:T(8,128)(2,1)}, u32[]{:S(2)}, u32[]{:S(2)}) collective-permute-start(bf16[512,1024]{1,0:T(8,128)(2,1)} %get-tuple-element.159), channel_id=1, source_target_pairs={{0,16},{16,0},{1,17},{17,1},{2,18},{18,2},{3,19},{19,3},{4,20},{20... | collective-permute-start | bytes 3145736 | tf_op jit(solution)/shard_map/ppermute | solution.py:34
  129.0 22.9 %collective-permute-start.34 = (bf16[256,1024]{1,0:T(8,128)(2,1)S(1)}, bf16[256,1024]{1,0:T(8,128)(2,1)S(1)}, u32[]{:S(2)}, u32[]{:S(2)}) collective-permute-start(bf16[256,1024]{1,0:T(8,128)(2,1)S(1)} %add_convert_fusion.1), channel_id=1, source_target_pairs={{0,3},{1,2},{2,1},{3,0},{4,7},{5,6},{6,5},{7,4},{8,11},{9,10},{10,... | collective-permute-start | bytes 1572872 | tf_op jit(solution)/shard_map/ppermute | solution.py:42
  135.4 16.5 %collective-permute-start.31 = (bf16[512,1024]{1,0:T(8,128)(2,1)S(1)}, bf16[512,1024]{1,0:T(8,128)(2,1)S(1)}, u32[]{:S(2)}, u32[]{:S(2)}) collective-permute-start(bf16[512,1024]{1,0:T(8,128)(2,1)S(1)} %add_convert_fusion), channel_id=1, source_target_pairs={{1,16},{2,19},{16,1},{19,2},{5,20},{6,23},{20,5},{23,6},{9,24},{10... | collective-permute-start | bytes 3145736 | tf_op jit(solution)/shard_map/ppermute | solution.py:30
  138.6 13.3 %collective-permute-start.33 = (bf16[256,1024]{1,0:T(8,128)(2,1)S(1)}, bf16[256,1024]{1,0:T(8,128)(2,1)S(1)}, u32[]{:S(2)}, u32[]{:S(2)}) collective-permute-start(bf16[256,1024]{1,0:T(8,128)(2,1)S(1)} %add_convert_fusion.2), channel_id=1, source_target_pairs={{4,8},{8,4},{5,9},{9,5},{6,10},{10,6},{7,11},{11,7},{20,24},{24,20... | collective-permute-start | bytes 1572872 | tf_op jit(solution)/shard_map/ppermute | solution.py:46
  139.8 14.2 %collective-permute-start.32 = (bf16[256,1024]{1,0:T(8,128)(2,1)S(1)}, bf16[256,1024]{1,0:T(8,128)(2,1)S(1)}, u32[]{:S(2)}, u32[]{:S(2)}) collective-permute-start(bf16[256,1024]{1,0:T(8,128)(2,1)S(1)} %add_convert_fusion.3), channel_id=1, source_target_pairs={{0,4},{4,0},{8,12},{12,8},{1,5},{5,1},{9,13},{13,9},{2,6},{6,2},{1... | collective-permute-start | bytes 1572872 | tf_op jit(solution)/shard_map/ppermute | solution.py:46
  154.5 10.6 %collective-permute-start.35 = (bf16[256,1024]{1,0:T(8,128)(2,1)S(1)}, bf16[256,1024]{1,0:T(8,128)(2,1)S(1)}, u32[]{:S(2)}, u32[]{:S(2)}) collective-permute-start(bf16[256,1024]{1,0:T(8,128)(2,1)S(1)} %get-tuple-element.142), channel_id=1, source_target_pairs={{1,16},{2,19},{16,1},{19,2},{5,20},{6,23},{20,5},{23,6},{9,24},{10... | collective-permute-start | bytes 1572872 | tf_op jit(solution)/shard_map/ppermute | solution.py:30
  (37 other events, 258.6 us)

commit v5 on v3

--- a/solution.py
+++ b/solution.py
@@ -58,26 +58,39 @@
     return lax.optimization_barrier(arrays)
 
 
-def move(_, a, b, to_a, to_b):
-    to_a[0] = a[...]
-    to_b[0] = b[...]
-
-
-def halves(tokens, blocks):
-    spec = lambda i: pl.BlockSpec((512, 256), lambda n, table: (0, table[i, n]))
-    out = pl.BlockSpec((1, 512, 256), lambda n, table: (n // 2, 0, n % 2))
+def sort_columns(table, tokens, give, own, sems):
+    copies = []
+    for half, out in enumerate((give, own)):
+        for n in range(8):
+            column = pl.multiple_of(table[half, n] * 256, 256)
+            copies.append(
+                pltpu.make_async_copy(
+                    tokens.at[:, pl.ds(column, 256)],
+                    out.at[n // 2, :, pl.ds(n % 2 * 256, 256)],
+                    sems.at[half, n],
+                )
+            )
+    for copy in copies:
+        copy.start()
+    for copy in copies:
+        copy.wait()
+
+
+def halves(tokens, table):
     kind = jax.ShapeDtypeStruct((4, 512, 512), bf16)
+    anywhere = pl.BlockSpec(memory_space=pl.ANY)
     return pl.pallas_call(
-        move,
+        sort_columns,
         grid_spec=pltpu.PrefetchScalarGridSpec(
             num_scalar_prefetch=1,
-            grid=(8,),
-            in_specs=[spec(0), spec(1)],
-            out_specs=[out, out],
+            grid=(1,),
+            in_specs=[anywhere],
+            out_specs=[anywhere, anywhere],
+            scratch_shapes=[pltpu.SemaphoreType.DMA((2, 8))],
         ),
         out_shape=[kind, kind],
-        cost_estimate=pl.CostEstimate(flops=0, bytes_accessed=16 << 20, transcendentals=0),
-    )(blocks, tokens, tokens)
+        cost_estimate=pl.CostEstimate(flops=0, bytes_accessed=8 << 20, transcendentals=0),
+    )(table, tokens)
 
 
 class Drift:
@@ -133,26 +146,34 @@
     ).reshape(2, 8)
 
     w = jnp.where(stays, weight, swap(weight))
-    g_sib = core(key_grad)
-    x_give, x_own = halves(tokens, blocks.astype(jnp.int32))
+    g_mine = lax.dynamic_slice_in_dim(key_grad, c * 256, 256, 0)
+    g_first = core(lax.dynamic_slice_in_dim(key_grad, (1 - c) * 256, 256, 0))
+    g_l = jnp.where(stays, g_first, g_mine)
+    drift = Drift(anchor - local_params[0].astype(f32), c, y)
+    d = drift.send()
+    blocks = blocks.astype(jnp.int32)
+    w, g_l, g_mine, g_first, blocks, d, drift.v = together(
+        w, g_l, g_mine, g_first, blocks, d, drift.v
+    )
+    drift.take(d)
+
+    x_give, x_own = halves(tokens, blocks)
     x_sib = core(x_give)
-    drift = Drift(anchor - local_params[0].astype(f32), c, y)
-    drift.take(drift.send())
-    g_a = jnp.where(stays, key_grad, g_sib)
-    g_l = lax.dynamic_slice_in_dim(jnp.where(stays, g_sib, key_grad), c * 256, 256, 0)
-
     got = (beside(g_l), line(w, PAIRS), line(w, MIDDLE), across(w), drift.send())
     leave = [jnp.where(stays, x_sib[k], x_own[k]) for k in range(4)]
     keep = [jnp.where(stays, x_own[k], x_sib[k]) for k in range(4)]
-    got, leave, drift.v = together(got, leave, drift.v)
+    got, leave, g_mine, drift.v = together(got, leave, g_mine, drift.v)
     g_half, e_own, m_own, q_own, d = got
     drift.take(d)
 
     got = (beside(leave[0]), line(m_own, ENDS_OUT), line(e_own, MIDDLE), across(e_own), drift.send())
-    g_rest = core(g_half)
-    g_b = jnp.where(
-        c == 0, jnp.concatenate([g_half, g_rest]), jnp.concatenate([g_rest, g_half])
-    )
+    rest = core(jnp.concatenate([g_half, g_mine]))
+
+    def in_order(a, b):
+        return jnp.where(c == 0, jnp.concatenate([a, b]), jnp.concatenate([b, a]))
+
+    g_b = in_order(g_half, rest[:256])
+    g_a = jnp.where(stays, key_grad, in_order(g_first, rest[256:]))
     base = [dot_t(k, g_a) for k in keep]
     sent = drift.v
     got, leave, sent, g_b, base = together(got, leave, sent, g_b, base)

time: 159 us -> 283 us (1.78)
  Pallas kernels: 7.37 us -> 129 us
  waiting for transfers between devices: 56.8 us -> 44.7 us
  local copies, waits for them, and re-layouts: 1.65 us -> 7.4 us
  matrix products: 12 us -> 16.3 us
  other arithmetic: 17.4 us -> 20.8 us
    pallas_call x1, Pallas kernels: 7.37 us -> 129 us  [halves(): pl.pallas_call(sort_columns, grid_spec=pltpu.PrefetchScalarGridSpec(num_s...]
    ppermute x7, waiting for transfers between devices: 8.57 us -> 3.46 us  [send(): return lax.ppermute(self.sent, axis, perm)]
    ppermute x3, waiting for transfers between devices: 12.7 us -> 8.86 us  [swap(): return lax.ppermute(v, ('c', 'x'), SWAP)]
    ppermute x6, waiting for transfers between devices: 19.2 us -> 15.7 us  [across(): return lax.ppermute(v, 'x', ACROSS)]
    select_n x1, other arithmetic: 0.33 us -> 3.26 us  [on_device(): keep = [jnp.where(stays, x_own[k], x_sib[k]) for k in range(4)]]
  transfers between devices with their start and end apart: 37 -> 37, of which waited for: 15 -> 16; matrix products, arithmetic and copies ran while one was open for 17% -> 13% of each run, Pallas kernels for 0% -> 0%
where the time goes in v5:
time: 283 us; the launch traced here: 282 us
  Pallas kernels  129 us (46%)
  starting transfers between devices  62.8 us (22%)
  waiting for transfers between devices  44.7 us (16%)
  other arithmetic  20.8 us (7%)
  matrix products  16.3 us (6%)
  local copies, waits for them, and re-layouts  7.4 us (3%)
    pallas_call x1, Pallas kernels, halves(): pl.pallas_call(sort_columns, grid_spec=pltpu.PrefetchScalarGridSpec(num_s...  129 us
    ppermute x12, starting transfers between devices, line(): return lax.ppermute(v, 'zl', pairs)  18.5 us
    ppermute x6, waiting for transfers between devices, across(): return lax.ppermute(v, 'x', ACROSS)  15.7 us
    ppermute x7, starting transfers between devices, send(): return lax.ppermute(self.sent, axis, perm)  12.4 us
    ppermute x12, waiting for transfers between devices, line(): return lax.ppermute(v, 'zl', pairs)  10.2 us
    ppermute x3, starting transfers between devices, swap(): return lax.ppermute(v, ('c', 'x'), SWAP)  9.85 us
    ppermute x6, starting transfers between devices, across(): return lax.ppermute(v, 'x', ACROSS)  9.43 us
    ppermute x4, starting transfers between devices, core(): return lax.ppermute(v, 'c', CORE)  9.31 us
  transfers between devices with their start and end apart: 37, of which 16 were waited for; matrix products, arithmetic and copies ran while one was open for 13% of the time, Pallas kernels for 0%

profile of v5, /device:TPU:1, one launch (start us, length us, event | category | flops | bytes accessed | tf_op | source)
XLA Modules:
  0.0 282.3 jit_solution(7114859922756415070)
XLA Ops:
  0.6 4.5 %collective-permute-start = (bf16[256,1024]{1,0:T(8,128)(2,1)}, bf16[256,1024]{1,0:T(8,128)(2,1)}, u32[]{:S(2)}, u32[]{:S(2)}) collective-permute-start(bf16[256,1024]{1,0:T(8,128)(2,1)} %bitcast.76), channel_id=1, source_target_pairs={{1,16},{2,19},{16,1},{19,2},{5,20},{6,23},{20,5},{23,6},{9,24},{10... | collective-permute-start | bytes 1572872 | tf_op jit(solution)/shard_map/ppermute | solution.py:30
  5.2 1.9 constant_dynamic-slice_fusion.4
  12.3 1.9 broadcast_select_fusion.8
  15.4 129.0 %shard_map.127 = (bf16[4,512,512]{2,1,0:T(8,128)(2,1)}, bf16[4,512,512]{2,1,0:T(8,128)(2,1)}) custom-call(s32[2,8]{1,0:T(2,128)} %reshape.37.table, bf16[512,4096]{1,0:T(8,128)(2,1)} %tokens.1), custom_call_target="tpu_custom_call" | custom-call | bytes 8388608 | tf_op jit(solution)/shard_map/pallas_call | solution.py:82
  144.6 2.5 collective-permute-start.6
  147.8 4.6 %collective-permute-start.4 = (bf16[256,1024]{1,0:T(8,128)(2,1)}, bf16[256,1024]{1,0:T(8,128)(2,1)S(1)}, u32[]{:S(2)}, u32[]{:S(2)}) collective-permute-start(bf16[256,1024]{1,0:T(8,128)(2,1)} %broadcast_select_fusion.8), channel_id=1, source_target_pairs={{0,4},{4,0},{8,12},{12,8},{1,5},{5,1},{9,13},{13,9},{2,6},{6,2},{1... | collective-permute-start | bytes 1572872 | tf_op jit(solution)/shard_map/ppermute | solution.py:46
  156.2 3.3 %select_bitcast_fusion = (bf16[512,512]{1,0:T(8,128)(2,1)}, bf16[512,512]{1,0:T(8,128)(2,1)}, bf16[512,512]{1,0:T(8,128)(2,1)}, bf16[512,512]{1,0:T(8,128)(2,1)}...) fusion(pred[]{:T(512)S(6)} %eq.37, bf16[4,512,512]{2,1,0:T(8,128)(2,1)} %collective-permute-done.8, ...), kind=kLoop, calls=%fused_computation.81 | loop fusion | flops 1572864 | bytes 7340033 | tf_op jit(solution)/shard_map/jit(_where)/select_n | solution.py:164
  159.4 2.0 collective-permute-done.7
  161.4 3.4 %collective-permute-done.3 = bf16[256,1024]{1,0:T(8,128)(2,1)S(1)} collective-permute-done((bf16[256,1024]{1,0:T(8,128)(2,1)}, bf16[256,1024]{1,0:T(8,128)(2,1)S(1)}, u32[]{:S(2)}, u32[]{:S(2)}) %collective-permute-start.3) | collective-permute-done | bytes 524320 | tf_op jit(solution)/shard_map/ppermute | solution.py:38
  166.7 2.2 collective-permute-start.14
  171.0 3.0 %collective-permute-start.13 = (f32[32,1024]{1,0:T(8,128)S(1)}, f32[32,1024]{1,0:T(8,128)S(1)}, u32[]{:S(2)}, u32[]{:S(2)}) collective-permute-start(f32[32,1024]{1,0:T(8,128)S(1)} %constant_dynamic-slice_fusion), channel_id=1, source_target_pairs={{0,64},{32,96},{64,0},{96,32},{1,65},{33,97},{65,1},{97,33},{2,66}... | collective-permute-start | bytes 393224 | tf_op jit(solution)/shard_map/ppermute | solution.py:114
  178.7 1.8 fusion.41
  181.3 1.8 fusion.44
  185.1 1.9 collective-permute-done.9
  186.9 1.9 collective-permute-done.10
  189.9 5.2 %collective-permute-start.19 = (bf16[32,1024]{1,0:T(8,128)(2,1)S(1)}, bf16[32,1024]{1,0:T(8,128)(2,1)S(1)}, u32[]{:S(2)}, u32[]{:S(2)}) collective-permute-start(bf16[32,1024]{1,0:T(8,128)(2,1)S(1)} %dynamic-slice_add_fusion.2), channel_id=1, source_target_pairs={{0,128},{128,0},{1,129},{129,1},{2,130},{130,2},{3,131},{131,3},{4... | collective-permute-start | bytes 196616 | tf_op jit(solution)/shard_map/ppermute | solution.py:114
  195.1 2.0 collective-permute-start.18
  201.3 6.3 %collective-permute-done.18 = bf16[256,1024]{1,0:T(8,128)(2,1)S(1)} collective-permute-done((bf16[256,1024]{1,0:T(8,128)(2,1)S(1)}, bf16[256,1024]{1,0:T(8,128)(2,1)S(1)}, u32[]{:S(2)}, u32[]{:S(2)}) %collective-permute-start.18) | collective-permute-done | bytes 524320 | tf_op jit(solution)/shard_map/ppermute | solution.py:42
  208.2 2.2 collective-permute-done.16
  215.9 6.2 %collective-permute-done.23 = bf16[256,1024]{1,0:T(8,128)(2,1)S(1)} collective-permute-done((bf16[256,1024]{1,0:T(8,128)(2,1)S(1)}, bf16[256,1024]{1,0:T(8,128)(2,1)S(1)}, u32[]{:S(2)}, u32[]{:S(2)}) %collective-permute-start.23) | collective-permute-done | bytes 524320 | tf_op jit(solution)/shard_map/ppermute | solution.py:42
  227.1 3.1 %collective-permute-start.26 = (bf16[256,1024]{1,0:T(8,128)(2,1)S(1)}, bf16[256,1024]{1,0:T(8,128)(2,1)S(1)}, u32[]{:S(2)}, u32[]{:S(2)}) collective-permute-start(bf16[256,1024]{1,0:T(8,128)(2,1)S(1)} %get-tuple-element.136), channel_id=1, source_target_pairs={{0,4},{4,0},{8,12},{12,8},{1,5},{5,1},{9,13},{13,9},{2,6},{6,2},{1... | collective-permute-start | bytes 1572872 | tf_op jit(solution)/shard_map/ppermute | solution.py:46
  234.8 2.3 collective-permute-done.26
  237.2 1.8 fusion.32
  240.3 6.8 %collective-permute-start.30 = (bf16[512,1024]{1,0:T(8,128)(2,1)S(1)}, bf16[512,1024]{1,0:T(8,128)(2,1)S(1)}, u32[]{:S(2)}, u32[]{:S(2)}) collective-permute-start(bf16[512,1024]{1,0:T(8,128)(2,1)S(1)} %get-tuple-element.153), channel_id=1, source_target_pairs={{0,16},{16,0},{1,17},{17,1},{2,18},{18,2},{3,19},{19,3},{4,20},{20... | collective-permute-start | bytes 3145736 | tf_op jit(solution)/shard_map/ppermute | solution.py:34
  247.6 1.9 collective-permute-start.32
  250.6 3.8 %collective-permute-start.33 = (bf16[256,1024]{1,0:T(8,128)(2,1)S(1)}, bf16[256,1024]{1,0:T(8,128)(2,1)S(1)}, u32[]{:S(2)}, u32[]{:S(2)}) collective-permute-start(bf16[256,1024]{1,0:T(8,128)(2,1)S(1)} %add_convert_fusion.2), channel_id=1, source_target_pairs={{0,4},{4,0},{8,12},{12,8},{1,5},{5,1},{9,13},{13,9},{2,6},{6,2},{1... | collective-permute-start | bytes 1572872 | tf_op jit(solution)/shard_map/ppermute | solution.py:46
  257.0 2.1 collective-permute-start.31
  259.2 3.3 %collective-permute-done.32 = bf16[256,1024]{1,0:T(8,128)(2,1)S(1)} collective-permute-done((bf16[256,1024]{1,0:T(8,128)(2,1)S(1)}, bf16[256,1024]{1,0:T(8,128)(2,1)S(1)}, u32[]{:S(2)}, u32[]{:S(2)}) %collective-permute-start.32) | collective-permute-done | bytes 524320 | tf_op jit(solution)/shard_map/ppermute | solution.py:42
  262.4 3.7 %collective-permute-done.33 = bf16[256,1024]{1,0:T(8,128)(2,1)S(1)} collective-permute-done((bf16[256,1024]{1,0:T(8,128)(2,1)S(1)}, bf16[256,1024]{1,0:T(8,128)(2,1)S(1)}, u32[]{:S(2)}, u32[]{:S(2)}) %collective-permute-start.33) | collective-permute-done | bytes 524320 | tf_op jit(solution)/shard_map/ppermute | solution.py:46
  266.6 3.2 %collective-permute-start.35 = (bf16[256,1024]{1,0:T(8,128)(2,1)S(1)}, bf16[256,1024]{1,0:T(8,128)(2,1)S(1)}, u32[]{:S(2)}, u32[]{:S(2)}) collective-permute-start(bf16[256,1024]{1,0:T(8,128)(2,1)S(1)} %get-tuple-element.134), channel_id=1, source_target_pairs={{1,16},{2,19},{16,1},{19,2},{5,20},{6,23},{20,5},{23,6},{9,24},{10... | collective-permute-start | bytes 1572872 | tf_op jit(solution)/shard_map/ppermute | solution.py:30
  271.6 7.3 %collective-permute-done.35 = bf16[256,1024]{1,0:T(8,128)(2,1)S(1)} collective-permute-done((bf16[256,1024]{1,0:T(8,128)(2,1)S(1)}, bf16[256,1024]{1,0:T(8,128)(2,1)S(1)}, u32[]{:S(2)}, u32[]{:S(2)}) %collective-permute-start.35) | collective-permute-done | bytes 524320 | tf_op jit(solution)/shard_map/ppermute | solution.py:30
  278.9 2.3 fusion.83
  (149 shorter events, 51.7 us)
Async XLA Ops:
  0.6 11.7 %collective-permute-start = (bf16[256,1024]{1,0:T(8,128)(2,1)}, bf16[256,1024]{1,0:T(8,128)(2,1)}, u32[]{:S(2)}, u32[]{:S(2)}) collective-permute-start(bf16[256,1024]{1,0:T(8,128)(2,1)} %bitcast.76), channel_id=1, source_target_pairs={{1,16},{2,19},{16,1},{19,2},{5,20},{6,23},{20,5},{23,6},{9,24},{10... | collective-permute-start | bytes 1572872 | tf_op jit(solution)/shard_map/ppermute | solution.py:30
  144.5 10.3 %collective-permute-start.8 = (bf16[4,512,512]{2,1,0:T(8,128)(2,1)}, bf16[4,512,512]{2,1,0:T(8,128)(2,1)}, u32[]{:S(2)}, u32[]{:S(2)}) collective-permute-start(bf16[4,512,512]{2,1,0:T(8,128)(2,1)} %get-tuple-element.74), channel_id=1, source_target_pairs={{0,16},{16,0},{1,17},{17,1},{2,18},{18,2},{3,19},{19,3},{4,20},{20... | collective-permute-start | bytes 6291464 | tf_op jit(solution)/shard_map/ppermute | solution.py:34
  144.6 20.2 %collective-permute-start.6 = (bf16[256,1024]{1,0:T(8,128)(2,1)}, bf16[256,1024]{1,0:T(8,128)(2,1)S(1)}, u32[]{:S(2)}, u32[]{:S(2)}) collective-permute-start(bf16[256,1024]{1,0:T(8,128)(2,1)} %broadcast_select_fusion.8), channel_id=1, source_target_pairs={{0,3},{1,2},{2,1},{3,0},{4,7},{5,6},{6,5},{7,4},{8,11},{9,10},{10,... | collective-permute-start | bytes 1572872 | tf_op jit(solution)/shard_map/ppermute | solution.py:42
  147.1 17.7 %collective-permute-start.5 = (bf16[256,1024]{1,0:T(8,128)(2,1)}, bf16[256,1024]{1,0:T(8,128)(2,1)S(1)}, u32[]{:S(2)}, u32[]{:S(2)}) collective-permute-start(bf16[256,1024]{1,0:T(8,128)(2,1)} %broadcast_select_fusion.8), channel_id=1, source_target_pairs={{4,8},{8,4},{5,9},{9,5},{6,10},{10,6},{7,11},{11,7},{20,24},{24,20... | collective-permute-start | bytes 1572872 | tf_op jit(solution)/shard_map/ppermute | solution.py:46
  147.8 17.0 %collective-permute-start.4 = (bf16[256,1024]{1,0:T(8,128)(2,1)}, bf16[256,1024]{1,0:T(8,128)(2,1)S(1)}, u32[]{:S(2)}, u32[]{:S(2)}) collective-permute-start(bf16[256,1024]{1,0:T(8,128)(2,1)} %broadcast_select_fusion.8), channel_id=1, source_target_pairs={{0,4},{4,0},{8,12},{12,8},{1,5},{5,1},{9,13},{13,9},{2,6},{6,2},{1... | collective-permute-start | bytes 1572872 | tf_op jit(solution)/shard_map/ppermute | solution.py:46
  152.4 12.4 %collective-permute-start.3 = (bf16[256,1024]{1,0:T(8,128)(2,1)}, bf16[256,1024]{1,0:T(8,128)(2,1)S(1)}, u32[]{:S(2)}, u32[]{:S(2)}) collective-permute-start(bf16[256,1024]{1,0:T(8,128)(2,1)} %get-tuple-element.69), channel_id=1, source_target_pairs={{0,1},{1,0},{2,3},{3,2},{4,5},{5,4},{6,7},{7,6},{8,9},{9,8},{10,11... | collective-permute-start | bytes 1572872 | tf_op jit(solution)/shard_map/ppermute | solution.py:38
  168.9 20.0 %collective-permute-start.12 = (bf16[256,1024]{1,0:T(8,128)(2,1)}, bf16[256,1024]{1,0:T(8,128)(2,1)S(1)}, u32[]{:S(2)}, u32[]{:S(2)}) collective-permute-start(bf16[256,1024]{1,0:T(8,128)(2,1)} %copy-done.25), channel_id=1, source_target_pairs={{0,3},{1,2},{2,1},{3,0},{4,7},{5,6},{6,5},{7,4},{8,11},{9,10},{10,... | collective-permute-start | bytes 1572872 | tf_op jit(solution)/shard_map/ppermute | solution.py:42
  169.3 19.6 %collective-permute-start.11 = (bf16[256,1024]{1,0:T(8,128)(2,1)}, bf16[256,1024]{1,0:T(8,128)(2,1)S(1)}, u32[]{:S(2)}, u32[]{:S(2)}) collective-permute-start(bf16[256,1024]{1,0:T(8,128)(2,1)} %copy-done.25), channel_id=1, source_target_pairs={{4,8},{8,4},{5,9},{9,5},{6,10},{10,6},{7,11},{11,7},{20,24},{24,20... | collective-permute-start | bytes 1572872 | tf_op jit(solution)/shard_map/ppermute | solution.py:46
  171.0 12.7 %collective-permute-start.13 = (f32[32,1024]{1,0:T(8,128)S(1)}, f32[32,1024]{1,0:T(8,128)S(1)}, u32[]{:S(2)}, u32[]{:S(2)}) collective-permute-start(f32[32,1024]{1,0:T(8,128)S(1)} %constant_dynamic-slice_fusion), channel_id=1, source_target_pairs={{0,64},{32,96},{64,0},{96,32},{1,65},{33,97},{65,1},{97,33},{2,66}... | collective-permute-start | bytes 393224 | tf_op jit(solution)/shard_map/ppermute | solution.py:114
  174.0 12.9 %collective-permute-start.9 = (bf16[512,512]{1,0:T(8,128)(2,1)}, bf16[512,512]{1,0:T(8,128)(2,1)S(1)}, u32[]{:S(2)}, u32[]{:S(2)}) collective-permute-start(bf16[512,512]{1,0:T(8,128)(2,1)} %get-tuple-element.77), channel_id=1, source_target_pairs={{0,1},{1,0},{2,3},{3,2},{4,5},{5,4},{6,7},{7,6},{8,9},{9,8},{10,11... | collective-permute-start | bytes 1572872 | tf_op jit(solution)/shard_map/ppermute | solution.py:38
  174.4 14.5 %collective-permute-start.10 = (bf16[256,1024]{1,0:T(8,128)(2,1)}, bf16[256,1024]{1,0:T(8,128)(2,1)S(1)}, u32[]{:S(2)}, u32[]{:S(2)}) collective-permute-start(bf16[256,1024]{1,0:T(8,128)(2,1)} %copy-done.18), channel_id=1, source_target_pairs={{4,0},{8,12},{5,1},{9,13},{6,2},{10,14},{7,3},{11,15},{20,16},{24,... | collective-permute-start | bytes 1572872 | tf_op jit(solution)/shard_map/ppermute | solution.py:46
  184.2 16.3 %collective-permute-start.17 = (bf16[256,1024]{1,0:T(8,128)(2,1)S(1)}, bf16[256,1024]{1,0:T(8,128)(2,1)S(1)}, u32[]{:S(2)}, u32[]{:S(2)}) collective-permute-start(bf16[256,1024]{1,0:T(8,128)(2,1)S(1)} %copy-done.24), channel_id=1, source_target_pairs={{4,8},{8,4},{5,9},{9,5},{6,10},{10,6},{7,11},{11,7},{20,24},{24,20... | collective-permute-start | bytes 1572872 | tf_op jit(solution)/shard_map/ppermute | solution.py:46
  189.9 11.3 %collective-permute-start.19 = (bf16[32,1024]{1,0:T(8,128)(2,1)S(1)}, bf16[32,1024]{1,0:T(8,128)(2,1)S(1)}, u32[]{:S(2)}, u32[]{:S(2)}) collective-permute-start(bf16[32,1024]{1,0:T(8,128)(2,1)S(1)} %dynamic-slice_add_fusion.2), channel_id=1, source_target_pairs={{0,128},{128,0},{1,129},{129,1},{2,130},{130,2},{3,131},{131,3},{4... | collective-permute-start | bytes 196616 | tf_op jit(solution)/shard_map/ppermute | solution.py:114
  195.1 12.4 %collective-permute-start.18 = (bf16[256,1024]{1,0:T(8,128)(2,1)S(1)}, bf16[256,1024]{1,0:T(8,128)(2,1)S(1)}, u32[]{:S(2)}, u32[]{:S(2)}) collective-permute-start(bf16[256,1024]{1,0:T(8,128)(2,1)S(1)} %add_convert_fusion.7), channel_id=1, source_target_pairs={{0,3},{1,2},{2,1},{3,0},{4,7},{5,6},{6,5},{7,4},{8,11},{9,10},{10,... | collective-permute-start | bytes 1572872 | tf_op jit(solution)/shard_map/ppermute | solution.py:42
  197.2 11.1 %collective-permute-start.15 = (bf16[512,512]{1,0:T(8,128)(2,1)S(1)}, bf16[512,512]{1,0:T(8,128)(2,1)S(1)}, u32[]{:S(2)}, u32[]{:S(2)}) collective-permute-start(bf16[512,512]{1,0:T(8,128)(2,1)S(1)} %copy-done.22), channel_id=1, source_target_pairs={{0,1},{1,0},{2,3},{3,2},{4,5},{5,4},{6,7},{7,6},{8,9},{9,8},{10,11... | collective-permute-start | bytes 1572872 | tf_op jit(solution)/shard_map/ppermute | solution.py:38
  197.9 12.5 %collective-permute-start.16 = (bf16[256,1024]{1,0:T(8,128)(2,1)S(1)}, bf16[256,1024]{1,0:T(8,128)(2,1)S(1)}, u32[]{:S(2)}, u32[]{:S(2)}) collective-permute-start(bf16[256,1024]{1,0:T(8,128)(2,1)S(1)} %collective-permute-done.11), channel_id=1, source_target_pairs={{4,0},{8,12},{5,1},{9,13},{6,2},{10,14},{7,3},{11,15},{20,16},{24,... | collective-permute-start | bytes 1572872 | tf_op jit(solution)/shard_map/ppermute | solution.py:46
  200.5 13.8 %collective-permute-start.22 = (bf16[256,1024]{1,0:T(8,128)(2,1)S(1)}, bf16[256,1024]{1,0:T(8,128)(2,1)S(1)}, u32[]{:S(2)}, u32[]{:S(2)}) collective-permute-start(bf16[256,1024]{1,0:T(8,128)(2,1)S(1)} %collective-permute-done.12), channel_id=1, source_target_pairs={{4,8},{8,4},{5,9},{9,5},{6,10},{10,6},{7,11},{11,7},{20,24},{24,20... | collective-permute-start | bytes 1572872 | tf_op jit(solution)/shard_map/ppermute | solution.py:46
  211.2 10.8 %collective-permute-start.23 = (bf16[256,1024]{1,0:T(8,128)(2,1)S(1)}, bf16[256,1024]{1,0:T(8,128)(2,1)S(1)}, u32[]{:S(2)}, u32[]{:S(2)}) collective-permute-start(bf16[256,1024]{1,0:T(8,128)(2,1)S(1)} %add_convert_fusion.6), channel_id=1, source_target_pairs={{0,3},{1,2},{2,1},{3,0},{4,7},{5,6},{6,5},{7,4},{8,11},{9,10},{10,... | collective-permute-start | bytes 1572872 | tf_op jit(solution)/shard_map/ppermute | solution.py:42
  212.4 9.6 %collective-permute-start.21 = (bf16[256,1024]{1,0:T(8,128)(2,1)S(1)}, bf16[256,1024]{1,0:T(8,128)(2,1)S(1)}, u32[]{:S(2)}, u32[]{:S(2)}) collective-permute-start(bf16[256,1024]{1,0:T(8,128)(2,1)S(1)} %get-tuple-element.138), channel_id=1, source_target_pairs={{0,4},{4,0},{8,12},{12,8},{1,5},{5,1},{9,13},{13,9},{2,6},{6,2},{1... | collective-permute-start | bytes 1572872 | tf_op jit(solution)/shard_map/ppermute | solution.py:46
  212.5 9.6 %collective-permute-start.20 = (bf16[512,512]{1,0:T(8,128)(2,1)S(1)}, bf16[512,512]{1,0:T(8,128)(2,1)S(1)}, u32[]{:S(2)}, u32[]{:S(2)}) collective-permute-start(bf16[512,512]{1,0:T(8,128)(2,1)S(1)} %copy-done.21), channel_id=1, source_target_pairs={{0,1},{1,0},{2,3},{3,2},{4,5},{5,4},{6,7},{7,6},{8,9},{9,8},{10,11... | collective-permute-start | bytes 1572872 | tf_op jit(solution)/shard_map/ppermute | solution.py:38
  222.2 12.1 %collective-permute-start.29 = (f32[64,1024]{1,0:T(8,128)S(1)}, f32[64,1024]{1,0:T(8,128)S(1)}, u32[]{:S(2)}, u32[]{:S(2)}) collective-permute-start(f32[64,1024]{1,0:T(8,128)S(1)} %maximum_select_fusion.3), channel_id=1, source_target_pairs={{0,32},{32,0},{64,96},{96,64},{1,33},{33,1},{65,97},{97,65},{2,34}... | collective-permute-start | bytes 786440 | tf_op jit(solution)/shard_map/ppermute | solution.py:114
  224.0 10.3 %collective-permute-start.28 = (bf16[256,1024]{1,0:T(8,128)(2,1)S(1)}, bf16[256,1024]{1,0:T(8,128)(2,1)S(1)}, u32[]{:S(2)}, u32[]{:S(2)}) collective-permute-start(bf16[256,1024]{1,0:T(8,128)(2,1)S(1)} %add_convert_fusion.4), channel_id=1, source_target_pairs={{0,3},{1,2},{2,1},{3,0},{4,7},{5,6},{6,5},{7,4},{8,11},{9,10},{10,... | collective-permute-start | bytes 1572872 | tf_op jit(solution)/shard_map/ppermute | solution.py:42
  225.7 8.7 %collective-permute-start.27 = (bf16[256,1024]{1,0:T(8,128)(2,1)S(1)}, bf16[256,1024]{1,0:T(8,128)(2,1)S(1)}, u32[]{:S(2)}, u32[]{:S(2)}) collective-permute-start(bf16[256,1024]{1,0:T(8,128)(2,1)S(1)} %add_convert_fusion.5), channel_id=1, source_target_pairs={{4,8},{8,4},{5,9},{9,5},{6,10},{10,6},{7,11},{11,7},{20,24},{24,20... | collective-permute-start | bytes 1572872 | tf_op jit(solution)/shard_map/ppermute | solution.py:46
  226.4 8.4 %collective-permute-start.25 = (bf16[512,512]{1,0:T(8,128)(2,1)S(1)}, bf16[512,512]{1,0:T(8,128)(2,1)S(1)}, u32[]{:S(2)}, u32[]{:S(2)}) collective-permute-start(bf16[512,512]{1,0:T(8,128)(2,1)S(1)} %copy-done.20), channel_id=1, source_target_pairs={{0,1},{1,0},{2,3},{3,2},{4,5},{5,4},{6,7},{7,6},{8,9},{9,8},{10,11... | collective-permute-start | bytes 1572872 | tf_op jit(solution)/shard_map/ppermute | solution.py:38
  227.1 10.0 %collective-permute-start.26 = (bf16[256,1024]{1,0:T(8,128)(2,1)S(1)}, bf16[256,1024]{1,0:T(8,128)(2,1)S(1)}, u32[]{:S(2)}, u32[]{:S(2)}) collective-permute-start(bf16[256,1024]{1,0:T(8,128)(2,1)S(1)} %get-tuple-element.136), channel_id=1, source_target_pairs={{0,4},{4,0},{8,12},{12,8},{1,5},{5,1},{9,13},{13,9},{2,6},{6,2},{1... | collective-permute-start | bytes 1572872 | tf_op jit(solution)/shard_map/ppermute | solution.py:46
  240.3 15.5 %collective-permute-start.30 = (bf16[512,1024]{1,0:T(8,128)(2,1)S(1)}, bf16[512,1024]{1,0:T(8,128)(2,1)S(1)}, u32[]{:S(2)}, u32[]{:S(2)}) collective-permute-start(bf16[512,1024]{1,0:T(8,128)(2,1)S(1)} %get-tuple-element.153), channel_id=1, source_target_pairs={{0,16},{16,0},{1,17},{17,1},{2,18},{18,2},{3,19},{19,3},{4,20},{20... | collective-permute-start | bytes 3145736 | tf_op jit(solution)/shard_map/ppermute | solution.py:34
  247.6 14.8 %collective-permute-start.32 = (bf16[256,1024]{1,0:T(8,128)(2,1)S(1)}, bf16[256,1024]{1,0:T(8,128)(2,1)S(1)}, u32[]{:S(2)}, u32[]{:S(2)}) collective-permute-start(bf16[256,1024]{1,0:T(8,128)(2,1)S(1)} %add_convert_fusion.3), channel_id=1, source_target_pairs={{0,3},{1,2},{2,1},{3,0},{4,7},{5,6},{6,5},{7,4},{8,11},{9,10},{10,... | collective-permute-start | bytes 1572872 | tf_op jit(solution)/shard_map/ppermute | solution.py:42
  249.6 12.8 %collective-permute-start.34 = (bf16[256,1024]{1,0:T(8,128)(2,1)S(1)}, bf16[256,1024]{1,0:T(8,128)(2,1)S(1)}, u32[]{:S(2)}, u32[]{:S(2)}) collective-permute-start(bf16[256,1024]{1,0:T(8,128)(2,1)S(1)} %add_convert_fusion.1), channel_id=1, source_target_pairs={{4,8},{8,4},{5,9},{9,5},{6,10},{10,6},{7,11},{11,7},{20,24},{24,20... | collective-permute-start | bytes 1572872 | tf_op jit(solution)/shard_map/ppermute | solution.py:46
  250.6 15.6 %collective-permute-start.33 = (bf16[256,1024]{1,0:T(8,128)(2,1)S(1)}, bf16[256,1024]{1,0:T(8,128)(2,1)S(1)}, u32[]{:S(2)}, u32[]{:S(2)}) collective-permute-start(bf16[256,1024]{1,0:T(8,128)(2,1)S(1)} %add_convert_fusion.2), channel_id=1, source_target_pairs={{0,4},{4,0},{8,12},{12,8},{1,5},{5,1},{9,13},{13,9},{2,6},{6,2},{1... | collective-permute-start | bytes 1572872 | tf_op jit(solution)/shard_map/ppermute | solution.py:46
  254.9 15.0 %collective-permute-start.36 = (f32[128,1024]{1,0:T(8,128)S(1)}, f32[128,1024]{1,0:T(8,128)S(1)}, u32[]{:S(2)}, u32[]{:S(2)}) collective-permute-start(f32[128,1024]{1,0:T(8,128)S(1)} %maximum_select_fusion.2), channel_id=1, source_target_pairs={{0,16},{16,0},{1,17},{17,1},{2,18},{18,2},{3,19},{19,3},{4,20},{20... | collective-permute-start | bytes 1572872 | tf_op jit(solution)/shard_map/ppermute | solution.py:114
  257.0 24.2 %collective-permute-start.31 = (bf16[512,1024]{1,0:T(8,128)(2,1)S(1)}, bf16[512,1024]{1,0:T(8,128)(2,1)S(1)}, u32[]{:S(2)}, u32[]{:S(2)}) collective-permute-start(bf16[512,1024]{1,0:T(8,128)(2,1)S(1)} %add_convert_fusion), channel_id=1, source_target_pairs={{1,16},{2,19},{16,1},{19,2},{5,20},{6,23},{20,5},{23,6},{9,24},{10... | collective-permute-start | bytes 3145736 | tf_op jit(solution)/shard_map/ppermute | solution.py:30
  266.6 12.3 %collective-permute-start.35 = (bf16[256,1024]{1,0:T(8,128)(2,1)S(1)}, bf16[256,1024]{1,0:T(8,128)(2,1)S(1)}, u32[]{:S(2)}, u32[]{:S(2)}) collective-permute-start(bf16[256,1024]{1,0:T(8,128)(2,1)S(1)} %get-tuple-element.134), channel_id=1, source_target_pairs={{1,16},{2,19},{16,1},{19,2},{5,20},{6,23},{20,5},{23,6},{9,24},{10... | collective-permute-start | bytes 1572872 | tf_op jit(solution)/shard_map/ppermute | solution.py:30
  (32 other events, 205.0 us)

commit v6 on v3

--- a/solution.py
+++ b/solution.py
@@ -56,6 +56,10 @@
 
 def together(*arrays):
     return lax.optimization_barrier(arrays)
+
+
+def after(array, *earlier):
+    return together(array, *earlier)[0]
 
 
 def move(_, a, b, to_a, to_b):
@@ -76,7 +80,7 @@
             out_specs=[out, out],
         ),
         out_shape=[kind, kind],
-        cost_estimate=pl.CostEstimate(flops=0, bytes_accessed=16 << 20, transcendentals=0),
+        cost_estimate=pl.CostEstimate(flops=0, bytes_accessed=0, transcendentals=0),
     )(blocks, tokens, tokens)
 
 
@@ -88,7 +92,8 @@
         self.steps = [("c", CORE, c), ("y", near, y % 2), ("y", wide, y // 2), ("zh", CORE, c)]
         self.at = 0
 
-    def send(self):
+    def send(self, earlier):
+        self.v = after(self.v, earlier)
         if self.at < 3:
             bit = self.steps[self.at][2]
             n = self.v.shape[0] // 2
@@ -133,33 +138,34 @@
     ).reshape(2, 8)
 
     w = jnp.where(stays, weight, swap(weight))
-    g_sib = core(key_grad)
-    x_give, x_own = halves(tokens, blocks.astype(jnp.int32))
+    g_mine = lax.dynamic_slice_in_dim(key_grad, c * 256, 256, 0)
+    g_first = core(lax.dynamic_slice_in_dim(key_grad, (1 - c) * 256, 256, 0))
+    g_l = jnp.where(stays, g_first, g_mine)
+    drift = Drift(anchor - local_params[0].astype(f32), c, y)
+    d = drift.send(g_l)
+    w, g_l, blocks, d = together(w, g_l, blocks.astype(jnp.int32), d)
+    drift.take(d)
+
+    g_half, e_own, m_own, q_own = beside(g_l), line(w, PAIRS), line(w, MIDDLE), across(w)
+    x_give, x_own = halves(tokens, blocks)
     x_sib = core(x_give)
-    drift = Drift(anchor - local_params[0].astype(f32), c, y)
-    drift.take(drift.send())
-    g_a = jnp.where(stays, key_grad, g_sib)
-    g_l = lax.dynamic_slice_in_dim(jnp.where(stays, g_sib, key_grad), c * 256, 256, 0)
-
-    got = (beside(g_l), line(w, PAIRS), line(w, MIDDLE), across(w), drift.send())
+    drift.take(drift.send(w))
     leave = [jnp.where(stays, x_sib[k], x_own[k]) for k in range(4)]
     keep = [jnp.where(stays, x_own[k], x_sib[k]) for k in range(4)]
-    got, leave, drift.v = together(got, leave, drift.v)
-    g_half, e_own, m_own, q_own, d = got
-    drift.take(d)
-
-    got = (beside(leave[0]), line(m_own, ENDS_OUT), line(e_own, MIDDLE), across(e_own), drift.send())
-    g_rest = core(g_half)
-    g_b = jnp.where(
-        c == 0, jnp.concatenate([g_half, g_rest]), jnp.concatenate([g_rest, g_half])
-    )
+
+    x_b = [beside(after(leave[0], g_half))]
+    e2 = line(after(m_own, e_own, g_half, leave[0]), ENDS_OUT)
+    m2 = line(after(e_own, m_own, g_half, leave[0]), MIDDLE)
+    q2 = across(after(e_own, q_own, g_half, leave[0]))
+    drift.take(drift.send(g_half))
+    rest = core(jnp.concatenate([g_half, g_mine]))
+
+    def in_order(a, b):
+        return jnp.where(c == 0, jnp.concatenate([a, b]), jnp.concatenate([b, a]))
+
+    g_b = in_order(g_half, rest[:256])
+    g_a = jnp.where(stays, key_grad, in_order(g_first, rest[256:]))
     base = [dot_t(k, g_a) for k in keep]
-    sent = drift.v
-    got, leave, sent, g_b, base = together(got, leave, sent, g_b, base)
-    drift.v = sent
-    x_b = [got[0]]
-    _, e2, m2, q2, d = got
-    drift.take(d)
     mid = jnp.where(end, e2, m_own)
 
     def going(k):
@@ -171,62 +177,44 @@
     def cat(*arrays):
         return jnp.concatenate(arrays, axis=-1)
 
-    got = (beside(leave[1]), line(m2, ENDS_OUT), line(q_own, MIDDLE), across(going(0)), drift.send())
+    x_b.append(beside(after(leave[1], x_b[0])))
+    e3 = line(after(m2, e2, x_b[0]), ENDS_OUT)
+    m3 = line(after(q_own, m2, x_b[0]), MIDDLE)
+    q3 = across(after(going(0), q2))
+    drift.take(drift.send(x_b[0]))
     rows = [None, None, jnp.concatenate([e_own, q2]), jnp.concatenate([w, q_own])]
     k_a = dot(cat(keep[2], keep[3]), jnp.concatenate(rows[2:]))
-    stay = staying(0)
-    got, leave, drift.v, drift.sent, stay, k_a = together(got, leave, drift.v, drift.sent, stay, k_a)
-    x_b.append(got[0])
-    _, e3, m3, q3, d = got
-    drift.take(d)
-    part0 = stay + q3.astype(f32)
-
-    got = (
-        beside(leave[2]),
-        line(jnp.where(end, part0.astype(bf16), m3), PAIRS),
-        line(q2, MIDDLE),
-        across(going(1)),
-        drift.send(),
-    )
-    stay = staying(1)
-    got, leave, drift.v, stay, part0 = together(got, leave, drift.v, stay, part0)
-    x_b.append(got[0])
-    _, e4, m4, q4, d = got
-    drift.take(d)
-    part1 = stay + q4.astype(f32)
-
-    got = (
-        beside(leave[3]),
-        line(jnp.where(end, part1.astype(bf16), m4), PAIRS),
-        line((part0 + e4.astype(f32)).astype(bf16), MIDDLE),
-        across(going(2)),
-        drift.send(),
-    )
+    part0 = staying(0) + q3.astype(f32)
+
+    x_b.append(beside(after(leave[2], x_b[1])))
+    e4 = line(after(jnp.where(end, part0.astype(bf16), m3), e3, x_b[1]), PAIRS)
+    m4 = line(after(q2, m3, x_b[1]), MIDDLE)
+    q4 = across(after(going(1), q3))
+    drift.take(drift.send(x_b[1]))
+    part1 = staying(1) + q4.astype(f32)
+
+    x_b.append(beside(after(leave[3], x_b[2])))
+    e5 = line(after(jnp.where(end, part1.astype(bf16), m4), e4, x_b[2]), PAIRS)
+    m5 = line(after((part0 + e4.astype(f32)).astype(bf16), m4, x_b[2]), MIDDLE)
+    q5 = across(after(going(2), q4))
+    drift.take(drift.send(x_b[2]))
     rows[1] = jnp.concatenate([mid, jnp.where(end, e4, m3)])
     k_a = k_a + dot(keep[1], rows[1])
     k_b = dot(cat(x_b[1], x_b[2]), jnp.concatenate(rows[1:3]))
-    stay = staying(2)
-    got, drift.v, stay, part1, k_a, k_b = together(got, drift.v, stay, part1, k_a, k_b)
-    x_b.append(got[0])
-    _, e5, m5, q5, d = got
-    drift.take(d)
-    part2 = stay + q5.astype(f32)
-
-    got = (
-        line((part2 + m5.astype(f32)).astype(bf16), PAIRS),
-        line((part1 + e5.astype(f32)).astype(bf16), MIDDLE),
-        across(going(3)),
-    )
+    part2 = staying(2) + q5.astype(f32)
+
+    e6 = line(after((part2 + m5.astype(f32)).astype(bf16), e5), PAIRS)
+    m6 = line(after((part1 + e5.astype(f32)).astype(bf16), m5), MIDDLE)
+    q6 = across(after(going(3), q5))
     rows[0] = jnp.concatenate([jnp.where(end, e3, m2), jnp.where(end, e5, m4)])
     k_a = k_a + dot(keep[0], rows[0])
     k_b = k_b + dot(cat(x_b[0], x_b[3]), jnp.concatenate([rows[0], rows[3]]))
     k_got = core(jnp.where(stays, k_b, k_a).astype(bf16))
     keys_work = (jnp.where(stays, k_a, k_b) + k_got.astype(f32)).astype(bf16)
     keys = jnp.where(stays, keys_work, swap(keys_work))
-    e6, m6, q6 = got
     total = staying(3) + q6.astype(f32) + e6.astype(f32) + m6.astype(f32)
     gradient = jnp.where(stays, total, swap(total.astype(bf16)).astype(f32))
-    drift.take(drift.send())
+    drift.take(drift.send(x_b[3]))
 
     new_first = first_decay * adam_first[0] + (1.0 - first_decay) * gradient
     new_second = second_decay * adam_second[0] + (1.0 - second_decay) * gradient * gradient

time: 159 us -> 183 us (1.15)
  matrix products: 12 us -> 27.3 us
  local copies, waits for them, and re-layouts: 1.65 us -> 6.38 us
  starting transfers between devices: 62 us -> 65.1 us
  other arithmetic: 17.4 us -> 19.9 us
  waiting for transfers between devices: 56.8 us -> 54.3 us
    ppermute x6, waiting for transfers between devices: 19.2 us -> 5.95 us  [across(): return lax.ppermute(v, 'x', ACROSS)]
    dot_general x12, matrix products: 6.66 us -> 19.2 us  [dot_t(): lax.dot_general(a, b, (((0,), (0,)), ((), ())), preferred_element_type=f32)]
    ppermute x5, waiting for transfers between devices: 5.14 us -> 15.3 us  [beside(): return lax.ppermute(v, 'x', BESIDE)]
    ppermute x4, starting transfers between devices: 10.6 us -> 14.9 us  [core(): return lax.ppermute(v, 'c', CORE)]
    ppermute x12, waiting for transfers between devices: 11.2 us -> 14 us  [line(): return lax.ppermute(v, 'zl', pairs)]
    dot_general x5, matrix products: 5.34 us -> 8.1 us  [dot(): return jnp.dot(a, b, preferred_element_type=f32)]
    concatenate x0 -> x1, other arithmetic: none -> 2.24 us  [on_device(): rest = core(jnp.concatenate([g_half, g_mine]))]
    select_n x5 -> x2, other arithmetic: 3.9 us -> 1.79 us  [the longest x1 1.21 us: on_device(): g_l = jnp.where(stays, g_first, g_mine)]
  transfers between devices with their start and end apart: 37 -> 37, of which waited for: 15 -> 13; matrix products, arithmetic and copies ran while one was open for 17% -> 27% of each run, Pallas kernels for 0% -> 4%
where the time goes in v6:
time: 183 us; the launch traced here: 182 us
  starting transfers between devices  65.1 us (36%)
  waiting for transfers between devices  54.3 us (30%)
  matrix products  27.3 us (15%)
  other arithmetic  19.9 us (11%)
  Pallas kernels  7.4 us (4%)
  local copies, waits for them, and re-layouts  6.38 us (3%)
    dot_general x12, matrix products, dot_t(): lax.dot_general(a, b, (((0,), (0,)), ((), ())), preferred_element_type=f32)  19.2 us
    ppermute x12, starting transfers between devices, line(): return lax.ppermute(v, 'zl', pairs)  18.3 us
    ppermute x5, waiting for transfers between devices, beside(): return lax.ppermute(v, 'x', BESIDE)  15.3 us
    ppermute x4, starting transfers between devices, core(): return lax.ppermute(v, 'c', CORE)  14.9 us
    ppermute x12, waiting for transfers between devices, line(): return lax.ppermute(v, 'zl', pairs)  14 us
    ppermute x7, starting transfers between devices, send(): return lax.ppermute(self.sent, axis, perm)  13 us
    ppermute x3, waiting for transfers between devices, swap(): return lax.ppermute(v, ('c', 'x'), SWAP)  12 us
    dot_general x5, matrix products, dot(): return jnp.dot(a, b, preferred_element_type=f32)  8.1 us
  transfers between devices with their start and end apart: 37, of which 13 were waited for; matrix products, arithmetic and copies ran while one was open for 27% of the time, Pallas kernels for 4%

profile of v6, /device:TPU:1, one launch (start us, length us, event | category | flops | bytes accessed | tf_op | source)
XLA Modules:
  0.0 181.6 jit_solution(16214440024666529114)
XLA Ops:
  0.7 2.0 %constant_dynamic-slice_fusion.4 = bf16[256,1024]{1,0:T(8,128)(2,1)} fusion(bf16[512,1024]{1,0:T(8,128)(2,1)} %param.9, s32[]{:T(128)S(6)} %select_n.224), kind=kLoop, calls=%fused_computation.133 | loop fusion | bytes 1048580 | tf_op jit(solution)/shard_map/dynamic_slice | solution.py:142
  2.6 3.2 %collective-permute-start.1 = (bf16[256,1024]{1,0:T(8,128)(2,1)}, bf16[256,1024]{1,0:T(8,128)(2,1)S(1)}, u32[]{:S(2)}, u32[]{:S(2)}) collective-permute-start(bf16[256,1024]{1,0:T(8,128)(2,1)} %constant_dynamic-slice_fusion.4), channel_id=1, source_target_pairs={{0,16},{16,0},{1,17},{17,1},{2,18},{18,2},{3,19},{19,3},{4,20},{20... | collective-permute-start | bytes 1572872 | tf_op jit(solution)/shard_map/ppermute | solution.py:34
  5.8 1.9 %collective-permute-start = (bf16[256,1024]{1,0:T(8,128)(2,1)}, bf16[256,1024]{1,0:T(8,128)(2,1)}, u32[]{:S(2)}, u32[]{:S(2)}) collective-permute-start(bf16[256,1024]{1,0:T(8,128)(2,1)} %bitcast.68), channel_id=1, source_target_pairs={{1,16},{2,19},{16,1},{19,2},{5,20},{6,23},{20,5},{23,6},{9,24},{10... | collective-permute-start | bytes 1572872 | tf_op jit(solution)/shard_map/ppermute | solution.py:30
  11.5 5.2 %collective-permute-done = bf16[256,1024]{1,0:T(8,128)(2,1)} collective-permute-done((bf16[256,1024]{1,0:T(8,128)(2,1)}, bf16[256,1024]{1,0:T(8,128)(2,1)}, u32[]{:S(2)}, u32[]{:S(2)}) %collective-permute-start) | collective-permute-done | bytes 524320 | tf_op jit(solution)/shard_map/ppermute | solution.py:30
  16.7 1.9 %broadcast_select_fusion.6 = bf16[256,1024]{1,0:T(8,128)(2,1)} fusion(bf16[256,1024]{1,0:T(8,128)(2,1)} %collective-permute-done, pred[]{:T(512)S(6)} %eq.37, bf16[1,256,1024]{2,1,0:T(8,128)(2,1)S(1)} %copy-done.10), kind=kLoop, calls=%fused_computation.104 | loop fusion | flops 262144 | bytes 1572865 | tf_op jit(solution)/shard_map/jit(_where)/select_n | solution.py:140
  18.7 7.4 %shard_map.127 = (bf16[4,512,512]{2,1,0:T(8,128)(2,1)}, bf16[4,512,512]{2,1,0:T(8,128)(2,1)}) custom-call(s32[2,8]{1,0:T(2,128)} %reshape.37._, bf16[512,4096]{1,0:T(8,128)(2,1)} %b.1, bf16[512,4096]{1,0:T(8,128)(2,1)} %b.1), custom_call_target="tpu_custom_call" | custom-call | tf_op jit(solution)/shard_map/pallas_call | solution.py:74
  27.6 3.9 %collective-permute-done.6 = bf16[256,1024]{1,0:T(8,128)(2,1)} collective-permute-done((bf16[256,1024]{1,0:T(8,128)(2,1)}, bf16[256,1024]{1,0:T(8,128)(2,1)}, u32[]{:S(2)}, u32[]{:S(2)}) %collective-permute-start.6) | collective-permute-done | bytes 524320 | tf_op jit(solution)/shard_map/ppermute | solution.py:38
  31.5 2.2 %pad_maximum_fusion.7 = bf16[512,1024]{1,0:T(8,128)(2,1)} fusion(bf16[256,1024]{1,0:T(8,128)(2,1)} %collective-permute-done.6, bf16[256,1024]{1,0:T(8,128)(2,1)} %get-tuple-element.73), kind=kLoop, calls=%fused_computation.28 | loop fusion | flops 2097152 | bytes 2097152 | tf_op jit(solution)/shard_map/concatenate | solution.py:161
  35.1 6.2 %collective-permute-done.31 = f32[64,1024]{1,0:T(8,128)} collective-permute-done((f32[64,1024]{1,0:T(8,128)S(1)}, f32[64,1024]{1,0:T(8,128)}, u32[]{:S(2)}, u32[]{:S(2)}) %collective-permute-start.31) | collective-permute-done | bytes 262176 | tf_op jit(solution)/shard_map/ppermute | solution.py:106
  43.1 3.3 %collective-permute-start.32 = (f32[32,1024]{1,0:T(8,128)}, f32[32,1024]{1,0:T(8,128)S(1)}, u32[]{:S(2)}, u32[]{:S(2)}) collective-permute-start(f32[32,1024]{1,0:T(8,128)} %constant_dynamic-slice_fusion), channel_id=1, source_target_pairs={{0,64},{32,96},{64,0},{96,32},{1,65},{33,97},{65,1},{97,33},{2,66}... | collective-permute-start | bytes 393224 | tf_op jit(solution)/shard_map/ppermute | solution.py:106
  48.9 3.7 %collective-permute-start.4 = (bf16[256,1024]{1,0:T(8,128)(2,1)}, bf16[256,1024]{1,0:T(8,128)(2,1)S(1)}, u32[]{:S(2)}, u32[]{:S(2)}) collective-permute-start(bf16[256,1024]{1,0:T(8,128)(2,1)} %broadcast_select_fusion.6), channel_id=1, source_target_pairs={{0,4},{4,0},{8,12},{12,8},{1,5},{5,1},{9,13},{13,9},{2,6},{6,2},{1... | collective-permute-start | bytes 1572872 | tf_op jit(solution)/shard_map/ppermute | solution.py:46
  56.4 6.4 %collective-permute-done.4 = bf16[256,1024]{1,0:T(8,128)(2,1)S(1)} collective-permute-done((bf16[256,1024]{1,0:T(8,128)(2,1)}, bf16[256,1024]{1,0:T(8,128)(2,1)S(1)}, u32[]{:S(2)}, u32[]{:S(2)}) %collective-permute-start.4) | collective-permute-done | bytes 524320 | tf_op jit(solution)/shard_map/ppermute | solution.py:46
  62.8 2.2 %collective-permute-start.7 = (bf16[256,1024]{1,0:T(8,128)(2,1)S(1)}, bf16[256,1024]{1,0:T(8,128)(2,1)S(1)}, u32[]{:S(2)}, u32[]{:S(2)}) collective-permute-start(bf16[256,1024]{1,0:T(8,128)(2,1)S(1)} %collective-permute-done.4), channel_id=1, source_target_pairs={{0,3},{1,2},{2,1},{3,0},{4,7},{5,6},{6,5},{7,4},{8,11},{9,10},{10,... | collective-permute-start | bytes 1572872 | tf_op jit(solution)/shard_map/ppermute | solution.py:42
  70.2 7.0 %collective-permute-done.11 = bf16[512,512]{1,0:T(8,128)(2,1)S(1)} collective-permute-done((bf16[512,512]{1,0:T(8,128)(2,1)S(1)}, bf16[512,512]{1,0:T(8,128)(2,1)S(1)}, u32[]{:S(2)}, u32[]{:S(2)}) %collective-permute-start.11) | collective-permute-done | bytes 524320 | tf_op jit(solution)/shard_map/ppermute | solution.py:38
  77.2 5.1 %collective-permute-start.33 = (bf16[32,1024]{1,0:T(8,128)(2,1)S(1)}, bf16[32,1024]{1,0:T(8,128)(2,1)S(1)}, u32[]{:S(2)}, u32[]{:S(2)}) collective-permute-start(bf16[32,1024]{1,0:T(8,128)(2,1)S(1)} %dynamic-slice_add_fusion.2), channel_id=1, source_target_pairs={{0,128},{128,0},{1,129},{129,1},{2,130},{130,2},{3,131},{131,3},{4... | collective-permute-start | bytes 196616 | tf_op jit(solution)/shard_map/ppermute | solution.py:106
  88.9 4.4 %collective-permute-done.16 = bf16[512,512]{1,0:T(8,128)(2,1)S(1)} collective-permute-done((bf16[512,512]{1,0:T(8,128)(2,1)S(1)}, bf16[512,512]{1,0:T(8,128)(2,1)S(1)}, u32[]{:S(2)}, u32[]{:S(2)}) %collective-permute-start.16) | collective-permute-done | bytes 524320 | tf_op jit(solution)/shard_map/ppermute | solution.py:38
  105.6 3.9 %collective-permute-done.17 = bf16[256,1024]{1,0:T(8,128)(2,1)S(1)} collective-permute-done((bf16[256,1024]{1,0:T(8,128)(2,1)S(1)}, bf16[256,1024]{1,0:T(8,128)(2,1)S(1)}, u32[]{:S(2)}, u32[]{:S(2)}) %collective-permute-start.17) | collective-permute-done | bytes 524320 | tf_op jit(solution)/shard_map/ppermute | solution.py:46
  113.2 2.6 %collective-permute-start.21 = (bf16[256,1024]{1,0:T(8,128)(2,1)S(1)}, bf16[256,1024]{1,0:T(8,128)(2,1)S(1)}, u32[]{:S(2)}, u32[]{:S(2)}) collective-permute-start(bf16[256,1024]{1,0:T(8,128)(2,1)S(1)} %get-tuple-element.56), channel_id=1, source_target_pairs={{0,4},{4,0},{8,12},{12,8},{1,5},{5,1},{9,13},{13,9},{2,6},{6,2},{1... | collective-permute-start | bytes 1572872 | tf_op jit(solution)/shard_map/ppermute | solution.py:46
  120.2 2.4 %collective-permute-done.21 = bf16[256,1024]{1,0:T(8,128)(2,1)S(1)} collective-permute-done((bf16[256,1024]{1,0:T(8,128)(2,1)S(1)}, bf16[256,1024]{1,0:T(8,128)(2,1)S(1)}, u32[]{:S(2)}, u32[]{:S(2)}) %collective-permute-start.21) | collective-permute-done | bytes 524320 | tf_op jit(solution)/shard_map/ppermute | solution.py:46
  124.0 1.9 %add_add_fusion = f32[512,1024]{1,0:T(8,128)S(1)} fusion(f32[512,1024]{1,0:T(8,128)S(1)} %fusion, f32[512,1024]{1,0:T(8,128)S(1)} %fusion.40, bf16[256,1024]{1,0:T(8,128)(2,1)S(1)} %broadcast_select_fusion.1, bf16[256,1024]{1,0:T(8,128)(2,1)S(1)} %broadcast_select_fusion.2, pred[]{:T(512)S(6)} %eq.37, bf16[4,512,512]{2,1,0:T(8,128)(2,1)} %copy-done.1, ...), kind=kOutput, calls=%fused_computation.22 | convolution fusion | flops 540278784 | bytes 8388609 | tf_op jit(solution)/shard_map/dot_general | solution.py:50
  125.8 3.0 %select_convert_fusion = (bf16[512,1024]{1,0:T(8,128)(2,1)}, f32[512,1024]{1,0:T(8,128)}) fusion(f32[512,1024]{1,0:T(8,128)S(1)} %add_add_fusion, pred[]{:T(512)S(6)} %eq.37, f32[512,1024]{1,0:T(8,128)S(1)} %fusion.1, bf16[256,1024]{1,0:T(8,128)(2,1)S(1)} %collective-permute-done.7, bf16[256,1024]{1,0:T(8,128)(2,1)S(1)} %collective-permute-done.4, ...), kind=kOutput, calls=%fused_computation.21 | convolution fusion | flops 1085276160 | bytes 10485761 | tf_op jit(solution)/shard_map/dot_general | solution.py:50
  128.8 11.3 %collective-permute-start.23 = (bf16[512,1024]{1,0:T(8,128)(2,1)}, bf16[512,1024]{1,0:T(8,128)(2,1)S(1)}, u32[]{:S(2)}, u32[]{:S(2)}) collective-permute-start(bf16[512,1024]{1,0:T(8,128)(2,1)} %get-tuple-element.89), channel_id=1, source_target_pairs={{0,16},{16,0},{1,17},{17,1},{2,18},{18,2},{3,19},{19,3},{4,20},{20... | collective-permute-start | bytes 3145736 | tf_op jit(solution)/shard_map/ppermute | solution.py:34
  142.6 2.6 %fusion.26 = bf16[256,1024]{1,0:T(8,128)(2,1)} fusion(f32[512,1024]{1,0:T(8,128)S(1)} %fusion.114, bf16[256,1024]{1,0:T(8,128)(2,1)S(1)} %collective-permute-done.27, bf16[256,1024]{1,0:T(8,128)(2,1)S(1)} %collective-permute-done.25, bf16[512,512]{1,0:T(8,128)(2,1)S(1)} %collective-permute-done.20, bf16[256,1024]{1,0:T(8,128)(2,1)} %collective-permute-done.6, ...), kind=kOutput, calls=%fused_computation.37 | convolution fusion | flops 274726912 | bytes 3932161 | tf_op jit(solution)/shard_map/dot_general | solution.py:54
  145.1 2.5 %fusion.28 = bf16[256,1024]{1,0:T(8,128)(2,1)} fusion(f32[512,1024]{1,0:T(8,128)S(1)} %fusion.113, bf16[512,512]{1,0:T(8,128)(2,1)S(1)} %collective-permute-done.22, bf16[256,1024]{1,0:T(8,128)(2,1)} %collective-permute-done.6, bf16[256,1024]{1,0:T(8,128)(2,1)S(1)} %get-tuple-element.83, pred[]{:T(512)S(6)} %eq.42), kind=kOutput, calls=%fused_computation.41 | convolution fusion | flops 273678336 | bytes 2883585 | tf_op jit(solution)/shard_map/dot_general | solution.py:54
  149.1 2.9 %collective-permute-start.28 = (bf16[256,1024]{1,0:T(8,128)(2,1)}, bf16[256,1024]{1,0:T(8,128)(2,1)}, u32[]{:S(2)}, u32[]{:S(2)}) collective-permute-start(bf16[256,1024]{1,0:T(8,128)(2,1)} %fusion.26), channel_id=1, source_target_pairs={{0,4},{4,0},{8,12},{12,8},{1,5},{5,1},{9,13},{13,9},{2,6},{6,2},{1... | collective-permute-start | bytes 1572872 | tf_op jit(solution)/shard_map/ppermute | solution.py:46
  154.0 2.4 %add_convert_fusion = bf16[512,1024]{1,0:T(8,128)(2,1)S(1)} fusion(bf16[512,1024]{1,0:T(8,128)(2,1)S(1)} %collective-permute-done.23, f32[512,1024]{1,0:T(8,128)S(1)} %add_add_fusion, f32[512,1024]{1,0:T(8,128)} %get-tuple-element.90, pred[]{:T(512)S(6)} %eq.37), kind=kLoop, calls=%fused_computation.20 | loop fusion | flops 2097152 | bytes 6291457 | tf_op jit(solution)/shard_map/convert_element_type | solution.py:213
  156.4 2.1 %collective-permute-start.24 = (bf16[512,1024]{1,0:T(8,128)(2,1)S(1)}, bf16[512,1024]{1,0:T(8,128)(2,1)S(1)}, u32[]{:S(2)}, u32[]{:S(2)}) collective-permute-start(bf16[512,1024]{1,0:T(8,128)(2,1)S(1)} %add_convert_fusion), channel_id=1, source_target_pairs={{1,16},{2,19},{16,1},{19,2},{5,20},{6,23},{20,5},{23,6},{9,24},{10... | collective-permute-start | bytes 3145736 | tf_op jit(solution)/shard_map/ppermute | solution.py:30
  158.5 4.2 %collective-permute-done.26 = bf16[256,1024]{1,0:T(8,128)(2,1)} collective-permute-done((bf16[256,1024]{1,0:T(8,128)(2,1)}, bf16[256,1024]{1,0:T(8,128)(2,1)}, u32[]{:S(2)}, u32[]{:S(2)}) %collective-permute-start.26) | collective-permute-done | bytes 524320 | tf_op jit(solution)/shard_map/ppermute | solution.py:42
  164.0 2.3 %fusion.112 = (bf16[256,1024]{1,0:T(8,128)(2,1)S(1)}, f32[256,1024]{1,0:T(8,128)S(1)}) fusion(bf16[256,1024]{1,0:T(8,128)(2,1)} %collective-permute-done.29, bf16[256,1024]{1,0:T(8,128)(2,1)} %collective-permute-done.28, bf16[256,1024]{1,0:T(8,128)(2,1)} %collective-permute-done.26, bf16[256,1024]{1,0:T(8,128)(2,1)} %collective-permute-done.6, ...), kind=kOutput, calls=%fused_computation.141 | convolution fusion | flops 275251200 | bytes 5505025 | tf_op jit(solution)/shard_map/dot_general | solution.py:54
  166.4 3.3 %collective-permute-start.30 = (bf16[256,1024]{1,0:T(8,128)(2,1)S(1)}, bf16[256,1024]{1,0:T(8,128)(2,1)S(1)}, u32[]{:S(2)}, u32[]{:S(2)}) collective-permute-start(bf16[256,1024]{1,0:T(8,128)(2,1)S(1)} %get-tuple-element.91), channel_id=1, source_target_pairs={{1,16},{2,19},{16,1},{19,2},{5,20},{6,23},{20,5},{23,6},{9,24},{10... | collective-permute-start | bytes 1572872 | tf_op jit(solution)/shard_map/ppermute | solution.py:30
  171.4 6.8 %collective-permute-done.30 = bf16[256,1024]{1,0:T(8,128)(2,1)S(1)} collective-permute-done((bf16[256,1024]{1,0:T(8,128)(2,1)S(1)}, bf16[256,1024]{1,0:T(8,128)(2,1)S(1)}, u32[]{:S(2)}, u32[]{:S(2)}) %collective-permute-start.30) | collective-permute-done | bytes 524320 | tf_op jit(solution)/shard_map/ppermute | solution.py:30
  178.2 2.3 %fusion.102 = (f32[1,256,1024]{2,1,0:T(8,128)}, bf16[1,256,1024]{2,1,0:T(8,128)(2,1)}, f32[1,256,1024]{2,1,0:T(8,128)}) fusion(f32[256,1024]{1,0:T(8,128)S(1)} %get-tuple-element.92, bf16[256,1024]{1,0:T(8,128)(2,1)S(1)} %collective-permute-done.30, pred[]{:T(512)S(6)} %eq.37, f32[1,256,1024]{2,1,0:T(8,128)S(1)} %copy-done.13, ...), kind=kLoop, calls=%fused_computation.139 | loop fusion | flops 4456448 | bytes 6815745 | tf_op jit(solution)/shard_map/broadcast_in_dim | solution.py:228
  (131 shorter events, 57.9 us)
Async XLA Ops:
  5.8 10.8 %collective-permute-start = (bf16[256,1024]{1,0:T(8,128)(2,1)}, bf16[256,1024]{1,0:T(8,128)(2,1)}, u32[]{:S(2)}, u32[]{:S(2)}) collective-permute-start(bf16[256,1024]{1,0:T(8,128)(2,1)} %bitcast.68), channel_id=1, source_target_pairs={{1,16},{2,19},{16,1},{19,2},{5,20},{6,23},{20,5},{23,6},{9,24},{10... | collective-permute-start | bytes 1572872 | tf_op jit(solution)/shard_map/ppermute | solution.py:30
  18.6 12.9 %collective-permute-start.6 = (bf16[256,1024]{1,0:T(8,128)(2,1)}, bf16[256,1024]{1,0:T(8,128)(2,1)}, u32[]{:S(2)}, u32[]{:S(2)}) collective-permute-start(bf16[256,1024]{1,0:T(8,128)(2,1)} %get-tuple-element.43), channel_id=1, source_target_pairs={{0,1},{1,0},{2,3},{3,2},{4,5},{5,4},{6,7},{7,6},{8,9},{9,8},{10,11... | collective-permute-start | bytes 1572872 | tf_op jit(solution)/shard_map/ppermute | solution.py:38
  26.1 28.4 %collective-permute-start.3 = (bf16[4,512,512]{2,1,0:T(8,128)(2,1)}, bf16[4,512,512]{2,1,0:T(8,128)(2,1)S(1)}, u32[]{:S(2)}, u32[]{:S(2)}) collective-permute-start(bf16[4,512,512]{2,1,0:T(8,128)(2,1)} %get-tuple-element.41), channel_id=1, source_target_pairs={{0,16},{16,0},{1,17},{17,1},{2,18},{18,2},{3,19},{19,3},{4,20},{20... | collective-permute-start | bytes 6291464 | tf_op jit(solution)/shard_map/ppermute | solution.py:34
  33.7 18.9 %collective-permute-start.10 = (bf16[512,1024]{1,0:T(8,128)(2,1)}, bf16[512,1024]{1,0:T(8,128)(2,1)}, u32[]{:S(2)}, u32[]{:S(2)}) collective-permute-start(bf16[512,1024]{1,0:T(8,128)(2,1)} %pad_maximum_fusion.7), channel_id=1, source_target_pairs={{0,16},{16,0},{1,17},{17,1},{2,18},{18,2},{3,19},{19,3},{4,20},{20... | collective-permute-start | bytes 3145736 | tf_op jit(solution)/shard_map/ppermute | solution.py:34
  46.3 10.1 %collective-permute-start.8 = (bf16[256,1024]{1,0:T(8,128)(2,1)}, bf16[256,1024]{1,0:T(8,128)(2,1)S(1)}, u32[]{:S(2)}, u32[]{:S(2)}) collective-permute-start(bf16[256,1024]{1,0:T(8,128)(2,1)} %broadcast_select_fusion.6), channel_id=1, source_target_pairs={{4,8},{8,4},{5,9},{9,5},{6,10},{10,6},{7,11},{11,7},{20,24},{24,20... | collective-permute-start | bytes 1572872 | tf_op jit(solution)/shard_map/ppermute | solution.py:46
  47.1 15.7 %collective-permute-start.5 = (bf16[256,1024]{1,0:T(8,128)(2,1)}, bf16[256,1024]{1,0:T(8,128)(2,1)S(1)}, u32[]{:S(2)}, u32[]{:S(2)}) collective-permute-start(bf16[256,1024]{1,0:T(8,128)(2,1)} %broadcast_select_fusion.6), channel_id=1, source_target_pairs={{0,3},{1,2},{2,1},{3,0},{4,7},{5,6},{6,5},{7,4},{8,11},{9,10},{10,... | collective-permute-start | bytes 1572872 | tf_op jit(solution)/shard_map/ppermute | solution.py:42
  48.9 14.0 %collective-permute-start.4 = (bf16[256,1024]{1,0:T(8,128)(2,1)}, bf16[256,1024]{1,0:T(8,128)(2,1)S(1)}, u32[]{:S(2)}, u32[]{:S(2)}) collective-permute-start(bf16[256,1024]{1,0:T(8,128)(2,1)} %broadcast_select_fusion.6), channel_id=1, source_target_pairs={{0,4},{4,0},{8,12},{12,8},{1,5},{5,1},{9,13},{13,9},{2,6},{6,2},{1... | collective-permute-start | bytes 1572872 | tf_op jit(solution)/shard_map/ppermute | solution.py:46
  62.8 21.2 %collective-permute-start.7 = (bf16[256,1024]{1,0:T(8,128)(2,1)S(1)}, bf16[256,1024]{1,0:T(8,128)(2,1)S(1)}, u32[]{:S(2)}, u32[]{:S(2)}) collective-permute-start(bf16[256,1024]{1,0:T(8,128)(2,1)S(1)} %collective-permute-done.4), channel_id=1, source_target_pairs={{0,3},{1,2},{2,1},{3,0},{4,7},{5,6},{6,5},{7,4},{8,11},{9,10},{10,... | collective-permute-start | bytes 1572872 | tf_op jit(solution)/shard_map/ppermute | solution.py:42
  65.1 20.5 %collective-permute-start.9 = (bf16[256,1024]{1,0:T(8,128)(2,1)S(1)}, bf16[256,1024]{1,0:T(8,128)(2,1)S(1)}, u32[]{:S(2)}, u32[]{:S(2)}) collective-permute-start(bf16[256,1024]{1,0:T(8,128)(2,1)S(1)} %collective-permute-done.8), channel_id=1, source_target_pairs={{4,0},{8,12},{5,1},{9,13},{6,2},{10,14},{7,3},{11,15},{20,16},{24,... | collective-permute-start | bytes 1572872 | tf_op jit(solution)/shard_map/ppermute | solution.py:46
  66.4 10.8 %collective-permute-start.11 = (bf16[512,512]{1,0:T(8,128)(2,1)S(1)}, bf16[512,512]{1,0:T(8,128)(2,1)S(1)}, u32[]{:S(2)}, u32[]{:S(2)}) collective-permute-start(bf16[512,512]{1,0:T(8,128)(2,1)S(1)} %get-tuple-element.46), channel_id=1, source_target_pairs={{0,1},{1,0},{2,3},{3,2},{4,5},{5,4},{6,7},{7,6},{8,9},{9,8},{10,11... | collective-permute-start | bytes 1572872 | tf_op jit(solution)/shard_map/ppermute | solution.py:38
  66.5 19.1 %collective-permute-start.13 = (bf16[256,1024]{1,0:T(8,128)(2,1)S(1)}, bf16[256,1024]{1,0:T(8,128)(2,1)S(1)}, u32[]{:S(2)}, u32[]{:S(2)}) collective-permute-start(bf16[256,1024]{1,0:T(8,128)(2,1)S(1)} %collective-permute-done.4), channel_id=1, source_target_pairs={{4,8},{8,4},{5,9},{9,5},{6,10},{10,6},{7,11},{11,7},{20,24},{24,20... | collective-permute-start | bytes 1572872 | tf_op jit(solution)/shard_map/ppermute | solution.py:46
  77.2 11.7 %collective-permute-start.33 = (bf16[32,1024]{1,0:T(8,128)(2,1)S(1)}, bf16[32,1024]{1,0:T(8,128)(2,1)S(1)}, u32[]{:S(2)}, u32[]{:S(2)}) collective-permute-start(bf16[32,1024]{1,0:T(8,128)(2,1)S(1)} %dynamic-slice_add_fusion.2), channel_id=1, source_target_pairs={{0,128},{128,0},{1,129},{129,1},{2,130},{130,2},{3,131},{131,3},{4... | collective-permute-start | bytes 196616 | tf_op jit(solution)/shard_map/ppermute | solution.py:106
  84.1 12.8 %collective-permute-start.12 = (bf16[256,1024]{1,0:T(8,128)(2,1)S(1)}, bf16[256,1024]{1,0:T(8,128)(2,1)S(1)}, u32[]{:S(2)}, u32[]{:S(2)}) collective-permute-start(bf16[256,1024]{1,0:T(8,128)(2,1)S(1)} %fusion.34), channel_id=1, source_target_pairs={{0,3},{1,2},{2,1},{3,0},{4,7},{5,6},{6,5},{7,4},{8,11},{9,10},{10,... | collective-permute-start | bytes 1572872 | tf_op jit(solution)/shard_map/ppermute | solution.py:42
  84.4 8.9 %collective-permute-start.16 = (bf16[512,512]{1,0:T(8,128)(2,1)S(1)}, bf16[512,512]{1,0:T(8,128)(2,1)S(1)}, u32[]{:S(2)}, u32[]{:S(2)}) collective-permute-start(bf16[512,512]{1,0:T(8,128)(2,1)S(1)} %get-tuple-element.51), channel_id=1, source_target_pairs={{0,1},{1,0},{2,3},{3,2},{4,5},{5,4},{6,7},{7,6},{8,9},{9,8},{10,11... | collective-permute-start | bytes 1572872 | tf_op jit(solution)/shard_map/ppermute | solution.py:38
  85.6 11.3 %collective-permute-start.14 = (bf16[256,1024]{1,0:T(8,128)(2,1)S(1)}, bf16[256,1024]{1,0:T(8,128)(2,1)S(1)}, u32[]{:S(2)}, u32[]{:S(2)}) collective-permute-start(bf16[256,1024]{1,0:T(8,128)(2,1)S(1)} %collective-permute-done.5), channel_id=1, source_target_pairs={{4,8},{8,4},{5,9},{9,5},{6,10},{10,6},{7,11},{11,7},{20,24},{24,20... | collective-permute-start | bytes 1572872 | tf_op jit(solution)/shard_map/ppermute | solution.py:46
  86.3 12.4 %collective-permute-start.15 = (bf16[256,1024]{1,0:T(8,128)(2,1)S(1)}, bf16[256,1024]{1,0:T(8,128)(2,1)S(1)}, u32[]{:S(2)}, u32[]{:S(2)}) collective-permute-start(bf16[256,1024]{1,0:T(8,128)(2,1)S(1)} %collective-permute-done.13), channel_id=1, source_target_pairs={{4,0},{8,12},{5,1},{9,13},{6,2},{10,14},{7,3},{11,15},{20,16},{24,... | collective-permute-start | bytes 1572872 | tf_op jit(solution)/shard_map/ppermute | solution.py:46
  93.3 11.0 %collective-permute-start.34 = (f32[32,1024]{1,0:T(8,128)S(1)}, f32[32,1024]{1,0:T(8,128)S(1)}, u32[]{:S(2)}, u32[]{:S(2)}) collective-permute-start(f32[32,1024]{1,0:T(8,128)S(1)} %convert_add_fusion), channel_id=1, source_target_pairs={{0,64},{32,96},{64,0},{96,32},{1,65},{33,97},{65,1},{97,33},{2,66}... | collective-permute-start | bytes 393224 | tf_op jit(solution)/shard_map/ppermute | solution.py:106
  95.1 9.3 %collective-permute-start.20 = (bf16[512,512]{1,0:T(8,128)(2,1)S(1)}, bf16[512,512]{1,0:T(8,128)(2,1)S(1)}, u32[]{:S(2)}, u32[]{:S(2)}) collective-permute-start(bf16[512,512]{1,0:T(8,128)(2,1)S(1)} %get-tuple-element.55), channel_id=1, source_target_pairs={{0,1},{1,0},{2,3},{3,2},{4,5},{5,4},{6,7},{7,6},{8,9},{9,8},{10,11... | collective-permute-start | bytes 1572872 | tf_op jit(solution)/shard_map/ppermute | solution.py:38
  98.7 10.7 %collective-permute-start.17 = (bf16[256,1024]{1,0:T(8,128)(2,1)S(1)}, bf16[256,1024]{1,0:T(8,128)(2,1)S(1)}, u32[]{:S(2)}, u32[]{:S(2)}) collective-permute-start(bf16[256,1024]{1,0:T(8,128)(2,1)S(1)} %get-tuple-element.52), channel_id=1, source_target_pairs={{0,4},{4,0},{8,12},{12,8},{1,5},{5,1},{9,13},{13,9},{2,6},{6,2},{1... | collective-permute-start | bytes 1572872 | tf_op jit(solution)/shard_map/ppermute | solution.py:46
  102.0 9.3 %collective-permute-start.18 = (bf16[256,1024]{1,0:T(8,128)(2,1)S(1)}, bf16[256,1024]{1,0:T(8,128)(2,1)S(1)}, u32[]{:S(2)}, u32[]{:S(2)}) collective-permute-start(bf16[256,1024]{1,0:T(8,128)(2,1)S(1)} %fusion.32), channel_id=1, source_target_pairs={{0,3},{1,2},{2,1},{3,0},{4,7},{5,6},{6,5},{7,4},{8,11},{9,10},{10,... | collective-permute-start | bytes 1572872 | tf_op jit(solution)/shard_map/ppermute | solution.py:42
  104.4 47.5 %collective-permute-start.35 = (f32[64,1024]{1,0:T(8,128)S(1)}, f32[64,1024]{1,0:T(8,128)}, u32[]{:S(2)}, u32[]{:S(2)}) collective-permute-start(f32[64,1024]{1,0:T(8,128)S(1)} %maximum_select_fusion.3), channel_id=1, source_target_pairs={{0,32},{32,0},{64,96},{96,64},{1,33},{33,1},{65,97},{97,65},{2,34}... | collective-permute-start | bytes 786440 | tf_op jit(solution)/shard_map/ppermute | solution.py:106
  104.9 17.8 %collective-permute-start.22 = (bf16[512,512]{1,0:T(8,128)(2,1)S(1)}, bf16[512,512]{1,0:T(8,128)(2,1)S(1)}, u32[]{:S(2)}, u32[]{:S(2)}) collective-permute-start(bf16[512,512]{1,0:T(8,128)(2,1)S(1)} %get-tuple-element.57), channel_id=1, source_target_pairs={{0,1},{1,0},{2,3},{3,2},{4,5},{5,4},{6,7},{7,6},{8,9},{9,8},{10,11... | collective-permute-start | bytes 1572872 | tf_op jit(solution)/shard_map/ppermute | solution.py:38
  113.2 9.4 %collective-permute-start.21 = (bf16[256,1024]{1,0:T(8,128)(2,1)S(1)}, bf16[256,1024]{1,0:T(8,128)(2,1)S(1)}, u32[]{:S(2)}, u32[]{:S(2)}) collective-permute-start(bf16[256,1024]{1,0:T(8,128)(2,1)S(1)} %get-tuple-element.56), channel_id=1, source_target_pairs={{0,4},{4,0},{8,12},{12,8},{1,5},{5,1},{9,13},{13,9},{2,6},{6,2},{1... | collective-permute-start | bytes 1572872 | tf_op jit(solution)/shard_map/ppermute | solution.py:46
  115.7 25.3 %collective-permute-start.27 = (bf16[256,1024]{1,0:T(8,128)(2,1)S(1)}, bf16[256,1024]{1,0:T(8,128)(2,1)S(1)}, u32[]{:S(2)}, u32[]{:S(2)}) collective-permute-start(bf16[256,1024]{1,0:T(8,128)(2,1)S(1)} %add_convert_fusion.2), channel_id=1, source_target_pairs={{4,8},{8,4},{5,9},{9,5},{6,10},{10,6},{7,11},{11,7},{20,24},{24,20... | collective-permute-start | bytes 1572872 | tf_op jit(solution)/shard_map/ppermute | solution.py:46
  118.2 24.4 %collective-permute-start.25 = (bf16[256,1024]{1,0:T(8,128)(2,1)S(1)}, bf16[256,1024]{1,0:T(8,128)(2,1)S(1)}, u32[]{:S(2)}, u32[]{:S(2)}) collective-permute-start(bf16[256,1024]{1,0:T(8,128)(2,1)S(1)} %fusion.27), channel_id=1, source_target_pairs={{0,3},{1,2},{2,1},{3,0},{4,7},{5,6},{6,5},{7,4},{8,11},{9,10},{10,... | collective-permute-start | bytes 1572872 | tf_op jit(solution)/shard_map/ppermute | solution.py:42
  128.8 25.1 %collective-permute-start.23 = (bf16[512,1024]{1,0:T(8,128)(2,1)}, bf16[512,1024]{1,0:T(8,128)(2,1)S(1)}, u32[]{:S(2)}, u32[]{:S(2)}) collective-permute-start(bf16[512,1024]{1,0:T(8,128)(2,1)} %get-tuple-element.89), channel_id=1, source_target_pairs={{0,16},{16,0},{1,17},{17,1},{2,18},{18,2},{3,19},{19,3},{4,20},{20... | collective-permute-start | bytes 3145736 | tf_op jit(solution)/shard_map/ppermute | solution.py:34
  141.1 17.4 %collective-permute-start.29 = (bf16[256,1024]{1,0:T(8,128)(2,1)}, bf16[256,1024]{1,0:T(8,128)(2,1)}, u32[]{:S(2)}, u32[]{:S(2)}) collective-permute-start(bf16[256,1024]{1,0:T(8,128)(2,1)} %add_convert_fusion.1), channel_id=1, source_target_pairs={{4,8},{8,4},{5,9},{9,5},{6,10},{10,6},{7,11},{11,7},{20,24},{24,20... | collective-permute-start | bytes 1572872 | tf_op jit(solution)/shard_map/ppermute | solution.py:46
  147.6 15.1 %collective-permute-start.26 = (bf16[256,1024]{1,0:T(8,128)(2,1)}, bf16[256,1024]{1,0:T(8,128)(2,1)}, u32[]{:S(2)}, u32[]{:S(2)}) collective-permute-start(bf16[256,1024]{1,0:T(8,128)(2,1)} %fusion.28), channel_id=1, source_target_pairs={{0,3},{1,2},{2,1},{3,0},{4,7},{5,6},{6,5},{7,4},{8,11},{9,10},{10,... | collective-permute-start | bytes 1572872 | tf_op jit(solution)/shard_map/ppermute | solution.py:42
  149.1 15.0 %collective-permute-start.28 = (bf16[256,1024]{1,0:T(8,128)(2,1)}, bf16[256,1024]{1,0:T(8,128)(2,1)}, u32[]{:S(2)}, u32[]{:S(2)}) collective-permute-start(bf16[256,1024]{1,0:T(8,128)(2,1)} %fusion.26), channel_id=1, source_target_pairs={{0,4},{4,0},{8,12},{12,8},{1,5},{5,1},{9,13},{13,9},{2,6},{6,2},{1... | collective-permute-start | bytes 1572872 | tf_op jit(solution)/shard_map/ppermute | solution.py:46
  153.0 16.7 %collective-permute-start.36 = (f32[128,1024]{1,0:T(8,128)S(1)}, f32[128,1024]{1,0:T(8,128)S(1)}, u32[]{:S(2)}, u32[]{:S(2)}) collective-permute-start(f32[128,1024]{1,0:T(8,128)S(1)} %maximum_select_fusion.2), channel_id=1, source_target_pairs={{0,16},{16,0},{1,17},{17,1},{2,18},{18,2},{3,19},{19,3},{4,20},{20... | collective-permute-start | bytes 1572872 | tf_op jit(solution)/shard_map/ppermute | solution.py:106
  156.4 24.2 %collective-permute-start.24 = (bf16[512,1024]{1,0:T(8,128)(2,1)S(1)}, bf16[512,1024]{1,0:T(8,128)(2,1)S(1)}, u32[]{:S(2)}, u32[]{:S(2)}) collective-permute-start(bf16[512,1024]{1,0:T(8,128)(2,1)S(1)} %add_convert_fusion), channel_id=1, source_target_pairs={{1,16},{2,19},{16,1},{19,2},{5,20},{6,23},{20,5},{23,6},{9,24},{10... | collective-permute-start | bytes 3145736 | tf_op jit(solution)/shard_map/ppermute | solution.py:30
  166.4 11.8 %collective-permute-start.30 = (bf16[256,1024]{1,0:T(8,128)(2,1)S(1)}, bf16[256,1024]{1,0:T(8,128)(2,1)S(1)}, u32[]{:S(2)}, u32[]{:S(2)}) collective-permute-start(bf16[256,1024]{1,0:T(8,128)(2,1)S(1)} %get-tuple-element.91), channel_id=1, source_target_pairs={{1,16},{2,19},{16,1},{19,2},{5,20},{6,23},{20,5},{23,6},{9,24},{10... | collective-permute-start | bytes 1572872 | tf_op jit(solution)/shard_map/ppermute | solution.py:30
  (26 other events, 454.5 us)

commit v7 on v6

--- a/solution.py
+++ b/solution.py
@@ -80,7 +80,7 @@
             out_specs=[out, out],
         ),
         out_shape=[kind, kind],
-        cost_estimate=pl.CostEstimate(flops=0, bytes_accessed=0, transcendentals=0),
+        cost_estimate=pl.CostEstimate(flops=0, bytes_accessed=16 << 20, transcendentals=0),
     )(blocks, tokens, tokens)
 
 
@@ -92,8 +92,8 @@
         self.steps = [("c", CORE, c), ("y", near, y % 2), ("y", wide, y // 2), ("zh", CORE, c)]
         self.at = 0
 
-    def send(self, earlier):
-        self.v = after(self.v, earlier)
+    def send(self, *earlier):
+        self.v = after(self.v, *earlier)
         if self.at < 3:
             bit = self.steps[self.at][2]
             n = self.v.shape[0] // 2
@@ -138,33 +138,29 @@
     ).reshape(2, 8)
 
     w = jnp.where(stays, weight, swap(weight))
-    g_mine = lax.dynamic_slice_in_dim(key_grad, c * 256, 256, 0)
-    g_first = core(lax.dynamic_slice_in_dim(key_grad, (1 - c) * 256, 256, 0))
-    g_l = jnp.where(stays, g_first, g_mine)
+    g_sib = core(key_grad)
+    x_give, x_own = halves(tokens, blocks.astype(jnp.int32))
+    x_sib = core(x_give)
     drift = Drift(anchor - local_params[0].astype(f32), c, y)
-    d = drift.send(g_l)
-    w, g_l, blocks, d = together(w, g_l, blocks.astype(jnp.int32), d)
-    drift.take(d)
-
-    g_half, e_own, m_own, q_own = beside(g_l), line(w, PAIRS), line(w, MIDDLE), across(w)
-    x_give, x_own = halves(tokens, blocks)
-    x_sib = core(x_give)
-    drift.take(drift.send(w))
+    drift.take(drift.send())
+    w, g_sib = together(w, g_sib)
+    g_a = jnp.where(stays, key_grad, g_sib)
+    g_l = lax.dynamic_slice_in_dim(jnp.where(stays, g_sib, key_grad), c * 256, 256, 0)
+
+    got = (beside(g_l), line(w, PAIRS), line(w, MIDDLE), across(w), drift.send())
     leave = [jnp.where(stays, x_sib[k], x_own[k]) for k in range(4)]
     keep = [jnp.where(stays, x_own[k], x_sib[k]) for k in range(4)]
-
-    x_b = [beside(after(leave[0], g_half))]
-    e2 = line(after(m_own, e_own, g_half, leave[0]), ENDS_OUT)
-    m2 = line(after(e_own, m_own, g_half, leave[0]), MIDDLE)
-    q2 = across(after(e_own, q_own, g_half, leave[0]))
+    got, leave, drift.v = together(got, leave, drift.v)
+    g_half, e_own, m_own, q_own, d = got
+    drift.take(d)
+
+    x_b = [beside(leave[0])]
+    e2, m2, q2 = line(m_own, ENDS_OUT), line(e_own, MIDDLE), across(e_own)
     drift.take(drift.send(g_half))
-    rest = core(jnp.concatenate([g_half, g_mine]))
-
-    def in_order(a, b):
-        return jnp.where(c == 0, jnp.concatenate([a, b]), jnp.concatenate([b, a]))
-
-    g_b = in_order(g_half, rest[:256])
-    g_a = jnp.where(stays, key_grad, in_order(g_first, rest[256:]))
+    g_rest = core(g_half)
+    g_b = jnp.where(
+        c == 0, jnp.concatenate([g_half, g_rest]), jnp.concatenate([g_rest, g_half])
+    )
     base = [dot_t(k, g_a) for k in keep]
     mid = jnp.where(end, e2, m_own)
 
@@ -202,19 +198,25 @@
     k_a = k_a + dot(keep[1], rows[1])
     k_b = dot(cat(x_b[1], x_b[2]), jnp.concatenate(rows[1:3]))
     part2 = staying(2) + q5.astype(f32)
-
-    e6 = line(after((part2 + m5.astype(f32)).astype(bf16), e5), PAIRS)
-    m6 = line(after((part1 + e5.astype(f32)).astype(bf16), m5), MIDDLE)
-    q6 = across(after(going(3), q5))
+    (x_b[3], e5, m5, q5), drift.v, part1, part2, k_a, k_b = together(
+        (x_b[3], e5, m5, q5), drift.v, part1, part2, k_a, k_b
+    )
+
+    got = (
+        line((part2 + m5.astype(f32)).astype(bf16), PAIRS),
+        line((part1 + e5.astype(f32)).astype(bf16), MIDDLE),
+        across(going(3)),
+    )
     rows[0] = jnp.concatenate([jnp.where(end, e3, m2), jnp.where(end, e5, m4)])
     k_a = k_a + dot(keep[0], rows[0])
     k_b = k_b + dot(cat(x_b[0], x_b[3]), jnp.concatenate([rows[0], rows[3]]))
     k_got = core(jnp.where(stays, k_b, k_a).astype(bf16))
     keys_work = (jnp.where(stays, k_a, k_b) + k_got.astype(f32)).astype(bf16)
     keys = jnp.where(stays, keys_work, swap(keys_work))
+    e6, m6, q6 = got
     total = staying(3) + q6.astype(f32) + e6.astype(f32) + m6.astype(f32)
     gradient = jnp.where(stays, total, swap(total.astype(bf16)).astype(f32))
-    drift.take(drift.send(x_b[3]))
+    drift.take(drift.send())
 
     new_first = first_decay * adam_first[0] + (1.0 - first_decay) * gradient
     new_second = second_decay * adam_second[0] + (1.0 - second_decay) * gradient * gradient

time: 183 us -> 159 us (0.87)
  waiting for transfers between devices: 54.3 us -> 71.5 us
  matrix products: 27.3 us -> 12.5 us
  starting transfers between devices: 65.1 us -> 50.5 us
  other arithmetic: 19.9 us -> 13.9 us
  local copies, waits for them, and re-layouts: 6.38 us -> 1.67 us
    dot_general x12, matrix products: 19.2 us -> 7.09 us  [dot_t(): lax.dot_general(a, b, (((0,), (0,)), ((), ())), preferred_element_type=f32)]
    ppermute x6, waiting for transfers between devices: 5.95 us -> 14.8 us  [across(): return lax.ppermute(v, 'x', ACROSS)]
    ppermute x12, waiting for transfers between devices: 14 us -> 21.4 us  [line(): return lax.ppermute(v, 'zl', pairs)]
    ppermute x4, starting transfers between devices: 14.9 us -> 9.56 us  [core(): return lax.ppermute(v, 'c', CORE)]
    ppermute x3, waiting for transfers between devices: 12 us -> 15.4 us  [swap(): return lax.ppermute(v, ('c', 'x'), SWAP)]
    ppermute x6, starting transfers between devices: 7.72 us -> 4.35 us  [across(): return lax.ppermute(v, 'x', ACROSS)]
    dot_general x5, matrix products: 8.1 us -> 5.41 us  [dot(): return jnp.dot(a, b, preferred_element_type=f32)]
    ppermute x5, waiting for transfers between devices: 15.3 us -> 12.6 us  [beside(): return lax.ppermute(v, 'x', BESIDE)]
  transfers between devices with their start and end apart: 37 -> 37, of which waited for: 13 -> 14; matrix products, arithmetic and copies ran while one was open for 27% -> 15% of each run, Pallas kernels for 4% -> 0%
where the time goes in v7:
time: 159 us
  waiting for transfers between devices  71.5 us (45%)
  starting transfers between devices  50.5 us (32%)
  other arithmetic  13.9 us (9%)
  matrix products  12.5 us (8%)
  Pallas kernels  7.36 us (5%)
  local copies, waits for them, and re-layouts  1.67 us (1%)
    ppermute x12, waiting for transfers between devices, line(): return lax.ppermute(v, 'zl', pairs)  21.4 us
    ppermute x12, starting transfers between devices, line(): return lax.ppermute(v, 'zl', pairs)  16.8 us
    ppermute x3, waiting for transfers between devices, swap(): return lax.ppermute(v, ('c', 'x'), SWAP)  15.4 us
    ppermute x6, waiting for transfers between devices, across(): return lax.ppermute(v, 'x', ACROSS)  14.8 us
    ppermute x5, waiting for transfers between devices, beside(): return lax.ppermute(v, 'x', BESIDE)  12.6 us
    ppermute x7, starting transfers between devices, send(): return lax.ppermute(self.sent, axis, perm)  12.5 us
    ppermute x4, starting transfers between devices, core(): return lax.ppermute(v, 'c', CORE)  9.56 us
    pallas_call x1, Pallas kernels, halves(): pl.pallas_call(move, grid_spec=pltpu.PrefetchScalarGridSpec(num_scalar_pr...  7.36 us
  transfers between devices with their start and end apart: 37, of which 14 were waited for; matrix products, arithmetic and copies ran while one was open for 15% of the time, Pallas kernels for 0%

profile of v7, /device:TPU:1, one launch (start us, length us, event | category | flops | bytes accessed | tf_op | source)
XLA Modules:
  0.0 158.7 jit_solution(4475576327086542993)
XLA Ops:
  1.4 7.4 %shard_map.127 = (bf16[4,512,512]{2,1,0:T(8,128)(2,1)}, bf16[4,512,512]{2,1,0:T(8,128)(2,1)}) custom-call(s32[2,8]{1,0:T(2,128)} %reshape.37._, bf16[512,4096]{1,0:T(8,128)(2,1)} %b.1, bf16[512,4096]{1,0:T(8,128)(2,1)} %b.1), custom_call_target="tpu_custom_call" | custom-call | bytes 16777216 | tf_op jit(solution)/shard_map/pallas_call | solution.py:74
  8.8 3.2 %collective-permute-start.8 = (bf16[4,512,512]{2,1,0:T(8,128)(2,1)}, bf16[4,512,512]{2,1,0:T(8,128)(2,1)S(1)}, u32[]{:S(2)}, u32[]{:S(2)}) collective-permute-start(bf16[4,512,512]{2,1,0:T(8,128)(2,1)} %get-tuple-element.46), channel_id=1, source_target_pairs={{0,16},{16,0},{1,17},{17,1},{2,18},{18,2},{3,19},{19,3},{4,20},{20... | collective-permute-start | bytes 6291464 | tf_op jit(solution)/shard_map/ppermute | solution.py:34
  12.0 1.5 convert_subtract_fusion.1
  14.9 1.9 %collective-permute-start = (bf16[256,1024]{1,0:T(8,128)(2,1)}, bf16[256,1024]{1,0:T(8,128)(2,1)}, u32[]{:S(2)}, u32[]{:S(2)}) collective-permute-start(bf16[256,1024]{1,0:T(8,128)(2,1)} %bitcast.68), channel_id=1, source_target_pairs={{1,16},{2,19},{16,1},{19,2},{5,20},{6,23},{20,5},{23,6},{9,24},{10... | collective-permute-start | bytes 1572872 | tf_op jit(solution)/shard_map/ppermute | solution.py:30
  18.2 7.7 %collective-permute-done = bf16[256,1024]{1,0:T(8,128)(2,1)} collective-permute-done((bf16[256,1024]{1,0:T(8,128)(2,1)}, bf16[256,1024]{1,0:T(8,128)(2,1)}, u32[]{:S(2)}, u32[]{:S(2)}) %collective-permute-start) | collective-permute-done | bytes 524320 | tf_op jit(solution)/shard_map/ppermute | solution.py:30
  28.5 4.6 %collective-permute-start.3 = (bf16[256,1024]{1,0:T(8,128)(2,1)S(1)}, bf16[256,1024]{1,0:T(8,128)(2,1)S(1)}, u32[]{:S(2)}, u32[]{:S(2)}) collective-permute-start(bf16[256,1024]{1,0:T(8,128)(2,1)S(1)} %broadcast_select_fusion.2), channel_id=1, source_target_pairs={{0,4},{4,0},{8,12},{12,8},{1,5},{5,1},{9,13},{13,9},{2,6},{6,2},{1... | collective-permute-start | bytes 1572872 | tf_op jit(solution)/shard_map/ppermute | solution.py:46
  34.5 1.3 broadcast_select_fusion
  35.8 1.4 collective-permute-start.7
  37.5 6.6 %collective-permute-done.7 = f32[64,1024]{1,0:T(8,128)S(1)} collective-permute-done((f32[64,1024]{1,0:T(8,128)S(1)}, f32[64,1024]{1,0:T(8,128)S(1)}, u32[]{:S(2)}, u32[]{:S(2)}) %collective-permute-start.7) | collective-permute-done | bytes 262176 | tf_op jit(solution)/shard_map/ppermute | solution.py:106
  44.1 3.3 %collective-permute-done.2 = bf16[256,1024]{1,0:T(8,128)(2,1)S(1)} collective-permute-done((bf16[256,1024]{1,0:T(8,128)(2,1)S(1)}, bf16[256,1024]{1,0:T(8,128)(2,1)S(1)}, u32[]{:S(2)}, u32[]{:S(2)}) %collective-permute-start.2) | collective-permute-done | bytes 524320 | tf_op jit(solution)/shard_map/ppermute | solution.py:38
  49.2 1.3 collective-permute-start.20
  53.7 8.3 %collective-permute-done.9 = bf16[512,512]{1,0:T(8,128)(2,1)S(1)} collective-permute-done((bf16[512,512]{1,0:T(8,128)(2,1)S(1)}, bf16[512,512]{1,0:T(8,128)(2,1)S(1)}, u32[]{:S(2)}, u32[]{:S(2)}) %collective-permute-start.9) | collective-permute-done | bytes 524320 | tf_op jit(solution)/shard_map/ppermute | solution.py:38
  62.0 2.9 %collective-permute-start.26 = (f32[32,1024]{1,0:T(8,128)S(1)}, f32[32,1024]{1,0:T(8,128)S(1)}, u32[]{:S(2)}, u32[]{:S(2)}) collective-permute-start(f32[32,1024]{1,0:T(8,128)S(1)} %constant_dynamic-slice_fusion), channel_id=1, source_target_pairs={{0,64},{32,96},{64,0},{96,32},{1,65},{33,97},{65,1},{97,33},{2,66}... | collective-permute-start | bytes 393224 | tf_op jit(solution)/shard_map/ppermute | solution.py:106
  66.3 1.9 %collective-permute-start.15 = (bf16[256,1024]{1,0:T(8,128)(2,1)S(1)}, bf16[256,1024]{1,0:T(8,128)(2,1)S(1)}, u32[]{:S(2)}, u32[]{:S(2)}) collective-permute-start(bf16[256,1024]{1,0:T(8,128)(2,1)S(1)} %fusion.28), channel_id=1, source_target_pairs={{0,3},{1,2},{2,1},{3,0},{4,7},{5,6},{6,5},{7,4},{8,11},{9,10},{10,... | collective-permute-start | bytes 1572872 | tf_op jit(solution)/shard_map/ppermute | solution.py:42
  68.3 5.2 %collective-permute-start.27 = (bf16[32,1024]{1,0:T(8,128)(2,1)S(1)}, bf16[32,1024]{1,0:T(8,128)(2,1)S(1)}, u32[]{:S(2)}, u32[]{:S(2)}) collective-permute-start(bf16[32,1024]{1,0:T(8,128)(2,1)S(1)} %dynamic-slice_add_fusion.2), channel_id=1, source_target_pairs={{0,128},{128,0},{1,129},{129,1},{2,130},{130,2},{3,131},{131,3},{4... | collective-permute-start | bytes 196616 | tf_op jit(solution)/shard_map/ppermute | solution.py:106
  73.5 1.3 collective-permute-start.21
  79.7 10.4 %collective-permute-done.21 = bf16[256,1024]{1,0:T(8,128)(2,1)S(1)} collective-permute-done((bf16[256,1024]{1,0:T(8,128)(2,1)S(1)}, bf16[256,1024]{1,0:T(8,128)(2,1)S(1)}, u32[]{:S(2)}, u32[]{:S(2)}) %collective-permute-start.21) | collective-permute-done | bytes 524320 | tf_op jit(solution)/shard_map/ppermute | solution.py:46
  92.6 8.7 %collective-permute-done.22 = bf16[256,1024]{1,0:T(8,128)(2,1)S(1)} collective-permute-done((bf16[256,1024]{1,0:T(8,128)(2,1)S(1)}, bf16[256,1024]{1,0:T(8,128)(2,1)S(1)}, u32[]{:S(2)}, u32[]{:S(2)}) %collective-permute-start.22) | collective-permute-done | bytes 524320 | tf_op jit(solution)/shard_map/ppermute | solution.py:46
  101.5 1.6 %collective-permute-done.16 = bf16[256,1024]{1,0:T(8,128)(2,1)S(1)} collective-permute-done((bf16[256,1024]{1,0:T(8,128)(2,1)S(1)}, bf16[256,1024]{1,0:T(8,128)(2,1)S(1)}, u32[]{:S(2)}, u32[]{:S(2)}) %collective-permute-start.16) | collective-permute-done | bytes 524320 | tf_op jit(solution)/shard_map/ppermute | solution.py:42
  107.0 1.3 fusion.16
  108.3 1.3 fusion.5
  109.7 7.4 %collective-permute-done.25 = bf16[256,1024]{1,0:T(8,128)(2,1)S(1)} collective-permute-done((bf16[256,1024]{1,0:T(8,128)(2,1)S(1)}, bf16[256,1024]{1,0:T(8,128)(2,1)S(1)}, u32[]{:S(2)}, u32[]{:S(2)}) %collective-permute-start.25) | collective-permute-done | bytes 524320 | tf_op jit(solution)/shard_map/ppermute | solution.py:42
  118.4 1.4 select_convert_fusion
  119.8 5.0 %collective-permute-start.30 = (bf16[512,1024]{1,0:T(8,128)(2,1)S(1)}, bf16[512,1024]{1,0:T(8,128)(2,1)S(1)}, u32[]{:S(2)}, u32[]{:S(2)}) collective-permute-start(bf16[512,1024]{1,0:T(8,128)(2,1)S(1)} %get-tuple-element.97), channel_id=1, source_target_pairs={{0,16},{16,0},{1,17},{17,1},{2,18},{18,2},{3,19},{19,3},{4,20},{20... | collective-permute-start | bytes 3145736 | tf_op jit(solution)/shard_map/ppermute | solution.py:34
  127.1 4.3 %collective-permute-start.33 = (bf16[256,1024]{1,0:T(8,128)(2,1)S(1)}, bf16[256,1024]{1,0:T(8,128)(2,1)S(1)}, u32[]{:S(2)}, u32[]{:S(2)}) collective-permute-start(bf16[256,1024]{1,0:T(8,128)(2,1)S(1)} %add_convert_fusion.2), channel_id=1, source_target_pairs={{0,4},{4,0},{8,12},{12,8},{1,5},{5,1},{9,13},{13,9},{2,6},{6,2},{1... | collective-permute-start | bytes 1572872 | tf_op jit(solution)/shard_map/ppermute | solution.py:46
  133.4 2.1 %collective-permute-start.31 = (bf16[512,1024]{1,0:T(8,128)(2,1)S(1)}, bf16[512,1024]{1,0:T(8,128)(2,1)S(1)}, u32[]{:S(2)}, u32[]{:S(2)}) collective-permute-start(bf16[512,1024]{1,0:T(8,128)(2,1)S(1)} %add_convert_fusion), channel_id=1, source_target_pairs={{1,16},{2,19},{16,1},{19,2},{5,20},{6,23},{20,5},{23,6},{9,24},{10... | collective-permute-start | bytes 3145736 | tf_op jit(solution)/shard_map/ppermute | solution.py:30
  135.5 5.4 %collective-permute-done.32 = bf16[256,1024]{1,0:T(8,128)(2,1)S(1)} collective-permute-done((bf16[256,1024]{1,0:T(8,128)(2,1)S(1)}, bf16[256,1024]{1,0:T(8,128)(2,1)S(1)}, u32[]{:S(2)}, u32[]{:S(2)}) %collective-permute-start.32) | collective-permute-done | bytes 524320 | tf_op jit(solution)/shard_map/ppermute | solution.py:42
  140.8 2.3 %collective-permute-done.33 = bf16[256,1024]{1,0:T(8,128)(2,1)S(1)} collective-permute-done((bf16[256,1024]{1,0:T(8,128)(2,1)S(1)}, bf16[256,1024]{1,0:T(8,128)(2,1)S(1)}, u32[]{:S(2)}, u32[]{:S(2)}) %collective-permute-start.33) | collective-permute-done | bytes 524320 | tf_op jit(solution)/shard_map/ppermute | solution.py:46
  143.8 2.1 %collective-permute-start.35 = (bf16[256,1024]{1,0:T(8,128)(2,1)S(1)}, bf16[256,1024]{1,0:T(8,128)(2,1)S(1)}, u32[]{:S(2)}, u32[]{:S(2)}) collective-permute-start(bf16[256,1024]{1,0:T(8,128)(2,1)S(1)} %get-tuple-element.99), channel_id=1, source_target_pairs={{1,16},{2,19},{16,1},{19,2},{5,20},{6,23},{20,5},{23,6},{9,24},{10... | collective-permute-start | bytes 1572872 | tf_op jit(solution)/shard_map/ppermute | solution.py:30
  145.9 1.7 %multiply_subtract_fusion = (f32[256,1024]{1,0:T(8,128)}, f32[256,1024]{1,0:T(8,128)}) fusion(f32[256,1024]{1,0:T(8,128)S(1)} %copy-done.1, f32[128,1024]{1,0:T(8,128)S(1)} %maximum_select_fusion.2, f32[128,1024]{1,0:T(8,128)S(1)} %collective-permute-done.36, pred[]{:T(512)S(6)} %eq.41, f32[256,1024]{1,0:T(8,128)S(1)} %copy-done.4), kind=kLoop, calls=%fused_computation.70 | loop fusion | flops 2621440 | bytes 5242881 | tf_op jit(solution)/shard_map/sub | solution.py:229
  147.6 7.7 %collective-permute-done.35 = bf16[256,1024]{1,0:T(8,128)(2,1)S(1)} collective-permute-done((bf16[256,1024]{1,0:T(8,128)(2,1)S(1)}, bf16[256,1024]{1,0:T(8,128)(2,1)S(1)}, u32[]{:S(2)}, u32[]{:S(2)}) %collective-permute-start.35) | collective-permute-done | bytes 524320 | tf_op jit(solution)/shard_map/ppermute | solution.py:30
  155.3 2.3 %fusion.94 = (f32[1,256,1024]{2,1,0:T(8,128)}, bf16[1,256,1024]{2,1,0:T(8,128)(2,1)}, f32[1,256,1024]{2,1,0:T(8,128)}) fusion(f32[256,1024]{1,0:T(8,128)S(1)} %get-tuple-element.100, bf16[256,1024]{1,0:T(8,128)(2,1)S(1)} %collective-permute-done.35, pred[]{:T(512)S(6)} %eq.36, f32[1,256,1024]{2,1,0:T(8,128)S(1)} %copy-done.5, ...), kind=kLoop, calls=%fused_computation.132 | loop fusion | flops 4456448 | bytes 6815745 | tf_op jit(solution)/shard_map/broadcast_in_dim | solution.py:230
  (101 shorter events, 32.8 us)
Async XLA Ops:
  8.8 27.0 %collective-permute-start.8 = (bf16[4,512,512]{2,1,0:T(8,128)(2,1)}, bf16[4,512,512]{2,1,0:T(8,128)(2,1)S(1)}, u32[]{:S(2)}, u32[]{:S(2)}) collective-permute-start(bf16[4,512,512]{2,1,0:T(8,128)(2,1)} %get-tuple-element.46), channel_id=1, source_target_pairs={{0,16},{16,0},{1,17},{17,1},{2,18},{18,2},{3,19},{19,3},{4,20},{20... | collective-permute-start | bytes 6291464 | tf_op jit(solution)/shard_map/ppermute | solution.py:34
  14.4 12.6 %collective-permute-start.1 = (bf16[512,1024]{1,0:T(8,128)(2,1)}, bf16[512,1024]{1,0:T(8,128)(2,1)}, u32[]{:S(2)}, u32[]{:S(2)}) collective-permute-start(bf16[512,1024]{1,0:T(8,128)(2,1)} %param.9), channel_id=1, source_target_pairs={{0,16},{16,0},{1,17},{17,1},{2,18},{18,2},{3,19},{19,3},{4,20},{20... | collective-permute-start | bytes 3145736 | tf_op jit(solution)/shard_map/ppermute | solution.py:34
  14.9 11.0 %collective-permute-start = (bf16[256,1024]{1,0:T(8,128)(2,1)}, bf16[256,1024]{1,0:T(8,128)(2,1)}, u32[]{:S(2)}, u32[]{:S(2)}) collective-permute-start(bf16[256,1024]{1,0:T(8,128)(2,1)} %bitcast.68), channel_id=1, source_target_pairs={{1,16},{2,19},{16,1},{19,2},{5,20},{6,23},{20,5},{23,6},{9,24},{10... | collective-permute-start | bytes 1572872 | tf_op jit(solution)/shard_map/ppermute | solution.py:30
  27.0 20.4 %collective-permute-start.5 = (bf16[256,1024]{1,0:T(8,128)(2,1)S(1)}, bf16[256,1024]{1,0:T(8,128)(2,1)S(1)}, u32[]{:S(2)}, u32[]{:S(2)}) collective-permute-start(bf16[256,1024]{1,0:T(8,128)(2,1)S(1)} %broadcast_select_fusion.2), channel_id=1, source_target_pairs={{0,3},{1,2},{2,1},{3,0},{4,7},{5,6},{6,5},{7,4},{8,11},{9,10},{10,... | collective-permute-start | bytes 1572872 | tf_op jit(solution)/shard_map/ppermute | solution.py:42
  27.8 19.6 %collective-permute-start.4 = (bf16[256,1024]{1,0:T(8,128)(2,1)S(1)}, bf16[256,1024]{1,0:T(8,128)(2,1)S(1)}, u32[]{:S(2)}, u32[]{:S(2)}) collective-permute-start(bf16[256,1024]{1,0:T(8,128)(2,1)S(1)} %broadcast_select_fusion.2), channel_id=1, source_target_pairs={{4,8},{8,4},{5,9},{9,5},{6,10},{10,6},{7,11},{11,7},{20,24},{24,20... | collective-permute-start | bytes 1572872 | tf_op jit(solution)/shard_map/ppermute | solution.py:46
  28.5 18.9 %collective-permute-start.3 = (bf16[256,1024]{1,0:T(8,128)(2,1)S(1)}, bf16[256,1024]{1,0:T(8,128)(2,1)S(1)}, u32[]{:S(2)}, u32[]{:S(2)}) collective-permute-start(bf16[256,1024]{1,0:T(8,128)(2,1)S(1)} %broadcast_select_fusion.2), channel_id=1, source_target_pairs={{0,4},{4,0},{8,12},{12,8},{1,5},{5,1},{9,13},{13,9},{2,6},{6,2},{1... | collective-permute-start | bytes 1572872 | tf_op jit(solution)/shard_map/ppermute | solution.py:46
  34.4 13.1 %collective-permute-start.2 = (bf16[256,1024]{1,0:T(8,128)(2,1)S(1)}, bf16[256,1024]{1,0:T(8,128)(2,1)S(1)}, u32[]{:S(2)}, u32[]{:S(2)}) collective-permute-start(bf16[256,1024]{1,0:T(8,128)(2,1)S(1)} %dynamic-slice_select_fusion), channel_id=1, source_target_pairs={{0,1},{1,0},{2,3},{3,2},{4,5},{5,4},{6,7},{7,6},{8,9},{9,8},{10,11... | collective-permute-start | bytes 1572872 | tf_op jit(solution)/shard_map/ppermute | solution.py:38
  47.4 17.5 %collective-permute-start.17 = (bf16[256,1024]{1,0:T(8,128)(2,1)S(1)}, bf16[256,1024]{1,0:T(8,128)(2,1)S(1)}, u32[]{:S(2)}, u32[]{:S(2)}) collective-permute-start(bf16[256,1024]{1,0:T(8,128)(2,1)S(1)} %collective-permute-done.3), channel_id=1, source_target_pairs={{4,8},{8,4},{5,9},{9,5},{6,10},{10,6},{7,11},{11,7},{20,24},{24,20... | collective-permute-start | bytes 1572872 | tf_op jit(solution)/shard_map/ppermute | solution.py:46
  48.1 18.2 %collective-permute-start.14 = (bf16[256,1024]{1,0:T(8,128)(2,1)S(1)}, bf16[256,1024]{1,0:T(8,128)(2,1)S(1)}, u32[]{:S(2)}, u32[]{:S(2)}) collective-permute-start(bf16[256,1024]{1,0:T(8,128)(2,1)S(1)} %collective-permute-done.3), channel_id=1, source_target_pairs={{0,3},{1,2},{2,1},{3,0},{4,7},{5,6},{6,5},{7,4},{8,11},{9,10},{10,... | collective-permute-start | bytes 1572872 | tf_op jit(solution)/shard_map/ppermute | solution.py:42
  49.2 12.8 %collective-permute-start.9 = (bf16[512,512]{1,0:T(8,128)(2,1)S(1)}, bf16[512,512]{1,0:T(8,128)(2,1)S(1)}, u32[]{:S(2)}, u32[]{:S(2)}) collective-permute-start(bf16[512,512]{1,0:T(8,128)(2,1)S(1)} %get-tuple-element.51), channel_id=1, source_target_pairs={{0,1},{1,0},{2,3},{3,2},{4,5},{5,4},{6,7},{7,6},{8,9},{9,8},{10,11... | collective-permute-start | bytes 1572872 | tf_op jit(solution)/shard_map/ppermute | solution.py:38
  49.2 24.3 %collective-permute-start.20 = (bf16[256,1024]{1,0:T(8,128)(2,1)S(1)}, bf16[256,1024]{1,0:T(8,128)(2,1)S(1)}, u32[]{:S(2)}, u32[]{:S(2)}) collective-permute-start(bf16[256,1024]{1,0:T(8,128)(2,1)S(1)} %collective-permute-done.4), channel_id=1, source_target_pairs={{4,0},{8,12},{5,1},{9,13},{6,2},{10,14},{7,3},{11,15},{20,16},{24,... | collective-permute-start | bytes 1572872 | tf_op jit(solution)/shard_map/ppermute | solution.py:46
  50.5 14.7 %collective-permute-start.13 = (bf16[256,1024]{1,0:T(8,128)(2,1)S(1)}, bf16[256,1024]{1,0:T(8,128)(2,1)S(1)}, u32[]{:S(2)}, u32[]{:S(2)}) collective-permute-start(bf16[256,1024]{1,0:T(8,128)(2,1)S(1)} %collective-permute-done.2), channel_id=1, source_target_pairs={{0,16},{16,0},{1,17},{17,1},{2,18},{18,2},{3,19},{19,3},{4,20},{20... | collective-permute-start | bytes 1572872 | tf_op jit(solution)/shard_map/ppermute | solution.py:34
  64.9 11.6 %collective-permute-start.10 = (bf16[512,512]{1,0:T(8,128)(2,1)S(1)}, bf16[512,512]{1,0:T(8,128)(2,1)S(1)}, u32[]{:S(2)}, u32[]{:S(2)}) collective-permute-start(bf16[512,512]{1,0:T(8,128)(2,1)S(1)} %get-tuple-element.52), channel_id=1, source_target_pairs={{0,1},{1,0},{2,3},{3,2},{4,5},{5,4},{6,7},{7,6},{8,9},{9,8},{10,11... | collective-permute-start | bytes 1572872 | tf_op jit(solution)/shard_map/ppermute | solution.py:38
  65.1 12.9 %collective-permute-start.18 = (bf16[256,1024]{1,0:T(8,128)(2,1)S(1)}, bf16[256,1024]{1,0:T(8,128)(2,1)S(1)}, u32[]{:S(2)}, u32[]{:S(2)}) collective-permute-start(bf16[256,1024]{1,0:T(8,128)(2,1)S(1)} %collective-permute-done.5), channel_id=1, source_target_pairs={{4,8},{8,4},{5,9},{9,5},{6,10},{10,6},{7,11},{11,7},{20,24},{24,20... | collective-permute-start | bytes 1572872 | tf_op jit(solution)/shard_map/ppermute | solution.py:46
  66.3 12.8 %collective-permute-start.15 = (bf16[256,1024]{1,0:T(8,128)(2,1)S(1)}, bf16[256,1024]{1,0:T(8,128)(2,1)S(1)}, u32[]{:S(2)}, u32[]{:S(2)}) collective-permute-start(bf16[256,1024]{1,0:T(8,128)(2,1)S(1)} %fusion.28), channel_id=1, source_target_pairs={{0,3},{1,2},{2,1},{3,0},{4,7},{5,6},{6,5},{7,4},{8,11},{9,10},{10,... | collective-permute-start | bytes 1572872 | tf_op jit(solution)/shard_map/ppermute | solution.py:42
  73.5 16.6 %collective-permute-start.21 = (bf16[256,1024]{1,0:T(8,128)(2,1)S(1)}, bf16[256,1024]{1,0:T(8,128)(2,1)S(1)}, u32[]{:S(2)}, u32[]{:S(2)}) collective-permute-start(bf16[256,1024]{1,0:T(8,128)(2,1)S(1)} %collective-permute-done.17), channel_id=1, source_target_pairs={{4,0},{8,12},{5,1},{9,13},{6,2},{10,14},{7,3},{11,15},{20,16},{24,... | collective-permute-start | bytes 1572872 | tf_op jit(solution)/shard_map/ppermute | solution.py:46
  76.5 14.5 %collective-permute-start.28 = (f32[32,1024]{1,0:T(8,128)S(1)}, f32[32,1024]{1,0:T(8,128)S(1)}, u32[]{:S(2)}, u32[]{:S(2)}) collective-permute-start(f32[32,1024]{1,0:T(8,128)S(1)} %convert_add_fusion), channel_id=1, source_target_pairs={{0,64},{32,96},{64,0},{96,32},{1,65},{33,97},{65,1},{97,33},{2,66}... | collective-permute-start | bytes 393224 | tf_op jit(solution)/shard_map/ppermute | solution.py:106
  77.8 13.3 %collective-permute-start.11 = (bf16[512,512]{1,0:T(8,128)(2,1)S(1)}, bf16[512,512]{1,0:T(8,128)(2,1)S(1)}, u32[]{:S(2)}, u32[]{:S(2)}) collective-permute-start(bf16[512,512]{1,0:T(8,128)(2,1)S(1)} %get-tuple-element.53), channel_id=1, source_target_pairs={{0,1},{1,0},{2,3},{3,2},{4,5},{5,4},{6,7},{7,6},{8,9},{9,8},{10,11... | collective-permute-start | bytes 1572872 | tf_op jit(solution)/shard_map/ppermute | solution.py:38
  78.0 23.4 %collective-permute-start.19 = (bf16[256,1024]{1,0:T(8,128)(2,1)S(1)}, bf16[256,1024]{1,0:T(8,128)(2,1)S(1)}, u32[]{:S(2)}, u32[]{:S(2)}) collective-permute-start(bf16[256,1024]{1,0:T(8,128)(2,1)S(1)} %collective-permute-done.14), channel_id=1, source_target_pairs={{4,8},{8,4},{5,9},{9,5},{6,10},{10,6},{7,11},{11,7},{20,24},{24,20... | collective-permute-start | bytes 1572872 | tf_op jit(solution)/shard_map/ppermute | solution.py:46
  90.1 11.2 %collective-permute-start.22 = (bf16[256,1024]{1,0:T(8,128)(2,1)S(1)}, bf16[256,1024]{1,0:T(8,128)(2,1)S(1)}, u32[]{:S(2)}, u32[]{:S(2)}) collective-permute-start(bf16[256,1024]{1,0:T(8,128)(2,1)S(1)} %get-tuple-element.64), channel_id=1, source_target_pairs={{0,4},{4,0},{8,12},{12,8},{1,5},{5,1},{9,13},{13,9},{2,6},{6,2},{1... | collective-permute-start | bytes 1572872 | tf_op jit(solution)/shard_map/ppermute | solution.py:46
  90.6 12.5 %collective-permute-start.16 = (bf16[256,1024]{1,0:T(8,128)(2,1)S(1)}, bf16[256,1024]{1,0:T(8,128)(2,1)S(1)}, u32[]{:S(2)}, u32[]{:S(2)}) collective-permute-start(bf16[256,1024]{1,0:T(8,128)(2,1)S(1)} %fusion.29), channel_id=1, source_target_pairs={{0,3},{1,2},{2,1},{3,0},{4,7},{5,6},{6,5},{7,4},{8,11},{9,10},{10,... | collective-permute-start | bytes 1572872 | tf_op jit(solution)/shard_map/ppermute | solution.py:42
  91.0 18.5 %collective-permute-start.29 = (f32[64,1024]{1,0:T(8,128)S(1)}, f32[64,1024]{1,0:T(8,128)S(1)}, u32[]{:S(2)}, u32[]{:S(2)}) collective-permute-start(f32[64,1024]{1,0:T(8,128)S(1)} %maximum_select_fusion.3), channel_id=1, source_target_pairs={{0,32},{32,0},{64,96},{96,64},{1,33},{33,1},{65,97},{97,65},{2,34}... | collective-permute-start | bytes 786440 | tf_op jit(solution)/shard_map/ppermute | solution.py:106
  92.0 25.6 %collective-permute-start.12 = (bf16[512,512]{1,0:T(8,128)(2,1)S(1)}, bf16[512,512]{1,0:T(8,128)(2,1)S(1)}, u32[]{:S(2)}, u32[]{:S(2)}) collective-permute-start(bf16[512,512]{1,0:T(8,128)(2,1)S(1)} %get-tuple-element.54), channel_id=1, source_target_pairs={{0,1},{1,0},{2,3},{3,2},{4,5},{5,4},{6,7},{7,6},{8,9},{9,8},{10,11... | collective-permute-start | bytes 1572872 | tf_op jit(solution)/shard_map/ppermute | solution.py:38
  103.7 13.9 %collective-permute-start.23 = (bf16[256,1024]{1,0:T(8,128)(2,1)S(1)}, bf16[256,1024]{1,0:T(8,128)(2,1)S(1)}, u32[]{:S(2)}, u32[]{:S(2)}) collective-permute-start(bf16[256,1024]{1,0:T(8,128)(2,1)S(1)} %get-tuple-element.65), channel_id=1, source_target_pairs={{0,4},{4,0},{8,12},{12,8},{1,5},{5,1},{9,13},{13,9},{2,6},{6,2},{1... | collective-permute-start | bytes 1572872 | tf_op jit(solution)/shard_map/ppermute | solution.py:46
  104.9 12.7 %collective-permute-start.24 = (bf16[256,1024]{1,0:T(8,128)(2,1)S(1)}, bf16[256,1024]{1,0:T(8,128)(2,1)S(1)}, u32[]{:S(2)}, u32[]{:S(2)}) collective-permute-start(bf16[256,1024]{1,0:T(8,128)(2,1)S(1)} %add_convert_fusion.3), channel_id=1, source_target_pairs={{4,8},{8,4},{5,9},{9,5},{6,10},{10,6},{7,11},{11,7},{20,24},{24,20... | collective-permute-start | bytes 1572872 | tf_op jit(solution)/shard_map/ppermute | solution.py:46
  119.8 12.4 %collective-permute-start.30 = (bf16[512,1024]{1,0:T(8,128)(2,1)S(1)}, bf16[512,1024]{1,0:T(8,128)(2,1)S(1)}, u32[]{:S(2)}, u32[]{:S(2)}) collective-permute-start(bf16[512,1024]{1,0:T(8,128)(2,1)S(1)} %get-tuple-element.97), channel_id=1, source_target_pairs={{0,16},{16,0},{1,17},{17,1},{2,18},{18,2},{3,19},{19,3},{4,20},{20... | collective-permute-start | bytes 3145736 | tf_op jit(solution)/shard_map/ppermute | solution.py:34
  126.0 14.8 %collective-permute-start.32 = (bf16[256,1024]{1,0:T(8,128)(2,1)S(1)}, bf16[256,1024]{1,0:T(8,128)(2,1)S(1)}, u32[]{:S(2)}, u32[]{:S(2)}) collective-permute-start(bf16[256,1024]{1,0:T(8,128)(2,1)S(1)} %fusion.21), channel_id=1, source_target_pairs={{0,3},{1,2},{2,1},{3,0},{4,7},{5,6},{6,5},{7,4},{8,11},{9,10},{10,... | collective-permute-start | bytes 1572872 | tf_op jit(solution)/shard_map/ppermute | solution.py:42
  126.2 14.6 %collective-permute-start.34 = (bf16[256,1024]{1,0:T(8,128)(2,1)S(1)}, bf16[256,1024]{1,0:T(8,128)(2,1)S(1)}, u32[]{:S(2)}, u32[]{:S(2)}) collective-permute-start(bf16[256,1024]{1,0:T(8,128)(2,1)S(1)} %add_convert_fusion.1), channel_id=1, source_target_pairs={{4,8},{8,4},{5,9},{9,5},{6,10},{10,6},{7,11},{11,7},{20,24},{24,20... | collective-permute-start | bytes 1572872 | tf_op jit(solution)/shard_map/ppermute | solution.py:46
  127.1 16.0 %collective-permute-start.33 = (bf16[256,1024]{1,0:T(8,128)(2,1)S(1)}, bf16[256,1024]{1,0:T(8,128)(2,1)S(1)}, u32[]{:S(2)}, u32[]{:S(2)}) collective-permute-start(bf16[256,1024]{1,0:T(8,128)(2,1)S(1)} %add_convert_fusion.2), channel_id=1, source_target_pairs={{0,4},{4,0},{8,12},{12,8},{1,5},{5,1},{9,13},{13,9},{2,6},{6,2},{1... | collective-permute-start | bytes 1572872 | tf_op jit(solution)/shard_map/ppermute | solution.py:46
  131.4 14.5 %collective-permute-start.36 = (f32[128,1024]{1,0:T(8,128)S(1)}, f32[128,1024]{1,0:T(8,128)S(1)}, u32[]{:S(2)}, u32[]{:S(2)}) collective-permute-start(f32[128,1024]{1,0:T(8,128)S(1)} %maximum_select_fusion.2), channel_id=1, source_target_pairs={{0,16},{16,0},{1,17},{17,1},{2,18},{18,2},{3,19},{19,3},{4,20},{20... | collective-permute-start | bytes 1572872 | tf_op jit(solution)/shard_map/ppermute | solution.py:106
  133.4 24.2 %collective-permute-start.31 = (bf16[512,1024]{1,0:T(8,128)(2,1)S(1)}, bf16[512,1024]{1,0:T(8,128)(2,1)S(1)}, u32[]{:S(2)}, u32[]{:S(2)}) collective-permute-start(bf16[512,1024]{1,0:T(8,128)(2,1)S(1)} %add_convert_fusion), channel_id=1, source_target_pairs={{1,16},{2,19},{16,1},{19,2},{5,20},{6,23},{20,5},{23,6},{9,24},{10... | collective-permute-start | bytes 3145736 | tf_op jit(solution)/shard_map/ppermute | solution.py:30
  143.8 11.5 %collective-permute-start.35 = (bf16[256,1024]{1,0:T(8,128)(2,1)S(1)}, bf16[256,1024]{1,0:T(8,128)(2,1)S(1)}, u32[]{:S(2)}, u32[]{:S(2)}) collective-permute-start(bf16[256,1024]{1,0:T(8,128)(2,1)S(1)} %get-tuple-element.99), channel_id=1, source_target_pairs={{1,16},{2,19},{16,1},{19,2},{5,20},{6,23},{20,5},{23,6},{9,24},{10... | collective-permute-start | bytes 1572872 | tf_op jit(solution)/shard_map/ppermute | solution.py:30
  (12 other events, 118.8 us)

commit v8 on v3

--- a/solution.py
+++ b/solution.py
@@ -58,6 +58,10 @@
     return lax.optimization_barrier(arrays)
 
 
+def after(array, *earlier):
+    return together(array, *earlier)[0]
+
+
 def move(_, a, b, to_a, to_b):
     to_a[0] = a[...]
     to_b[0] = b[...]
@@ -66,17 +70,18 @@
 def halves(tokens, blocks):
     spec = lambda i: pl.BlockSpec((512, 256), lambda n, table: (0, table[i, n]))
     out = pl.BlockSpec((1, 512, 256), lambda n, table: (n // 2, 0, n % 2))
-    kind = jax.ShapeDtypeStruct((4, 512, 512), bf16)
+    steps = blocks.shape[1]
+    kind = jax.ShapeDtypeStruct((steps // 2, 512, 512), bf16)
     return pl.pallas_call(
         move,
         grid_spec=pltpu.PrefetchScalarGridSpec(
             num_scalar_prefetch=1,
-            grid=(8,),
+            grid=(steps,),
             in_specs=[spec(0), spec(1)],
             out_specs=[out, out],
         ),
         out_shape=[kind, kind],
-        cost_estimate=pl.CostEstimate(flops=0, bytes_accessed=16 << 20, transcendentals=0),
+        cost_estimate=pl.CostEstimate(flops=0, bytes_accessed=0, transcendentals=0),
     )(blocks, tokens, tokens)
 
 
@@ -132,31 +137,44 @@
         [4 * order[k] + q for half in (theirs, mine) for k in range(4) for q in (half, 3 - half)]
     ).reshape(2, 8)
 
-    w = jnp.where(stays, weight, swap(weight))
-    g_sib = core(key_grad)
-    x_give, x_own = halves(tokens, blocks.astype(jnp.int32))
-    x_sib = core(x_give)
-    drift = Drift(anchor - local_params[0].astype(f32), c, y)
+    w = swap(weight)
+    g_mine = lax.dynamic_slice_in_dim(key_grad, c * 256, 256, 0)
+    g_first = core(lax.dynamic_slice_in_dim(key_grad, (1 - c) * 256, 256, 0))
+    g_l = jnp.where(stays, g_first, g_mine)
+    g_half0 = beside(g_l[:128])
+    blocks = blocks.astype(jnp.int32)
+    w, g_half0, blocks = together(w, g_half0, blocks)
+    w = jnp.where(stays, weight, w)
+    drift = Drift(after(anchor - local_params[0].astype(f32), g_l), c, y)
     drift.take(drift.send())
-    g_a = jnp.where(stays, key_grad, g_sib)
-    g_l = lax.dynamic_slice_in_dim(jnp.where(stays, g_sib, key_grad), c * 256, 256, 0)
-
-    got = (beside(g_l), line(w, PAIRS), line(w, MIDDLE), across(w), drift.send())
-    leave = [jnp.where(stays, x_sib[k], x_own[k]) for k in range(4)]
-    keep = [jnp.where(stays, x_own[k], x_sib[k]) for k in range(4)]
-    got, leave, drift.v = together(got, leave, drift.v)
+
+    give0, own0 = halves(tokens, blocks[:, :2])
+    sib0 = core(give0)
+    give, own = halves(tokens, after(blocks[:, 2:], sib0))
+    drift.take(drift.send())
+    got = (beside(g_l[128:]), line(w, PAIRS), line(w, MIDDLE), across(w), drift.send())
+    leave = [jnp.where(stays, sib0[0], own0[0])]
+    keep = [jnp.where(stays, own0[0], sib0[0])]
+    sib = core(give)
+    got, leave, sib, own, g_mine, drift.v = together(got, leave, sib, own, g_mine, drift.v)
     g_half, e_own, m_own, q_own, d = got
-    drift.take(d)
-
-    got = (beside(leave[0]), line(m_own, ENDS_OUT), line(e_own, MIDDLE), across(e_own), drift.send())
-    g_rest = core(g_half)
-    g_b = jnp.where(
-        c == 0, jnp.concatenate([g_half, g_rest]), jnp.concatenate([g_rest, g_half])
-    )
+    g_half = jnp.concatenate([g_half0, g_half])
+    drift.take(d)
+
+    got = (beside(leave[0]), line(m_own, ENDS_OUT), line(e_own, MIDDLE), across(e_own))
+    leave += [jnp.where(stays, sib[k], own[k]) for k in range(3)]
+    keep += [jnp.where(stays, own[k], sib[k]) for k in range(3)]
+    rest = core(jnp.concatenate([g_half, g_mine]))
+
+    def in_order(a, b):
+        return jnp.where(c == 0, jnp.concatenate([a, b]), jnp.concatenate([b, a]))
+
+    g_b = in_order(g_half, rest[:256])
+    g_a = jnp.where(stays, key_grad, in_order(g_first, rest[256:]))
     base = [dot_t(k, g_a) for k in keep]
-    sent = drift.v
-    got, leave, sent, g_b, base = together(got, leave, sent, g_b, base)
-    drift.v = sent
+    drift.v = after(drift.v, g_b)
+    got += (drift.send(),)
+    got, leave, drift.sent, g_b, base = together(got, leave, drift.sent, g_b, base)
     x_b = [got[0]]
     _, e2, m2, q2, d = got
     drift.take(d)
@@ -175,7 +193,7 @@
     rows = [None, None, jnp.concatenate([e_own, q2]), jnp.concatenate([w, q_own])]
     k_a = dot(cat(keep[2], keep[3]), jnp.concatenate(rows[2:]))
     stay = staying(0)
-    got, leave, drift.v, drift.sent, stay, k_a = together(got, leave, drift.v, drift.sent, stay, k_a)
+    got, leave, drift.v, stay, k_a = together(got, leave, drift.v, stay, k_a)
     x_b.append(got[0])
     _, e3, m3, q3, d = got
     drift.take(d)
@@ -226,8 +244,6 @@
     e6, m6, q6 = got
     total = staying(3) + q6.astype(f32) + e6.astype(f32) + m6.astype(f32)
     gradient = jnp.where(stays, total, swap(total.astype(bf16)).astype(f32))
-    drift.take(drift.send())
-
     new_first = first_decay * adam_first[0] + (1.0 - first_decay) * gradient
     new_second = second_decay * adam_second[0] + (1.0 - second_decay) * gradient * gradient
     master = weight.astype(f32)

time: 159 us -> 177 us (1.11)
  waiting for transfers between devices: 56.8 us -> 63.8 us
  local copies, waits for them, and re-layouts: 1.65 us -> 6.24 us
  matrix products: 12 us -> 14.1 us
    ppermute x12, waiting for transfers between devices: 11.2 us -> 17.4 us  [line(): return lax.ppermute(v, 'zl', pairs)]
    ppermute x7, starting transfers between devices: 14.5 us -> 18.5 us  [send(): return lax.ppermute(self.sent, axis, perm)]
    ppermute x7, waiting for transfers between devices: 8.57 us -> 4.69 us  [send(): return lax.ppermute(self.sent, axis, perm)]
    ppermute x12, starting transfers between devices: 18.5 us -> 14.7 us  [line(): return lax.ppermute(v, 'zl', pairs)]
    unnamed x10 -> x54, local copies, waits for them, and re-layouts: 0.03 us -> 2.79 us
    ppermute x6, waiting for transfers between devices: 19.2 us -> 21.8 us  [across(): return lax.ppermute(v, 'x', ACROSS)]
    select_n x5 -> x6, other arithmetic: 4.96 us -> 7.54 us  [the longest x1 2.26 us: on_device(): g_l = jnp.where(stays, g_first, g_mine)]
    pallas_call x1 -> x2, Pallas kernels: 7.37 us -> 8.93 us  [halves(): pl.pallas_call(move, grid_spec=pltpu.PrefetchScalarGridSpec(num_scalar_pr...]
  transfers between devices with their start and end apart: 37 -> 39, of which waited for: 15 -> 18; matrix products, arithmetic and copies ran while one was open for 17% -> 17% of each run, Pallas kernels for 0% -> 3%
where the time goes in v8:
time: 177 us; the launch traced here: 176 us
  waiting for transfers between devices  63.8 us (36%)
  starting transfers between devices  62.7 us (35%)
  other arithmetic  18.7 us (11%)
  matrix products  14.1 us (8%)
  Pallas kernels  8.93 us (5%)
  local copies, waits for them, and re-layouts  6.24 us (4%)
    ppermute x6, waiting for transfers between devices, across(): return lax.ppermute(v, 'x', ACROSS)  21.8 us
    ppermute x7, starting transfers between devices, send(): return lax.ppermute(self.sent, axis, perm)  18.5 us
    ppermute x12, waiting for transfers between devices, line(): return lax.ppermute(v, 'zl', pairs)  17.4 us
    ppermute x12, starting transfers between devices, line(): return lax.ppermute(v, 'zl', pairs)  14.7 us
    ppermute x3, waiting for transfers between devices, swap(): return lax.ppermute(v, ('c', 'x'), SWAP)  13.9 us
    ppermute x5, starting transfers between devices, core(): return lax.ppermute(v, 'c', CORE)  10 us
    ppermute x3, starting transfers between devices, swap(): return lax.ppermute(v, ('c', 'x'), SWAP)  9.44 us
    pallas_call x2, Pallas kernels, halves(): pl.pallas_call(move, grid_spec=pltpu.PrefetchScalarGridSpec(num_scalar_pr...  8.93 us
  transfers between devices with their start and end apart: 39, of which 18 were waited for; matrix products, arithmetic and copies ran while one was open for 17% of the time, Pallas kernels for 3%

profile of v8, /device:TPU:1, one launch (start us, length us, event | category | flops | bytes accessed | tf_op | source)
XLA Modules:
  0.0 175.8 jit_solution(10593837339629415286)
XLA Ops:
  1.7 3.3 %collective-permute-start = (bf16[256,1024]{1,0:T(8,128)(2,1)S(1)}, bf16[256,1024]{1,0:T(8,128)(2,1)S(1)}, u32[]{:S(2)}, u32[]{:S(2)}) collective-permute-start(bf16[256,1024]{1,0:T(8,128)(2,1)S(1)} %constant_dynamic-slice_fusion.4), channel_id=1, source_target_pairs={{0,16},{16,0},{1,17},{17,1},{2,18},{18,2},{3,19},{19,3},{4,20},{20... | collective-permute-start | bytes 1572872 | tf_op jit(solution)/shard_map/ppermute | solution.py:34
  5.1 1.9 %collective-permute-start.2 = (bf16[256,1024]{1,0:T(8,128)(2,1)}, bf16[256,1024]{1,0:T(8,128)(2,1)S(1)}, u32[]{:S(2)}, u32[]{:S(2)}) collective-permute-start(bf16[256,1024]{1,0:T(8,128)(2,1)} %bitcast.77), channel_id=1, source_target_pairs={{1,16},{2,19},{16,1},{19,2},{5,20},{6,23},{20,5},{23,6},{9,24},{10... | collective-permute-start | bytes 1572872 | tf_op jit(solution)/shard_map/ppermute | solution.py:30
  7.0 2.3 %broadcast_select_fusion.8 = (bf16[256,1024]{1,0:T(8,128)(2,1)S(1)}, bf16[256,1024]{1,0:T(8,128)(2,1)}) fusion(bf16[256,1024]{1,0:T(8,128)(2,1)S(1)} %collective-permute-done, pred[]{:T(512)S(6)} %eq.37, bf16[512,1024]{1,0:T(8,128)(2,1)} %param.9, s32[]{:T(128)S(6)} %select_n.223), kind=kLoop, calls=%fused_computation.95 | loop fusion | flops 262144 | bytes 2097157 | tf_op jit(solution)/shard_map/jit(_where)/select_n | solution.py:143
  10.2 8.3 %collective-permute-done.2 = bf16[256,1024]{1,0:T(8,128)(2,1)S(1)} collective-permute-done((bf16[256,1024]{1,0:T(8,128)(2,1)}, bf16[256,1024]{1,0:T(8,128)(2,1)S(1)}, u32[]{:S(2)}, u32[]{:S(2)}) %collective-permute-start.2) | collective-permute-done | bytes 524320 | tf_op jit(solution)/shard_map/ppermute | solution.py:30
  19.6 2.9 %shard_map.127 = (bf16[1,512,512]{2,1,0:T(8,128)(2,1)}, bf16[1,512,512]{2,1,0:T(8,128)(2,1)}) custom-call(s32[2,2]{1,0:T(2,128)} %bitcast.78, bf16[512,4096]{1,0:T(8,128)(2,1)} %b.3, bf16[512,4096]{1,0:T(8,128)(2,1)} %b.3), custom_call_target="tpu_custom_call" | custom-call | tf_op jit(solution)/shard_map/pallas_call | solution.py:75
  22.5 3.2 %collective-permute-start.10 = (bf16[1,512,512]{2,1,0:T(8,128)(2,1)}, bf16[1,512,512]{2,1,0:T(8,128)(2,1)S(1)}, u32[]{:S(2)}, u32[]{:S(2)}) collective-permute-start(bf16[1,512,512]{2,1,0:T(8,128)(2,1)} %get-tuple-element.72), channel_id=1, source_target_pairs={{0,16},{16,0},{1,17},{17,1},{2,18},{18,2},{3,19},{19,3},{4,20},{20... | collective-permute-start | bytes 1572872 | tf_op jit(solution)/shard_map/ppermute | solution.py:34
  27.5 6.0 %shard_map.128 = (bf16[3,512,512]{2,1,0:T(8,128)(2,1)}, bf16[3,512,512]{2,1,0:T(8,128)(2,1)}) custom-call(s32[2,6]{1,0:T(2,128)} %slice.93._, bf16[512,4096]{1,0:T(8,128)(2,1)} %b.3, bf16[512,4096]{1,0:T(8,128)(2,1)} %b.3), custom_call_target="tpu_custom_call" | custom-call | tf_op jit(solution)/shard_map/pallas_call | solution.py:75
  36.6 2.0 %collective-permute-start.6 = (bf16[256,1024]{1,0:T(8,128)(2,1)S(1)}, bf16[256,1024]{1,0:T(8,128)(2,1)S(1)}, u32[]{:S(2)}, u32[]{:S(2)}) collective-permute-start(bf16[256,1024]{1,0:T(8,128)(2,1)S(1)} %broadcast_select_fusion.7), channel_id=1, source_target_pairs={{0,3},{1,2},{2,1},{3,0},{4,7},{5,6},{6,5},{7,4},{8,11},{9,10},{10,... | collective-permute-start | bytes 1572872 | tf_op jit(solution)/shard_map/ppermute | solution.py:42
  39.3 3.7 %collective-permute-done.8 = f32[64,1024]{1,0:T(8,128)S(1)} collective-permute-done((f32[64,1024]{1,0:T(8,128)S(1)}, f32[64,1024]{1,0:T(8,128)S(1)}, u32[]{:S(2)}, u32[]{:S(2)}) %collective-permute-start.8) | collective-permute-done | bytes 262176 | tf_op jit(solution)/shard_map/ppermute | solution.py:106
  44.0 2.7 %collective-permute-start.9 = (f32[32,1024]{1,0:T(8,128)S(1)}, f32[32,1024]{1,0:T(8,128)S(1)}, u32[]{:S(2)}, u32[]{:S(2)}) collective-permute-start(f32[32,1024]{1,0:T(8,128)S(1)} %constant_dynamic-slice_fusion), channel_id=1, source_target_pairs={{0,64},{32,96},{64,0},{96,32},{1,65},{33,97},{65,1},{97,33},{2,66}... | collective-permute-start | bytes 393224 | tf_op jit(solution)/shard_map/ppermute | solution.py:106
  47.5 3.7 %collective-permute-done.6 = bf16[256,1024]{1,0:T(8,128)(2,1)S(1)} collective-permute-done((bf16[256,1024]{1,0:T(8,128)(2,1)S(1)}, bf16[256,1024]{1,0:T(8,128)(2,1)S(1)}, u32[]{:S(2)}, u32[]{:S(2)}) %collective-permute-start.6) | collective-permute-done | bytes 524320 | tf_op jit(solution)/shard_map/ppermute | solution.py:42
  51.2 4.2 %collective-permute-done.4 = bf16[256,1024]{1,0:T(8,128)(2,1)S(1)} collective-permute-done((bf16[256,1024]{1,0:T(8,128)(2,1)S(1)}, bf16[256,1024]{1,0:T(8,128)(2,1)S(1)}, u32[]{:S(2)}, u32[]{:S(2)}) %collective-permute-start.4) | collective-permute-done | bytes 524320 | tf_op jit(solution)/shard_map/ppermute | solution.py:46
  57.3 1.9 %collective-permute-start.16 = (bf16[512,1024]{1,0:T(8,128)(2,1)}, bf16[512,1024]{1,0:T(8,128)(2,1)S(1)}, u32[]{:S(2)}, u32[]{:S(2)}) collective-permute-start(bf16[512,1024]{1,0:T(8,128)(2,1)} %pad_maximum_fusion.6), channel_id=1, source_target_pairs={{0,16},{16,0},{1,17},{17,1},{2,18},{18,2},{3,19},{19,3},{4,20},{20... | collective-permute-start | bytes 3145736 | tf_op jit(solution)/shard_map/ppermute | solution.py:34
  62.7 2.0 %select_bitcast_fusion = (bf16[512,512]{1,0:T(8,128)(2,1)S(1)}, bf16[512,512]{1,0:T(8,128)(2,1)S(1)}, bf16[512,512]{1,0:T(8,128)(2,1)S(1)}, bf16[512,512]{1,0:T(8,128)(2,1)S(1)}, bf16[512,512]{1,0:T(8,128)(2,1)S(1)}) fusion(pred[]{:T(512)S(6)} %eq.37, bf16[3,512,512]{2,1,0:T(8,128)(2,1)} %get-tuple-element.87, bf16[3,512,512]{2,1,0:T(8,128)(2,1)} %collective-permute-done.11), kind=kLoop, calls=%fused_computation.81 | loop fusion | flops 1310720 | bytes 5767169 | tf_op jit(solution)/shard_map/jit(_where)/select_n | solution.py:166
  66.2 7.0 %collective-permute-start.17 = (bf16[32,1024]{1,0:T(8,128)(2,1)S(1)}, bf16[32,1024]{1,0:T(8,128)(2,1)S(1)}, u32[]{:S(2)}, u32[]{:S(2)}) collective-permute-start(bf16[32,1024]{1,0:T(8,128)(2,1)S(1)} %dynamic-slice_add_fusion.2), channel_id=1, source_target_pairs={{0,128},{128,0},{1,129},{129,1},{2,130},{130,2},{3,131},{131,3},{4... | collective-permute-start | bytes 196616 | tf_op jit(solution)/shard_map/ppermute | solution.py:106
  73.9 1.8 %fusion.40 = f32[512,1024]{1,0:T(8,128)S(1)} fusion(bf16[512,1024]{1,0:T(8,128)(2,1)S(1)} %fusion.20, pred[]{:T(512)S(6)} %eq.37, bf16[3,512,512]{2,1,0:T(8,128)(2,1)S(1)} %copy-done.3, bf16[3,512,512]{2,1,0:T(8,128)(2,1)} %collective-permute-done.11), kind=kOutput, calls=%fused_computation.74 | convolution fusion | flops 537133056 | bytes 4194305 | tf_op jit(solution)/shard_map/dot_general | solution.py:54
  81.2 3.0 %collective-permute-start.22 = (f32[32,1024]{1,0:T(8,128)S(1)}, f32[32,1024]{1,0:T(8,128)S(1)}, u32[]{:S(2)}, u32[]{:S(2)}) collective-permute-start(f32[32,1024]{1,0:T(8,128)S(1)} %convert_add_fusion.3), channel_id=1, source_target_pairs={{0,64},{32,96},{64,0},{96,32},{1,65},{33,97},{65,1},{97,33},{2,66}... | collective-permute-start | bytes 393224 | tf_op jit(solution)/shard_map/ppermute | solution.py:106
  88.6 7.9 %collective-permute-done.21 = bf16[256,1024]{1,0:T(8,128)(2,1)S(1)} collective-permute-done((bf16[256,1024]{1,0:T(8,128)(2,1)S(1)}, bf16[256,1024]{1,0:T(8,128)(2,1)S(1)}, u32[]{:S(2)}, u32[]{:S(2)}) %collective-permute-start.21) | collective-permute-done | bytes 524320 | tf_op jit(solution)/shard_map/ppermute | solution.py:42
  96.4 5.9 %collective-permute-done.19 = bf16[256,1024]{1,0:T(8,128)(2,1)S(1)} collective-permute-done((bf16[256,1024]{1,0:T(8,128)(2,1)S(1)}, bf16[256,1024]{1,0:T(8,128)(2,1)S(1)}, u32[]{:S(2)}, u32[]{:S(2)}) %collective-permute-start.19) | collective-permute-done | bytes 524320 | tf_op jit(solution)/shard_map/ppermute | solution.py:46
  103.3 1.9 %collective-permute-start.26 = (bf16[256,1024]{1,0:T(8,128)(2,1)S(1)}, bf16[256,1024]{1,0:T(8,128)(2,1)S(1)}, u32[]{:S(2)}, u32[]{:S(2)}) collective-permute-start(bf16[256,1024]{1,0:T(8,128)(2,1)S(1)} %add_convert_fusion.6), channel_id=1, source_target_pairs={{0,3},{1,2},{2,1},{3,0},{4,7},{5,6},{6,5},{7,4},{8,11},{9,10},{10,... | collective-permute-start | bytes 1572872 | tf_op jit(solution)/shard_map/ppermute | solution.py:42
  107.7 7.1 %collective-permute-done.26 = bf16[256,1024]{1,0:T(8,128)(2,1)S(1)} collective-permute-done((bf16[256,1024]{1,0:T(8,128)(2,1)S(1)}, bf16[256,1024]{1,0:T(8,128)(2,1)S(1)}, u32[]{:S(2)}, u32[]{:S(2)}) %collective-permute-start.26) | collective-permute-done | bytes 524320 | tf_op jit(solution)/shard_map/ppermute | solution.py:42
  118.0 5.2 %collective-permute-start.32 = (f32[128,1024]{1,0:T(8,128)S(1)}, f32[128,1024]{1,0:T(8,128)S(1)}, u32[]{:S(2)}, u32[]{:S(2)}) collective-permute-start(f32[128,1024]{1,0:T(8,128)S(1)} %maximum_select_fusion.3), channel_id=1, source_target_pairs={{0,16},{16,0},{1,17},{17,1},{2,18},{18,2},{3,19},{19,3},{4,20},{20... | collective-permute-start | bytes 1572872 | tf_op jit(solution)/shard_map/ppermute | solution.py:106
  123.4 3.5 %collective-permute-start.29 = (bf16[256,1024]{1,0:T(8,128)(2,1)S(1)}, bf16[256,1024]{1,0:T(8,128)(2,1)S(1)}, u32[]{:S(2)}, u32[]{:S(2)}) collective-permute-start(bf16[256,1024]{1,0:T(8,128)(2,1)S(1)} %get-tuple-element.136), channel_id=1, source_target_pairs={{0,4},{4,0},{8,12},{12,8},{1,5},{5,1},{9,13},{13,9},{2,6},{6,2},{1... | collective-permute-start | bytes 1572872 | tf_op jit(solution)/shard_map/ppermute | solution.py:46
  131.1 5.3 %collective-permute-done.28 = bf16[512,512]{1,0:T(8,128)(2,1)S(1)} collective-permute-done((bf16[512,512]{1,0:T(8,128)(2,1)S(1)}, bf16[512,512]{1,0:T(8,128)(2,1)S(1)}, u32[]{:S(2)}, u32[]{:S(2)}) %collective-permute-start.28) | collective-permute-done | bytes 524320 | tf_op jit(solution)/shard_map/ppermute | solution.py:38
  136.3 2.4 %collective-permute-done.29 = bf16[256,1024]{1,0:T(8,128)(2,1)S(1)} collective-permute-done((bf16[256,1024]{1,0:T(8,128)(2,1)S(1)}, bf16[256,1024]{1,0:T(8,128)(2,1)S(1)}, u32[]{:S(2)}, u32[]{:S(2)}) %collective-permute-start.29) | collective-permute-done | bytes 524320 | tf_op jit(solution)/shard_map/ppermute | solution.py:46
  145.4 3.5 %collective-permute-start.36 = (bf16[256,1024]{1,0:T(8,128)(2,1)S(1)}, bf16[256,1024]{1,0:T(8,128)(2,1)S(1)}, u32[]{:S(2)}, u32[]{:S(2)}) collective-permute-start(bf16[256,1024]{1,0:T(8,128)(2,1)S(1)} %add_convert_fusion.2), channel_id=1, source_target_pairs={{0,4},{4,0},{8,12},{12,8},{1,5},{5,1},{9,13},{13,9},{2,6},{6,2},{1... | collective-permute-start | bytes 1572872 | tf_op jit(solution)/shard_map/ppermute | solution.py:46
  150.5 3.6 %collective-permute-start.34 = (bf16[512,1024]{1,0:T(8,128)(2,1)S(1)}, bf16[512,1024]{1,0:T(8,128)(2,1)S(1)}, u32[]{:S(2)}, u32[]{:S(2)}) collective-permute-start(bf16[512,1024]{1,0:T(8,128)(2,1)S(1)} %add_convert_fusion), channel_id=1, source_target_pairs={{1,16},{2,19},{16,1},{19,2},{5,20},{6,23},{20,5},{23,6},{9,24},{10... | collective-permute-start | bytes 3145736 | tf_op jit(solution)/shard_map/ppermute | solution.py:30
  154.2 3.2 %collective-permute-done.35 = bf16[256,1024]{1,0:T(8,128)(2,1)S(1)} collective-permute-done((bf16[256,1024]{1,0:T(8,128)(2,1)S(1)}, bf16[256,1024]{1,0:T(8,128)(2,1)S(1)}, u32[]{:S(2)}, u32[]{:S(2)}) %collective-permute-start.35) | collective-permute-done | bytes 524320 | tf_op jit(solution)/shard_map/ppermute | solution.py:42
  157.4 3.2 %collective-permute-done.36 = bf16[256,1024]{1,0:T(8,128)(2,1)S(1)} collective-permute-done((bf16[256,1024]{1,0:T(8,128)(2,1)S(1)}, bf16[256,1024]{1,0:T(8,128)(2,1)S(1)}, u32[]{:S(2)}, u32[]{:S(2)}) %collective-permute-start.36) | collective-permute-done | bytes 524320 | tf_op jit(solution)/shard_map/ppermute | solution.py:46
  161.2 3.9 %collective-permute-start.38 = (bf16[256,1024]{1,0:T(8,128)(2,1)S(1)}, bf16[256,1024]{1,0:T(8,128)(2,1)S(1)}, u32[]{:S(2)}, u32[]{:S(2)}) collective-permute-start(bf16[256,1024]{1,0:T(8,128)(2,1)S(1)} %get-tuple-element.134), channel_id=1, source_target_pairs={{1,16},{2,19},{16,1},{19,2},{5,20},{6,23},{20,5},{23,6},{9,24},{10... | collective-permute-start | bytes 1572872 | tf_op jit(solution)/shard_map/ppermute | solution.py:30
  166.8 5.6 %collective-permute-done.38 = bf16[256,1024]{1,0:T(8,128)(2,1)S(1)} collective-permute-done((bf16[256,1024]{1,0:T(8,128)(2,1)S(1)}, bf16[256,1024]{1,0:T(8,128)(2,1)S(1)}, u32[]{:S(2)}, u32[]{:S(2)}) %collective-permute-start.38) | collective-permute-done | bytes 524320 | tf_op jit(solution)/shard_map/ppermute | solution.py:30
  172.4 2.3 %fusion.82 = (f32[1,256,1024]{2,1,0:T(8,128)}, bf16[1,256,1024]{2,1,0:T(8,128)(2,1)}, f32[1,256,1024]{2,1,0:T(8,128)}) fusion(f32[256,1024]{1,0:T(8,128)S(1)} %get-tuple-element.135, bf16[256,1024]{1,0:T(8,128)(2,1)S(1)} %collective-permute-done.38, pred[]{:T(512)S(6)} %eq.37, f32[1,256,1024]{2,1,0:T(8,128)S(1)} %copy-done.9, ...), kind=kLoop, calls=%fused_computation.128 | loop fusion | flops 4456448 | bytes 6815745 | tf_op jit(solution)/shard_map/broadcast_in_dim | solution.py:256
  (157 shorter events, 49.9 us)
Async XLA Ops:
  5.1 13.5 %collective-permute-start.2 = (bf16[256,1024]{1,0:T(8,128)(2,1)}, bf16[256,1024]{1,0:T(8,128)(2,1)S(1)}, u32[]{:S(2)}, u32[]{:S(2)}) collective-permute-start(bf16[256,1024]{1,0:T(8,128)(2,1)} %bitcast.77), channel_id=1, source_target_pairs={{1,16},{2,19},{16,1},{19,2},{5,20},{6,23},{20,5},{23,6},{9,24},{10... | collective-permute-start | bytes 1572872 | tf_op jit(solution)/shard_map/ppermute | solution.py:30
  9.3 9.6 %collective-permute-start.3 = (bf16[128,1024]{1,0:T(8,128)(2,1)S(1)}, bf16[128,1024]{1,0:T(8,128)(2,1)S(1)}, u32[]{:S(2)}, u32[]{:S(2)}) collective-permute-start(bf16[128,1024]{1,0:T(8,128)(2,1)S(1)} %get-tuple-element.152), channel_id=1, source_target_pairs={{0,1},{1,0},{2,3},{3,2},{4,5},{5,4},{6,7},{7,6},{8,9},{9,8},{10,11... | collective-permute-start | bytes 786440 | tf_op jit(solution)/shard_map/ppermute | solution.py:38
  33.5 22.7 %collective-permute-start.11 = (bf16[3,512,512]{2,1,0:T(8,128)(2,1)}, bf16[3,512,512]{2,1,0:T(8,128)(2,1)}, u32[]{:S(2)}, u32[]{:S(2)}) collective-permute-start(bf16[3,512,512]{2,1,0:T(8,128)(2,1)} %get-tuple-element.75), channel_id=1, source_target_pairs={{0,16},{16,0},{1,17},{17,1},{2,18},{18,2},{3,19},{19,3},{4,20},{20... | collective-permute-start | bytes 4718600 | tf_op jit(solution)/shard_map/ppermute | solution.py:34
  33.9 10.1 %collective-permute-start.1 = (bf16[128,1024]{1,0:T(8,128)(2,1)S(1)}, bf16[128,1024]{1,0:T(8,128)(2,1)S(1)}, u32[]{:S(2)}, u32[]{:S(2)}) collective-permute-start(bf16[128,1024]{1,0:T(8,128)(2,1)S(1)} %get-tuple-element.153), channel_id=1, source_target_pairs={{0,1},{1,0},{2,3},{3,2},{4,5},{5,4},{6,7},{7,6},{8,9},{9,8},{10,11... | collective-permute-start | bytes 786440 | tf_op jit(solution)/shard_map/ppermute | solution.py:38
  36.6 14.7 %collective-permute-start.6 = (bf16[256,1024]{1,0:T(8,128)(2,1)S(1)}, bf16[256,1024]{1,0:T(8,128)(2,1)S(1)}, u32[]{:S(2)}, u32[]{:S(2)}) collective-permute-start(bf16[256,1024]{1,0:T(8,128)(2,1)S(1)} %broadcast_select_fusion.7), channel_id=1, source_target_pairs={{0,3},{1,2},{2,1},{3,0},{4,7},{5,6},{6,5},{7,4},{8,11},{9,10},{10,... | collective-permute-start | bytes 1572872 | tf_op jit(solution)/shard_map/ppermute | solution.py:42
  38.6 12.6 %collective-permute-start.5 = (bf16[256,1024]{1,0:T(8,128)(2,1)S(1)}, bf16[256,1024]{1,0:T(8,128)(2,1)S(1)}, u32[]{:S(2)}, u32[]{:S(2)}) collective-permute-start(bf16[256,1024]{1,0:T(8,128)(2,1)S(1)} %broadcast_select_fusion.7), channel_id=1, source_target_pairs={{4,8},{8,4},{5,9},{9,5},{6,10},{10,6},{7,11},{11,7},{20,24},{24,20... | collective-permute-start | bytes 1572872 | tf_op jit(solution)/shard_map/ppermute | solution.py:46
  43.0 12.5 %collective-permute-start.4 = (bf16[256,1024]{1,0:T(8,128)(2,1)S(1)}, bf16[256,1024]{1,0:T(8,128)(2,1)S(1)}, u32[]{:S(2)}, u32[]{:S(2)}) collective-permute-start(bf16[256,1024]{1,0:T(8,128)(2,1)S(1)} %broadcast_select_fusion.7), channel_id=1, source_target_pairs={{0,4},{4,0},{8,12},{12,8},{1,5},{5,1},{9,13},{13,9},{2,6},{6,2},{1... | collective-permute-start | bytes 1572872 | tf_op jit(solution)/shard_map/ppermute | solution.py:46
  44.0 11.5 %collective-permute-start.9 = (f32[32,1024]{1,0:T(8,128)S(1)}, f32[32,1024]{1,0:T(8,128)S(1)}, u32[]{:S(2)}, u32[]{:S(2)}) collective-permute-start(f32[32,1024]{1,0:T(8,128)S(1)} %constant_dynamic-slice_fusion), channel_id=1, source_target_pairs={{0,64},{32,96},{64,0},{96,32},{1,65},{33,97},{65,1},{97,33},{2,66}... | collective-permute-start | bytes 393224 | tf_op jit(solution)/shard_map/ppermute | solution.py:106
  59.2 21.0 %collective-permute-start.15 = (bf16[256,1024]{1,0:T(8,128)(2,1)}, bf16[256,1024]{1,0:T(8,128)(2,1)S(1)}, u32[]{:S(2)}, u32[]{:S(2)}) collective-permute-start(bf16[256,1024]{1,0:T(8,128)(2,1)} %copy-done.25), channel_id=1, source_target_pairs={{0,3},{1,2},{2,1},{3,0},{4,7},{5,6},{6,5},{7,4},{8,11},{9,10},{10,... | collective-permute-start | bytes 1572872 | tf_op jit(solution)/shard_map/ppermute | solution.py:42
  60.1 20.1 %collective-permute-start.14 = (bf16[256,1024]{1,0:T(8,128)(2,1)}, bf16[256,1024]{1,0:T(8,128)(2,1)S(1)}, u32[]{:S(2)}, u32[]{:S(2)}) collective-permute-start(bf16[256,1024]{1,0:T(8,128)(2,1)} %copy-done.25), channel_id=1, source_target_pairs={{4,8},{8,4},{5,9},{9,5},{6,10},{10,6},{7,11},{11,7},{20,24},{24,20... | collective-permute-start | bytes 1572872 | tf_op jit(solution)/shard_map/ppermute | solution.py:46
  60.8 17.1 %collective-permute-start.12 = (bf16[512,512]{1,0:T(8,128)(2,1)}, bf16[512,512]{1,0:T(8,128)(2,1)S(1)}, u32[]{:S(2)}, u32[]{:S(2)}) collective-permute-start(bf16[512,512]{1,0:T(8,128)(2,1)} %select_bitcast_fusion.5), channel_id=1, source_target_pairs={{0,1},{1,0},{2,3},{3,2},{4,5},{5,4},{6,7},{7,6},{8,9},{9,8},{10,11... | collective-permute-start | bytes 1572872 | tf_op jit(solution)/shard_map/ppermute | solution.py:38
  61.4 18.8 %collective-permute-start.13 = (bf16[256,1024]{1,0:T(8,128)(2,1)}, bf16[256,1024]{1,0:T(8,128)(2,1)S(1)}, u32[]{:S(2)}, u32[]{:S(2)}) collective-permute-start(bf16[256,1024]{1,0:T(8,128)(2,1)} %copy-done.20), channel_id=1, source_target_pairs={{4,0},{8,12},{5,1},{9,13},{6,2},{10,14},{7,3},{11,15},{20,16},{24,... | collective-permute-start | bytes 1572872 | tf_op jit(solution)/shard_map/ppermute | solution.py:46
  66.2 14.0 %collective-permute-start.17 = (bf16[32,1024]{1,0:T(8,128)(2,1)S(1)}, bf16[32,1024]{1,0:T(8,128)(2,1)S(1)}, u32[]{:S(2)}, u32[]{:S(2)}) collective-permute-start(bf16[32,1024]{1,0:T(8,128)(2,1)S(1)} %dynamic-slice_add_fusion.2), channel_id=1, source_target_pairs={{0,128},{128,0},{1,129},{129,1},{2,130},{130,2},{3,131},{131,3},{4... | collective-permute-start | bytes 196616 | tf_op jit(solution)/shard_map/ppermute | solution.py:106
  78.2 9.6 %collective-permute-start.20 = (bf16[256,1024]{1,0:T(8,128)(2,1)S(1)}, bf16[256,1024]{1,0:T(8,128)(2,1)S(1)}, u32[]{:S(2)}, u32[]{:S(2)}) collective-permute-start(bf16[256,1024]{1,0:T(8,128)(2,1)S(1)} %copy-done.24), channel_id=1, source_target_pairs={{4,8},{8,4},{5,9},{9,5},{6,10},{10,6},{7,11},{11,7},{20,24},{24,20... | collective-permute-start | bytes 1572872 | tf_op jit(solution)/shard_map/ppermute | solution.py:46
  84.2 12.2 %collective-permute-start.21 = (bf16[256,1024]{1,0:T(8,128)(2,1)S(1)}, bf16[256,1024]{1,0:T(8,128)(2,1)S(1)}, u32[]{:S(2)}, u32[]{:S(2)}) collective-permute-start(bf16[256,1024]{1,0:T(8,128)(2,1)S(1)} %add_convert_fusion.7), channel_id=1, source_target_pairs={{0,3},{1,2},{2,1},{3,0},{4,7},{5,6},{6,5},{7,4},{8,11},{9,10},{10,... | collective-permute-start | bytes 1572872 | tf_op jit(solution)/shard_map/ppermute | solution.py:42
  85.1 11.3 %collective-permute-start.18 = (bf16[512,512]{1,0:T(8,128)(2,1)S(1)}, bf16[512,512]{1,0:T(8,128)(2,1)S(1)}, u32[]{:S(2)}, u32[]{:S(2)}) collective-permute-start(bf16[512,512]{1,0:T(8,128)(2,1)S(1)} %get-tuple-element.88), channel_id=1, source_target_pairs={{0,1},{1,0},{2,3},{3,2},{4,5},{5,4},{6,7},{7,6},{8,9},{9,8},{10,11... | collective-permute-start | bytes 1572872 | tf_op jit(solution)/shard_map/ppermute | solution.py:38
  85.2 17.2 %collective-permute-start.19 = (bf16[256,1024]{1,0:T(8,128)(2,1)S(1)}, bf16[256,1024]{1,0:T(8,128)(2,1)S(1)}, u32[]{:S(2)}, u32[]{:S(2)}) collective-permute-start(bf16[256,1024]{1,0:T(8,128)(2,1)S(1)} %collective-permute-done.14), channel_id=1, source_target_pairs={{4,0},{8,12},{5,1},{9,13},{6,2},{10,14},{7,3},{11,15},{20,16},{24,... | collective-permute-start | bytes 1572872 | tf_op jit(solution)/shard_map/ppermute | solution.py:46
  87.9 18.8 %collective-permute-start.25 = (bf16[256,1024]{1,0:T(8,128)(2,1)S(1)}, bf16[256,1024]{1,0:T(8,128)(2,1)S(1)}, u32[]{:S(2)}, u32[]{:S(2)}) collective-permute-start(bf16[256,1024]{1,0:T(8,128)(2,1)S(1)} %collective-permute-done.15), channel_id=1, source_target_pairs={{4,8},{8,4},{5,9},{9,5},{6,10},{10,6},{7,11},{11,7},{20,24},{24,20... | collective-permute-start | bytes 1572872 | tf_op jit(solution)/shard_map/ppermute | solution.py:46
  103.3 11.4 %collective-permute-start.26 = (bf16[256,1024]{1,0:T(8,128)(2,1)S(1)}, bf16[256,1024]{1,0:T(8,128)(2,1)S(1)}, u32[]{:S(2)}, u32[]{:S(2)}) collective-permute-start(bf16[256,1024]{1,0:T(8,128)(2,1)S(1)} %add_convert_fusion.6), channel_id=1, source_target_pairs={{0,3},{1,2},{2,1},{3,0},{4,7},{5,6},{6,5},{7,4},{8,11},{9,10},{10,... | collective-permute-start | bytes 1572872 | tf_op jit(solution)/shard_map/ppermute | solution.py:42
  105.5 9.6 %collective-permute-start.24 = (bf16[256,1024]{1,0:T(8,128)(2,1)S(1)}, bf16[256,1024]{1,0:T(8,128)(2,1)S(1)}, u32[]{:S(2)}, u32[]{:S(2)}) collective-permute-start(bf16[256,1024]{1,0:T(8,128)(2,1)S(1)} %get-tuple-element.138), channel_id=1, source_target_pairs={{0,4},{4,0},{8,12},{12,8},{1,5},{5,1},{9,13},{13,9},{2,6},{6,2},{1... | collective-permute-start | bytes 1572872 | tf_op jit(solution)/shard_map/ppermute | solution.py:46
  105.6 9.6 %collective-permute-start.23 = (bf16[512,512]{1,0:T(8,128)(2,1)S(1)}, bf16[512,512]{1,0:T(8,128)(2,1)S(1)}, u32[]{:S(2)}, u32[]{:S(2)}) collective-permute-start(bf16[512,512]{1,0:T(8,128)(2,1)S(1)} %get-tuple-element.99), channel_id=1, source_target_pairs={{0,1},{1,0},{2,3},{3,2},{4,5},{5,4},{6,7},{7,6},{8,9},{9,8},{10,11... | collective-permute-start | bytes 1572872 | tf_op jit(solution)/shard_map/ppermute | solution.py:38
  115.9 15.1 %collective-permute-start.31 = (bf16[256,1024]{1,0:T(8,128)(2,1)S(1)}, bf16[256,1024]{1,0:T(8,128)(2,1)S(1)}, u32[]{:S(2)}, u32[]{:S(2)}) collective-permute-start(bf16[256,1024]{1,0:T(8,128)(2,1)S(1)} %add_convert_fusion.4), channel_id=1, source_target_pairs={{0,3},{1,2},{2,1},{3,0},{4,7},{5,6},{6,5},{7,4},{8,11},{9,10},{10,... | collective-permute-start | bytes 1572872 | tf_op jit(solution)/shard_map/ppermute | solution.py:42
  117.2 13.8 %collective-permute-start.30 = (bf16[256,1024]{1,0:T(8,128)(2,1)S(1)}, bf16[256,1024]{1,0:T(8,128)(2,1)S(1)}, u32[]{:S(2)}, u32[]{:S(2)}) collective-permute-start(bf16[256,1024]{1,0:T(8,128)(2,1)S(1)} %add_convert_fusion.5), channel_id=1, source_target_pairs={{4,8},{8,4},{5,9},{9,5},{6,10},{10,6},{7,11},{11,7},{20,24},{24,20... | collective-permute-start | bytes 1572872 | tf_op jit(solution)/shard_map/ppermute | solution.py:46
  118.0 13.1 %collective-permute-start.32 = (f32[128,1024]{1,0:T(8,128)S(1)}, f32[128,1024]{1,0:T(8,128)S(1)}, u32[]{:S(2)}, u32[]{:S(2)}) collective-permute-start(f32[128,1024]{1,0:T(8,128)S(1)} %maximum_select_fusion.3), channel_id=1, source_target_pairs={{0,16},{16,0},{1,17},{17,1},{2,18},{18,2},{3,19},{19,3},{4,20},{20... | collective-permute-start | bytes 1572872 | tf_op jit(solution)/shard_map/ppermute | solution.py:106
  123.1 13.2 %collective-permute-start.28 = (bf16[512,512]{1,0:T(8,128)(2,1)S(1)}, bf16[512,512]{1,0:T(8,128)(2,1)S(1)}, u32[]{:S(2)}, u32[]{:S(2)}) collective-permute-start(bf16[512,512]{1,0:T(8,128)(2,1)S(1)} %get-tuple-element.108), channel_id=1, source_target_pairs={{0,1},{1,0},{2,3},{3,2},{4,5},{5,4},{6,7},{7,6},{8,9},{9,8},{10,11... | collective-permute-start | bytes 1572872 | tf_op jit(solution)/shard_map/ppermute | solution.py:38
  123.4 15.3 %collective-permute-start.29 = (bf16[256,1024]{1,0:T(8,128)(2,1)S(1)}, bf16[256,1024]{1,0:T(8,128)(2,1)S(1)}, u32[]{:S(2)}, u32[]{:S(2)}) collective-permute-start(bf16[256,1024]{1,0:T(8,128)(2,1)S(1)} %get-tuple-element.136), channel_id=1, source_target_pairs={{0,4},{4,0},{8,12},{12,8},{1,5},{5,1},{9,13},{13,9},{2,6},{6,2},{1... | collective-permute-start | bytes 1572872 | tf_op jit(solution)/shard_map/ppermute | solution.py:46
  140.9 8.5 %collective-permute-start.33 = (bf16[512,1024]{1,0:T(8,128)(2,1)S(1)}, bf16[512,1024]{1,0:T(8,128)(2,1)S(1)}, u32[]{:S(2)}, u32[]{:S(2)}) collective-permute-start(bf16[512,1024]{1,0:T(8,128)(2,1)S(1)} %get-tuple-element.154), channel_id=1, source_target_pairs={{0,16},{16,0},{1,17},{17,1},{2,18},{18,2},{3,19},{19,3},{4,20},{20... | collective-permute-start | bytes 3145736 | tf_op jit(solution)/shard_map/ppermute | solution.py:34
  142.6 14.8 %collective-permute-start.35 = (bf16[256,1024]{1,0:T(8,128)(2,1)S(1)}, bf16[256,1024]{1,0:T(8,128)(2,1)S(1)}, u32[]{:S(2)}, u32[]{:S(2)}) collective-permute-start(bf16[256,1024]{1,0:T(8,128)(2,1)S(1)} %add_convert_fusion.3), channel_id=1, source_target_pairs={{0,3},{1,2},{2,1},{3,0},{4,7},{5,6},{6,5},{7,4},{8,11},{9,10},{10,... | collective-permute-start | bytes 1572872 | tf_op jit(solution)/shard_map/ppermute | solution.py:42
  144.4 13.0 %collective-permute-start.37 = (bf16[256,1024]{1,0:T(8,128)(2,1)S(1)}, bf16[256,1024]{1,0:T(8,128)(2,1)S(1)}, u32[]{:S(2)}, u32[]{:S(2)}) collective-permute-start(bf16[256,1024]{1,0:T(8,128)(2,1)S(1)} %add_convert_fusion.1), channel_id=1, source_target_pairs={{4,8},{8,4},{5,9},{9,5},{6,10},{10,6},{7,11},{11,7},{20,24},{24,20... | collective-permute-start | bytes 1572872 | tf_op jit(solution)/shard_map/ppermute | solution.py:46
  145.4 15.3 %collective-permute-start.36 = (bf16[256,1024]{1,0:T(8,128)(2,1)S(1)}, bf16[256,1024]{1,0:T(8,128)(2,1)S(1)}, u32[]{:S(2)}, u32[]{:S(2)}) collective-permute-start(bf16[256,1024]{1,0:T(8,128)(2,1)S(1)} %add_convert_fusion.2), channel_id=1, source_target_pairs={{0,4},{4,0},{8,12},{12,8},{1,5},{5,1},{9,13},{13,9},{2,6},{6,2},{1... | collective-permute-start | bytes 1572872 | tf_op jit(solution)/shard_map/ppermute | solution.py:46
  150.5 24.2 %collective-permute-start.34 = (bf16[512,1024]{1,0:T(8,128)(2,1)S(1)}, bf16[512,1024]{1,0:T(8,128)(2,1)S(1)}, u32[]{:S(2)}, u32[]{:S(2)}) collective-permute-start(bf16[512,1024]{1,0:T(8,128)(2,1)S(1)} %add_convert_fusion), channel_id=1, source_target_pairs={{1,16},{2,19},{16,1},{19,2},{5,20},{6,23},{20,5},{23,6},{9,24},{10... | collective-permute-start | bytes 3145736 | tf_op jit(solution)/shard_map/ppermute | solution.py:30
  161.2 11.2 %collective-permute-start.38 = (bf16[256,1024]{1,0:T(8,128)(2,1)S(1)}, bf16[256,1024]{1,0:T(8,128)(2,1)S(1)}, u32[]{:S(2)}, u32[]{:S(2)}) collective-permute-start(bf16[256,1024]{1,0:T(8,128)(2,1)S(1)} %get-tuple-element.134), channel_id=1, source_target_pairs={{1,16},{2,19},{16,1},{19,2},{5,20},{6,23},{20,5},{23,6},{9,24},{10... | collective-permute-start | bytes 1572872 | tf_op jit(solution)/shard_map/ppermute | solution.py:30
  (34 other events, 270.9 us)

commit v9 on v3

--- a/solution.py
+++ b/solution.py
@@ -58,26 +58,30 @@
     return lax.optimization_barrier(arrays)
 
 
-def move(_, a, b, to_a, to_b):
-    to_a[0] = a[...]
-    to_b[0] = b[...]
+def move(_, a0, a1, b0, b1, to_a, to_b):
+    to_a[0, :, :256] = a0[...]
+    to_a[0, :, 256:] = a1[...]
+    to_b[0, :, :256] = b0[...]
+    to_b[0, :, 256:] = b1[...]
 
 
 def halves(tokens, blocks):
-    spec = lambda i: pl.BlockSpec((512, 256), lambda n, table: (0, table[i, n]))
-    out = pl.BlockSpec((1, 512, 256), lambda n, table: (n // 2, 0, n % 2))
+    def spec(half, place):
+        return pl.BlockSpec((512, 256), lambda n, table: (0, table[half, 2 * n + place]))
+
+    out = pl.BlockSpec((1, 512, 512), lambda n, table: (n, 0, 0))
     kind = jax.ShapeDtypeStruct((4, 512, 512), bf16)
     return pl.pallas_call(
         move,
         grid_spec=pltpu.PrefetchScalarGridSpec(
             num_scalar_prefetch=1,
-            grid=(8,),
-            in_specs=[spec(0), spec(1)],
+            grid=(4,),
+            in_specs=[spec(half, place) for half in range(2) for place in range(2)],
             out_specs=[out, out],
         ),
         out_shape=[kind, kind],
         cost_estimate=pl.CostEstimate(flops=0, bytes_accessed=16 << 20, transcendentals=0),
-    )(blocks, tokens, tokens)
+    )(blocks, tokens, tokens, tokens, tokens)
 
 
 class Drift:
@@ -88,7 +92,9 @@
         self.steps = [("c", CORE, c), ("y", near, y % 2), ("y", wide, y // 2), ("zh", CORE, c)]
         self.at = 0
 
-    def send(self):
+    def send(self, earlier=None):
+        if earlier is not None:
+            self.v, _ = together(self.v, earlier)
         if self.at < 3:
             bit = self.steps[self.at][2]
             n = self.v.shape[0] // 2
@@ -171,7 +177,8 @@
     def cat(*arrays):
         return jnp.concatenate(arrays, axis=-1)
 
-    got = (beside(leave[1]), line(m2, ENDS_OUT), line(q_own, MIDDLE), across(going(0)), drift.send())
+    m3 = line(q_own, MIDDLE)
+    got = (beside(leave[1]), line(m2, ENDS_OUT), m3, across(going(0)), drift.send(m3))
     rows = [None, None, jnp.concatenate([e_own, q2]), jnp.concatenate([w, q_own])]
     k_a = dot(cat(keep[2], keep[3]), jnp.concatenate(rows[2:]))
     stay = staying(0)
@@ -181,12 +188,13 @@
     drift.take(d)
     part0 = stay + q3.astype(f32)
 
+    m4 = line(q2, MIDDLE)
     got = (
         beside(leave[2]),
         line(jnp.where(end, part0.astype(bf16), m3), PAIRS),
-        line(q2, MIDDLE),
+        m4,
         across(going(1)),
-        drift.send(),
+        drift.send(m4),
     )
     stay = staying(1)
     got, leave, drift.v, stay, part0 = together(got, leave, drift.v, stay, part0)
@@ -225,7 +233,8 @@
     keys = jnp.where(stays, keys_work, swap(keys_work))
     e6, m6, q6 = got
     total = staying(3) + q6.astype(f32) + e6.astype(f32) + m6.astype(f32)
-    gradient = jnp.where(stays, total, swap(total.astype(bf16)).astype(f32))
+    back, keys = together(swap(total.astype(bf16)), keys)
+    gradient = jnp.where(stays, total, back.astype(f32))
     drift.take(drift.send())
 
     new_first = first_decay * adam_first[0] + (1.0 - first_decay) * gradient

time: 159 us -> 170 us (1.069)
  starting transfers between devices: 62 us -> 68.9 us
  other arithmetic: 17.4 us -> 21.9 us
  waiting for transfers between devices: 56.8 us -> 52.3 us
  matrix products: 12 us -> 16 us
  Pallas kernels: 7.37 us -> 5.48 us
    ppermute x6, waiting for transfers between devices: 19.2 us -> 1.39 us  [across(): return lax.ppermute(v, 'x', ACROSS)]
    ppermute x12, waiting for transfers between devices: 11.2 us -> 22 us  [line(): return lax.ppermute(v, 'zl', pairs)]
    ppermute x12, starting transfers between devices: 18.5 us -> 27.7 us  [line(): return lax.ppermute(v, 'zl', pairs)]
    convert_element_type x1, other arithmetic: 1.16 us -> 3.73 us  [on_device(): keys_work = (jnp.where(stays, k_a, k_b) + k_got.astype(f32)).astype(bf16)]
    dot_general x12, matrix products: 6.66 us -> 8.93 us  [dot_t(): lax.dot_general(a, b, (((0,), (0,)), ((), ())), preferred_element_type=f32)]
    ppermute x7, waiting for transfers between devices: 8.57 us -> 10.6 us  [send(): return lax.ppermute(self.sent, axis, perm)]
    pallas_call x1, Pallas kernels: 7.37 us -> 5.48 us  [halves(): pl.pallas_call(move, grid_spec=pltpu.PrefetchScalarGridSpec(num_scalar_pr...]
  transfers between devices with their start and end apart: 37 -> 37, of which waited for: 15 -> 14; matrix products, arithmetic and copies ran while one was open for 17% -> 19% of each run, Pallas kernels for 0% -> 0%
where the time goes in v9:
time: 170 us; the launch traced here: 169 us
  starting transfers between devices  68.9 us (41%)
  waiting for transfers between devices  52.3 us (31%)
  other arithmetic  21.9 us (13%)
  matrix products  16 us (9%)
  Pallas kernels  5.48 us (3%)
  local copies, waits for them, and re-layouts  3.3 us (2%)
    ppermute x12, starting transfers between devices, line(): return lax.ppermute(v, 'zl', pairs)  27.7 us
    ppermute x12, waiting for transfers between devices, line(): return lax.ppermute(v, 'zl', pairs)  22 us
    ppermute x7, starting transfers between devices, send(): return lax.ppermute(self.sent, axis, perm)  13.7 us
    ppermute x3, waiting for transfers between devices, swap(): return lax.ppermute(v, ('c', 'x'), SWAP)  12.8 us
    ppermute x7, waiting for transfers between devices, send(): return lax.ppermute(self.sent, axis, perm)  10.6 us
    ppermute x3, starting transfers between devices, swap(): return lax.ppermute(v, ('c', 'x'), SWAP)  9.25 us
    ppermute x4, starting transfers between devices, core(): return lax.ppermute(v, 'c', CORE)  9.07 us
    dot_general x12, matrix products, dot_t(): lax.dot_general(a, b, (((0,), (0,)), ((), ())), preferred_element_type=f32)  8.93 us
  transfers between devices with their start and end apart: 37, of which 14 were waited for; matrix products, arithmetic and copies ran while one was open for 19% of the time, Pallas kernels for 0%

profile of v9, /device:TPU:1, one launch (start us, length us, event | category | flops | bytes accessed | tf_op | source)
XLA Modules:
  0.0 169.2 jit_solution(7497855542275584462)
XLA Ops:
  1.4 5.5 %shard_map.127 = (bf16[4,512,512]{2,1,0:T(8,128)(2,1)}, bf16[4,512,512]{2,1,0:T(8,128)(2,1)}) custom-call(s32[2,8]{1,0:T(2,128)} %reshape.37._, bf16[512,4096]{1,0:T(8,128)(2,1)} %b1.1, bf16[512,4096]{1,0:T(8,128)(2,1)} %b1.1, bf16[512,4096]{1,0:T(8,128)(2,1)} %b1.1, bf16[512,4096]{1,0:T(8,128)(2,1)} %b1.1), custom_call_target="tpu_custom_call" | custom-call | bytes 16777216 | tf_op jit(solution)/shard_map/pallas_call | solution.py:74
  6.9 3.2 %collective-permute-start.8 = (bf16[4,512,512]{2,1,0:T(8,128)(2,1)}, bf16[4,512,512]{2,1,0:T(8,128)(2,1)S(1)}, u32[]{:S(2)}, u32[]{:S(2)}) collective-permute-start(bf16[4,512,512]{2,1,0:T(8,128)(2,1)} %get-tuple-element.65), channel_id=1, source_target_pairs={{0,16},{16,0},{1,17},{17,1},{2,18},{18,2},{3,19},{19,3},{4,20},{20... | collective-permute-start | bytes 6291464 | tf_op jit(solution)/shard_map/ppermute | solution.py:34
  10.1 1.9 %collective-permute-start.2 = (bf16[256,1024]{1,0:T(8,128)(2,1)}, bf16[256,1024]{1,0:T(8,128)(2,1)}, u32[]{:S(2)}, u32[]{:S(2)}) collective-permute-start(bf16[256,1024]{1,0:T(8,128)(2,1)} %bitcast), channel_id=1, source_target_pairs={{1,16},{2,19},{16,1},{19,2},{5,20},{6,23},{20,5},{23,6},{9,24},{10... | collective-permute-start | bytes 1572872 | tf_op jit(solution)/shard_map/ppermute | solution.py:30
  15.0 6.1 %collective-permute-done.2 = bf16[256,1024]{1,0:T(8,128)(2,1)} collective-permute-done((bf16[256,1024]{1,0:T(8,128)(2,1)}, bf16[256,1024]{1,0:T(8,128)(2,1)}, u32[]{:S(2)}, u32[]{:S(2)}) %collective-permute-start.2) | collective-permute-done | bytes 524320 | tf_op jit(solution)/shard_map/ppermute | solution.py:30
  23.9 4.6 %collective-permute-start.3 = (bf16[256,1024]{1,0:T(8,128)(2,1)S(1)}, bf16[256,1024]{1,0:T(8,128)(2,1)S(1)}, u32[]{:S(2)}, u32[]{:S(2)}) collective-permute-start(bf16[256,1024]{1,0:T(8,128)(2,1)S(1)} %broadcast_select_fusion.2), channel_id=1, source_target_pairs={{0,4},{4,0},{8,12},{12,8},{1,5},{5,1},{9,13},{13,9},{2,6},{6,2},{1... | collective-permute-start | bytes 1572872 | tf_op jit(solution)/shard_map/ppermute | solution.py:46
  34.4 5.3 %collective-permute-done.7 = f32[64,1024]{1,0:T(8,128)S(1)} collective-permute-done((f32[64,1024]{1,0:T(8,128)S(1)}, f32[64,1024]{1,0:T(8,128)S(1)}, u32[]{:S(2)}, u32[]{:S(2)}) %collective-permute-start.7) | collective-permute-done | bytes 262176 | tf_op jit(solution)/shard_map/ppermute | solution.py:107
  39.8 4.5 %collective-permute-done.1 = bf16[256,1024]{1,0:T(8,128)(2,1)S(1)} collective-permute-done((bf16[256,1024]{1,0:T(8,128)(2,1)S(1)}, bf16[256,1024]{1,0:T(8,128)(2,1)S(1)}, u32[]{:S(2)}, u32[]{:S(2)}) %collective-permute-start.1) | collective-permute-done | bytes 524320 | tf_op jit(solution)/shard_map/ppermute | solution.py:38
  52.0 3.0 %collective-permute-start.13 = (f32[32,1024]{1,0:T(8,128)S(1)}, f32[32,1024]{1,0:T(8,128)S(1)}, u32[]{:S(2)}, u32[]{:S(2)}) collective-permute-start(f32[32,1024]{1,0:T(8,128)S(1)} %constant_dynamic-slice_fusion), channel_id=1, source_target_pairs={{0,64},{32,96},{64,0},{96,32},{1,65},{33,97},{65,1},{97,33},{2,66}... | collective-permute-start | bytes 393224 | tf_op jit(solution)/shard_map/ppermute | solution.py:107
  55.5 3.2 %collective-permute-done.13 = f32[32,1024]{1,0:T(8,128)S(1)} collective-permute-done((f32[32,1024]{1,0:T(8,128)S(1)}, f32[32,1024]{1,0:T(8,128)S(1)}, u32[]{:S(2)}, u32[]{:S(2)}) %collective-permute-start.13) | collective-permute-done | bytes 131104 | tf_op jit(solution)/shard_map/ppermute | solution.py:107
  62.8 1.6 collective-permute-start.15
  67.7 5.2 %collective-permute-start.19 = (bf16[32,1024]{1,0:T(8,128)(2,1)S(1)}, bf16[32,1024]{1,0:T(8,128)(2,1)S(1)}, u32[]{:S(2)}, u32[]{:S(2)}) collective-permute-start(bf16[32,1024]{1,0:T(8,128)(2,1)S(1)} %dynamic-slice_add_fusion.2), channel_id=1, source_target_pairs={{0,128},{128,0},{1,129},{129,1},{2,130},{130,2},{3,131},{131,3},{4... | collective-permute-start | bytes 196616 | tf_op jit(solution)/shard_map/ppermute | solution.py:107
  72.9 2.0 %collective-permute-done.19 = bf16[32,1024]{1,0:T(8,128)(2,1)S(1)} collective-permute-done((bf16[32,1024]{1,0:T(8,128)(2,1)S(1)}, bf16[32,1024]{1,0:T(8,128)(2,1)S(1)}, u32[]{:S(2)}, u32[]{:S(2)}) %collective-permute-start.19) | collective-permute-done | bytes 65568 | tf_op jit(solution)/shard_map/ppermute | solution.py:107
  74.9 5.3 %collective-permute-done.16 = bf16[256,1024]{1,0:T(8,128)(2,1)S(1)} collective-permute-done((bf16[256,1024]{1,0:T(8,128)(2,1)S(1)}, bf16[256,1024]{1,0:T(8,128)(2,1)S(1)}, u32[]{:S(2)}, u32[]{:S(2)}) %collective-permute-start.16) | collective-permute-done | bytes 524320 | tf_op jit(solution)/shard_map/ppermute | solution.py:46
  80.2 3.0 %collective-permute-start.24 = (f32[32,1024]{1,0:T(8,128)S(1)}, f32[32,1024]{1,0:T(8,128)S(1)}, u32[]{:S(2)}, u32[]{:S(2)}) collective-permute-start(f32[32,1024]{1,0:T(8,128)S(1)} %convert_add_fusion.3), channel_id=1, source_target_pairs={{0,64},{32,96},{64,0},{96,32},{1,65},{33,97},{65,1},{97,33},{2,66}... | collective-permute-start | bytes 393224 | tf_op jit(solution)/shard_map/ppermute | solution.py:107
  85.4 10.5 %collective-permute-start.21 = (bf16[256,1024]{1,0:T(8,128)(2,1)S(1)}, bf16[256,1024]{1,0:T(8,128)(2,1)S(1)}, u32[]{:S(2)}, u32[]{:S(2)}) collective-permute-start(bf16[256,1024]{1,0:T(8,128)(2,1)S(1)} %get-tuple-element.130), channel_id=1, source_target_pairs={{0,4},{4,0},{8,12},{12,8},{1,5},{5,1},{9,13},{13,9},{2,6},{6,2},{1... | collective-permute-start | bytes 1572872 | tf_op jit(solution)/shard_map/ppermute | solution.py:46
  96.6 9.3 %collective-permute-done.21 = bf16[256,1024]{1,0:T(8,128)(2,1)S(1)} collective-permute-done((bf16[256,1024]{1,0:T(8,128)(2,1)S(1)}, bf16[256,1024]{1,0:T(8,128)(2,1)S(1)}, u32[]{:S(2)}, u32[]{:S(2)}) %collective-permute-start.21) | collective-permute-done | bytes 524320 | tf_op jit(solution)/shard_map/ppermute | solution.py:46
  111.0 2.4 %collective-permute-start.26 = (bf16[256,1024]{1,0:T(8,128)(2,1)S(1)}, bf16[256,1024]{1,0:T(8,128)(2,1)S(1)}, u32[]{:S(2)}, u32[]{:S(2)}) collective-permute-start(bf16[256,1024]{1,0:T(8,128)(2,1)S(1)} %get-tuple-element.128), channel_id=1, source_target_pairs={{0,4},{4,0},{8,12},{12,8},{1,5},{5,1},{9,13},{13,9},{2,6},{6,2},{1... | collective-permute-start | bytes 1572872 | tf_op jit(solution)/shard_map/ppermute | solution.py:46
  114.6 1.7 slice_add_fusion
  119.0 2.7 %collective-permute-done.26 = bf16[256,1024]{1,0:T(8,128)(2,1)S(1)} collective-permute-done((bf16[256,1024]{1,0:T(8,128)(2,1)S(1)}, bf16[256,1024]{1,0:T(8,128)(2,1)S(1)}, u32[]{:S(2)}, u32[]{:S(2)}) %collective-permute-start.26) | collective-permute-done | bytes 524320 | tf_op jit(solution)/shard_map/ppermute | solution.py:46
  123.3 3.1 %select_convert_fusion = (bf16[512,1024]{1,0:T(8,128)(2,1)}, f32[512,1024]{1,0:T(8,128)}) fusion(pred[]{:T(512)S(6)} %eq.36, f32[512,1024]{1,0:T(8,128)S(1)} %fusion.5, f32[512,1024]{1,0:T(8,128)S(1)} %add.211, f32[512,1024]{1,0:T(8,128)S(1)} %fusion.30, bf16[256,1024]{1,0:T(8,128)(2,1)S(1)} %collective-permute-done.5, ...), kind=kOutput, calls=%fused_computation.21 | convolution fusion | flops 1086324736 | bytes 12582913 | tf_op jit(solution)/shard_map/dot_general | solution.py:50
  126.4 4.8 %collective-permute-start.34 = (bf16[512,1024]{1,0:T(8,128)(2,1)}, bf16[512,1024]{1,0:T(8,128)(2,1)}, u32[]{:S(2)}, u32[]{:S(2)}) collective-permute-start(bf16[512,1024]{1,0:T(8,128)(2,1)} %get-tuple-element.141), channel_id=1, source_target_pairs={{0,16},{16,0},{1,17},{17,1},{2,18},{18,2},{3,19},{19,3},{4,20},{20... | collective-permute-start | bytes 3145736 | tf_op jit(solution)/shard_map/ppermute | solution.py:34
  131.2 1.6 add_convert_fusion.3
  132.8 1.7 %collective-permute-start.30 = (bf16[256,1024]{1,0:T(8,128)(2,1)S(1)}, bf16[256,1024]{1,0:T(8,128)(2,1)S(1)}, u32[]{:S(2)}, u32[]{:S(2)}) collective-permute-start(bf16[256,1024]{1,0:T(8,128)(2,1)S(1)} %add_convert_fusion.3), channel_id=1, source_target_pairs={{0,3},{1,2},{2,1},{3,0},{4,7},{5,6},{6,5},{7,4},{8,11},{9,10},{10,... | collective-permute-start | bytes 1572872 | tf_op jit(solution)/shard_map/ppermute | solution.py:42
  136.7 3.6 %collective-permute-start.31 = (bf16[256,1024]{1,0:T(8,128)(2,1)S(1)}, bf16[256,1024]{1,0:T(8,128)(2,1)S(1)}, u32[]{:S(2)}, u32[]{:S(2)}) collective-permute-start(bf16[256,1024]{1,0:T(8,128)(2,1)S(1)} %add_convert_fusion.2), channel_id=1, source_target_pairs={{0,4},{4,0},{8,12},{12,8},{1,5},{5,1},{9,13},{13,9},{2,6},{6,2},{1... | collective-permute-start | bytes 1572872 | tf_op jit(solution)/shard_map/ppermute | solution.py:46
  140.3 3.7 %add_convert_fusion = bf16[512,1024]{1,0:T(8,128)(2,1)S(1)} fusion(bf16[512,1024]{1,0:T(8,128)(2,1)} %collective-permute-done.34, pred[]{:T(512)S(6)} %eq.36, f32[512,1024]{1,0:T(8,128)S(1)} %copy-done.11, f32[512,1024]{1,0:T(8,128)} %get-tuple-element.142, f32[512,1024]{1,0:T(8,128)S(1)} %copy-done.1, f32[512,1024]{1,0:T(8,128)} %copy-done.12), kind=kLoop, calls=%fused_computation.20 | loop fusion | flops 3145728 | bytes 10485761 | tf_op jit(solution)/shard_map/convert_element_type | solution.py:232
  144.1 3.5 %collective-permute-start.35 = (bf16[512,1024]{1,0:T(8,128)(2,1)S(1)}, bf16[512,1024]{1,0:T(8,128)(2,1)S(1)}, u32[]{:S(2)}, u32[]{:S(2)}) collective-permute-start(bf16[512,1024]{1,0:T(8,128)(2,1)S(1)} %add_convert_fusion), channel_id=1, source_target_pairs={{1,16},{2,19},{16,1},{19,2},{5,20},{6,23},{20,5},{23,6},{9,24},{10... | collective-permute-start | bytes 3145736 | tf_op jit(solution)/shard_map/ppermute | solution.py:30
  148.3 3.7 %collective-permute-done.31 = bf16[256,1024]{1,0:T(8,128)(2,1)S(1)} collective-permute-done((bf16[256,1024]{1,0:T(8,128)(2,1)S(1)}, bf16[256,1024]{1,0:T(8,128)(2,1)S(1)}, u32[]{:S(2)}, u32[]{:S(2)}) %collective-permute-start.31) | collective-permute-done | bytes 524320 | tf_op jit(solution)/shard_map/ppermute | solution.py:46
  152.5 3.8 %collective-permute-start.33 = (bf16[256,1024]{1,0:T(8,128)(2,1)S(1)}, bf16[256,1024]{1,0:T(8,128)(2,1)S(1)}, u32[]{:S(2)}, u32[]{:S(2)}) collective-permute-start(bf16[256,1024]{1,0:T(8,128)(2,1)S(1)} %get-tuple-element.126), channel_id=1, source_target_pairs={{1,16},{2,19},{16,1},{19,2},{5,20},{6,23},{20,5},{23,6},{9,24},{10... | collective-permute-start | bytes 1572872 | tf_op jit(solution)/shard_map/ppermute | solution.py:30
  156.3 1.7 %multiply_subtract_fusion = (f32[256,1024]{1,0:T(8,128)}, f32[256,1024]{1,0:T(8,128)}) fusion(f32[256,1024]{1,0:T(8,128)S(1)} %copy-done.6, f32[128,1024]{1,0:T(8,128)S(1)} %maximum_select_fusion.2, f32[128,1024]{1,0:T(8,128)S(1)} %collective-permute-done.36, pred[]{:T(512)S(6)} %eq.40, f32[256,1024]{1,0:T(8,128)S(1)} %copy-done.13), kind=kLoop, calls=%fused_computation.51 | loop fusion | flops 2621440 | bytes 5242881 | tf_op jit(solution)/shard_map/sub | solution.py:248
  158.0 2.2 %collective-permute-done.35 = bf16[512,1024]{1,0:T(8,128)(2,1)S(1)} collective-permute-done((bf16[512,1024]{1,0:T(8,128)(2,1)S(1)}, bf16[512,1024]{1,0:T(8,128)(2,1)S(1)}, u32[]{:S(2)}, u32[]{:S(2)}) %collective-permute-start.35) | collective-permute-done | bytes 1048608 | tf_op jit(solution)/shard_map/ppermute | solution.py:30
  161.3 4.5 %collective-permute-done.33 = bf16[256,1024]{1,0:T(8,128)(2,1)S(1)} collective-permute-done((bf16[256,1024]{1,0:T(8,128)(2,1)S(1)}, bf16[256,1024]{1,0:T(8,128)(2,1)S(1)}, u32[]{:S(2)}, u32[]{:S(2)}) %collective-permute-start.33) | collective-permute-done | bytes 524320 | tf_op jit(solution)/shard_map/ppermute | solution.py:30
  165.8 3.4 %fusion.81 = (f32[1,256,1024]{2,1,0:T(8,128)}, bf16[1,256,1024]{2,1,0:T(8,128)(2,1)}, f32[1,256,1024]{2,1,0:T(8,128)}) fusion(f32[256,1024]{1,0:T(8,128)S(1)} %get-tuple-element.127, bf16[256,1024]{1,0:T(8,128)(2,1)S(1)} %collective-permute-done.33, pred[]{:T(512)S(6)} %eq.36, f32[1,256,1024]{2,1,0:T(8,128)S(1)} %copy-done.14, ...), kind=kLoop, calls=%fused_computation.123 | loop fusion | flops 4456448 | bytes 6815745 | tf_op jit(solution)/shard_map/broadcast_in_dim | solution.py:249
  (138 shorter events, 45.4 us)
Async XLA Ops:
  6.9 25.8 %collective-permute-start.8 = (bf16[4,512,512]{2,1,0:T(8,128)(2,1)}, bf16[4,512,512]{2,1,0:T(8,128)(2,1)S(1)}, u32[]{:S(2)}, u32[]{:S(2)}) collective-permute-start(bf16[4,512,512]{2,1,0:T(8,128)(2,1)} %get-tuple-element.65), channel_id=1, source_target_pairs={{0,16},{16,0},{1,17},{17,1},{2,18},{18,2},{3,19},{19,3},{4,20},{20... | collective-permute-start | bytes 6291464 | tf_op jit(solution)/shard_map/ppermute | solution.py:34
  10.1 11.0 %collective-permute-start.2 = (bf16[256,1024]{1,0:T(8,128)(2,1)}, bf16[256,1024]{1,0:T(8,128)(2,1)}, u32[]{:S(2)}, u32[]{:S(2)}) collective-permute-start(bf16[256,1024]{1,0:T(8,128)(2,1)} %bitcast), channel_id=1, source_target_pairs={{1,16},{2,19},{16,1},{19,2},{5,20},{6,23},{20,5},{23,6},{9,24},{10... | collective-permute-start | bytes 1572872 | tf_op jit(solution)/shard_map/ppermute | solution.py:30
  12.1 17.6 %collective-permute-start = (bf16[512,1024]{1,0:T(8,128)(2,1)}, bf16[512,1024]{1,0:T(8,128)(2,1)}, u32[]{:S(2)}, u32[]{:S(2)}) collective-permute-start(bf16[512,1024]{1,0:T(8,128)(2,1)} %param.9), channel_id=1, source_target_pairs={{0,16},{16,0},{1,17},{17,1},{2,18},{18,2},{3,19},{19,3},{4,20},{20... | collective-permute-start | bytes 3145736 | tf_op jit(solution)/shard_map/ppermute | solution.py:34
  14.5 9.4 %collective-permute-start.6 = (f32[128,1024]{1,0:T(8,128)}, f32[128,1024]{1,0:T(8,128)}, u32[]{:S(2)}, u32[]{:S(2)}) collective-permute-start(f32[128,1024]{1,0:T(8,128)} %constant_dynamic-slice_fusion.2), channel_id=1, source_target_pairs={{0,16},{16,0},{1,17},{17,1},{2,18},{18,2},{3,19},{19,3},{4,20},{20... | collective-permute-start | bytes 1572872 | tf_op jit(solution)/shard_map/ppermute | solution.py:107
  22.4 17.3 %collective-permute-start.5 = (bf16[256,1024]{1,0:T(8,128)(2,1)S(1)}, bf16[256,1024]{1,0:T(8,128)(2,1)S(1)}, u32[]{:S(2)}, u32[]{:S(2)}) collective-permute-start(bf16[256,1024]{1,0:T(8,128)(2,1)S(1)} %broadcast_select_fusion.2), channel_id=1, source_target_pairs={{0,3},{1,2},{2,1},{3,0},{4,7},{5,6},{6,5},{7,4},{8,11},{9,10},{10,... | collective-permute-start | bytes 1572872 | tf_op jit(solution)/shard_map/ppermute | solution.py:42
  23.2 16.5 %collective-permute-start.4 = (bf16[256,1024]{1,0:T(8,128)(2,1)S(1)}, bf16[256,1024]{1,0:T(8,128)(2,1)S(1)}, u32[]{:S(2)}, u32[]{:S(2)}) collective-permute-start(bf16[256,1024]{1,0:T(8,128)(2,1)S(1)} %broadcast_select_fusion.2), channel_id=1, source_target_pairs={{4,8},{8,4},{5,9},{9,5},{6,10},{10,6},{7,11},{11,7},{20,24},{24,20... | collective-permute-start | bytes 1572872 | tf_op jit(solution)/shard_map/ppermute | solution.py:46
  23.9 15.8 %collective-permute-start.3 = (bf16[256,1024]{1,0:T(8,128)(2,1)S(1)}, bf16[256,1024]{1,0:T(8,128)(2,1)S(1)}, u32[]{:S(2)}, u32[]{:S(2)}) collective-permute-start(bf16[256,1024]{1,0:T(8,128)(2,1)S(1)} %broadcast_select_fusion.2), channel_id=1, source_target_pairs={{0,4},{4,0},{8,12},{12,8},{1,5},{5,1},{9,13},{13,9},{2,6},{6,2},{1... | collective-permute-start | bytes 1572872 | tf_op jit(solution)/shard_map/ppermute | solution.py:46
  31.2 13.1 %collective-permute-start.1 = (bf16[256,1024]{1,0:T(8,128)(2,1)S(1)}, bf16[256,1024]{1,0:T(8,128)(2,1)S(1)}, u32[]{:S(2)}, u32[]{:S(2)}) collective-permute-start(bf16[256,1024]{1,0:T(8,128)(2,1)S(1)} %dynamic-slice_select_fusion), channel_id=1, source_target_pairs={{0,1},{1,0},{2,3},{3,2},{4,5},{5,4},{6,7},{7,6},{8,9},{9,8},{10,11... | collective-permute-start | bytes 1572872 | tf_op jit(solution)/shard_map/ppermute | solution.py:38
  44.3 16.1 %collective-permute-start.12 = (bf16[256,1024]{1,0:T(8,128)(2,1)S(1)}, bf16[256,1024]{1,0:T(8,128)(2,1)S(1)}, u32[]{:S(2)}, u32[]{:S(2)}) collective-permute-start(bf16[256,1024]{1,0:T(8,128)(2,1)S(1)} %collective-permute-done.3), channel_id=1, source_target_pairs={{0,3},{1,2},{2,1},{3,0},{4,7},{5,6},{6,5},{7,4},{8,11},{9,10},{10,... | collective-permute-start | bytes 1572872 | tf_op jit(solution)/shard_map/ppermute | solution.py:42
  45.1 15.3 %collective-permute-start.11 = (bf16[256,1024]{1,0:T(8,128)(2,1)S(1)}, bf16[256,1024]{1,0:T(8,128)(2,1)S(1)}, u32[]{:S(2)}, u32[]{:S(2)}) collective-permute-start(bf16[256,1024]{1,0:T(8,128)(2,1)S(1)} %collective-permute-done.3), channel_id=1, source_target_pairs={{4,8},{8,4},{5,9},{9,5},{6,10},{10,6},{7,11},{11,7},{20,24},{24,20... | collective-permute-start | bytes 1572872 | tf_op jit(solution)/shard_map/ppermute | solution.py:46
  45.8 13.6 %collective-permute-start.9 = (bf16[512,512]{1,0:T(8,128)(2,1)S(1)}, bf16[512,512]{1,0:T(8,128)(2,1)S(1)}, u32[]{:S(2)}, u32[]{:S(2)}) collective-permute-start(bf16[512,512]{1,0:T(8,128)(2,1)S(1)} %get-tuple-element.67), channel_id=1, source_target_pairs={{0,1},{1,0},{2,3},{3,2},{4,5},{5,4},{6,7},{7,6},{8,9},{9,8},{10,11... | collective-permute-start | bytes 1572872 | tf_op jit(solution)/shard_map/ppermute | solution.py:38
  45.9 14.5 %collective-permute-start.10 = (bf16[256,1024]{1,0:T(8,128)(2,1)S(1)}, bf16[256,1024]{1,0:T(8,128)(2,1)S(1)}, u32[]{:S(2)}, u32[]{:S(2)}) collective-permute-start(bf16[256,1024]{1,0:T(8,128)(2,1)S(1)} %collective-permute-done.4), channel_id=1, source_target_pairs={{4,0},{8,12},{5,1},{9,13},{6,2},{10,14},{7,3},{11,15},{20,16},{24,... | collective-permute-start | bytes 1572872 | tf_op jit(solution)/shard_map/ppermute | solution.py:46
  58.7 8.9 %collective-permute-start.17 = (bf16[256,1024]{1,0:T(8,128)(2,1)S(1)}, bf16[256,1024]{1,0:T(8,128)(2,1)S(1)}, u32[]{:S(2)}, u32[]{:S(2)}) collective-permute-start(bf16[256,1024]{1,0:T(8,128)(2,1)S(1)} %collective-permute-done.5), channel_id=1, source_target_pairs={{4,8},{8,4},{5,9},{9,5},{6,10},{10,6},{7,11},{11,7},{20,24},{24,20... | collective-permute-start | bytes 1572872 | tf_op jit(solution)/shard_map/ppermute | solution.py:46
  61.4 13.6 %collective-permute-start.18 = (bf16[256,1024]{1,0:T(8,128)(2,1)S(1)}, bf16[256,1024]{1,0:T(8,128)(2,1)S(1)}, u32[]{:S(2)}, u32[]{:S(2)}) collective-permute-start(bf16[256,1024]{1,0:T(8,128)(2,1)S(1)} %add_convert_fusion.7), channel_id=1, source_target_pairs={{0,3},{1,2},{2,1},{3,0},{4,7},{5,6},{6,5},{7,4},{8,11},{9,10},{10,... | collective-permute-start | bytes 1572872 | tf_op jit(solution)/shard_map/ppermute | solution.py:42
  62.8 12.1 %collective-permute-start.15 = (bf16[512,512]{1,0:T(8,128)(2,1)S(1)}, bf16[512,512]{1,0:T(8,128)(2,1)S(1)}, u32[]{:S(2)}, u32[]{:S(2)}) collective-permute-start(bf16[512,512]{1,0:T(8,128)(2,1)S(1)} %get-tuple-element.77), channel_id=1, source_target_pairs={{0,1},{1,0},{2,3},{3,2},{4,5},{5,4},{6,7},{7,6},{8,9},{9,8},{10,11... | collective-permute-start | bytes 1572872 | tf_op jit(solution)/shard_map/ppermute | solution.py:38
  64.4 15.8 %collective-permute-start.16 = (bf16[256,1024]{1,0:T(8,128)(2,1)S(1)}, bf16[256,1024]{1,0:T(8,128)(2,1)S(1)}, u32[]{:S(2)}, u32[]{:S(2)}) collective-permute-start(bf16[256,1024]{1,0:T(8,128)(2,1)S(1)} %collective-permute-done.11), channel_id=1, source_target_pairs={{4,0},{8,12},{5,1},{9,13},{6,2},{10,14},{7,3},{11,15},{20,16},{24,... | collective-permute-start | bytes 1572872 | tf_op jit(solution)/shard_map/ppermute | solution.py:46
  65.7 14.6 %collective-permute-start.22 = (bf16[256,1024]{1,0:T(8,128)(2,1)S(1)}, bf16[256,1024]{1,0:T(8,128)(2,1)S(1)}, u32[]{:S(2)}, u32[]{:S(2)}) collective-permute-start(bf16[256,1024]{1,0:T(8,128)(2,1)S(1)} %collective-permute-done.12), channel_id=1, source_target_pairs={{4,8},{8,4},{5,9},{9,5},{6,10},{10,6},{7,11},{11,7},{20,24},{24,20... | collective-permute-start | bytes 1572872 | tf_op jit(solution)/shard_map/ppermute | solution.py:46
  80.2 16.3 %collective-permute-start.24 = (f32[32,1024]{1,0:T(8,128)S(1)}, f32[32,1024]{1,0:T(8,128)S(1)}, u32[]{:S(2)}, u32[]{:S(2)}) collective-permute-start(f32[32,1024]{1,0:T(8,128)S(1)} %convert_add_fusion.3), channel_id=1, source_target_pairs={{0,64},{32,96},{64,0},{96,32},{1,65},{33,97},{65,1},{97,33},{2,66}... | collective-permute-start | bytes 393224 | tf_op jit(solution)/shard_map/ppermute | solution.py:107
  83.7 12.8 %collective-permute-start.23 = (bf16[256,1024]{1,0:T(8,128)(2,1)S(1)}, bf16[256,1024]{1,0:T(8,128)(2,1)S(1)}, u32[]{:S(2)}, u32[]{:S(2)}) collective-permute-start(bf16[256,1024]{1,0:T(8,128)(2,1)S(1)} %add_convert_fusion.6), channel_id=1, source_target_pairs={{0,3},{1,2},{2,1},{3,0},{4,7},{5,6},{6,5},{7,4},{8,11},{9,10},{10,... | collective-permute-start | bytes 1572872 | tf_op jit(solution)/shard_map/ppermute | solution.py:42
  85.4 20.4 %collective-permute-start.21 = (bf16[256,1024]{1,0:T(8,128)(2,1)S(1)}, bf16[256,1024]{1,0:T(8,128)(2,1)S(1)}, u32[]{:S(2)}, u32[]{:S(2)}) collective-permute-start(bf16[256,1024]{1,0:T(8,128)(2,1)S(1)} %get-tuple-element.130), channel_id=1, source_target_pairs={{0,4},{4,0},{8,12},{12,8},{1,5},{5,1},{9,13},{13,9},{2,6},{6,2},{1... | collective-permute-start | bytes 1572872 | tf_op jit(solution)/shard_map/ppermute | solution.py:46
  95.8 10.9 %collective-permute-start.20 = (bf16[512,512]{1,0:T(8,128)(2,1)S(1)}, bf16[512,512]{1,0:T(8,128)(2,1)S(1)}, u32[]{:S(2)}, u32[]{:S(2)}) collective-permute-start(bf16[512,512]{1,0:T(8,128)(2,1)S(1)} %get-tuple-element.89), channel_id=1, source_target_pairs={{0,1},{1,0},{2,3},{3,2},{4,5},{5,4},{6,7},{7,6},{8,9},{9,8},{10,11... | collective-permute-start | bytes 1572872 | tf_op jit(solution)/shard_map/ppermute | solution.py:38
  106.8 10.7 %collective-permute-start.29 = (f32[64,1024]{1,0:T(8,128)S(1)}, f32[64,1024]{1,0:T(8,128)S(1)}, u32[]{:S(2)}, u32[]{:S(2)}) collective-permute-start(f32[64,1024]{1,0:T(8,128)S(1)} %maximum_select_fusion.3), channel_id=1, source_target_pairs={{0,32},{32,0},{64,96},{96,64},{1,33},{33,1},{65,97},{97,65},{2,34}... | collective-permute-start | bytes 786440 | tf_op jit(solution)/shard_map/ppermute | solution.py:107
  108.0 11.0 %collective-permute-start.28 = (bf16[256,1024]{1,0:T(8,128)(2,1)S(1)}, bf16[256,1024]{1,0:T(8,128)(2,1)S(1)}, u32[]{:S(2)}, u32[]{:S(2)}) collective-permute-start(bf16[256,1024]{1,0:T(8,128)(2,1)S(1)} %add_convert_fusion.4), channel_id=1, source_target_pairs={{0,3},{1,2},{2,1},{3,0},{4,7},{5,6},{6,5},{7,4},{8,11},{9,10},{10,... | collective-permute-start | bytes 1572872 | tf_op jit(solution)/shard_map/ppermute | solution.py:42
  108.4 10.5 %collective-permute-start.27 = (bf16[256,1024]{1,0:T(8,128)(2,1)S(1)}, bf16[256,1024]{1,0:T(8,128)(2,1)S(1)}, u32[]{:S(2)}, u32[]{:S(2)}) collective-permute-start(bf16[256,1024]{1,0:T(8,128)(2,1)S(1)} %add_convert_fusion.5), channel_id=1, source_target_pairs={{4,8},{8,4},{5,9},{9,5},{6,10},{10,6},{7,11},{11,7},{20,24},{24,20... | collective-permute-start | bytes 1572872 | tf_op jit(solution)/shard_map/ppermute | solution.py:46
  109.1 9.9 %collective-permute-start.25 = (bf16[512,512]{1,0:T(8,128)(2,1)S(1)}, bf16[512,512]{1,0:T(8,128)(2,1)S(1)}, u32[]{:S(2)}, u32[]{:S(2)}) collective-permute-start(bf16[512,512]{1,0:T(8,128)(2,1)S(1)} %get-tuple-element.99), channel_id=1, source_target_pairs={{0,1},{1,0},{2,3},{3,2},{4,5},{5,4},{6,7},{7,6},{8,9},{9,8},{10,11... | collective-permute-start | bytes 1572872 | tf_op jit(solution)/shard_map/ppermute | solution.py:38
  111.0 10.8 %collective-permute-start.26 = (bf16[256,1024]{1,0:T(8,128)(2,1)S(1)}, bf16[256,1024]{1,0:T(8,128)(2,1)S(1)}, u32[]{:S(2)}, u32[]{:S(2)}) collective-permute-start(bf16[256,1024]{1,0:T(8,128)(2,1)S(1)} %get-tuple-element.128), channel_id=1, source_target_pairs={{0,4},{4,0},{8,12},{12,8},{1,5},{5,1},{9,13},{13,9},{2,6},{6,2},{1... | collective-permute-start | bytes 1572872 | tf_op jit(solution)/shard_map/ppermute | solution.py:46
  126.4 13.9 %collective-permute-start.34 = (bf16[512,1024]{1,0:T(8,128)(2,1)}, bf16[512,1024]{1,0:T(8,128)(2,1)}, u32[]{:S(2)}, u32[]{:S(2)}) collective-permute-start(bf16[512,1024]{1,0:T(8,128)(2,1)} %get-tuple-element.141), channel_id=1, source_target_pairs={{0,16},{16,0},{1,17},{17,1},{2,18},{18,2},{3,19},{19,3},{4,20},{20... | collective-permute-start | bytes 3145736 | tf_op jit(solution)/shard_map/ppermute | solution.py:34
  132.8 15.5 %collective-permute-start.30 = (bf16[256,1024]{1,0:T(8,128)(2,1)S(1)}, bf16[256,1024]{1,0:T(8,128)(2,1)S(1)}, u32[]{:S(2)}, u32[]{:S(2)}) collective-permute-start(bf16[256,1024]{1,0:T(8,128)(2,1)S(1)} %add_convert_fusion.3), channel_id=1, source_target_pairs={{0,3},{1,2},{2,1},{3,0},{4,7},{5,6},{6,5},{7,4},{8,11},{9,10},{10,... | collective-permute-start | bytes 1572872 | tf_op jit(solution)/shard_map/ppermute | solution.py:42
  134.7 13.6 %collective-permute-start.32 = (bf16[256,1024]{1,0:T(8,128)(2,1)S(1)}, bf16[256,1024]{1,0:T(8,128)(2,1)S(1)}, u32[]{:S(2)}, u32[]{:S(2)}) collective-permute-start(bf16[256,1024]{1,0:T(8,128)(2,1)S(1)} %add_convert_fusion.1), channel_id=1, source_target_pairs={{4,8},{8,4},{5,9},{9,5},{6,10},{10,6},{7,11},{11,7},{20,24},{24,20... | collective-permute-start | bytes 1572872 | tf_op jit(solution)/shard_map/ppermute | solution.py:46
  136.7 15.3 %collective-permute-start.31 = (bf16[256,1024]{1,0:T(8,128)(2,1)S(1)}, bf16[256,1024]{1,0:T(8,128)(2,1)S(1)}, u32[]{:S(2)}, u32[]{:S(2)}) collective-permute-start(bf16[256,1024]{1,0:T(8,128)(2,1)S(1)} %add_convert_fusion.2), channel_id=1, source_target_pairs={{0,4},{4,0},{8,12},{12,8},{1,5},{5,1},{9,13},{13,9},{2,6},{6,2},{1... | collective-permute-start | bytes 1572872 | tf_op jit(solution)/shard_map/ppermute | solution.py:46
  144.1 16.1 %collective-permute-start.35 = (bf16[512,1024]{1,0:T(8,128)(2,1)S(1)}, bf16[512,1024]{1,0:T(8,128)(2,1)S(1)}, u32[]{:S(2)}, u32[]{:S(2)}) collective-permute-start(bf16[512,1024]{1,0:T(8,128)(2,1)S(1)} %add_convert_fusion), channel_id=1, source_target_pairs={{1,16},{2,19},{16,1},{19,2},{5,20},{6,23},{20,5},{23,6},{9,24},{10... | collective-permute-start | bytes 3145736 | tf_op jit(solution)/shard_map/ppermute | solution.py:30
  152.5 13.3 %collective-permute-start.33 = (bf16[256,1024]{1,0:T(8,128)(2,1)S(1)}, bf16[256,1024]{1,0:T(8,128)(2,1)S(1)}, u32[]{:S(2)}, u32[]{:S(2)}) collective-permute-start(bf16[256,1024]{1,0:T(8,128)(2,1)S(1)} %get-tuple-element.126), channel_id=1, source_target_pairs={{1,16},{2,19},{16,1},{19,2},{5,20},{6,23},{20,5},{23,6},{9,24},{10... | collective-permute-start | bytes 1572872 | tf_op jit(solution)/shard_map/ppermute | solution.py:30
  (28 other events, 164.9 us)

commit v10 on v7

--- a/solution.py
+++ b/solution.py
@@ -143,7 +143,6 @@
     x_sib = core(x_give)
     drift = Drift(anchor - local_params[0].astype(f32), c, y)
     drift.take(drift.send())
-    w, g_sib = together(w, g_sib)
     g_a = jnp.where(stays, key_grad, g_sib)
     g_l = lax.dynamic_slice_in_dim(jnp.where(stays, g_sib, key_grad), c * 256, 256, 0)
 
@@ -156,7 +155,7 @@
 
     x_b = [beside(leave[0])]
     e2, m2, q2 = line(m_own, ENDS_OUT), line(e_own, MIDDLE), across(e_own)
-    drift.take(drift.send(g_half))
+    drift.take(drift.send(m2))
     g_rest = core(g_half)
     g_b = jnp.where(
         c == 0, jnp.concatenate([g_half, g_rest]), jnp.concatenate([g_rest, g_half])
@@ -177,7 +176,7 @@
     e3 = line(after(m2, e2, x_b[0]), ENDS_OUT)
     m3 = line(after(q_own, m2, x_b[0]), MIDDLE)
     q3 = across(after(going(0), q2))
-    drift.take(drift.send(x_b[0]))
+    drift.take(drift.send(m3))
     rows = [None, None, jnp.concatenate([e_own, q2]), jnp.concatenate([w, q_own])]
     k_a = dot(cat(keep[2], keep[3]), jnp.concatenate(rows[2:]))
     part0 = staying(0) + q3.astype(f32)
@@ -186,14 +185,14 @@
     e4 = line(after(jnp.where(end, part0.astype(bf16), m3), e3, x_b[1]), PAIRS)
     m4 = line(after(q2, m3, x_b[1]), MIDDLE)
     q4 = across(after(going(1), q3))
-    drift.take(drift.send(x_b[1]))
+    drift.take(drift.send(m4))
     part1 = staying(1) + q4.astype(f32)
 
     x_b.append(beside(after(leave[3], x_b[2])))
     e5 = line(after(jnp.where(end, part1.astype(bf16), m4), e4, x_b[2]), PAIRS)
     m5 = line(after((part0 + e4.astype(f32)).astype(bf16), m4, x_b[2]), MIDDLE)
     q5 = across(after(going(2), q4))
-    drift.take(drift.send(x_b[2]))
+    drift.take(drift.send(q4))
     rows[1] = jnp.concatenate([mid, jnp.where(end, e4, m3)])
     k_a = k_a + dot(keep[1], rows[1])
     k_b = dot(cat(x_b[1], x_b[2]), jnp.concatenate(rows[1:3]))

time: 159 us -> 157 us (0.987)
  waiting for transfers between devices: 71.5 us -> 54.6 us
  starting transfers between devices: 50.5 us -> 63.5 us
    ppermute x6, waiting for transfers between devices: 14.8 us -> 4 us  [across(): return lax.ppermute(v, 'x', ACROSS)]
    ppermute x12, waiting for transfers between devices: 21.4 us -> 11.6 us  [line(): return lax.ppermute(v, 'zl', pairs)]
    ppermute x6, starting transfers between devices: 4.35 us -> 13.9 us  [across(): return lax.ppermute(v, 'x', ACROSS)]
    ppermute x7, waiting for transfers between devices: 7.27 us -> 10.5 us  [send(): return lax.ppermute(self.sent, axis, perm)]
    ppermute x5, waiting for transfers between devices: 12.6 us -> 15.1 us  [beside(): return lax.ppermute(v, 'x', BESIDE)]
    ppermute x3, waiting for transfers between devices: 15.4 us -> 13.3 us  [swap(): return lax.ppermute(v, ('c', 'x'), SWAP)]
  transfers between devices with their start and end apart: 37 -> 37, of which waited for: 14 -> 14; matrix products, arithmetic and copies ran while one was open for 15% -> 16% of each run, Pallas kernels for 0% -> 0%
where the time goes in v10:
time: 157 us; the launch traced here: 156 us
  starting transfers between devices  63.5 us (40%)
  waiting for transfers between devices  54.6 us (35%)
  other arithmetic  15.3 us (10%)
  matrix products  12.4 us (8%)
  Pallas kernels  7.37 us (5%)
  local copies, waits for them, and re-layouts  1.64 us (1%)
    ppermute x12, starting transfers between devices, line(): return lax.ppermute(v, 'zl', pairs)  17.9 us
    ppermute x5, waiting for transfers between devices, beside(): return lax.ppermute(v, 'x', BESIDE)  15.1 us
    ppermute x7, starting transfers between devices, send(): return lax.ppermute(self.sent, axis, perm)  14 us
    ppermute x6, starting transfers between devices, across(): return lax.ppermute(v, 'x', ACROSS)  13.9 us
    ppermute x3, waiting for transfers between devices, swap(): return lax.ppermute(v, ('c', 'x'), SWAP)  13.3 us
    ppermute x12, waiting for transfers between devices, line(): return lax.ppermute(v, 'zl', pairs)  11.6 us
    ppermute x7, waiting for transfers between devices, send(): return lax.ppermute(self.sent, axis, perm)  10.5 us
    ppermute x4, starting transfers between devices, core(): return lax.ppermute(v, 'c', CORE)  9.43 us
  transfers between devices with their start and end apart: 37, of which 14 were waited for; matrix products, arithmetic and copies ran while one was open for 16% of the time, Pallas kernels for 0%

profile of v10, /device:TPU:1, one launch (start us, length us, event | category | flops | bytes accessed | tf_op | source)
XLA Modules:
  0.0 155.9 jit_solution(16497264700052298850)
XLA Ops:
  1.4 7.4 %shard_map.127 = (bf16[4,512,512]{2,1,0:T(8,128)(2,1)}, bf16[4,512,512]{2,1,0:T(8,128)(2,1)}) custom-call(s32[2,8]{1,0:T(2,128)} %reshape.37._, bf16[512,4096]{1,0:T(8,128)(2,1)} %b.1, bf16[512,4096]{1,0:T(8,128)(2,1)} %b.1), custom_call_target="tpu_custom_call" | custom-call | bytes 16777216 | tf_op jit(solution)/shard_map/pallas_call | solution.py:74
  8.8 3.2 %collective-permute-start.8 = (bf16[4,512,512]{2,1,0:T(8,128)(2,1)}, bf16[4,512,512]{2,1,0:T(8,128)(2,1)S(1)}, u32[]{:S(2)}, u32[]{:S(2)}) collective-permute-start(bf16[4,512,512]{2,1,0:T(8,128)(2,1)} %get-tuple-element.42), channel_id=1, source_target_pairs={{0,16},{16,0},{1,17},{17,1},{2,18},{18,2},{3,19},{19,3},{4,20},{20... | collective-permute-start | bytes 6291464 | tf_op jit(solution)/shard_map/ppermute | solution.py:34
  12.0 1.9 %collective-permute-start.2 = (bf16[256,1024]{1,0:T(8,128)(2,1)}, bf16[256,1024]{1,0:T(8,128)(2,1)}, u32[]{:S(2)}, u32[]{:S(2)}) collective-permute-start(bf16[256,1024]{1,0:T(8,128)(2,1)} %bitcast), channel_id=1, source_target_pairs={{1,16},{2,19},{16,1},{19,2},{5,20},{6,23},{20,5},{23,6},{9,24},{10... | collective-permute-start | bytes 1572872 | tf_op jit(solution)/shard_map/ppermute | solution.py:30
  14.1 1.5 convert_subtract_fusion.1
  16.9 6.1 %collective-permute-done.2 = bf16[256,1024]{1,0:T(8,128)(2,1)} collective-permute-done((bf16[256,1024]{1,0:T(8,128)(2,1)}, bf16[256,1024]{1,0:T(8,128)(2,1)}, u32[]{:S(2)}, u32[]{:S(2)}) %collective-permute-start.2) | collective-permute-done | bytes 524320 | tf_op jit(solution)/shard_map/ppermute | solution.py:30
  25.8 4.6 %collective-permute-start.3 = (bf16[256,1024]{1,0:T(8,128)(2,1)S(1)}, bf16[256,1024]{1,0:T(8,128)(2,1)S(1)}, u32[]{:S(2)}, u32[]{:S(2)}) collective-permute-start(bf16[256,1024]{1,0:T(8,128)(2,1)S(1)} %broadcast_select_fusion.2), channel_id=1, source_target_pairs={{0,4},{4,0},{8,12},{12,8},{1,5},{5,1},{9,13},{13,9},{2,6},{6,2},{1... | collective-permute-start | bytes 1572872 | tf_op jit(solution)/shard_map/ppermute | solution.py:46
  31.6 1.5 dynamic-slice_select_fusion
  34.6 1.4 collective-permute-start.7
  36.3 5.3 %collective-permute-done.7 = f32[64,1024]{1,0:T(8,128)S(1)} collective-permute-done((f32[64,1024]{1,0:T(8,128)S(1)}, f32[64,1024]{1,0:T(8,128)S(1)}, u32[]{:S(2)}, u32[]{:S(2)}) %collective-permute-start.7) | collective-permute-done | bytes 262176 | tf_op jit(solution)/shard_map/ppermute | solution.py:106
  41.6 4.5 %collective-permute-done.1 = bf16[256,1024]{1,0:T(8,128)(2,1)S(1)} collective-permute-done((bf16[256,1024]{1,0:T(8,128)(2,1)S(1)}, bf16[256,1024]{1,0:T(8,128)(2,1)S(1)}, u32[]{:S(2)}, u32[]{:S(2)}) %collective-permute-start.1) | collective-permute-done | bytes 524320 | tf_op jit(solution)/shard_map/ppermute | solution.py:38
  52.4 8.0 %collective-permute-done.9 = bf16[512,512]{1,0:T(8,128)(2,1)S(1)} collective-permute-done((bf16[512,512]{1,0:T(8,128)(2,1)S(1)}, bf16[512,512]{1,0:T(8,128)(2,1)S(1)}, u32[]{:S(2)}, u32[]{:S(2)}) %collective-permute-start.9) | collective-permute-done | bytes 524320 | tf_op jit(solution)/shard_map/ppermute | solution.py:38
  61.8 2.3 %collective-permute-start.15 = (bf16[256,1024]{1,0:T(8,128)(2,1)S(1)}, bf16[256,1024]{1,0:T(8,128)(2,1)S(1)}, u32[]{:S(2)}, u32[]{:S(2)}) collective-permute-start(bf16[256,1024]{1,0:T(8,128)(2,1)S(1)} %fusion.28), channel_id=1, source_target_pairs={{0,3},{1,2},{2,1},{3,0},{4,7},{5,6},{6,5},{7,4},{8,11},{9,10},{10,... | collective-permute-start | bytes 1572872 | tf_op jit(solution)/shard_map/ppermute | solution.py:42
  64.1 3.0 %collective-permute-start.26 = (f32[32,1024]{1,0:T(8,128)S(1)}, f32[32,1024]{1,0:T(8,128)S(1)}, u32[]{:S(2)}, u32[]{:S(2)}) collective-permute-start(f32[32,1024]{1,0:T(8,128)S(1)} %constant_dynamic-slice_fusion), channel_id=1, source_target_pairs={{0,64},{32,96},{64,0},{96,32},{1,65},{33,97},{65,1},{97,33},{2,66}... | collective-permute-start | bytes 393224 | tf_op jit(solution)/shard_map/ppermute | solution.py:106
  69.6 2.6 %collective-permute-done.10 = bf16[512,512]{1,0:T(8,128)(2,1)S(1)} collective-permute-done((bf16[512,512]{1,0:T(8,128)(2,1)S(1)}, bf16[512,512]{1,0:T(8,128)(2,1)S(1)}, u32[]{:S(2)}, u32[]{:S(2)}) %collective-permute-start.10) | collective-permute-done | bytes 524320 | tf_op jit(solution)/shard_map/ppermute | solution.py:38
  72.6 5.1 %collective-permute-start.27 = (bf16[32,1024]{1,0:T(8,128)(2,1)S(1)}, bf16[32,1024]{1,0:T(8,128)(2,1)S(1)}, u32[]{:S(2)}, u32[]{:S(2)}) collective-permute-start(bf16[32,1024]{1,0:T(8,128)(2,1)S(1)} %dynamic-slice_add_fusion.2), channel_id=1, source_target_pairs={{0,128},{128,0},{1,129},{129,1},{2,130},{130,2},{3,131},{131,3},{4... | collective-permute-start | bytes 196616 | tf_op jit(solution)/shard_map/ppermute | solution.py:106
  78.9 3.8 %collective-permute-done.21 = bf16[256,1024]{1,0:T(8,128)(2,1)S(1)} collective-permute-done((bf16[256,1024]{1,0:T(8,128)(2,1)S(1)}, bf16[256,1024]{1,0:T(8,128)(2,1)S(1)}, u32[]{:S(2)}, u32[]{:S(2)}) %collective-permute-start.21) | collective-permute-done | bytes 524320 | tf_op jit(solution)/shard_map/ppermute | solution.py:46
  84.2 3.3 %collective-permute-start.16 = (bf16[256,1024]{1,0:T(8,128)(2,1)S(1)}, bf16[256,1024]{1,0:T(8,128)(2,1)S(1)}, u32[]{:S(2)}, u32[]{:S(2)}) collective-permute-start(bf16[256,1024]{1,0:T(8,128)(2,1)S(1)} %fusion.29), channel_id=1, source_target_pairs={{0,3},{1,2},{2,1},{3,0},{4,7},{5,6},{6,5},{7,4},{8,11},{9,10},{10,... | collective-permute-start | bytes 1572872 | tf_op jit(solution)/shard_map/ppermute | solution.py:42
  88.5 2.9 %collective-permute-start.28 = (f32[32,1024]{1,0:T(8,128)S(1)}, f32[32,1024]{1,0:T(8,128)S(1)}, u32[]{:S(2)}, u32[]{:S(2)}) collective-permute-start(f32[32,1024]{1,0:T(8,128)S(1)} %convert_add_fusion), channel_id=1, source_target_pairs={{0,64},{32,96},{64,0},{96,32},{1,65},{33,97},{65,1},{97,33},{2,66}... | collective-permute-start | bytes 393224 | tf_op jit(solution)/shard_map/ppermute | solution.py:106
  91.4 3.1 %collective-permute-done.22 = bf16[256,1024]{1,0:T(8,128)(2,1)S(1)} collective-permute-done((bf16[256,1024]{1,0:T(8,128)(2,1)S(1)}, bf16[256,1024]{1,0:T(8,128)(2,1)S(1)}, u32[]{:S(2)}, u32[]{:S(2)}) %collective-permute-start.22) | collective-permute-done | bytes 524320 | tf_op jit(solution)/shard_map/ppermute | solution.py:46
  95.9 1.7 %collective-permute-start.23 = (bf16[256,1024]{1,0:T(8,128)(2,1)S(1)}, bf16[256,1024]{1,0:T(8,128)(2,1)S(1)}, u32[]{:S(2)}, u32[]{:S(2)}) collective-permute-start(bf16[256,1024]{1,0:T(8,128)(2,1)S(1)} %get-tuple-element.61), channel_id=1, source_target_pairs={{0,4},{4,0},{8,12},{12,8},{1,5},{5,1},{9,13},{13,9},{2,6},{6,2},{1... | collective-permute-start | bytes 1572872 | tf_op jit(solution)/shard_map/ppermute | solution.py:46
  98.7 3.9 %collective-permute-start.25 = (bf16[256,1024]{1,0:T(8,128)(2,1)S(1)}, bf16[256,1024]{1,0:T(8,128)(2,1)S(1)}, u32[]{:S(2)}, u32[]{:S(2)}) collective-permute-start(bf16[256,1024]{1,0:T(8,128)(2,1)S(1)} %fusion.26), channel_id=1, source_target_pairs={{0,3},{1,2},{2,1},{3,0},{4,7},{5,6},{6,5},{7,4},{8,11},{9,10},{10,... | collective-permute-start | bytes 1572872 | tf_op jit(solution)/shard_map/ppermute | solution.py:42
  106.2 4.1 %collective-permute-done.29 = f32[64,1024]{1,0:T(8,128)S(1)} collective-permute-done((f32[64,1024]{1,0:T(8,128)S(1)}, f32[64,1024]{1,0:T(8,128)S(1)}, u32[]{:S(2)}, u32[]{:S(2)}) %collective-permute-start.29) | collective-permute-done | bytes 262176 | tf_op jit(solution)/shard_map/ppermute | solution.py:106
  113.5 5.1 %collective-permute-start.30 = (bf16[512,1024]{1,0:T(8,128)(2,1)S(1)}, bf16[512,1024]{1,0:T(8,128)(2,1)S(1)}, u32[]{:S(2)}, u32[]{:S(2)}) collective-permute-start(bf16[512,1024]{1,0:T(8,128)(2,1)S(1)} %get-tuple-element.93), channel_id=1, source_target_pairs={{0,16},{16,0},{1,17},{17,1},{2,18},{18,2},{3,19},{19,3},{4,20},{20... | collective-permute-start | bytes 3145736 | tf_op jit(solution)/shard_map/ppermute | solution.py:34
  119.8 2.7 %collective-permute-start.32 = (bf16[256,1024]{1,0:T(8,128)(2,1)S(1)}, bf16[256,1024]{1,0:T(8,128)(2,1)S(1)}, u32[]{:S(2)}, u32[]{:S(2)}) collective-permute-start(bf16[256,1024]{1,0:T(8,128)(2,1)S(1)} %fusion.21), channel_id=1, source_target_pairs={{0,3},{1,2},{2,1},{3,0},{4,7},{5,6},{6,5},{7,4},{8,11},{9,10},{10,... | collective-permute-start | bytes 1572872 | tf_op jit(solution)/shard_map/ppermute | solution.py:42
  123.5 4.0 %collective-permute-start.33 = (bf16[256,1024]{1,0:T(8,128)(2,1)S(1)}, bf16[256,1024]{1,0:T(8,128)(2,1)S(1)}, u32[]{:S(2)}, u32[]{:S(2)}) collective-permute-start(bf16[256,1024]{1,0:T(8,128)(2,1)S(1)} %add_convert_fusion.2), channel_id=1, source_target_pairs={{0,4},{4,0},{8,12},{12,8},{1,5},{5,1},{9,13},{13,9},{2,6},{6,2},{1... | collective-permute-start | bytes 1572872 | tf_op jit(solution)/shard_map/ppermute | solution.py:46
  129.6 2.1 %collective-permute-start.31 = (bf16[512,1024]{1,0:T(8,128)(2,1)S(1)}, bf16[512,1024]{1,0:T(8,128)(2,1)S(1)}, u32[]{:S(2)}, u32[]{:S(2)}) collective-permute-start(bf16[512,1024]{1,0:T(8,128)(2,1)S(1)} %add_convert_fusion), channel_id=1, source_target_pairs={{1,16},{2,19},{16,1},{19,2},{5,20},{6,23},{20,5},{23,6},{9,24},{10... | collective-permute-start | bytes 3145736 | tf_op jit(solution)/shard_map/ppermute | solution.py:30
  131.7 3.0 %collective-permute-done.32 = bf16[256,1024]{1,0:T(8,128)(2,1)S(1)} collective-permute-done((bf16[256,1024]{1,0:T(8,128)(2,1)S(1)}, bf16[256,1024]{1,0:T(8,128)(2,1)S(1)}, u32[]{:S(2)}, u32[]{:S(2)}) %collective-permute-start.32) | collective-permute-done | bytes 524320 | tf_op jit(solution)/shard_map/ppermute | solution.py:42
  134.7 4.6 %collective-permute-done.33 = bf16[256,1024]{1,0:T(8,128)(2,1)S(1)} collective-permute-done((bf16[256,1024]{1,0:T(8,128)(2,1)S(1)}, bf16[256,1024]{1,0:T(8,128)(2,1)S(1)}, u32[]{:S(2)}, u32[]{:S(2)}) %collective-permute-start.33) | collective-permute-done | bytes 524320 | tf_op jit(solution)/shard_map/ppermute | solution.py:46
  139.9 2.7 %collective-permute-start.35 = (bf16[256,1024]{1,0:T(8,128)(2,1)S(1)}, bf16[256,1024]{1,0:T(8,128)(2,1)S(1)}, u32[]{:S(2)}, u32[]{:S(2)}) collective-permute-start(bf16[256,1024]{1,0:T(8,128)(2,1)S(1)} %get-tuple-element.95), channel_id=1, source_target_pairs={{1,16},{2,19},{16,1},{19,2},{5,20},{6,23},{20,5},{23,6},{9,24},{10... | collective-permute-start | bytes 1572872 | tf_op jit(solution)/shard_map/ppermute | solution.py:30
  142.7 1.7 %multiply_subtract_fusion = (f32[256,1024]{1,0:T(8,128)}, f32[256,1024]{1,0:T(8,128)}) fusion(f32[256,1024]{1,0:T(8,128)S(1)} %copy-done.1, f32[128,1024]{1,0:T(8,128)S(1)} %maximum_select_fusion.2, f32[128,1024]{1,0:T(8,128)S(1)} %collective-permute-done.36, pred[]{:T(512)S(6)} %eq.41, f32[256,1024]{1,0:T(8,128)S(1)} %copy-done.2), kind=kLoop, calls=%fused_computation.70 | loop fusion | flops 2621440 | bytes 5242881 | tf_op jit(solution)/shard_map/sub | solution.py:228
  144.4 7.1 %collective-permute-done.35 = bf16[256,1024]{1,0:T(8,128)(2,1)S(1)} collective-permute-done((bf16[256,1024]{1,0:T(8,128)(2,1)S(1)}, bf16[256,1024]{1,0:T(8,128)(2,1)S(1)}, u32[]{:S(2)}, u32[]{:S(2)}) %collective-permute-start.35) | collective-permute-done | bytes 524320 | tf_op jit(solution)/shard_map/ppermute | solution.py:30
  151.5 3.4 %fusion.94 = (f32[1,256,1024]{2,1,0:T(8,128)}, bf16[1,256,1024]{2,1,0:T(8,128)(2,1)}, f32[1,256,1024]{2,1,0:T(8,128)}) fusion(f32[256,1024]{1,0:T(8,128)S(1)} %get-tuple-element.96, bf16[256,1024]{1,0:T(8,128)(2,1)S(1)} %collective-permute-done.35, pred[]{:T(512)S(6)} %eq.36, f32[1,256,1024]{2,1,0:T(8,128)S(1)} %copy-done.3, ...), kind=kLoop, calls=%fused_computation.132 | loop fusion | flops 4456448 | bytes 6815745 | tf_op jit(solution)/shard_map/broadcast_in_dim | solution.py:229
  (97 shorter events, 37.0 us)
Async XLA Ops:
  8.8 25.8 %collective-permute-start.8 = (bf16[4,512,512]{2,1,0:T(8,128)(2,1)}, bf16[4,512,512]{2,1,0:T(8,128)(2,1)S(1)}, u32[]{:S(2)}, u32[]{:S(2)}) collective-permute-start(bf16[4,512,512]{2,1,0:T(8,128)(2,1)} %get-tuple-element.42), channel_id=1, source_target_pairs={{0,16},{16,0},{1,17},{17,1},{2,18},{18,2},{3,19},{19,3},{4,20},{20... | collective-permute-start | bytes 6291464 | tf_op jit(solution)/shard_map/ppermute | solution.py:34
  12.0 11.0 %collective-permute-start.2 = (bf16[256,1024]{1,0:T(8,128)(2,1)}, bf16[256,1024]{1,0:T(8,128)(2,1)}, u32[]{:S(2)}, u32[]{:S(2)}) collective-permute-start(bf16[256,1024]{1,0:T(8,128)(2,1)} %bitcast), channel_id=1, source_target_pairs={{1,16},{2,19},{16,1},{19,2},{5,20},{6,23},{20,5},{23,6},{9,24},{10... | collective-permute-start | bytes 1572872 | tf_op jit(solution)/shard_map/ppermute | solution.py:30
  14.0 17.6 %collective-permute-start = (bf16[512,1024]{1,0:T(8,128)(2,1)}, bf16[512,1024]{1,0:T(8,128)(2,1)}, u32[]{:S(2)}, u32[]{:S(2)}) collective-permute-start(bf16[512,1024]{1,0:T(8,128)(2,1)} %param.9), channel_id=1, source_target_pairs={{0,16},{16,0},{1,17},{17,1},{2,18},{18,2},{3,19},{19,3},{4,20},{20... | collective-permute-start | bytes 3145736 | tf_op jit(solution)/shard_map/ppermute | solution.py:34
  24.3 17.3 %collective-permute-start.5 = (bf16[256,1024]{1,0:T(8,128)(2,1)S(1)}, bf16[256,1024]{1,0:T(8,128)(2,1)S(1)}, u32[]{:S(2)}, u32[]{:S(2)}) collective-permute-start(bf16[256,1024]{1,0:T(8,128)(2,1)S(1)} %broadcast_select_fusion.2), channel_id=1, source_target_pairs={{0,3},{1,2},{2,1},{3,0},{4,7},{5,6},{6,5},{7,4},{8,11},{9,10},{10,... | collective-permute-start | bytes 1572872 | tf_op jit(solution)/shard_map/ppermute | solution.py:42
  25.1 16.5 %collective-permute-start.4 = (bf16[256,1024]{1,0:T(8,128)(2,1)S(1)}, bf16[256,1024]{1,0:T(8,128)(2,1)S(1)}, u32[]{:S(2)}, u32[]{:S(2)}) collective-permute-start(bf16[256,1024]{1,0:T(8,128)(2,1)S(1)} %broadcast_select_fusion.2), channel_id=1, source_target_pairs={{4,8},{8,4},{5,9},{9,5},{6,10},{10,6},{7,11},{11,7},{20,24},{24,20... | collective-permute-start | bytes 1572872 | tf_op jit(solution)/shard_map/ppermute | solution.py:46
  25.8 15.8 %collective-permute-start.3 = (bf16[256,1024]{1,0:T(8,128)(2,1)S(1)}, bf16[256,1024]{1,0:T(8,128)(2,1)S(1)}, u32[]{:S(2)}, u32[]{:S(2)}) collective-permute-start(bf16[256,1024]{1,0:T(8,128)(2,1)S(1)} %broadcast_select_fusion.2), channel_id=1, source_target_pairs={{0,4},{4,0},{8,12},{12,8},{1,5},{5,1},{9,13},{13,9},{2,6},{6,2},{1... | collective-permute-start | bytes 1572872 | tf_op jit(solution)/shard_map/ppermute | solution.py:46
  33.1 13.1 %collective-permute-start.1 = (bf16[256,1024]{1,0:T(8,128)(2,1)S(1)}, bf16[256,1024]{1,0:T(8,128)(2,1)S(1)}, u32[]{:S(2)}, u32[]{:S(2)}) collective-permute-start(bf16[256,1024]{1,0:T(8,128)(2,1)S(1)} %dynamic-slice_select_fusion), channel_id=1, source_target_pairs={{0,1},{1,0},{2,3},{3,2},{4,5},{5,4},{6,7},{7,6},{8,9},{9,8},{10,11... | collective-permute-start | bytes 1572872 | tf_op jit(solution)/shard_map/ppermute | solution.py:38
  46.2 14.5 %collective-permute-start.17 = (bf16[256,1024]{1,0:T(8,128)(2,1)S(1)}, bf16[256,1024]{1,0:T(8,128)(2,1)S(1)}, u32[]{:S(2)}, u32[]{:S(2)}) collective-permute-start(bf16[256,1024]{1,0:T(8,128)(2,1)S(1)} %collective-permute-done.3), channel_id=1, source_target_pairs={{4,8},{8,4},{5,9},{9,5},{6,10},{10,6},{7,11},{11,7},{20,24},{24,20... | collective-permute-start | bytes 1572872 | tf_op jit(solution)/shard_map/ppermute | solution.py:46
  46.9 15.0 %collective-permute-start.14 = (bf16[256,1024]{1,0:T(8,128)(2,1)S(1)}, bf16[256,1024]{1,0:T(8,128)(2,1)S(1)}, u32[]{:S(2)}, u32[]{:S(2)}) collective-permute-start(bf16[256,1024]{1,0:T(8,128)(2,1)S(1)} %collective-permute-done.3), channel_id=1, source_target_pairs={{0,3},{1,2},{2,1},{3,0},{4,7},{5,6},{6,5},{7,4},{8,11},{9,10},{10,... | collective-permute-start | bytes 1572872 | tf_op jit(solution)/shard_map/ppermute | solution.py:42
  47.8 12.6 %collective-permute-start.9 = (bf16[512,512]{1,0:T(8,128)(2,1)S(1)}, bf16[512,512]{1,0:T(8,128)(2,1)S(1)}, u32[]{:S(2)}, u32[]{:S(2)}) collective-permute-start(bf16[512,512]{1,0:T(8,128)(2,1)S(1)} %get-tuple-element.47), channel_id=1, source_target_pairs={{0,1},{1,0},{2,3},{3,2},{4,5},{5,4},{6,7},{7,6},{8,9},{9,8},{10,11... | collective-permute-start | bytes 1572872 | tf_op jit(solution)/shard_map/ppermute | solution.py:38
  47.8 16.3 %collective-permute-start.20 = (bf16[256,1024]{1,0:T(8,128)(2,1)S(1)}, bf16[256,1024]{1,0:T(8,128)(2,1)S(1)}, u32[]{:S(2)}, u32[]{:S(2)}) collective-permute-start(bf16[256,1024]{1,0:T(8,128)(2,1)S(1)} %collective-permute-done.4), channel_id=1, source_target_pairs={{4,0},{8,12},{5,1},{9,13},{6,2},{10,14},{7,3},{11,15},{20,16},{24,... | collective-permute-start | bytes 1572872 | tf_op jit(solution)/shard_map/ppermute | solution.py:46
  49.1 12.3 %collective-permute-start.13 = (bf16[256,1024]{1,0:T(8,128)(2,1)S(1)}, bf16[256,1024]{1,0:T(8,128)(2,1)S(1)}, u32[]{:S(2)}, u32[]{:S(2)}) collective-permute-start(bf16[256,1024]{1,0:T(8,128)(2,1)S(1)} %collective-permute-done.1), channel_id=1, source_target_pairs={{0,16},{16,0},{1,17},{17,1},{2,18},{18,2},{3,19},{19,3},{4,20},{20... | collective-permute-start | bytes 1572872 | tf_op jit(solution)/shard_map/ppermute | solution.py:34
  60.4 11.7 %collective-permute-start.10 = (bf16[512,512]{1,0:T(8,128)(2,1)S(1)}, bf16[512,512]{1,0:T(8,128)(2,1)S(1)}, u32[]{:S(2)}, u32[]{:S(2)}) collective-permute-start(bf16[512,512]{1,0:T(8,128)(2,1)S(1)} %get-tuple-element.48), channel_id=1, source_target_pairs={{0,1},{1,0},{2,3},{3,2},{4,5},{5,4},{6,7},{7,6},{8,9},{9,8},{10,11... | collective-permute-start | bytes 1572872 | tf_op jit(solution)/shard_map/ppermute | solution.py:38
  60.6 11.9 %collective-permute-start.18 = (bf16[256,1024]{1,0:T(8,128)(2,1)S(1)}, bf16[256,1024]{1,0:T(8,128)(2,1)S(1)}, u32[]{:S(2)}, u32[]{:S(2)}) collective-permute-start(bf16[256,1024]{1,0:T(8,128)(2,1)S(1)} %collective-permute-done.5), channel_id=1, source_target_pairs={{4,8},{8,4},{5,9},{9,5},{6,10},{10,6},{7,11},{11,7},{20,24},{24,20... | collective-permute-start | bytes 1572872 | tf_op jit(solution)/shard_map/ppermute | solution.py:46
  61.8 16.5 %collective-permute-start.15 = (bf16[256,1024]{1,0:T(8,128)(2,1)S(1)}, bf16[256,1024]{1,0:T(8,128)(2,1)S(1)}, u32[]{:S(2)}, u32[]{:S(2)}) collective-permute-start(bf16[256,1024]{1,0:T(8,128)(2,1)S(1)} %fusion.28), channel_id=1, source_target_pairs={{0,3},{1,2},{2,1},{3,0},{4,7},{5,6},{6,5},{7,4},{8,11},{9,10},{10,... | collective-permute-start | bytes 1572872 | tf_op jit(solution)/shard_map/ppermute | solution.py:42
  67.1 15.7 %collective-permute-start.21 = (bf16[256,1024]{1,0:T(8,128)(2,1)S(1)}, bf16[256,1024]{1,0:T(8,128)(2,1)S(1)}, u32[]{:S(2)}, u32[]{:S(2)}) collective-permute-start(bf16[256,1024]{1,0:T(8,128)(2,1)S(1)} %collective-permute-done.17), channel_id=1, source_target_pairs={{4,0},{8,12},{5,1},{9,13},{6,2},{10,14},{7,3},{11,15},{20,16},{24,... | collective-permute-start | bytes 1572872 | tf_op jit(solution)/shard_map/ppermute | solution.py:46
  72.1 15.5 %collective-permute-start.11 = (bf16[512,512]{1,0:T(8,128)(2,1)S(1)}, bf16[512,512]{1,0:T(8,128)(2,1)S(1)}, u32[]{:S(2)}, u32[]{:S(2)}) collective-permute-start(bf16[512,512]{1,0:T(8,128)(2,1)S(1)} %get-tuple-element.49), channel_id=1, source_target_pairs={{0,1},{1,0},{2,3},{3,2},{4,5},{5,4},{6,7},{7,6},{8,9},{9,8},{10,11... | collective-permute-start | bytes 1572872 | tf_op jit(solution)/shard_map/ppermute | solution.py:38
  72.6 15.0 %collective-permute-start.27 = (bf16[32,1024]{1,0:T(8,128)(2,1)S(1)}, bf16[32,1024]{1,0:T(8,128)(2,1)S(1)}, u32[]{:S(2)}, u32[]{:S(2)}) collective-permute-start(bf16[32,1024]{1,0:T(8,128)(2,1)S(1)} %dynamic-slice_add_fusion.2), channel_id=1, source_target_pairs={{0,128},{128,0},{1,129},{129,1},{2,130},{130,2},{3,131},{131,3},{4... | collective-permute-start | bytes 196616 | tf_op jit(solution)/shard_map/ppermute | solution.py:106
  82.8 11.8 %collective-permute-start.22 = (bf16[256,1024]{1,0:T(8,128)(2,1)S(1)}, bf16[256,1024]{1,0:T(8,128)(2,1)S(1)}, u32[]{:S(2)}, u32[]{:S(2)}) collective-permute-start(bf16[256,1024]{1,0:T(8,128)(2,1)S(1)} %get-tuple-element.60), channel_id=1, source_target_pairs={{0,4},{4,0},{8,12},{12,8},{1,5},{5,1},{9,13},{13,9},{2,6},{6,2},{1... | collective-permute-start | bytes 1572872 | tf_op jit(solution)/shard_map/ppermute | solution.py:46
  84.2 11.1 %collective-permute-start.16 = (bf16[256,1024]{1,0:T(8,128)(2,1)S(1)}, bf16[256,1024]{1,0:T(8,128)(2,1)S(1)}, u32[]{:S(2)}, u32[]{:S(2)}) collective-permute-start(bf16[256,1024]{1,0:T(8,128)(2,1)S(1)} %fusion.29), channel_id=1, source_target_pairs={{0,3},{1,2},{2,1},{3,0},{4,7},{5,6},{6,5},{7,4},{8,11},{9,10},{10,... | collective-permute-start | bytes 1572872 | tf_op jit(solution)/shard_map/ppermute | solution.py:42
  87.6 23.8 %collective-permute-start.12 = (bf16[512,512]{1,0:T(8,128)(2,1)S(1)}, bf16[512,512]{1,0:T(8,128)(2,1)S(1)}, u32[]{:S(2)}, u32[]{:S(2)}) collective-permute-start(bf16[512,512]{1,0:T(8,128)(2,1)S(1)} %get-tuple-element.50), channel_id=1, source_target_pairs={{0,1},{1,0},{2,3},{3,2},{4,5},{5,4},{6,7},{7,6},{8,9},{9,8},{10,11... | collective-permute-start | bytes 1572872 | tf_op jit(solution)/shard_map/ppermute | solution.py:38
  88.5 16.2 %collective-permute-start.28 = (f32[32,1024]{1,0:T(8,128)S(1)}, f32[32,1024]{1,0:T(8,128)S(1)}, u32[]{:S(2)}, u32[]{:S(2)}) collective-permute-start(f32[32,1024]{1,0:T(8,128)S(1)} %convert_add_fusion), channel_id=1, source_target_pairs={{0,64},{32,96},{64,0},{96,32},{1,65},{33,97},{65,1},{97,33},{2,66}... | collective-permute-start | bytes 393224 | tf_op jit(solution)/shard_map/ppermute | solution.py:106
  95.9 15.5 %collective-permute-start.23 = (bf16[256,1024]{1,0:T(8,128)(2,1)S(1)}, bf16[256,1024]{1,0:T(8,128)(2,1)S(1)}, u32[]{:S(2)}, u32[]{:S(2)}) collective-permute-start(bf16[256,1024]{1,0:T(8,128)(2,1)S(1)} %get-tuple-element.61), channel_id=1, source_target_pairs={{0,4},{4,0},{8,12},{12,8},{1,5},{5,1},{9,13},{13,9},{2,6},{6,2},{1... | collective-permute-start | bytes 1572872 | tf_op jit(solution)/shard_map/ppermute | solution.py:46
  97.6 13.8 %collective-permute-start.24 = (bf16[256,1024]{1,0:T(8,128)(2,1)S(1)}, bf16[256,1024]{1,0:T(8,128)(2,1)S(1)}, u32[]{:S(2)}, u32[]{:S(2)}) collective-permute-start(bf16[256,1024]{1,0:T(8,128)(2,1)S(1)} %add_convert_fusion.3), channel_id=1, source_target_pairs={{4,8},{8,4},{5,9},{9,5},{6,10},{10,6},{7,11},{11,7},{20,24},{24,20... | collective-permute-start | bytes 1572872 | tf_op jit(solution)/shard_map/ppermute | solution.py:46
  98.7 12.1 %collective-permute-start.25 = (bf16[256,1024]{1,0:T(8,128)(2,1)S(1)}, bf16[256,1024]{1,0:T(8,128)(2,1)S(1)}, u32[]{:S(2)}, u32[]{:S(2)}) collective-permute-start(bf16[256,1024]{1,0:T(8,128)(2,1)S(1)} %fusion.26), channel_id=1, source_target_pairs={{0,3},{1,2},{2,1},{3,0},{4,7},{5,6},{6,5},{7,4},{8,11},{9,10},{10,... | collective-permute-start | bytes 1572872 | tf_op jit(solution)/shard_map/ppermute | solution.py:42
  113.5 14.9 %collective-permute-start.30 = (bf16[512,1024]{1,0:T(8,128)(2,1)S(1)}, bf16[512,1024]{1,0:T(8,128)(2,1)S(1)}, u32[]{:S(2)}, u32[]{:S(2)}) collective-permute-start(bf16[512,1024]{1,0:T(8,128)(2,1)S(1)} %get-tuple-element.93), channel_id=1, source_target_pairs={{0,16},{16,0},{1,17},{17,1},{2,18},{18,2},{3,19},{19,3},{4,20},{20... | collective-permute-start | bytes 3145736 | tf_op jit(solution)/shard_map/ppermute | solution.py:34
  119.8 14.8 %collective-permute-start.32 = (bf16[256,1024]{1,0:T(8,128)(2,1)S(1)}, bf16[256,1024]{1,0:T(8,128)(2,1)S(1)}, u32[]{:S(2)}, u32[]{:S(2)}) collective-permute-start(bf16[256,1024]{1,0:T(8,128)(2,1)S(1)} %fusion.21), channel_id=1, source_target_pairs={{0,3},{1,2},{2,1},{3,0},{4,7},{5,6},{6,5},{7,4},{8,11},{9,10},{10,... | collective-permute-start | bytes 1572872 | tf_op jit(solution)/shard_map/ppermute | solution.py:42
  122.6 12.0 %collective-permute-start.34 = (bf16[256,1024]{1,0:T(8,128)(2,1)S(1)}, bf16[256,1024]{1,0:T(8,128)(2,1)S(1)}, u32[]{:S(2)}, u32[]{:S(2)}) collective-permute-start(bf16[256,1024]{1,0:T(8,128)(2,1)S(1)} %add_convert_fusion.1), channel_id=1, source_target_pairs={{4,8},{8,4},{5,9},{9,5},{6,10},{10,6},{7,11},{11,7},{20,24},{24,20... | collective-permute-start | bytes 1572872 | tf_op jit(solution)/shard_map/ppermute | solution.py:46
  123.5 15.8 %collective-permute-start.33 = (bf16[256,1024]{1,0:T(8,128)(2,1)S(1)}, bf16[256,1024]{1,0:T(8,128)(2,1)S(1)}, u32[]{:S(2)}, u32[]{:S(2)}) collective-permute-start(bf16[256,1024]{1,0:T(8,128)(2,1)S(1)} %add_convert_fusion.2), channel_id=1, source_target_pairs={{0,4},{4,0},{8,12},{12,8},{1,5},{5,1},{9,13},{13,9},{2,6},{6,2},{1... | collective-permute-start | bytes 1572872 | tf_op jit(solution)/shard_map/ppermute | solution.py:46
  127.5 15.1 %collective-permute-start.36 = (f32[128,1024]{1,0:T(8,128)S(1)}, f32[128,1024]{1,0:T(8,128)S(1)}, u32[]{:S(2)}, u32[]{:S(2)}) collective-permute-start(f32[128,1024]{1,0:T(8,128)S(1)} %maximum_select_fusion.2), channel_id=1, source_target_pairs={{0,16},{16,0},{1,17},{17,1},{2,18},{18,2},{3,19},{19,3},{4,20},{20... | collective-permute-start | bytes 1572872 | tf_op jit(solution)/shard_map/ppermute | solution.py:106
  129.6 25.3 %collective-permute-start.31 = (bf16[512,1024]{1,0:T(8,128)(2,1)S(1)}, bf16[512,1024]{1,0:T(8,128)(2,1)S(1)}, u32[]{:S(2)}, u32[]{:S(2)}) collective-permute-start(bf16[512,1024]{1,0:T(8,128)(2,1)S(1)} %add_convert_fusion), channel_id=1, source_target_pairs={{1,16},{2,19},{16,1},{19,2},{5,20},{6,23},{20,5},{23,6},{9,24},{10... | collective-permute-start | bytes 3145736 | tf_op jit(solution)/shard_map/ppermute | solution.py:30
  139.9 11.6 %collective-permute-start.35 = (bf16[256,1024]{1,0:T(8,128)(2,1)S(1)}, bf16[256,1024]{1,0:T(8,128)(2,1)S(1)}, u32[]{:S(2)}, u32[]{:S(2)}) collective-permute-start(bf16[256,1024]{1,0:T(8,128)(2,1)S(1)} %get-tuple-element.95), channel_id=1, source_target_pairs={{1,16},{2,19},{16,1},{19,2},{5,20},{6,23},{20,5},{23,6},{9,24},{10... | collective-permute-start | bytes 1572872 | tf_op jit(solution)/shard_map/ppermute | solution.py:30
  (10 other events, 92.0 us)

commit v11 on v10

--- a/solution.py
+++ b/solution.py
@@ -62,26 +62,30 @@
     return together(array, *earlier)[0]
 
 
-def move(_, a, b, to_a, to_b):
-    to_a[0] = a[...]
-    to_b[0] = b[...]
+def move(_, a0, a1, b0, b1, to_a, to_b):
+    to_a[0, :, :256] = a0[...]
+    to_a[0, :, 256:] = a1[...]
+    to_b[0, :, :256] = b0[...]
+    to_b[0, :, 256:] = b1[...]
 
 
 def halves(tokens, blocks):
-    spec = lambda i: pl.BlockSpec((512, 256), lambda n, table: (0, table[i, n]))
-    out = pl.BlockSpec((1, 512, 256), lambda n, table: (n // 2, 0, n % 2))
+    def spec(half, place):
+        return pl.BlockSpec((512, 256), lambda n, table: (0, table[half, 2 * n + place]))
+
+    out = pl.BlockSpec((1, 512, 512), lambda n, table: (n, 0, 0))
     kind = jax.ShapeDtypeStruct((4, 512, 512), bf16)
     return pl.pallas_call(
         move,
         grid_spec=pltpu.PrefetchScalarGridSpec(
             num_scalar_prefetch=1,
-            grid=(8,),
-            in_specs=[spec(0), spec(1)],
+            grid=(4,),
+            in_specs=[spec(half, place) for half in range(2) for place in range(2)],
             out_specs=[out, out],
         ),
         out_shape=[kind, kind],
         cost_estimate=pl.CostEstimate(flops=0, bytes_accessed=16 << 20, transcendentals=0),
-    )(blocks, tokens, tokens)
+    )(blocks, tokens, tokens, tokens, tokens)
 
 
 class Drift:
@@ -137,14 +141,16 @@
         [4 * order[k] + q for half in (theirs, mine) for k in range(4) for q in (half, 3 - half)]
     ).reshape(2, 8)
 
-    w = jnp.where(stays, weight, swap(weight))
-    g_sib = core(key_grad)
-    x_give, x_own = halves(tokens, blocks.astype(jnp.int32))
-    x_sib = core(x_give)
     drift = Drift(anchor - local_params[0].astype(f32), c, y)
-    drift.take(drift.send())
+    w, g_sib, d, blocks, drift.v = together(
+        swap(weight), core(key_grad), drift.send(), blocks.astype(jnp.int32), drift.v
+    )
+    drift.take(d)
+    w = jnp.where(stays, weight, w)
     g_a = jnp.where(stays, key_grad, g_sib)
     g_l = lax.dynamic_slice_in_dim(jnp.where(stays, g_sib, key_grad), c * 256, 256, 0)
+    x_give, x_own = halves(tokens, blocks)
+    x_sib = core(x_give)
 
     got = (beside(g_l), line(w, PAIRS), line(w, MIDDLE), across(w), drift.send())
     leave = [jnp.where(stays, x_sib[k], x_own[k]) for k in range(4)]

time: 157 us -> 148 us (0.943)
  waiting for transfers between devices: 54.6 us -> 50.5 us
  other arithmetic: 15.3 us -> 11.9 us
  Pallas kernels: 7.37 us -> 5.44 us
    ppermute x6, starting transfers between devices: 13.9 us -> 8.06 us  [across(): return lax.ppermute(v, 'x', ACROSS)]
    ppermute x5, waiting for transfers between devices: 15.1 us -> 11.3 us  [beside(): return lax.ppermute(v, 'x', BESIDE)]
    ppermute x4, starting transfers between devices: 9.43 us -> 13 us  [core(): return lax.ppermute(v, 'c', CORE)]
    ppermute x12, starting transfers between devices: 17.9 us -> 20.4 us  [line(): return lax.ppermute(v, 'zl', pairs)]
    pallas_call x1, Pallas kernels: 7.37 us -> 5.44 us  [halves(): pl.pallas_call(move, grid_spec=pltpu.PrefetchScalarGridSpec(num_scalar_pr...]
  transfers between devices with their start and end apart: 37 -> 37, of which waited for: 14 -> 13; matrix products, arithmetic and copies ran while one was open for 16% -> 15% of each run, Pallas kernels for 0% -> 0%
where the time goes in v11:
time: 148 us; the launch traced here: 147 us
  starting transfers between devices  63.9 us (43%)
  waiting for transfers between devices  50.5 us (34%)
  matrix products  12.5 us (8%)
  other arithmetic  11.9 us (8%)
  Pallas kernels  5.44 us (4%)
  local copies, waits for them, and re-layouts  1.68 us (1%)
    ppermute x12, starting transfers between devices, line(): return lax.ppermute(v, 'zl', pairs)  20.4 us
    ppermute x7, starting transfers between devices, send(): return lax.ppermute(self.sent, axis, perm)  14.1 us
    ppermute x3, waiting for transfers between devices, swap(): return lax.ppermute(v, ('c', 'x'), SWAP)  13.4 us
    ppermute x4, starting transfers between devices, core(): return lax.ppermute(v, 'c', CORE)  13 us
    ppermute x12, waiting for transfers between devices, line(): return lax.ppermute(v, 'zl', pairs)  12.6 us
    ppermute x5, waiting for transfers between devices, beside(): return lax.ppermute(v, 'x', BESIDE)  11.3 us
    ppermute x7, waiting for transfers between devices, send(): return lax.ppermute(self.sent, axis, perm)  9.61 us
    ppermute x6, starting transfers between devices, across(): return lax.ppermute(v, 'x', ACROSS)  8.06 us
  transfers between devices with their start and end apart: 37, of which 13 were waited for; matrix products, arithmetic and copies ran while one was open for 15% of the time, Pallas kernels for 0%

profile of v11, /device:TPU:1, one launch (start us, length us, event | category | flops | bytes accessed | tf_op | source)
XLA Modules:
  0.0 147.2 jit_solution(9930663534827026717)
XLA Ops:
  0.6 3.3 %collective-permute-start.1 = (bf16[512,1024]{1,0:T(8,128)(2,1)}, bf16[512,1024]{1,0:T(8,128)(2,1)S(1)}, u32[]{:S(2)}, u32[]{:S(2)}) collective-permute-start(bf16[512,1024]{1,0:T(8,128)(2,1)} %param.9), channel_id=1, source_target_pairs={{0,16},{16,0},{1,17},{17,1},{2,18},{18,2},{3,19},{19,3},{4,20},{20... | collective-permute-start | bytes 3145736 | tf_op jit(solution)/shard_map/ppermute | solution.py:34
  4.0 1.9 %collective-permute-start = (bf16[256,1024]{1,0:T(8,128)(2,1)}, bf16[256,1024]{1,0:T(8,128)(2,1)S(1)}, u32[]{:S(2)}, u32[]{:S(2)}) collective-permute-start(bf16[256,1024]{1,0:T(8,128)(2,1)} %bitcast.68), channel_id=1, source_target_pairs={{1,16},{2,19},{16,1},{19,2},{5,20},{6,23},{20,5},{23,6},{9,24},{10... | collective-permute-start | bytes 1572872 | tf_op jit(solution)/shard_map/ppermute | solution.py:30
  5.9 1.5 %convert_subtract_fusion.1 = f32[256,1024]{1,0:T(8,128)S(1)} fusion(f32[256,1024]{1,0:T(8,128)} %param.14, bf16[1,256,1024]{2,1,0:T(8,128)(2,1)} %param.13), kind=kLoop, calls=%fused_computation.68 | loop fusion | flops 524288 | bytes 2621440 | tf_op jit(solution)/shard_map/sub | solution.py:144
  9.0 5.7 %collective-permute-done = bf16[256,1024]{1,0:T(8,128)(2,1)S(1)} collective-permute-done((bf16[256,1024]{1,0:T(8,128)(2,1)}, bf16[256,1024]{1,0:T(8,128)(2,1)S(1)}, u32[]{:S(2)}, u32[]{:S(2)}) %collective-permute-start) | collective-permute-done | bytes 524320 | tf_op jit(solution)/shard_map/ppermute | solution.py:30
  14.7 5.4 %shard_map.127 = (bf16[4,512,512]{2,1,0:T(8,128)(2,1)}, bf16[4,512,512]{2,1,0:T(8,128)(2,1)}) custom-call(s32[2,8]{1,0:T(2,128)} %reshape.37._, bf16[512,4096]{1,0:T(8,128)(2,1)} %b1.1, bf16[512,4096]{1,0:T(8,128)(2,1)} %b1.1, bf16[512,4096]{1,0:T(8,128)(2,1)} %b1.1, bf16[512,4096]{1,0:T(8,128)(2,1)} %b1.1), custom_call_target="tpu_custom_call" | custom-call | bytes 16777216 | tf_op jit(solution)/shard_map/pallas_call | solution.py:78
  20.3 1.4 broadcast_select_fusion.2
  23.3 4.6 %collective-permute-start.4 = (bf16[256,1024]{1,0:T(8,128)(2,1)S(1)}, bf16[256,1024]{1,0:T(8,128)(2,1)S(1)}, u32[]{:S(2)}, u32[]{:S(2)}) collective-permute-start(bf16[256,1024]{1,0:T(8,128)(2,1)S(1)} %broadcast_select_fusion.2), channel_id=1, source_target_pairs={{0,4},{4,0},{8,12},{12,8},{1,5},{5,1},{9,13},{13,9},{2,6},{6,2},{1... | collective-permute-start | bytes 1572872 | tf_op jit(solution)/shard_map/ppermute | solution.py:46
  27.9 1.4 dynamic-slice_select_fusion
  29.6 1.4 collective-permute-start.7
  31.4 5.1 %collective-permute-done.7 = f32[64,1024]{1,0:T(8,128)S(1)} collective-permute-done((f32[64,1024]{1,0:T(8,128)S(1)}, f32[64,1024]{1,0:T(8,128)S(1)}, u32[]{:S(2)}, u32[]{:S(2)}) %collective-permute-start.7) | collective-permute-done | bytes 262176 | tf_op jit(solution)/shard_map/ppermute | solution.py:110
  36.4 5.2 %collective-permute-done.3 = bf16[256,1024]{1,0:T(8,128)(2,1)S(1)} collective-permute-done((bf16[256,1024]{1,0:T(8,128)(2,1)S(1)}, bf16[256,1024]{1,0:T(8,128)(2,1)S(1)}, u32[]{:S(2)}, u32[]{:S(2)}) %collective-permute-start.3) | collective-permute-done | bytes 524320 | tf_op jit(solution)/shard_map/ppermute | solution.py:38
  44.2 2.2 %collective-permute-start.13 = (bf16[256,1024]{1,0:T(8,128)(2,1)S(1)}, bf16[256,1024]{1,0:T(8,128)(2,1)S(1)}, u32[]{:S(2)}, u32[]{:S(2)}) collective-permute-start(bf16[256,1024]{1,0:T(8,128)(2,1)S(1)} %collective-permute-done.3), channel_id=1, source_target_pairs={{0,16},{16,0},{1,17},{17,1},{2,18},{18,2},{3,19},{19,3},{4,20},{20... | collective-permute-start | bytes 1572872 | tf_op jit(solution)/shard_map/ppermute | solution.py:34
  48.7 5.1 %collective-permute-done.9 = bf16[512,512]{1,0:T(8,128)(2,1)S(1)} collective-permute-done((bf16[512,512]{1,0:T(8,128)(2,1)S(1)}, bf16[512,512]{1,0:T(8,128)(2,1)S(1)}, u32[]{:S(2)}, u32[]{:S(2)}) %collective-permute-start.9) | collective-permute-done | bytes 524320 | tf_op jit(solution)/shard_map/ppermute | solution.py:38
  55.7 2.2 %collective-permute-start.15 = (bf16[256,1024]{1,0:T(8,128)(2,1)S(1)}, bf16[256,1024]{1,0:T(8,128)(2,1)S(1)}, u32[]{:S(2)}, u32[]{:S(2)}) collective-permute-start(bf16[256,1024]{1,0:T(8,128)(2,1)S(1)} %fusion.28), channel_id=1, source_target_pairs={{0,3},{1,2},{2,1},{3,0},{4,7},{5,6},{6,5},{7,4},{8,11},{9,10},{10,... | collective-permute-start | bytes 1572872 | tf_op jit(solution)/shard_map/ppermute | solution.py:42
  57.9 3.0 %collective-permute-start.26 = (f32[32,1024]{1,0:T(8,128)S(1)}, f32[32,1024]{1,0:T(8,128)S(1)}, u32[]{:S(2)}, u32[]{:S(2)}) collective-permute-start(f32[32,1024]{1,0:T(8,128)S(1)} %constant_dynamic-slice_fusion), channel_id=1, source_target_pairs={{0,64},{32,96},{64,0},{96,32},{1,65},{33,97},{65,1},{97,33},{2,66}... | collective-permute-start | bytes 393224 | tf_op jit(solution)/shard_map/ppermute | solution.py:110
  65.2 5.1 %collective-permute-start.27 = (bf16[32,1024]{1,0:T(8,128)(2,1)S(1)}, bf16[32,1024]{1,0:T(8,128)(2,1)S(1)}, u32[]{:S(2)}, u32[]{:S(2)}) collective-permute-start(bf16[32,1024]{1,0:T(8,128)(2,1)S(1)} %dynamic-slice_add_fusion.2), channel_id=1, source_target_pairs={{0,128},{128,0},{1,129},{129,1},{2,130},{130,2},{3,131},{131,3},{4... | collective-permute-start | bytes 196616 | tf_op jit(solution)/shard_map/ppermute | solution.py:110
  71.5 3.8 %collective-permute-done.21 = bf16[256,1024]{1,0:T(8,128)(2,1)S(1)} collective-permute-done((bf16[256,1024]{1,0:T(8,128)(2,1)S(1)}, bf16[256,1024]{1,0:T(8,128)(2,1)S(1)}, u32[]{:S(2)}, u32[]{:S(2)}) %collective-permute-start.21) | collective-permute-done | bytes 524320 | tf_op jit(solution)/shard_map/ppermute | solution.py:46
  75.3 2.9 %collective-permute-start.22 = (bf16[256,1024]{1,0:T(8,128)(2,1)S(1)}, bf16[256,1024]{1,0:T(8,128)(2,1)S(1)}, u32[]{:S(2)}, u32[]{:S(2)}) collective-permute-start(bf16[256,1024]{1,0:T(8,128)(2,1)S(1)} %get-tuple-element.70), channel_id=1, source_target_pairs={{0,4},{4,0},{8,12},{12,8},{1,5},{5,1},{9,13},{13,9},{2,6},{6,2},{1... | collective-permute-start | bytes 1572872 | tf_op jit(solution)/shard_map/ppermute | solution.py:46
  78.7 2.0 %collective-permute-start.16 = (bf16[256,1024]{1,0:T(8,128)(2,1)S(1)}, bf16[256,1024]{1,0:T(8,128)(2,1)S(1)}, u32[]{:S(2)}, u32[]{:S(2)}) collective-permute-start(bf16[256,1024]{1,0:T(8,128)(2,1)S(1)} %fusion.29), channel_id=1, source_target_pairs={{0,3},{1,2},{2,1},{3,0},{4,7},{5,6},{6,5},{7,4},{8,11},{9,10},{10,... | collective-permute-start | bytes 1572872 | tf_op jit(solution)/shard_map/ppermute | solution.py:42
  81.2 2.9 %collective-permute-start.28 = (f32[32,1024]{1,0:T(8,128)S(1)}, f32[32,1024]{1,0:T(8,128)S(1)}, u32[]{:S(2)}, u32[]{:S(2)}) collective-permute-start(f32[32,1024]{1,0:T(8,128)S(1)} %convert_add_fusion), channel_id=1, source_target_pairs={{0,64},{32,96},{64,0},{96,32},{1,65},{33,97},{65,1},{97,33},{2,66}... | collective-permute-start | bytes 393224 | tf_op jit(solution)/shard_map/ppermute | solution.py:110
  84.1 4.5 %collective-permute-done.22 = bf16[256,1024]{1,0:T(8,128)(2,1)S(1)} collective-permute-done((bf16[256,1024]{1,0:T(8,128)(2,1)S(1)}, bf16[256,1024]{1,0:T(8,128)(2,1)S(1)}, u32[]{:S(2)}, u32[]{:S(2)}) %collective-permute-start.22) | collective-permute-done | bytes 524320 | tf_op jit(solution)/shard_map/ppermute | solution.py:46
  97.4 3.5 %collective-permute-done.29 = f32[64,1024]{1,0:T(8,128)S(1)} collective-permute-done((f32[64,1024]{1,0:T(8,128)S(1)}, f32[64,1024]{1,0:T(8,128)S(1)}, u32[]{:S(2)}, u32[]{:S(2)}) %collective-permute-start.29) | collective-permute-done | bytes 262176 | tf_op jit(solution)/shard_map/ppermute | solution.py:110
  103.8 7.4 %collective-permute-start.30 = (bf16[512,1024]{1,0:T(8,128)(2,1)S(1)}, bf16[512,1024]{1,0:T(8,128)(2,1)S(1)}, u32[]{:S(2)}, u32[]{:S(2)}) collective-permute-start(bf16[512,1024]{1,0:T(8,128)(2,1)S(1)} %get-tuple-element.103), channel_id=1, source_target_pairs={{0,16},{16,0},{1,17},{17,1},{2,18},{18,2},{3,19},{19,3},{4,20},{20... | collective-permute-start | bytes 3145736 | tf_op jit(solution)/shard_map/ppermute | solution.py:34
  112.5 1.5 %collective-permute-start.32 = (bf16[256,1024]{1,0:T(8,128)(2,1)S(1)}, bf16[256,1024]{1,0:T(8,128)(2,1)S(1)}, u32[]{:S(2)}, u32[]{:S(2)}) collective-permute-start(bf16[256,1024]{1,0:T(8,128)(2,1)S(1)} %fusion.21), channel_id=1, source_target_pairs={{0,3},{1,2},{2,1},{3,0},{4,7},{5,6},{6,5},{7,4},{8,11},{9,10},{10,... | collective-permute-start | bytes 1572872 | tf_op jit(solution)/shard_map/ppermute | solution.py:42
  115.0 4.9 %collective-permute-start.33 = (bf16[256,1024]{1,0:T(8,128)(2,1)S(1)}, bf16[256,1024]{1,0:T(8,128)(2,1)S(1)}, u32[]{:S(2)}, u32[]{:S(2)}) collective-permute-start(bf16[256,1024]{1,0:T(8,128)(2,1)S(1)} %add_convert_fusion.2), channel_id=1, source_target_pairs={{0,4},{4,0},{8,12},{12,8},{1,5},{5,1},{9,13},{13,9},{2,6},{6,2},{1... | collective-permute-start | bytes 1572872 | tf_op jit(solution)/shard_map/ppermute | solution.py:46
  121.9 2.1 %collective-permute-start.31 = (bf16[512,1024]{1,0:T(8,128)(2,1)S(1)}, bf16[512,1024]{1,0:T(8,128)(2,1)S(1)}, u32[]{:S(2)}, u32[]{:S(2)}) collective-permute-start(bf16[512,1024]{1,0:T(8,128)(2,1)S(1)} %add_convert_fusion), channel_id=1, source_target_pairs={{1,16},{2,19},{16,1},{19,2},{5,20},{6,23},{20,5},{23,6},{9,24},{10... | collective-permute-start | bytes 3145736 | tf_op jit(solution)/shard_map/ppermute | solution.py:30
  124.0 3.3 %collective-permute-done.32 = bf16[256,1024]{1,0:T(8,128)(2,1)S(1)} collective-permute-done((bf16[256,1024]{1,0:T(8,128)(2,1)S(1)}, bf16[256,1024]{1,0:T(8,128)(2,1)S(1)}, u32[]{:S(2)}, u32[]{:S(2)}) %collective-permute-start.32) | collective-permute-done | bytes 524320 | tf_op jit(solution)/shard_map/ppermute | solution.py:42
  127.3 4.3 %collective-permute-done.33 = bf16[256,1024]{1,0:T(8,128)(2,1)S(1)} collective-permute-done((bf16[256,1024]{1,0:T(8,128)(2,1)S(1)}, bf16[256,1024]{1,0:T(8,128)(2,1)S(1)}, u32[]{:S(2)}, u32[]{:S(2)}) %collective-permute-start.33) | collective-permute-done | bytes 524320 | tf_op jit(solution)/shard_map/ppermute | solution.py:46
  132.3 2.1 %collective-permute-start.35 = (bf16[256,1024]{1,0:T(8,128)(2,1)S(1)}, bf16[256,1024]{1,0:T(8,128)(2,1)S(1)}, u32[]{:S(2)}, u32[]{:S(2)}) collective-permute-start(bf16[256,1024]{1,0:T(8,128)(2,1)S(1)} %get-tuple-element.105), channel_id=1, source_target_pairs={{1,16},{2,19},{16,1},{19,2},{5,20},{6,23},{20,5},{23,6},{9,24},{10... | collective-permute-start | bytes 1572872 | tf_op jit(solution)/shard_map/ppermute | solution.py:30
  134.4 1.7 %multiply_subtract_fusion = (f32[256,1024]{1,0:T(8,128)}, f32[256,1024]{1,0:T(8,128)}) fusion(f32[256,1024]{1,0:T(8,128)S(1)} %copy-done.1, f32[128,1024]{1,0:T(8,128)S(1)} %maximum_select_fusion.2, f32[128,1024]{1,0:T(8,128)S(1)} %collective-permute-done.36, pred[]{:T(512)S(6)} %eq.41, f32[256,1024]{1,0:T(8,128)S(1)} %copy-done.6), kind=kLoop, calls=%fused_computation.70 | loop fusion | flops 2621440 | bytes 5242881 | tf_op jit(solution)/shard_map/sub | solution.py:234
  136.1 7.7 %collective-permute-done.35 = bf16[256,1024]{1,0:T(8,128)(2,1)S(1)} collective-permute-done((bf16[256,1024]{1,0:T(8,128)(2,1)S(1)}, bf16[256,1024]{1,0:T(8,128)(2,1)S(1)}, u32[]{:S(2)}, u32[]{:S(2)}) %collective-permute-start.35) | collective-permute-done | bytes 524320 | tf_op jit(solution)/shard_map/ppermute | solution.py:30
  143.8 2.3 %fusion.94 = (f32[1,256,1024]{2,1,0:T(8,128)}, bf16[1,256,1024]{2,1,0:T(8,128)(2,1)}, f32[1,256,1024]{2,1,0:T(8,128)}) fusion(f32[256,1024]{1,0:T(8,128)S(1)} %get-tuple-element.106, bf16[256,1024]{1,0:T(8,128)(2,1)S(1)} %collective-permute-done.35, pred[]{:T(512)S(6)} %eq.36, f32[1,256,1024]{2,1,0:T(8,128)S(1)} %copy-done.7, ...), kind=kLoop, calls=%fused_computation.132 | loop fusion | flops 4456448 | bytes 6815745 | tf_op jit(solution)/shard_map/broadcast_in_dim | solution.py:235
  (111 shorter events, 34.6 us)
Async XLA Ops:
  0.6 14.0 %collective-permute-start.1 = (bf16[512,1024]{1,0:T(8,128)(2,1)}, bf16[512,1024]{1,0:T(8,128)(2,1)S(1)}, u32[]{:S(2)}, u32[]{:S(2)}) collective-permute-start(bf16[512,1024]{1,0:T(8,128)(2,1)} %param.9), channel_id=1, source_target_pairs={{0,16},{16,0},{1,17},{17,1},{2,18},{18,2},{3,19},{19,3},{4,20},{20... | collective-permute-start | bytes 3145736 | tf_op jit(solution)/shard_map/ppermute | solution.py:34
  4.0 10.7 %collective-permute-start = (bf16[256,1024]{1,0:T(8,128)(2,1)}, bf16[256,1024]{1,0:T(8,128)(2,1)S(1)}, u32[]{:S(2)}, u32[]{:S(2)}) collective-permute-start(bf16[256,1024]{1,0:T(8,128)(2,1)} %bitcast.68), channel_id=1, source_target_pairs={{1,16},{2,19},{16,1},{19,2},{5,20},{6,23},{20,5},{23,6},{9,24},{10... | collective-permute-start | bytes 1572872 | tf_op jit(solution)/shard_map/ppermute | solution.py:30
  20.1 9.5 %collective-permute-start.8 = (bf16[4,512,512]{2,1,0:T(8,128)(2,1)}, bf16[4,512,512]{2,1,0:T(8,128)(2,1)S(1)}, u32[]{:S(2)}, u32[]{:S(2)}) collective-permute-start(bf16[4,512,512]{2,1,0:T(8,128)(2,1)} %get-tuple-element.52), channel_id=1, source_target_pairs={{0,16},{16,0},{1,17},{17,1},{2,18},{18,2},{3,19},{19,3},{4,20},{20... | collective-permute-start | bytes 6291464 | tf_op jit(solution)/shard_map/ppermute | solution.py:34
  21.8 19.9 %collective-permute-start.6 = (bf16[256,1024]{1,0:T(8,128)(2,1)S(1)}, bf16[256,1024]{1,0:T(8,128)(2,1)S(1)}, u32[]{:S(2)}, u32[]{:S(2)}) collective-permute-start(bf16[256,1024]{1,0:T(8,128)(2,1)S(1)} %broadcast_select_fusion.2), channel_id=1, source_target_pairs={{0,3},{1,2},{2,1},{3,0},{4,7},{5,6},{6,5},{7,4},{8,11},{9,10},{10,... | collective-permute-start | bytes 1572872 | tf_op jit(solution)/shard_map/ppermute | solution.py:42
  22.6 19.1 %collective-permute-start.5 = (bf16[256,1024]{1,0:T(8,128)(2,1)S(1)}, bf16[256,1024]{1,0:T(8,128)(2,1)S(1)}, u32[]{:S(2)}, u32[]{:S(2)}) collective-permute-start(bf16[256,1024]{1,0:T(8,128)(2,1)S(1)} %broadcast_select_fusion.2), channel_id=1, source_target_pairs={{4,8},{8,4},{5,9},{9,5},{6,10},{10,6},{7,11},{11,7},{20,24},{24,20... | collective-permute-start | bytes 1572872 | tf_op jit(solution)/shard_map/ppermute | solution.py:46
  23.3 18.4 %collective-permute-start.4 = (bf16[256,1024]{1,0:T(8,128)(2,1)S(1)}, bf16[256,1024]{1,0:T(8,128)(2,1)S(1)}, u32[]{:S(2)}, u32[]{:S(2)}) collective-permute-start(bf16[256,1024]{1,0:T(8,128)(2,1)S(1)} %broadcast_select_fusion.2), channel_id=1, source_target_pairs={{0,4},{4,0},{8,12},{12,8},{1,5},{5,1},{9,13},{13,9},{2,6},{6,2},{1... | collective-permute-start | bytes 1572872 | tf_op jit(solution)/shard_map/ppermute | solution.py:46
  29.3 12.4 %collective-permute-start.3 = (bf16[256,1024]{1,0:T(8,128)(2,1)S(1)}, bf16[256,1024]{1,0:T(8,128)(2,1)S(1)}, u32[]{:S(2)}, u32[]{:S(2)}) collective-permute-start(bf16[256,1024]{1,0:T(8,128)(2,1)S(1)} %dynamic-slice_select_fusion), channel_id=1, source_target_pairs={{0,1},{1,0},{2,3},{3,2},{4,5},{5,4},{6,7},{7,6},{8,9},{9,8},{10,11... | collective-permute-start | bytes 1572872 | tf_op jit(solution)/shard_map/ppermute | solution.py:38
  41.7 12.8 %collective-permute-start.17 = (bf16[256,1024]{1,0:T(8,128)(2,1)S(1)}, bf16[256,1024]{1,0:T(8,128)(2,1)S(1)}, u32[]{:S(2)}, u32[]{:S(2)}) collective-permute-start(bf16[256,1024]{1,0:T(8,128)(2,1)S(1)} %collective-permute-done.4), channel_id=1, source_target_pairs={{4,8},{8,4},{5,9},{9,5},{6,10},{10,6},{7,11},{11,7},{20,24},{24,20... | collective-permute-start | bytes 1572872 | tf_op jit(solution)/shard_map/ppermute | solution.py:46
  42.4 13.3 %collective-permute-start.14 = (bf16[256,1024]{1,0:T(8,128)(2,1)S(1)}, bf16[256,1024]{1,0:T(8,128)(2,1)S(1)}, u32[]{:S(2)}, u32[]{:S(2)}) collective-permute-start(bf16[256,1024]{1,0:T(8,128)(2,1)S(1)} %collective-permute-done.4), channel_id=1, source_target_pairs={{0,3},{1,2},{2,1},{3,0},{4,7},{5,6},{6,5},{7,4},{8,11},{9,10},{10,... | collective-permute-start | bytes 1572872 | tf_op jit(solution)/shard_map/ppermute | solution.py:42
  42.7 11.1 %collective-permute-start.9 = (bf16[512,512]{1,0:T(8,128)(2,1)S(1)}, bf16[512,512]{1,0:T(8,128)(2,1)S(1)}, u32[]{:S(2)}, u32[]{:S(2)}) collective-permute-start(bf16[512,512]{1,0:T(8,128)(2,1)S(1)} %get-tuple-element.57), channel_id=1, source_target_pairs={{0,1},{1,0},{2,3},{3,2},{4,5},{5,4},{6,7},{7,6},{8,9},{9,8},{10,11... | collective-permute-start | bytes 1572872 | tf_op jit(solution)/shard_map/ppermute | solution.py:38
  42.9 15.0 %collective-permute-start.20 = (bf16[256,1024]{1,0:T(8,128)(2,1)S(1)}, bf16[256,1024]{1,0:T(8,128)(2,1)S(1)}, u32[]{:S(2)}, u32[]{:S(2)}) collective-permute-start(bf16[256,1024]{1,0:T(8,128)(2,1)S(1)} %collective-permute-done.5), channel_id=1, source_target_pairs={{4,0},{8,12},{5,1},{9,13},{6,2},{10,14},{7,3},{11,15},{20,16},{24,... | collective-permute-start | bytes 1572872 | tf_op jit(solution)/shard_map/ppermute | solution.py:46
  44.2 11.0 %collective-permute-start.13 = (bf16[256,1024]{1,0:T(8,128)(2,1)S(1)}, bf16[256,1024]{1,0:T(8,128)(2,1)S(1)}, u32[]{:S(2)}, u32[]{:S(2)}) collective-permute-start(bf16[256,1024]{1,0:T(8,128)(2,1)S(1)} %collective-permute-done.3), channel_id=1, source_target_pairs={{0,16},{16,0},{1,17},{17,1},{2,18},{18,2},{3,19},{19,3},{4,20},{20... | collective-permute-start | bytes 1572872 | tf_op jit(solution)/shard_map/ppermute | solution.py:34
  53.8 10.4 %collective-permute-start.10 = (bf16[512,512]{1,0:T(8,128)(2,1)S(1)}, bf16[512,512]{1,0:T(8,128)(2,1)S(1)}, u32[]{:S(2)}, u32[]{:S(2)}) collective-permute-start(bf16[512,512]{1,0:T(8,128)(2,1)S(1)} %get-tuple-element.58), channel_id=1, source_target_pairs={{0,1},{1,0},{2,3},{3,2},{4,5},{5,4},{6,7},{7,6},{8,9},{9,8},{10,11... | collective-permute-start | bytes 1572872 | tf_op jit(solution)/shard_map/ppermute | solution.py:38
  54.5 10.7 %collective-permute-start.18 = (bf16[256,1024]{1,0:T(8,128)(2,1)S(1)}, bf16[256,1024]{1,0:T(8,128)(2,1)S(1)}, u32[]{:S(2)}, u32[]{:S(2)}) collective-permute-start(bf16[256,1024]{1,0:T(8,128)(2,1)S(1)} %collective-permute-done.6), channel_id=1, source_target_pairs={{4,8},{8,4},{5,9},{9,5},{6,10},{10,6},{7,11},{11,7},{20,24},{24,20... | collective-permute-start | bytes 1572872 | tf_op jit(solution)/shard_map/ppermute | solution.py:46
  55.7 15.3 %collective-permute-start.15 = (bf16[256,1024]{1,0:T(8,128)(2,1)S(1)}, bf16[256,1024]{1,0:T(8,128)(2,1)S(1)}, u32[]{:S(2)}, u32[]{:S(2)}) collective-permute-start(bf16[256,1024]{1,0:T(8,128)(2,1)S(1)} %fusion.28), channel_id=1, source_target_pairs={{0,3},{1,2},{2,1},{3,0},{4,7},{5,6},{6,5},{7,4},{8,11},{9,10},{10,... | collective-permute-start | bytes 1572872 | tf_op jit(solution)/shard_map/ppermute | solution.py:42
  60.9 14.4 %collective-permute-start.21 = (bf16[256,1024]{1,0:T(8,128)(2,1)S(1)}, bf16[256,1024]{1,0:T(8,128)(2,1)S(1)}, u32[]{:S(2)}, u32[]{:S(2)}) collective-permute-start(bf16[256,1024]{1,0:T(8,128)(2,1)S(1)} %collective-permute-done.17), channel_id=1, source_target_pairs={{4,0},{8,12},{5,1},{9,13},{6,2},{10,14},{7,3},{11,15},{20,16},{24,... | collective-permute-start | bytes 1572872 | tf_op jit(solution)/shard_map/ppermute | solution.py:46
  64.2 16.6 %collective-permute-start.11 = (bf16[512,512]{1,0:T(8,128)(2,1)S(1)}, bf16[512,512]{1,0:T(8,128)(2,1)S(1)}, u32[]{:S(2)}, u32[]{:S(2)}) collective-permute-start(bf16[512,512]{1,0:T(8,128)(2,1)S(1)} %get-tuple-element.59), channel_id=1, source_target_pairs={{0,1},{1,0},{2,3},{3,2},{4,5},{5,4},{6,7},{7,6},{8,9},{9,8},{10,11... | collective-permute-start | bytes 1572872 | tf_op jit(solution)/shard_map/ppermute | solution.py:38
  65.2 15.6 %collective-permute-start.27 = (bf16[32,1024]{1,0:T(8,128)(2,1)S(1)}, bf16[32,1024]{1,0:T(8,128)(2,1)S(1)}, u32[]{:S(2)}, u32[]{:S(2)}) collective-permute-start(bf16[32,1024]{1,0:T(8,128)(2,1)S(1)} %dynamic-slice_add_fusion.2), channel_id=1, source_target_pairs={{0,128},{128,0},{1,129},{129,1},{2,130},{130,2},{3,131},{131,3},{4... | collective-permute-start | bytes 196616 | tf_op jit(solution)/shard_map/ppermute | solution.py:110
  70.3 10.9 %collective-permute-start.19 = (bf16[256,1024]{1,0:T(8,128)(2,1)S(1)}, bf16[256,1024]{1,0:T(8,128)(2,1)S(1)}, u32[]{:S(2)}, u32[]{:S(2)}) collective-permute-start(bf16[256,1024]{1,0:T(8,128)(2,1)S(1)} %collective-permute-done.14), channel_id=1, source_target_pairs={{4,8},{8,4},{5,9},{9,5},{6,10},{10,6},{7,11},{11,7},{20,24},{24,20... | collective-permute-start | bytes 1572872 | tf_op jit(solution)/shard_map/ppermute | solution.py:46
  75.3 13.2 %collective-permute-start.22 = (bf16[256,1024]{1,0:T(8,128)(2,1)S(1)}, bf16[256,1024]{1,0:T(8,128)(2,1)S(1)}, u32[]{:S(2)}, u32[]{:S(2)}) collective-permute-start(bf16[256,1024]{1,0:T(8,128)(2,1)S(1)} %get-tuple-element.70), channel_id=1, source_target_pairs={{0,4},{4,0},{8,12},{12,8},{1,5},{5,1},{9,13},{13,9},{2,6},{6,2},{1... | collective-permute-start | bytes 1572872 | tf_op jit(solution)/shard_map/ppermute | solution.py:46
  78.7 10.0 %collective-permute-start.16 = (bf16[256,1024]{1,0:T(8,128)(2,1)S(1)}, bf16[256,1024]{1,0:T(8,128)(2,1)S(1)}, u32[]{:S(2)}, u32[]{:S(2)}) collective-permute-start(bf16[256,1024]{1,0:T(8,128)(2,1)S(1)} %fusion.29), channel_id=1, source_target_pairs={{0,3},{1,2},{2,1},{3,0},{4,7},{5,6},{6,5},{7,4},{8,11},{9,10},{10,... | collective-permute-start | bytes 1572872 | tf_op jit(solution)/shard_map/ppermute | solution.py:42
  80.8 20.9 %collective-permute-start.12 = (bf16[512,512]{1,0:T(8,128)(2,1)S(1)}, bf16[512,512]{1,0:T(8,128)(2,1)S(1)}, u32[]{:S(2)}, u32[]{:S(2)}) collective-permute-start(bf16[512,512]{1,0:T(8,128)(2,1)S(1)} %get-tuple-element.60), channel_id=1, source_target_pairs={{0,1},{1,0},{2,3},{3,2},{4,5},{5,4},{6,7},{7,6},{8,9},{9,8},{10,11... | collective-permute-start | bytes 1572872 | tf_op jit(solution)/shard_map/ppermute | solution.py:38
  81.2 14.0 %collective-permute-start.28 = (f32[32,1024]{1,0:T(8,128)S(1)}, f32[32,1024]{1,0:T(8,128)S(1)}, u32[]{:S(2)}, u32[]{:S(2)}) collective-permute-start(f32[32,1024]{1,0:T(8,128)S(1)} %convert_add_fusion), channel_id=1, source_target_pairs={{0,64},{32,96},{64,0},{96,32},{1,65},{33,97},{65,1},{97,33},{2,66}... | collective-permute-start | bytes 393224 | tf_op jit(solution)/shard_map/ppermute | solution.py:110
  89.3 12.4 %collective-permute-start.23 = (bf16[256,1024]{1,0:T(8,128)(2,1)S(1)}, bf16[256,1024]{1,0:T(8,128)(2,1)S(1)}, u32[]{:S(2)}, u32[]{:S(2)}) collective-permute-start(bf16[256,1024]{1,0:T(8,128)(2,1)S(1)} %get-tuple-element.71), channel_id=1, source_target_pairs={{0,4},{4,0},{8,12},{12,8},{1,5},{5,1},{9,13},{13,9},{2,6},{6,2},{1... | collective-permute-start | bytes 1572872 | tf_op jit(solution)/shard_map/ppermute | solution.py:46
  90.7 11.0 %collective-permute-start.24 = (bf16[256,1024]{1,0:T(8,128)(2,1)S(1)}, bf16[256,1024]{1,0:T(8,128)(2,1)S(1)}, u32[]{:S(2)}, u32[]{:S(2)}) collective-permute-start(bf16[256,1024]{1,0:T(8,128)(2,1)S(1)} %add_convert_fusion.3), channel_id=1, source_target_pairs={{4,8},{8,4},{5,9},{9,5},{6,10},{10,6},{7,11},{11,7},{20,24},{24,20... | collective-permute-start | bytes 1572872 | tf_op jit(solution)/shard_map/ppermute | solution.py:46
  103.8 16.9 %collective-permute-start.30 = (bf16[512,1024]{1,0:T(8,128)(2,1)S(1)}, bf16[512,1024]{1,0:T(8,128)(2,1)S(1)}, u32[]{:S(2)}, u32[]{:S(2)}) collective-permute-start(bf16[512,1024]{1,0:T(8,128)(2,1)S(1)} %get-tuple-element.103), channel_id=1, source_target_pairs={{0,16},{16,0},{1,17},{17,1},{2,18},{18,2},{3,19},{19,3},{4,20},{20... | collective-permute-start | bytes 3145736 | tf_op jit(solution)/shard_map/ppermute | solution.py:34
  112.5 14.8 %collective-permute-start.32 = (bf16[256,1024]{1,0:T(8,128)(2,1)S(1)}, bf16[256,1024]{1,0:T(8,128)(2,1)S(1)}, u32[]{:S(2)}, u32[]{:S(2)}) collective-permute-start(bf16[256,1024]{1,0:T(8,128)(2,1)S(1)} %fusion.21), channel_id=1, source_target_pairs={{0,3},{1,2},{2,1},{3,0},{4,7},{5,6},{6,5},{7,4},{8,11},{9,10},{10,... | collective-permute-start | bytes 1572872 | tf_op jit(solution)/shard_map/ppermute | solution.py:42
  114.2 13.1 %collective-permute-start.34 = (bf16[256,1024]{1,0:T(8,128)(2,1)S(1)}, bf16[256,1024]{1,0:T(8,128)(2,1)S(1)}, u32[]{:S(2)}, u32[]{:S(2)}) collective-permute-start(bf16[256,1024]{1,0:T(8,128)(2,1)S(1)} %add_convert_fusion.1), channel_id=1, source_target_pairs={{4,8},{8,4},{5,9},{9,5},{6,10},{10,6},{7,11},{11,7},{20,24},{24,20... | collective-permute-start | bytes 1572872 | tf_op jit(solution)/shard_map/ppermute | solution.py:46
  115.0 16.6 %collective-permute-start.33 = (bf16[256,1024]{1,0:T(8,128)(2,1)S(1)}, bf16[256,1024]{1,0:T(8,128)(2,1)S(1)}, u32[]{:S(2)}, u32[]{:S(2)}) collective-permute-start(bf16[256,1024]{1,0:T(8,128)(2,1)S(1)} %add_convert_fusion.2), channel_id=1, source_target_pairs={{0,4},{4,0},{8,12},{12,8},{1,5},{5,1},{9,13},{13,9},{2,6},{6,2},{1... | collective-permute-start | bytes 1572872 | tf_op jit(solution)/shard_map/ppermute | solution.py:46
  119.9 14.5 %collective-permute-start.36 = (f32[128,1024]{1,0:T(8,128)S(1)}, f32[128,1024]{1,0:T(8,128)S(1)}, u32[]{:S(2)}, u32[]{:S(2)}) collective-permute-start(f32[128,1024]{1,0:T(8,128)S(1)} %maximum_select_fusion.2), channel_id=1, source_target_pairs={{0,16},{16,0},{1,17},{17,1},{2,18},{18,2},{3,19},{19,3},{4,20},{20... | collective-permute-start | bytes 1572872 | tf_op jit(solution)/shard_map/ppermute | solution.py:110
  121.9 24.2 %collective-permute-start.31 = (bf16[512,1024]{1,0:T(8,128)(2,1)S(1)}, bf16[512,1024]{1,0:T(8,128)(2,1)S(1)}, u32[]{:S(2)}, u32[]{:S(2)}) collective-permute-start(bf16[512,1024]{1,0:T(8,128)(2,1)S(1)} %add_convert_fusion), channel_id=1, source_target_pairs={{1,16},{2,19},{16,1},{19,2},{5,20},{6,23},{20,5},{23,6},{9,24},{10... | collective-permute-start | bytes 3145736 | tf_op jit(solution)/shard_map/ppermute | solution.py:30
  132.3 11.5 %collective-permute-start.35 = (bf16[256,1024]{1,0:T(8,128)(2,1)S(1)}, bf16[256,1024]{1,0:T(8,128)(2,1)S(1)}, u32[]{:S(2)}, u32[]{:S(2)}) collective-permute-start(bf16[256,1024]{1,0:T(8,128)(2,1)S(1)} %get-tuple-element.105), channel_id=1, source_target_pairs={{1,16},{2,19},{16,1},{19,2},{5,20},{6,23},{20,5},{23,6},{9,24},{10... | collective-permute-start | bytes 1572872 | tf_op jit(solution)/shard_map/ppermute | solution.py:30
  (17 other events, 137.1 us)

commit v12 on v11

--- a/solution.py
+++ b/solution.py
@@ -142,14 +142,15 @@
     ).reshape(2, 8)
 
     drift = Drift(anchor - local_params[0].astype(f32), c, y)
-    w, g_sib, d, blocks, drift.v = together(
-        swap(weight), core(key_grad), drift.send(), blocks.astype(jnp.int32), drift.v
+    g_sib = core(key_grad)
+    x_give, x_own = halves(tokens, after(blocks.astype(jnp.int32), g_sib))
+    w, g_sib, d, x_give, x_own, drift.v = together(
+        swap(weight), g_sib, drift.send(), x_give, x_own, drift.v
     )
     drift.take(d)
     w = jnp.where(stays, weight, w)
     g_a = jnp.where(stays, key_grad, g_sib)
     g_l = lax.dynamic_slice_in_dim(jnp.where(stays, g_sib, key_grad), c * 256, 256, 0)
-    x_give, x_own = halves(tokens, blocks)
     x_sib = core(x_give)
 
     got = (beside(g_l), line(w, PAIRS), line(w, MIDDLE), across(w), drift.send())

time: 148 us -> 145 us (0.980)
  waiting for transfers between devices: 50.5 us -> 47.1 us
    ppermute x3, waiting for transfers between devices: 13.4 us -> 7.96 us  [swap(): return lax.ppermute(v, ('c', 'x'), SWAP)]
    ppermute x5, waiting for transfers between devices: 11.3 us -> 14.1 us  [beside(): return lax.ppermute(v, 'x', BESIDE)]
  transfers between devices with their start and end apart: 37 -> 37, of which waited for: 13 -> 13; matrix products, arithmetic and copies ran while one was open for 15% -> 16% of each run, Pallas kernels for 0% -> 4%
where the time goes in v12:
time: 145 us
  starting transfers between devices  63.9 us (44%)
  waiting for transfers between devices  47.1 us (32%)
  matrix products  12.5 us (9%)
  other arithmetic  11.9 us (8%)
  Pallas kernels  5.43 us (4%)
  local copies, waits for them, and re-layouts  2.63 us (2%)
    ppermute x12, starting transfers between devices, line(): return lax.ppermute(v, 'zl', pairs)  20 us
    ppermute x7, starting transfers between devices, send(): return lax.ppermute(self.sent, axis, perm)  14.2 us
    ppermute x5, waiting for transfers between devices, beside(): return lax.ppermute(v, 'x', BESIDE)  14.1 us
    ppermute x4, starting transfers between devices, core(): return lax.ppermute(v, 'c', CORE)  12.8 us
    ppermute x12, waiting for transfers between devices, line(): return lax.ppermute(v, 'zl', pairs)  12.6 us
    ppermute x6, starting transfers between devices, across(): return lax.ppermute(v, 'x', ACROSS)  9.46 us
    ppermute x7, waiting for transfers between devices, send(): return lax.ppermute(self.sent, axis, perm)  8.87 us
    ppermute x3, waiting for transfers between devices, swap(): return lax.ppermute(v, ('c', 'x'), SWAP)  7.96 us
  transfers between devices with their start and end apart: 37, of which 13 were waited for; matrix products, arithmetic and copies ran while one was open for 16% of the time, Pallas kernels for 4%

profile of v12, /device:TPU:1, one launch (start us, length us, event | category | flops | bytes accessed | tf_op | source)
XLA Modules:
  0.0 144.5 jit_solution(7753236626647860327)
XLA Ops:
  0.6 3.3 %collective-permute-start.1 = (bf16[512,1024]{1,0:T(8,128)(2,1)}, bf16[512,1024]{1,0:T(8,128)(2,1)S(1)}, u32[]{:S(2)}, u32[]{:S(2)}) collective-permute-start(bf16[512,1024]{1,0:T(8,128)(2,1)} %param.9), channel_id=1, source_target_pairs={{0,16},{16,0},{1,17},{17,1},{2,18},{18,2},{3,19},{19,3},{4,20},{20... | collective-permute-start | bytes 3145736 | tf_op jit(solution)/shard_map/ppermute | solution.py:34
  4.0 1.9 %collective-permute-start = (bf16[256,1024]{1,0:T(8,128)(2,1)}, bf16[256,1024]{1,0:T(8,128)(2,1)S(1)}, u32[]{:S(2)}, u32[]{:S(2)}) collective-permute-start(bf16[256,1024]{1,0:T(8,128)(2,1)} %bitcast.68), channel_id=1, source_target_pairs={{1,16},{2,19},{16,1},{19,2},{5,20},{6,23},{20,5},{23,6},{9,24},{10... | collective-permute-start | bytes 1572872 | tf_op jit(solution)/shard_map/ppermute | solution.py:30
  5.9 1.5 %convert_subtract_fusion.1 = f32[256,1024]{1,0:T(8,128)S(1)} fusion(f32[256,1024]{1,0:T(8,128)} %param.14, bf16[1,256,1024]{2,1,0:T(8,128)(2,1)} %param.13), kind=kLoop, calls=%fused_computation.68 | loop fusion | flops 524288 | bytes 2621440 | tf_op jit(solution)/shard_map/sub | solution.py:144
  9.0 5.4 %shard_map.127 = (bf16[4,512,512]{2,1,0:T(8,128)(2,1)}, bf16[4,512,512]{2,1,0:T(8,128)(2,1)}) custom-call(s32[2,8]{1,0:T(2,128)} %reshape.37._, bf16[512,4096]{1,0:T(8,128)(2,1)} %b1.1, bf16[512,4096]{1,0:T(8,128)(2,1)} %b1.1, bf16[512,4096]{1,0:T(8,128)(2,1)} %b1.1, bf16[512,4096]{1,0:T(8,128)(2,1)} %b1.1), custom_call_target="tpu_custom_call" | custom-call | bytes 16777216 | tf_op jit(solution)/shard_map/pallas_call | solution.py:78
  15.9 1.4 broadcast_select_fusion.2
  19.3 4.6 %collective-permute-start.4 = (bf16[256,1024]{1,0:T(8,128)(2,1)S(1)}, bf16[256,1024]{1,0:T(8,128)(2,1)S(1)}, u32[]{:S(2)}, u32[]{:S(2)}) collective-permute-start(bf16[256,1024]{1,0:T(8,128)(2,1)S(1)} %broadcast_select_fusion.2), channel_id=1, source_target_pairs={{0,4},{4,0},{8,12},{12,8},{1,5},{5,1},{9,13},{13,9},{2,6},{6,2},{1... | collective-permute-start | bytes 1572872 | tf_op jit(solution)/shard_map/ppermute | solution.py:46
  23.9 1.4 dynamic-slice_select_fusion
  27.5 4.4 %collective-permute-done.7 = f32[64,1024]{1,0:T(8,128)S(1)} collective-permute-done((f32[64,1024]{1,0:T(8,128)S(1)}, f32[64,1024]{1,0:T(8,128)S(1)}, u32[]{:S(2)}, u32[]{:S(2)}) %collective-permute-start.7) | collective-permute-done | bytes 262176 | tf_op jit(solution)/shard_map/ppermute | solution.py:110
  31.8 6.3 %collective-permute-done.3 = bf16[256,1024]{1,0:T(8,128)(2,1)S(1)} collective-permute-done((bf16[256,1024]{1,0:T(8,128)(2,1)S(1)}, bf16[256,1024]{1,0:T(8,128)(2,1)S(1)}, u32[]{:S(2)}, u32[]{:S(2)}) %collective-permute-start.3) | collective-permute-done | bytes 524320 | tf_op jit(solution)/shard_map/ppermute | solution.py:38
  41.1 2.0 %collective-permute-start.13 = (bf16[256,1024]{1,0:T(8,128)(2,1)S(1)}, bf16[256,1024]{1,0:T(8,128)(2,1)S(1)}, u32[]{:S(2)}, u32[]{:S(2)}) collective-permute-start(bf16[256,1024]{1,0:T(8,128)(2,1)S(1)} %collective-permute-done.3), channel_id=1, source_target_pairs={{0,16},{16,0},{1,17},{17,1},{2,18},{18,2},{3,19},{19,3},{4,20},{20... | collective-permute-start | bytes 1572872 | tf_op jit(solution)/shard_map/ppermute | solution.py:34
  45.3 6.0 %collective-permute-done.9 = bf16[512,512]{1,0:T(8,128)(2,1)S(1)} collective-permute-done((bf16[512,512]{1,0:T(8,128)(2,1)S(1)}, bf16[512,512]{1,0:T(8,128)(2,1)S(1)}, u32[]{:S(2)}, u32[]{:S(2)}) %collective-permute-start.9) | collective-permute-done | bytes 524320 | tf_op jit(solution)/shard_map/ppermute | solution.py:38
  52.8 1.9 %collective-permute-start.15 = (bf16[256,1024]{1,0:T(8,128)(2,1)S(1)}, bf16[256,1024]{1,0:T(8,128)(2,1)S(1)}, u32[]{:S(2)}, u32[]{:S(2)}) collective-permute-start(bf16[256,1024]{1,0:T(8,128)(2,1)S(1)} %fusion.28), channel_id=1, source_target_pairs={{0,3},{1,2},{2,1},{3,0},{4,7},{5,6},{6,5},{7,4},{8,11},{9,10},{10,... | collective-permute-start | bytes 1572872 | tf_op jit(solution)/shard_map/ppermute | solution.py:42
  54.7 3.0 %collective-permute-start.26 = (f32[32,1024]{1,0:T(8,128)S(1)}, f32[32,1024]{1,0:T(8,128)S(1)}, u32[]{:S(2)}, u32[]{:S(2)}) collective-permute-start(f32[32,1024]{1,0:T(8,128)S(1)} %constant_dynamic-slice_fusion), channel_id=1, source_target_pairs={{0,64},{32,96},{64,0},{96,32},{1,65},{33,97},{65,1},{97,33},{2,66}... | collective-permute-start | bytes 393224 | tf_op jit(solution)/shard_map/ppermute | solution.py:110
  60.2 1.8 %collective-permute-done.10 = bf16[512,512]{1,0:T(8,128)(2,1)S(1)} collective-permute-done((bf16[512,512]{1,0:T(8,128)(2,1)S(1)}, bf16[512,512]{1,0:T(8,128)(2,1)S(1)}, u32[]{:S(2)}, u32[]{:S(2)}) %collective-permute-start.10) | collective-permute-done | bytes 524320 | tf_op jit(solution)/shard_map/ppermute | solution.py:38
  62.5 5.1 %collective-permute-start.27 = (bf16[32,1024]{1,0:T(8,128)(2,1)S(1)}, bf16[32,1024]{1,0:T(8,128)(2,1)S(1)}, u32[]{:S(2)}, u32[]{:S(2)}) collective-permute-start(bf16[32,1024]{1,0:T(8,128)(2,1)S(1)} %dynamic-slice_add_fusion.2), channel_id=1, source_target_pairs={{0,128},{128,0},{1,129},{129,1},{2,130},{130,2},{3,131},{131,3},{4... | collective-permute-start | bytes 196616 | tf_op jit(solution)/shard_map/ppermute | solution.py:110
  68.9 3.7 %collective-permute-done.21 = bf16[256,1024]{1,0:T(8,128)(2,1)S(1)} collective-permute-done((bf16[256,1024]{1,0:T(8,128)(2,1)S(1)}, bf16[256,1024]{1,0:T(8,128)(2,1)S(1)}, u32[]{:S(2)}, u32[]{:S(2)}) %collective-permute-start.21) | collective-permute-done | bytes 524320 | tf_op jit(solution)/shard_map/ppermute | solution.py:46
  72.6 3.0 %collective-permute-start.22 = (bf16[256,1024]{1,0:T(8,128)(2,1)S(1)}, bf16[256,1024]{1,0:T(8,128)(2,1)S(1)}, u32[]{:S(2)}, u32[]{:S(2)}) collective-permute-start(bf16[256,1024]{1,0:T(8,128)(2,1)S(1)} %get-tuple-element.74), channel_id=1, source_target_pairs={{0,4},{4,0},{8,12},{12,8},{1,5},{5,1},{9,13},{13,9},{2,6},{6,2},{1... | collective-permute-start | bytes 1572872 | tf_op jit(solution)/shard_map/ppermute | solution.py:46
  76.1 1.9 %collective-permute-start.16 = (bf16[256,1024]{1,0:T(8,128)(2,1)S(1)}, bf16[256,1024]{1,0:T(8,128)(2,1)S(1)}, u32[]{:S(2)}, u32[]{:S(2)}) collective-permute-start(bf16[256,1024]{1,0:T(8,128)(2,1)S(1)} %fusion.29), channel_id=1, source_target_pairs={{0,3},{1,2},{2,1},{3,0},{4,7},{5,6},{6,5},{7,4},{8,11},{9,10},{10,... | collective-permute-start | bytes 1572872 | tf_op jit(solution)/shard_map/ppermute | solution.py:42
  78.5 2.9 %collective-permute-start.28 = (f32[32,1024]{1,0:T(8,128)S(1)}, f32[32,1024]{1,0:T(8,128)S(1)}, u32[]{:S(2)}, u32[]{:S(2)}) collective-permute-start(f32[32,1024]{1,0:T(8,128)S(1)} %convert_add_fusion), channel_id=1, source_target_pairs={{0,64},{32,96},{64,0},{96,32},{1,65},{33,97},{65,1},{97,33},{2,66}... | collective-permute-start | bytes 393224 | tf_op jit(solution)/shard_map/ppermute | solution.py:110
  81.4 4.5 %collective-permute-done.22 = bf16[256,1024]{1,0:T(8,128)(2,1)S(1)} collective-permute-done((bf16[256,1024]{1,0:T(8,128)(2,1)S(1)}, bf16[256,1024]{1,0:T(8,128)(2,1)S(1)}, u32[]{:S(2)}, u32[]{:S(2)}) %collective-permute-start.22) | collective-permute-done | bytes 524320 | tf_op jit(solution)/shard_map/ppermute | solution.py:46
  88.9 1.9 %collective-permute-start.25 = (bf16[256,1024]{1,0:T(8,128)(2,1)S(1)}, bf16[256,1024]{1,0:T(8,128)(2,1)S(1)}, u32[]{:S(2)}, u32[]{:S(2)}) collective-permute-start(bf16[256,1024]{1,0:T(8,128)(2,1)S(1)} %fusion.26), channel_id=1, source_target_pairs={{0,3},{1,2},{2,1},{3,0},{4,7},{5,6},{6,5},{7,4},{8,11},{9,10},{10,... | collective-permute-start | bytes 1572872 | tf_op jit(solution)/shard_map/ppermute | solution.py:42
  95.1 3.4 %collective-permute-done.29 = f32[64,1024]{1,0:T(8,128)S(1)} collective-permute-done((f32[64,1024]{1,0:T(8,128)S(1)}, f32[64,1024]{1,0:T(8,128)S(1)}, u32[]{:S(2)}, u32[]{:S(2)}) %collective-permute-start.29) | collective-permute-done | bytes 262176 | tf_op jit(solution)/shard_map/ppermute | solution.py:110
  101.3 7.2 %collective-permute-start.30 = (bf16[512,1024]{1,0:T(8,128)(2,1)S(1)}, bf16[512,1024]{1,0:T(8,128)(2,1)S(1)}, u32[]{:S(2)}, u32[]{:S(2)}) collective-permute-start(bf16[512,1024]{1,0:T(8,128)(2,1)S(1)} %get-tuple-element.107), channel_id=1, source_target_pairs={{0,16},{16,0},{1,17},{17,1},{2,18},{18,2},{3,19},{19,3},{4,20},{20... | collective-permute-start | bytes 3145736 | tf_op jit(solution)/shard_map/ppermute | solution.py:34
  109.7 1.5 %collective-permute-start.32 = (bf16[256,1024]{1,0:T(8,128)(2,1)S(1)}, bf16[256,1024]{1,0:T(8,128)(2,1)S(1)}, u32[]{:S(2)}, u32[]{:S(2)}) collective-permute-start(bf16[256,1024]{1,0:T(8,128)(2,1)S(1)} %fusion.21), channel_id=1, source_target_pairs={{0,3},{1,2},{2,1},{3,0},{4,7},{5,6},{6,5},{7,4},{8,11},{9,10},{10,... | collective-permute-start | bytes 1572872 | tf_op jit(solution)/shard_map/ppermute | solution.py:42
  112.3 4.9 %collective-permute-start.33 = (bf16[256,1024]{1,0:T(8,128)(2,1)S(1)}, bf16[256,1024]{1,0:T(8,128)(2,1)S(1)}, u32[]{:S(2)}, u32[]{:S(2)}) collective-permute-start(bf16[256,1024]{1,0:T(8,128)(2,1)S(1)} %add_convert_fusion.2), channel_id=1, source_target_pairs={{0,4},{4,0},{8,12},{12,8},{1,5},{5,1},{9,13},{13,9},{2,6},{6,2},{1... | collective-permute-start | bytes 1572872 | tf_op jit(solution)/shard_map/ppermute | solution.py:46
  119.2 2.1 %collective-permute-start.31 = (bf16[512,1024]{1,0:T(8,128)(2,1)S(1)}, bf16[512,1024]{1,0:T(8,128)(2,1)S(1)}, u32[]{:S(2)}, u32[]{:S(2)}) collective-permute-start(bf16[512,1024]{1,0:T(8,128)(2,1)S(1)} %add_convert_fusion), channel_id=1, source_target_pairs={{1,16},{2,19},{16,1},{19,2},{5,20},{6,23},{20,5},{23,6},{9,24},{10... | collective-permute-start | bytes 3145736 | tf_op jit(solution)/shard_map/ppermute | solution.py:30
  121.3 3.3 %collective-permute-done.32 = bf16[256,1024]{1,0:T(8,128)(2,1)S(1)} collective-permute-done((bf16[256,1024]{1,0:T(8,128)(2,1)S(1)}, bf16[256,1024]{1,0:T(8,128)(2,1)S(1)}, u32[]{:S(2)}, u32[]{:S(2)}) %collective-permute-start.32) | collective-permute-done | bytes 524320 | tf_op jit(solution)/shard_map/ppermute | solution.py:42
  124.6 4.3 %collective-permute-done.33 = bf16[256,1024]{1,0:T(8,128)(2,1)S(1)} collective-permute-done((bf16[256,1024]{1,0:T(8,128)(2,1)S(1)}, bf16[256,1024]{1,0:T(8,128)(2,1)S(1)}, u32[]{:S(2)}, u32[]{:S(2)}) %collective-permute-start.33) | collective-permute-done | bytes 524320 | tf_op jit(solution)/shard_map/ppermute | solution.py:46
  129.6 2.1 %collective-permute-start.35 = (bf16[256,1024]{1,0:T(8,128)(2,1)S(1)}, bf16[256,1024]{1,0:T(8,128)(2,1)S(1)}, u32[]{:S(2)}, u32[]{:S(2)}) collective-permute-start(bf16[256,1024]{1,0:T(8,128)(2,1)S(1)} %get-tuple-element.109), channel_id=1, source_target_pairs={{1,16},{2,19},{16,1},{19,2},{5,20},{6,23},{20,5},{23,6},{9,24},{10... | collective-permute-start | bytes 1572872 | tf_op jit(solution)/shard_map/ppermute | solution.py:30
  131.7 1.7 %multiply_subtract_fusion = (f32[256,1024]{1,0:T(8,128)}, f32[256,1024]{1,0:T(8,128)}) fusion(f32[256,1024]{1,0:T(8,128)S(1)} %copy-done.1, f32[128,1024]{1,0:T(8,128)S(1)} %maximum_select_fusion.2, f32[128,1024]{1,0:T(8,128)S(1)} %collective-permute-done.36, pred[]{:T(512)S(6)} %eq.41, f32[256,1024]{1,0:T(8,128)S(1)} %copy-done.6), kind=kLoop, calls=%fused_computation.70 | loop fusion | flops 2621440 | bytes 5242881 | tf_op jit(solution)/shard_map/sub | solution.py:235
  133.4 7.7 %collective-permute-done.35 = bf16[256,1024]{1,0:T(8,128)(2,1)S(1)} collective-permute-done((bf16[256,1024]{1,0:T(8,128)(2,1)S(1)}, bf16[256,1024]{1,0:T(8,128)(2,1)S(1)}, u32[]{:S(2)}, u32[]{:S(2)}) %collective-permute-start.35) | collective-permute-done | bytes 524320 | tf_op jit(solution)/shard_map/ppermute | solution.py:30
  141.1 2.3 %fusion.94 = (f32[1,256,1024]{2,1,0:T(8,128)}, bf16[1,256,1024]{2,1,0:T(8,128)(2,1)}, f32[1,256,1024]{2,1,0:T(8,128)}) fusion(f32[256,1024]{1,0:T(8,128)S(1)} %get-tuple-element.110, bf16[256,1024]{1,0:T(8,128)(2,1)S(1)} %collective-permute-done.35, pred[]{:T(512)S(6)} %eq.36, f32[1,256,1024]{2,1,0:T(8,128)S(1)} %copy-done.7, ...), kind=kLoop, calls=%fused_computation.132 | loop fusion | flops 4456448 | bytes 6815745 | tf_op jit(solution)/shard_map/broadcast_in_dim | solution.py:236
  (111 shorter events, 34.9 us)
Async XLA Ops:
  4.0 10.7 %collective-permute-start = (bf16[256,1024]{1,0:T(8,128)(2,1)}, bf16[256,1024]{1,0:T(8,128)(2,1)S(1)}, u32[]{:S(2)}, u32[]{:S(2)}) collective-permute-start(bf16[256,1024]{1,0:T(8,128)(2,1)} %bitcast.68), channel_id=1, source_target_pairs={{1,16},{2,19},{16,1},{19,2},{5,20},{6,23},{20,5},{23,6},{9,24},{10... | collective-permute-start | bytes 1572872 | tf_op jit(solution)/shard_map/ppermute | solution.py:30
  15.6 10.1 %collective-permute-start.8 = (bf16[4,512,512]{2,1,0:T(8,128)(2,1)}, bf16[4,512,512]{2,1,0:T(8,128)(2,1)S(1)}, u32[]{:S(2)}, u32[]{:S(2)}) collective-permute-start(bf16[4,512,512]{2,1,0:T(8,128)(2,1)} %get-tuple-element.56), channel_id=1, source_target_pairs={{0,16},{16,0},{1,17},{17,1},{2,18},{18,2},{3,19},{19,3},{4,20},{20... | collective-permute-start | bytes 6291464 | tf_op jit(solution)/shard_map/ppermute | solution.py:34
  17.3 20.8 %collective-permute-start.6 = (bf16[256,1024]{1,0:T(8,128)(2,1)S(1)}, bf16[256,1024]{1,0:T(8,128)(2,1)S(1)}, u32[]{:S(2)}, u32[]{:S(2)}) collective-permute-start(bf16[256,1024]{1,0:T(8,128)(2,1)S(1)} %broadcast_select_fusion.2), channel_id=1, source_target_pairs={{0,3},{1,2},{2,1},{3,0},{4,7},{5,6},{6,5},{7,4},{8,11},{9,10},{10,... | collective-permute-start | bytes 1572872 | tf_op jit(solution)/shard_map/ppermute | solution.py:42
  18.6 19.5 %collective-permute-start.5 = (bf16[256,1024]{1,0:T(8,128)(2,1)S(1)}, bf16[256,1024]{1,0:T(8,128)(2,1)S(1)}, u32[]{:S(2)}, u32[]{:S(2)}) collective-permute-start(bf16[256,1024]{1,0:T(8,128)(2,1)S(1)} %broadcast_select_fusion.2), channel_id=1, source_target_pairs={{4,8},{8,4},{5,9},{9,5},{6,10},{10,6},{7,11},{11,7},{20,24},{24,20... | collective-permute-start | bytes 1572872 | tf_op jit(solution)/shard_map/ppermute | solution.py:46
  19.3 18.8 %collective-permute-start.4 = (bf16[256,1024]{1,0:T(8,128)(2,1)S(1)}, bf16[256,1024]{1,0:T(8,128)(2,1)S(1)}, u32[]{:S(2)}, u32[]{:S(2)}) collective-permute-start(bf16[256,1024]{1,0:T(8,128)(2,1)S(1)} %broadcast_select_fusion.2), channel_id=1, source_target_pairs={{0,4},{4,0},{8,12},{12,8},{1,5},{5,1},{9,13},{13,9},{2,6},{6,2},{1... | collective-permute-start | bytes 1572872 | tf_op jit(solution)/shard_map/ppermute | solution.py:46
  25.3 12.8 %collective-permute-start.3 = (bf16[256,1024]{1,0:T(8,128)(2,1)S(1)}, bf16[256,1024]{1,0:T(8,128)(2,1)S(1)}, u32[]{:S(2)}, u32[]{:S(2)}) collective-permute-start(bf16[256,1024]{1,0:T(8,128)(2,1)S(1)} %dynamic-slice_select_fusion), channel_id=1, source_target_pairs={{0,1},{1,0},{2,3},{3,2},{4,5},{5,4},{6,7},{7,6},{8,9},{9,8},{10,11... | collective-permute-start | bytes 1572872 | tf_op jit(solution)/shard_map/ppermute | solution.py:38
  38.1 13.5 %collective-permute-start.17 = (bf16[256,1024]{1,0:T(8,128)(2,1)S(1)}, bf16[256,1024]{1,0:T(8,128)(2,1)S(1)}, u32[]{:S(2)}, u32[]{:S(2)}) collective-permute-start(bf16[256,1024]{1,0:T(8,128)(2,1)S(1)} %collective-permute-done.4), channel_id=1, source_target_pairs={{4,8},{8,4},{5,9},{9,5},{6,10},{10,6},{7,11},{11,7},{20,24},{24,20... | collective-permute-start | bytes 1572872 | tf_op jit(solution)/shard_map/ppermute | solution.py:46
  38.8 14.0 %collective-permute-start.14 = (bf16[256,1024]{1,0:T(8,128)(2,1)S(1)}, bf16[256,1024]{1,0:T(8,128)(2,1)S(1)}, u32[]{:S(2)}, u32[]{:S(2)}) collective-permute-start(bf16[256,1024]{1,0:T(8,128)(2,1)S(1)} %collective-permute-done.4), channel_id=1, source_target_pairs={{0,3},{1,2},{2,1},{3,0},{4,7},{5,6},{6,5},{7,4},{8,11},{9,10},{10,... | collective-permute-start | bytes 1572872 | tf_op jit(solution)/shard_map/ppermute | solution.py:42
  39.8 11.6 %collective-permute-start.9 = (bf16[512,512]{1,0:T(8,128)(2,1)S(1)}, bf16[512,512]{1,0:T(8,128)(2,1)S(1)}, u32[]{:S(2)}, u32[]{:S(2)}) collective-permute-start(bf16[512,512]{1,0:T(8,128)(2,1)S(1)} %get-tuple-element.61), channel_id=1, source_target_pairs={{0,1},{1,0},{2,3},{3,2},{4,5},{5,4},{6,7},{7,6},{8,9},{9,8},{10,11... | collective-permute-start | bytes 1572872 | tf_op jit(solution)/shard_map/ppermute | solution.py:38
  39.8 15.0 %collective-permute-start.20 = (bf16[256,1024]{1,0:T(8,128)(2,1)S(1)}, bf16[256,1024]{1,0:T(8,128)(2,1)S(1)}, u32[]{:S(2)}, u32[]{:S(2)}) collective-permute-start(bf16[256,1024]{1,0:T(8,128)(2,1)S(1)} %collective-permute-done.5), channel_id=1, source_target_pairs={{4,0},{8,12},{5,1},{9,13},{6,2},{10,14},{7,3},{11,15},{20,16},{24,... | collective-permute-start | bytes 1572872 | tf_op jit(solution)/shard_map/ppermute | solution.py:46
  41.1 11.2 %collective-permute-start.13 = (bf16[256,1024]{1,0:T(8,128)(2,1)S(1)}, bf16[256,1024]{1,0:T(8,128)(2,1)S(1)}, u32[]{:S(2)}, u32[]{:S(2)}) collective-permute-start(bf16[256,1024]{1,0:T(8,128)(2,1)S(1)} %collective-permute-done.3), channel_id=1, source_target_pairs={{0,16},{16,0},{1,17},{17,1},{2,18},{18,2},{3,19},{19,3},{4,20},{20... | collective-permute-start | bytes 1572872 | tf_op jit(solution)/shard_map/ppermute | solution.py:34
  51.3 10.6 %collective-permute-start.10 = (bf16[512,512]{1,0:T(8,128)(2,1)S(1)}, bf16[512,512]{1,0:T(8,128)(2,1)S(1)}, u32[]{:S(2)}, u32[]{:S(2)}) collective-permute-start(bf16[512,512]{1,0:T(8,128)(2,1)S(1)} %get-tuple-element.62), channel_id=1, source_target_pairs={{0,1},{1,0},{2,3},{3,2},{4,5},{5,4},{6,7},{7,6},{8,9},{9,8},{10,11... | collective-permute-start | bytes 1572872 | tf_op jit(solution)/shard_map/ppermute | solution.py:38
  51.6 10.9 %collective-permute-start.18 = (bf16[256,1024]{1,0:T(8,128)(2,1)S(1)}, bf16[256,1024]{1,0:T(8,128)(2,1)S(1)}, u32[]{:S(2)}, u32[]{:S(2)}) collective-permute-start(bf16[256,1024]{1,0:T(8,128)(2,1)S(1)} %collective-permute-done.6), channel_id=1, source_target_pairs={{4,8},{8,4},{5,9},{9,5},{6,10},{10,6},{7,11},{11,7},{20,24},{24,20... | collective-permute-start | bytes 1572872 | tf_op jit(solution)/shard_map/ppermute | solution.py:46
  52.8 15.5 %collective-permute-start.15 = (bf16[256,1024]{1,0:T(8,128)(2,1)S(1)}, bf16[256,1024]{1,0:T(8,128)(2,1)S(1)}, u32[]{:S(2)}, u32[]{:S(2)}) collective-permute-start(bf16[256,1024]{1,0:T(8,128)(2,1)S(1)} %fusion.28), channel_id=1, source_target_pairs={{0,3},{1,2},{2,1},{3,0},{4,7},{5,6},{6,5},{7,4},{8,11},{9,10},{10,... | collective-permute-start | bytes 1572872 | tf_op jit(solution)/shard_map/ppermute | solution.py:42
  57.7 14.9 %collective-permute-start.21 = (bf16[256,1024]{1,0:T(8,128)(2,1)S(1)}, bf16[256,1024]{1,0:T(8,128)(2,1)S(1)}, u32[]{:S(2)}, u32[]{:S(2)}) collective-permute-start(bf16[256,1024]{1,0:T(8,128)(2,1)S(1)} %collective-permute-done.17), channel_id=1, source_target_pairs={{4,0},{8,12},{5,1},{9,13},{6,2},{10,14},{7,3},{11,15},{20,16},{24,... | collective-permute-start | bytes 1572872 | tf_op jit(solution)/shard_map/ppermute | solution.py:46
  62.0 16.1 %collective-permute-start.11 = (bf16[512,512]{1,0:T(8,128)(2,1)S(1)}, bf16[512,512]{1,0:T(8,128)(2,1)S(1)}, u32[]{:S(2)}, u32[]{:S(2)}) collective-permute-start(bf16[512,512]{1,0:T(8,128)(2,1)S(1)} %get-tuple-element.63), channel_id=1, source_target_pairs={{0,1},{1,0},{2,3},{3,2},{4,5},{5,4},{6,7},{7,6},{8,9},{9,8},{10,11... | collective-permute-start | bytes 1572872 | tf_op jit(solution)/shard_map/ppermute | solution.py:38
  62.5 15.5 %collective-permute-start.27 = (bf16[32,1024]{1,0:T(8,128)(2,1)S(1)}, bf16[32,1024]{1,0:T(8,128)(2,1)S(1)}, u32[]{:S(2)}, u32[]{:S(2)}) collective-permute-start(bf16[32,1024]{1,0:T(8,128)(2,1)S(1)} %dynamic-slice_add_fusion.2), channel_id=1, source_target_pairs={{0,128},{128,0},{1,129},{129,1},{2,130},{130,2},{3,131},{131,3},{4... | collective-permute-start | bytes 196616 | tf_op jit(solution)/shard_map/ppermute | solution.py:110
  67.6 10.8 %collective-permute-start.19 = (bf16[256,1024]{1,0:T(8,128)(2,1)S(1)}, bf16[256,1024]{1,0:T(8,128)(2,1)S(1)}, u32[]{:S(2)}, u32[]{:S(2)}) collective-permute-start(bf16[256,1024]{1,0:T(8,128)(2,1)S(1)} %collective-permute-done.14), channel_id=1, source_target_pairs={{4,8},{8,4},{5,9},{9,5},{6,10},{10,6},{7,11},{11,7},{20,24},{24,20... | collective-permute-start | bytes 1572872 | tf_op jit(solution)/shard_map/ppermute | solution.py:46
  72.6 13.3 %collective-permute-start.22 = (bf16[256,1024]{1,0:T(8,128)(2,1)S(1)}, bf16[256,1024]{1,0:T(8,128)(2,1)S(1)}, u32[]{:S(2)}, u32[]{:S(2)}) collective-permute-start(bf16[256,1024]{1,0:T(8,128)(2,1)S(1)} %get-tuple-element.74), channel_id=1, source_target_pairs={{0,4},{4,0},{8,12},{12,8},{1,5},{5,1},{9,13},{13,9},{2,6},{6,2},{1... | collective-permute-start | bytes 1572872 | tf_op jit(solution)/shard_map/ppermute | solution.py:46
  76.1 10.2 %collective-permute-start.16 = (bf16[256,1024]{1,0:T(8,128)(2,1)S(1)}, bf16[256,1024]{1,0:T(8,128)(2,1)S(1)}, u32[]{:S(2)}, u32[]{:S(2)}) collective-permute-start(bf16[256,1024]{1,0:T(8,128)(2,1)S(1)} %fusion.29), channel_id=1, source_target_pairs={{0,3},{1,2},{2,1},{3,0},{4,7},{5,6},{6,5},{7,4},{8,11},{9,10},{10,... | collective-permute-start | bytes 1572872 | tf_op jit(solution)/shard_map/ppermute | solution.py:42
  78.1 21.0 %collective-permute-start.12 = (bf16[512,512]{1,0:T(8,128)(2,1)S(1)}, bf16[512,512]{1,0:T(8,128)(2,1)S(1)}, u32[]{:S(2)}, u32[]{:S(2)}) collective-permute-start(bf16[512,512]{1,0:T(8,128)(2,1)S(1)} %get-tuple-element.64), channel_id=1, source_target_pairs={{0,1},{1,0},{2,3},{3,2},{4,5},{5,4},{6,7},{7,6},{8,9},{9,8},{10,11... | collective-permute-start | bytes 1572872 | tf_op jit(solution)/shard_map/ppermute | solution.py:38
  78.5 14.4 %collective-permute-start.28 = (f32[32,1024]{1,0:T(8,128)S(1)}, f32[32,1024]{1,0:T(8,128)S(1)}, u32[]{:S(2)}, u32[]{:S(2)}) collective-permute-start(f32[32,1024]{1,0:T(8,128)S(1)} %convert_add_fusion), channel_id=1, source_target_pairs={{0,64},{32,96},{64,0},{96,32},{1,65},{33,97},{65,1},{97,33},{2,66}... | collective-permute-start | bytes 393224 | tf_op jit(solution)/shard_map/ppermute | solution.py:110
  86.8 12.3 %collective-permute-start.23 = (bf16[256,1024]{1,0:T(8,128)(2,1)S(1)}, bf16[256,1024]{1,0:T(8,128)(2,1)S(1)}, u32[]{:S(2)}, u32[]{:S(2)}) collective-permute-start(bf16[256,1024]{1,0:T(8,128)(2,1)S(1)} %get-tuple-element.75), channel_id=1, source_target_pairs={{0,4},{4,0},{8,12},{12,8},{1,5},{5,1},{9,13},{13,9},{2,6},{6,2},{1... | collective-permute-start | bytes 1572872 | tf_op jit(solution)/shard_map/ppermute | solution.py:46
  87.7 11.4 %collective-permute-start.24 = (bf16[256,1024]{1,0:T(8,128)(2,1)S(1)}, bf16[256,1024]{1,0:T(8,128)(2,1)S(1)}, u32[]{:S(2)}, u32[]{:S(2)}) collective-permute-start(bf16[256,1024]{1,0:T(8,128)(2,1)S(1)} %add_convert_fusion.3), channel_id=1, source_target_pairs={{4,8},{8,4},{5,9},{9,5},{6,10},{10,6},{7,11},{11,7},{20,24},{24,20... | collective-permute-start | bytes 1572872 | tf_op jit(solution)/shard_map/ppermute | solution.py:46
  88.9 9.7 %collective-permute-start.25 = (bf16[256,1024]{1,0:T(8,128)(2,1)S(1)}, bf16[256,1024]{1,0:T(8,128)(2,1)S(1)}, u32[]{:S(2)}, u32[]{:S(2)}) collective-permute-start(bf16[256,1024]{1,0:T(8,128)(2,1)S(1)} %fusion.26), channel_id=1, source_target_pairs={{0,3},{1,2},{2,1},{3,0},{4,7},{5,6},{6,5},{7,4},{8,11},{9,10},{10,... | collective-permute-start | bytes 1572872 | tf_op jit(solution)/shard_map/ppermute | solution.py:42
  101.3 16.7 %collective-permute-start.30 = (bf16[512,1024]{1,0:T(8,128)(2,1)S(1)}, bf16[512,1024]{1,0:T(8,128)(2,1)S(1)}, u32[]{:S(2)}, u32[]{:S(2)}) collective-permute-start(bf16[512,1024]{1,0:T(8,128)(2,1)S(1)} %get-tuple-element.107), channel_id=1, source_target_pairs={{0,16},{16,0},{1,17},{17,1},{2,18},{18,2},{3,19},{19,3},{4,20},{20... | collective-permute-start | bytes 3145736 | tf_op jit(solution)/shard_map/ppermute | solution.py:34
  109.7 14.8 %collective-permute-start.32 = (bf16[256,1024]{1,0:T(8,128)(2,1)S(1)}, bf16[256,1024]{1,0:T(8,128)(2,1)S(1)}, u32[]{:S(2)}, u32[]{:S(2)}) collective-permute-start(bf16[256,1024]{1,0:T(8,128)(2,1)S(1)} %fusion.21), channel_id=1, source_target_pairs={{0,3},{1,2},{2,1},{3,0},{4,7},{5,6},{6,5},{7,4},{8,11},{9,10},{10,... | collective-permute-start | bytes 1572872 | tf_op jit(solution)/shard_map/ppermute | solution.py:42
  111.4 13.2 %collective-permute-start.34 = (bf16[256,1024]{1,0:T(8,128)(2,1)S(1)}, bf16[256,1024]{1,0:T(8,128)(2,1)S(1)}, u32[]{:S(2)}, u32[]{:S(2)}) collective-permute-start(bf16[256,1024]{1,0:T(8,128)(2,1)S(1)} %add_convert_fusion.1), channel_id=1, source_target_pairs={{4,8},{8,4},{5,9},{9,5},{6,10},{10,6},{7,11},{11,7},{20,24},{24,20... | collective-permute-start | bytes 1572872 | tf_op jit(solution)/shard_map/ppermute | solution.py:46
  112.3 16.6 %collective-permute-start.33 = (bf16[256,1024]{1,0:T(8,128)(2,1)S(1)}, bf16[256,1024]{1,0:T(8,128)(2,1)S(1)}, u32[]{:S(2)}, u32[]{:S(2)}) collective-permute-start(bf16[256,1024]{1,0:T(8,128)(2,1)S(1)} %add_convert_fusion.2), channel_id=1, source_target_pairs={{0,4},{4,0},{8,12},{12,8},{1,5},{5,1},{9,13},{13,9},{2,6},{6,2},{1... | collective-permute-start | bytes 1572872 | tf_op jit(solution)/shard_map/ppermute | solution.py:46
  117.2 14.5 %collective-permute-start.36 = (f32[128,1024]{1,0:T(8,128)S(1)}, f32[128,1024]{1,0:T(8,128)S(1)}, u32[]{:S(2)}, u32[]{:S(2)}) collective-permute-start(f32[128,1024]{1,0:T(8,128)S(1)} %maximum_select_fusion.2), channel_id=1, source_target_pairs={{0,16},{16,0},{1,17},{17,1},{2,18},{18,2},{3,19},{19,3},{4,20},{20... | collective-permute-start | bytes 1572872 | tf_op jit(solution)/shard_map/ppermute | solution.py:110
  119.2 24.2 %collective-permute-start.31 = (bf16[512,1024]{1,0:T(8,128)(2,1)S(1)}, bf16[512,1024]{1,0:T(8,128)(2,1)S(1)}, u32[]{:S(2)}, u32[]{:S(2)}) collective-permute-start(bf16[512,1024]{1,0:T(8,128)(2,1)S(1)} %add_convert_fusion), channel_id=1, source_target_pairs={{1,16},{2,19},{16,1},{19,2},{5,20},{6,23},{20,5},{23,6},{9,24},{10... | collective-permute-start | bytes 3145736 | tf_op jit(solution)/shard_map/ppermute | solution.py:30
  129.6 11.5 %collective-permute-start.35 = (bf16[256,1024]{1,0:T(8,128)(2,1)S(1)}, bf16[256,1024]{1,0:T(8,128)(2,1)S(1)}, u32[]{:S(2)}, u32[]{:S(2)}) collective-permute-start(bf16[256,1024]{1,0:T(8,128)(2,1)S(1)} %get-tuple-element.109), channel_id=1, source_target_pairs={{1,16},{2,19},{16,1},{19,2},{5,20},{6,23},{20,5},{23,6},{9,24},{10... | collective-permute-start | bytes 1572872 | tf_op jit(solution)/shard_map/ppermute | solution.py:30
  (17 other events, 128.0 us)
